TPU v7x, 512 devices: a whole 4x4x16 slice. The times are simulated.
512 devices in a mesh: dp: 32 (over x, z_hi, core), mp: 4 (over y), root: 4 (over z_lo).
Axes of the slice: x: 4, y: 4, z: 16 (z_hi: 4, z_lo: 4; z = z_hi * 4 + z_lo), core: 2. Of those that a mesh axis runs over, the one named last changes fastest.
Arguments:
- acts: bfloat16 [32768, 2048], P('dp', 'mp'), may hold values from -6 to 6
- grads_out: bfloat16 [32768, 4096], P('dp', 'root'), may hold values from -6 to 6
- prec_left: bfloat16 [4, 8, 512, 512], P('mp', 'root', 'dp')
- prec_right: bfloat16 [4, 8, 512, 512], P('mp', 'root', 'dp')
- stats_old: float32 [32, 512, 512], P('dp', 'mp')
- listed: int32 [16], replicated, may hold values from 0 to 31, as said below
- owner: int32 [16], replicated, may hold values from 0 to 3
Outputs:
- update: bfloat16 [4, 512, 4096], P('mp', 'dp', 'root')
- new_stats: float32 [4, 32, 512, 512], P('root', 'dp', 'mp')
- new_roots: float32 [4, 32, 512, 512], P('root', 'dp', 'mp')
Inputs may be any that keep to these rules, and one draw needn't show every extreme that they name: `listed`: 16 distinct block numbers; block 0 and block 31 are always among them.
All inputs are finite; a program needn't handle non-finite values.
Results may differ from a plain program's by a relative error of at most 0.0057.
Values may be sent and summed in bfloat16 or wider, within the bound.
No kernel may reach another device: no remote copies, remote signals or barrier semaphores. Data moves between devices by JAX's collectives and lax.ppermute only.
A program may use at most 64 MiB of HBM per device.

v0:
```python
import jax
import jax.numpy as jnp
from jax import lax
from jax.sharding import PartitionSpec as P

B = 512
ITERS = 2


decay_rate = 0.6


def spread(value, axis, source):
    kept = jnp.where(lax.axis_index(axis) == source, value, 0).astype(value.dtype)
    return lax.psum(kept, axis)


def matmul_high(left, right):
    return jnp.dot(left, right, precision=lax.Precision.HIGHEST, preferred_element_type=jnp.float32)


def local(acts, grads_out, prec_left, prec_right, stats_old, listed, owner):
    dp_count = lax.axis_size("dp")
    mp_count = lax.axis_size("mp")
    root_count = lax.axis_size("root")
    dp_index = lax.axis_index("dp")
    mp_index = lax.axis_index("mp")
    root_index = lax.axis_index("root")
    block_rows = B // dp_count
    scale = (acts.shape[0] * dp_count) ** (-0.5)
    summed = lax.psum_scatter(
        lax.dot_general(
            acts, grads_out, (((0,), (0,)), ((), ())), preferred_element_type=jnp.float32
        ),
        "dp",
        scatter_dimension=0,
        tiled=True,
    )
    grad_part = (summed * scale).astype(jnp.bfloat16)
    grad_full = lax.all_gather(grad_part, "dp", axis=0, tiled=True)
    grad_three = grad_full.reshape(B, 2, B)
    left_part = jnp.einsum(
        "crk,kcx->crx", prec_left[0], grad_three, preferred_element_type=jnp.float32
    ).astype(jnp.bfloat16)
    right_total = jnp.einsum(
        "crk,ckx->crx",
        left_part,
        lax.all_gather(prec_right, "dp", axis=2, tiled=True)[0],
        preferred_element_type=jnp.float32,
    )
    update = right_total.astype(jnp.bfloat16).transpose(1, 0, 2).reshape(1, block_rows, 2 * B)
    slot_count = stats_old.shape[0]
    quarter = B // mp_count
    col_blocks = 2 * root_count
    identity = jnp.eye(B, dtype=jnp.float32)

    def refresh_preconditioners(slot_pos, outputs):
        stats_store, roots_store = outputs
        global_slot = dp_index * slot_count + slot_pos
        block_id = listed[global_slot // 2]
        block_row = block_id // col_blocks
        block_col = block_id % col_blocks
        holder = block_row * root_count + block_col // 2
        payload = lax.dynamic_slice_in_dim(grad_full, block_col % 2 * B, B, 1)
        chosen = spread(payload, ("mp", "root"), holder)
        side = jnp.where(global_slot % 2 == 0, chosen, chosen.T)
        own_rows = lax.dynamic_slice_in_dim(side, mp_index * quarter, quarter, 0)
        product = lax.dot_general(
            own_rows, side, (((1,), (1,)), ((), ())), preferred_element_type=jnp.float32
        )
        old_rows = lax.dynamic_index_in_dim(stats_old, slot_pos, 0, keepdims=False)
        stats_rows = decay_rate * old_rows + (1.0 - decay_rate) / B * product
        full_stats = lax.all_gather(
            stats_rows.astype(jnp.bfloat16), "mp", axis=0, tiled=True
        ).astype(stats_rows.dtype)
        norm_value = jnp.sqrt(jnp.sum(full_stats * full_stats))
        factor = 2.5 / norm_value
        iterate = jnp.sqrt(jnp.sqrt(factor)) * identity
        coupled = factor * full_stats
        for step in range(ITERS):
            factor_matrix = (5.0 * identity - coupled) * 0.25
            iterate = matmul_high(iterate, factor_matrix)
            for power in range(4):
                coupled = matmul_high(coupled, factor_matrix)
        root_rows = lax.dynamic_slice_in_dim(iterate, mp_index * quarter, quarter, 0)
        owned = owner[global_slot // 2] == root_index
        zero_rows = jnp.zeros((quarter, B), jnp.float32)
        stats_store = lax.dynamic_update_index_in_dim(
            stats_store, jnp.where(owned, stats_rows, zero_rows), slot_pos, 0
        )
        roots_store = lax.dynamic_update_index_in_dim(
            roots_store, jnp.where(owned, root_rows, zero_rows), slot_pos, 0
        )
        return (stats_store, roots_store)

    blank = jnp.zeros((slot_count, quarter, B), jnp.float32)
    stats_new, roots_new = lax.fori_loop(0, slot_count, refresh_preconditioners, (blank, blank))
    return (update, stats_new[None], roots_new[None])


def solution(mesh):
    in_specs = (
        P("dp", "mp"),
        P("dp", "root"),
        P("mp", "root", "dp", None),
        P("mp", "root", "dp", None),
        P("dp", "mp", None),
        P(),
        P(),
    )
    out_specs = (P("mp", "dp", "root"), P("root", "dp", "mp", None), P("root", "dp", "mp", None))
    return jax.shard_map(local, mesh=mesh, in_specs=in_specs, out_specs=out_specs, check_vma=False)
```

profile of v0, /device:TPU:6, one launch (start us, length us, event | category | flops | bytes accessed | tf_op | source)
XLA Modules:
  0.0 484.0 jit_solution(10124901325183584620)
XLA Ops:
  7.2 0.0 copy-start
  7.2 0.0 reduce-scatter.2.cloned.1.call-start
  7.2 1.5 copy-done
  8.8 3.8 fusion.59
  12.6 0.0 copy-start.4
  12.6 0.0 copy-start.5
  12.6 0.0 reduce-scatter.2.cloned.1.call-update
  12.6 0.0 copy-start.3
  12.6 0.0 all-gather.3.cloned.1.call-start
  12.7 125.0 %reduce-scatter.2.cloned.1.call-done = f32[16,1024]{1,0:T(8,128)} async-done(((f32[512,1024]{1,0:T(8,128)}), f32[16,1024]{1,0:T(8,128)}) %reduce-scatter.2.cloned.1.call-update) | async-done | bytes 65552 | tf_op jit(solution)/shard_map/reduce_scatter | solution.py:31
  137.7 1.5 multiply_convert_fusion
  139.2 0.0 all-gather.3.cloned.1.call-update
  139.2 0.0 all-gather.5.cloned.1.call-start
  139.3 0.7 all-gather.5.cloned.1.call-update
  140.0 0.0 all-reduce.2.cloned.1.call-start
  140.0 0.0 copy-done.4
  140.0 0.6 dynamic_slice.24
  143.3 63.8 %all-gather.3.cloned.1.call-done = bf16[512,1024]{1,0:T(8,128)(2,1)} async-done(((bf16[16,1024]{1,0:T(8,128)(2,1)}), bf16[512,1024]{1,0:T(8,128)(2,1)}) %all-gather.3.cloned.1.call-update) | async-done | bytes 1048592 | tf_op jit(solution)/shard_map/all_gather | solution.py:40
  207.1 1.9 dynamic-slice_select_fusion
  209.0 0.0 all-reduce.2.cloned.1.call-update
  209.1 0.0 copy-done.5
  209.1 0.6 dynamic_slice.23
  210.3 1.5 copy.14
  211.8 64.0 %all-gather.5.cloned.1.call-done = bf16[1,2,512,512]{3,2,1,0:T(8,128)(2,1)} async-done(((bf16[1,2,16,512]{3,2,1,0:T(8,128)(2,1)}), bf16[1,2,512,512]{3,2,1,0:T(8,128)(2,1)}) %all-gather.5.cloned.1.call-update) | async-done | bytes 1048592 | tf_op jit(solution)/shard_map/all_gather | solution.py:48
  275.9 0.0 copy-done.3
  275.9 0.0 copy-start.2
  275.9 1.8 fusion.3
  277.7 0.6 reshape.17
  278.3 167.7 %all-reduce.2.cloned.1.call-done = bf16[512,512]{1,0:T(8,128)(2,1)} async-done(((bf16[512,512]{1,0:T(8,128)(2,1)}), bf16[512,512]{1,0:T(8,128)(2,1)}) %all-reduce.2.cloned.1.call-update) | async-done | bytes 524304 | tf_op jit(solution)/shard_map/while/body/eval_jaxpr/psum | solution.py:15
  446.0 1.3 copy.12
  447.3 1.1 bitcast_select_fusion
  448.4 0.0 copy-done.2
  448.4 1.0 fusion.56
  449.4 13.0 %all_gather.12 = bf16[512,512]{1,0:T(8,128)(2,1)S(1)} all-gather(bf16[128,512]{1,0:T(8,128)(2,1)S(1)} %get-tuple-element.27), channel_id=1, replica_groups=mesh['dp'=32,'mp'=4,'root'=4] {'mp'}, dimensions={0}, use_global_device_ids=true | all-gather | bytes 655360 | tf_op jit(solution)/shard_map/while/body/eval_jaxpr/all_gather | solution.py:73
  462.4 0.9 fusion.4
  464.0 3.0 fusion.1
  467.1 0.0 copy-start.1
  467.1 1.9 fusion.7
  469.0 0.0 copy-done.1
  469.0 2.0 fusion.12
  471.0 2.0 fusion.10
  472.9 2.0 fusion
  474.9 1.8 fusion.60
  476.8 0.7 select_bitcast_fusion
  (1 shorter events, 0.0 us)
Async XLA Ops:
  7.2 1.6 copy-start
  7.2 130.5 %reduce-scatter.2.cloned.1.call-start = ((), (), s32[]{:S(2)}) async-start(), calls=%async_computation.1 | async-start | bytes 2162688 | tf_op jit(solution)/shard_map/reduce_scatter | solution.py:31
  12.6 127.4 %copy-start.4 = (s32[16]{0:T(128)S(1)}, s32[16]{0:T(128)}, u32[]{:S(2)}) copy-start(s32[16]{0:T(128)} %param.12) | copy-start | bytes 196
  12.6 196.5 %copy-start.5 = (s32[16]{0:T(128)S(1)}, s32[16]{0:T(128)}, u32[]{:S(2)}) copy-start(s32[16]{0:T(128)} %param.13) | copy-start | bytes 196
  12.6 263.2 %copy-start.3 = (bf16[1,2,16,512]{3,2,1,0:T(8,128)(2,1)S(1)}, bf16[1,2,16,512]{3,2,1,0:T(8,128)(2,1)}, u32[]{:S(2)}) copy-start(bf16[1,2,16,512]{3,2,1,0:T(8,128)(2,1)} %param.9) | copy-start | bytes 98308
  12.6 194.5 %all-gather.3.cloned.1.call-start = ((), (), s32[]{:S(2)}) async-start(), calls=%async_computation.2 | async-start | bytes 1081344 | tf_op jit(solution)/shard_map/all_gather | solution.py:40
  139.2 136.6 %all-gather.5.cloned.1.call-start = ((), (), s32[]{:S(2)}) async-start(), calls=%async_computation.3 | async-start | bytes 1081344 | tf_op jit(solution)/shard_map/all_gather | solution.py:48
  140.0 306.1 %all-reduce.2.cloned.1.call-start = ((), (), s32[]{:S(2)}) async-start(), calls=%async_computation.4 | async-start | bytes 1048576 | tf_op jit(solution)/shard_map/while/body/eval_jaxpr/psum | solution.py:15
  275.9 172.5 %copy-start.2 = (f32[1,128,512]{2,1,0:T(8,128)S(1)}, f32[1,128,512]{2,1,0:T(8,128)}, u32[]{:S(2)}) copy-start(f32[1,128,512]{2,1,0:T(8,128)} %param.11) | copy-start | bytes 786436
  467.1 1.9 copy-start.1
Sparse Core Ops, SparseCore 0:
  12.7 124.9 reduce-scatter.1
  141.4 65.6 all-gather.2
  210.4 65.4 all-gather.4
  278.6 167.3 all-reduce.1
where the time goes:
time: 485 us; the launch traced here: 484 us
  waiting for transfers between devices  421 us (87%)
  matrix products  19.3 us (4%)
  between operations  18 us (4%)
  blocking collectives  13 us (3%)
  local copies, waits for them, and re-layouts  6.17 us (1%)
  other arithmetic  6.09 us (1%)
    psum x1, waiting for transfers between devices, spread(): return lax.psum(kept, axis)  168 us
    reduce_scatter x1, waiting for transfers between devices, local(): lax.psum_scatter(lax.dot_general(acts, grads_out, (((0,), (0,)), ((), ())...  125 us
    all_gather x1, waiting for transfers between devices, local(): lax.all_gather(prec_right, 'dp', axis=2, tiled=True)[0]  64 us
    all_gather x1, waiting for transfers between devices, local(): grad_full = lax.all_gather(grad_part, 'dp', axis=0, tiled=True)  63.8 us
    all_gather x1, blocking collectives, refresh_preconditioners(): lax.all_gather(stats_rows.astype(jnp.bfloat16), 'mp', axis=0, tiled=True)  13 us
    dot_general x6, matrix products, matmul_high(): jnp.dot(left, right, precision=lax.Precision.HIGHEST, preferred_element_t...  12.7 us
  transfers between devices with their start and end apart: 4, of which 4 were waited for; matrix products, arithmetic and copies ran while one was open for 1% of the time, Pallas kernels for 0%

commit v1 on v0

v1 whole, which is shorter than its diff:
```python
import functools

import jax
import jax.numpy as jnp
from jax import lax
from jax.experimental import pallas as pl
from jax.experimental.pallas import tpu as pltpu
from jax.sharding import Mesh, PartitionSpec as P

B = 512
DECAY = 0.6
KAPPA = 1.25 ** 4
X, ZH, CORE = 4, 4, 2
CHIPS = X * ZH
PART = B // X
ROWS = B // CHIPS
GRID = ("x", "zh")
F32, BF16 = jnp.float32, jnp.bfloat16
VMEM = pl.BlockSpec(memory_space=pltpu.VMEM)
SMEM = pl.BlockSpec(memory_space=pltpu.SMEM)


def dot(left, right, left_dim=1, right_dim=0):
    dims = (((left_dim,), (right_dim,)), ((), ()))
    return lax.dot_general(left, right, dims, preferred_element_type=F32)


def params():
    return pltpu.CompilerParams(vmem_limit_bytes=32 * 1024 * 1024)


def cost(flops, nbytes):
    return pl.CostEstimate(flops=flops, bytes_accessed=nbytes, transcendentals=0)


def shape(dims, dtype=BF16):
    return jax.ShapeDtypeStruct(dims, dtype)


def accumulate(total, part):
    @pl.when(pl.program_id(0) == 0)
    def _():
        total[...] = part

    @pl.when(pl.program_id(0) > 0)
    def _():
        total[...] += part


def other_kernel(index_ref, acts_ref, grads_ref, left_ref, right_ref, turned_ref, out_ref, total):
    other = index_ref[0]
    turned = acts_ref[...].T
    turned_ref[...] = turned
    accumulate(total, dot(turned, grads_ref[...]))

    @pl.when(pl.program_id(0) == pl.num_programs(0) - 1)
    def _():
        rows = left_ref.shape[2]
        out_ref[:B] = total[...].astype(BF16)
        out_ref[B : B + rows] = left_ref[0, other]
        out_ref[B + rows :] = right_ref[0, other]


def other_half(acts, grads, prec_left, prec_right, index):
    tokens, rows = acts.shape[0], prec_left.shape[2]
    steps = 4
    piece = tokens // steps
    whole = lambda *dims: pl.BlockSpec(dims, lambda k, index: (0,) * len(dims))
    return pl.pallas_call(
        other_kernel,
        grid_spec=pltpu.PrefetchScalarGridSpec(
            num_scalar_prefetch=1,
            grid=(steps,),
            in_specs=[
                pl.BlockSpec((piece, B), lambda k, index: (k, 0)),
                pl.BlockSpec((piece, B), lambda k, index: (k, index[0])),
                whole(*prec_left.shape),
                whole(*prec_right.shape),
            ],
            out_specs=[
                pl.BlockSpec((B, piece), lambda k, index: (0, k)),
                whole(B + 2 * rows, B),
            ],
            scratch_shapes=[pltpu.VMEM((B, B), F32)],
        ),
        out_shape=[shape((B, tokens)), shape((B + 2 * rows, B))],
        cost_estimate=cost(2 * tokens * B * B, 4 * tokens * B),
        name="other_half",
    )(index.reshape(1), acts, grads, prec_left, prec_right)


def own_kernel(index_ref, turned_ref, grads_ref, out_ref):
    at = pl.multiple_of(index_ref[0] * B, B)
    out_ref[...] = dot(turned_ref[...], grads_ref[:, pl.ds(at, B)])


def join_kernel(index_ref, own_ref, got_ref, left_ref, right_ref, out_ref, left_out, right_out):
    core = index_ref[0]
    rows = left_ref.shape[2]
    out_ref[...] = (own_ref[...] + got_ref[:B].astype(F32)).astype(BF16).T
    mine = pl.ds(pl.multiple_of(core * rows, rows), rows)
    theirs = pl.ds(pl.multiple_of((1 - core) * rows, rows), rows)
    left_out[mine, :] = left_ref[0, core]
    left_out[theirs, :] = got_ref[B : B + rows]
    right_out[mine, :] = right_ref[0, core]
    right_out[theirs, :] = got_ref[B + rows :]


def shifted(value, axis):
    size = lax.axis_size(axis)
    return [
        lax.ppermute(value, axis, [(at, (at + step) % size) for at in range(size)])
        for step in range(1, size)
    ]


def place(out_ref, parts, index):
    rows = parts[0].shape[0]
    for step, part in enumerate(parts):
        at = (index + len(parts) - step) % len(parts) * rows
        out_ref[pl.ds(pl.multiple_of(at, rows), rows), :] = part[...]


def part_kernel(axis_at, info_ref, one, two, three, four, out_ref):
    place(out_ref, (one, two, three, four), info_ref[axis_at])


def added(parts_ref):
    total = parts_ref[0].astype(F32)
    for part in range(1, parts_ref.shape[0]):
        total = total + parts_ref[part].astype(F32)
    return total


def sum_kernel(parts_ref, out_ref):
    out_ref[...] = added(parts_ref).astype(BF16)


def pack_kernel(scale, parts_ref, *refs):
    grad_ref, pieces_ref = refs[-2:]
    grad = (added(parts_ref) * scale).astype(BF16)
    grad_ref[...] = grad
    cores, n_mp, n_root, rows, lanes = pieces_ref.shape
    for c in range(cores):
        for m in range(n_mp):
            piece = grad[c * rows : (c + 1) * rows, m * lanes : (m + 1) * lanes]
            for r in range(n_root):
                pieces_ref[c, m, r] = piece


def left_kernel(info_ref, grad_ref, own_ref, one, two, three, out_ref, low, high, prec):
    x, zh = info_ref[1], info_ref[2]
    half, lanes = out_ref.shape[1:]
    for ref, slot in ((low, zh), (high, (zh + 2) % ZH)):
        ref[...] = jnp.zeros_like(ref)
        ref[pl.ds(pl.multiple_of(slot * ROWS, ROWS), ROWS), :] = grad_ref[...]
    place(prec, (own_ref, one, two, three), x)
    rows = prec[...].reshape(CHIPS, ROWS, B)
    out = dot(rows[:, :half].reshape(CHIPS * half, B), low[...], 1, 1)
    out = out + dot(rows[:, half:].reshape(CHIPS * half, B), high[...], 1, 1)
    out_ref[...] = out.astype(BF16).reshape(CHIPS, half, lanes)


def choose_kernel(place_ref, blocks_ref, left_ref, *refs):
    half, out_ref = left_ref.shape[1], refs[-1]
    for j in range(CHIPS):
        out_ref[j, :half] = blocks_ref[place_ref[j]]
        out_ref[j, half:] = left_ref[j]


def spread_kernel(parts_ref, *refs):
    half, out_ref = parts_ref.shape[1] // 2, refs[-1]
    for peer in range(out_ref.shape[0]):
        out_ref[peer] = parts_ref[:, :half]


def update_kernel(info_ref, parts_ref, own_ref, one, two, three, keep_ref, send_ref, left, prec):
    core, x = info_ref[0], info_ref[1]
    half, lanes = keep_ref.shape[0], parts_ref.shape[2]
    place(prec, (own_ref, one, two, three), x)
    slot = lax.broadcasted_iota(jnp.int32, (half, lanes), 1) // ROWS
    for w in range(X):
        low = jnp.zeros((half, lanes), F32)
        high = jnp.zeros((half, lanes), F32)
        for z in range(ZH):
            part = parts_ref[w * ZH + z, half:].astype(F32)
            low = low + jnp.where(slot == z, part, 0.0)
            high = high + jnp.where(slot == (z + 2) % ZH, part, 0.0)
        at = slice(w * lanes, (w + 1) * lanes)
        left[:half, at] = low.astype(BF16)
        left[half:, at] = pltpu.roll(high, lanes // 2, 1).astype(BF16)
    out = dot(left[...], prec[...])
    keep_ref[...] = jnp.where(core == 0, out[:half], out[half:]).astype(BF16)
    send_ref[...] = jnp.where(core == 0, out[half:], out[:half]).astype(BF16)


def refresh_kernel(info_ref, owner_ref, pieces_ref, own_ref, low_ref, one, two, three, stats_ref, roots_ref, block, product, old):
    core, x, zh, mp, root = (info_ref[at] for at in range(5))
    n_mp = pieces_ref.shape[1]
    rows, lanes = pieces_ref.shape[3:]
    quarter = own_ref.shape[0]
    for c in range(CORE):
        for m in range(n_mp):
            for j in range(CHIPS):
                at = j * ROWS + c * rows
                block[at : at + rows, m * lanes : (m + 1) * lanes] = pieces_ref[c, m, j]

    place(old, (low_ref, one, two, three), mp)

    @pl.when(core == 0)
    def _():
        value = block[...]
        product[...] = dot(value, value, 0, 0) * ((1.0 - DECAY) / B)

    @pl.when(core != 0)
    def _():
        value = block[...]
        product[...] = dot(value, value, 1, 1) * ((1.0 - DECAY) / B)

    mine = pl.ds(pl.multiple_of(mp * quarter, quarter), quarter)
    stats_rows = DECAY * own_ref[...] + product[mine, :]
    full = DECAY * old[...].astype(F32) + product[...]
    square = jnp.sum(full * full, axis=0, keepdims=True)
    factor = 2.5 / jnp.sqrt(jnp.sum(square, axis=1, keepdims=True))
    block[...] = (full * (factor * 0.2)).astype(BF16)
    e_rows = stats_rows * (factor * 0.2)
    y = e_rows
    for _ in range(5):
        y = y - dot(y.astype(BF16), block[...])
    line = lax.broadcasted_iota(jnp.int32, (quarter, B), 0) + mp * quarter
    unit = jnp.where(line == lax.broadcasted_iota(jnp.int32, (quarter, B), 1), 1.0, 0.0)
    roots_rows = (jnp.sqrt(jnp.sqrt(factor)) * 1.5625) * (unit - e_rows - KAPPA * y)
    owned = owner_ref[x * ZH + zh] == root
    stats_ref[...] = jnp.where(owned, stats_rows, 0.0)
    roots_ref[...] = jnp.where(owned, roots_rows, 0.0)


def kernel_call(kernel, name, in_specs, out_shape, scratch=(), work=None, awaited=0):
    return pl.pallas_call(
        kernel,
        in_specs=in_specs + [pl.BlockSpec(memory_space=pl.ANY)] * awaited,
        out_specs=[VMEM] * len(out_shape),
        out_shape=out_shape,
        scratch_shapes=list(scratch),
        compiler_params=params(),
        cost_estimate=work,
        name=name,
    )


def local(acts, grads_out, prec_left, prec_right, stats_old, listed, owner):
    x, zh, core = (lax.axis_index(name) for name in ("x", "zh", "core"))
    mp, root = lax.axis_index("mp"), lax.axis_index("root")
    n_mp, n_root = lax.axis_size("mp"), lax.axis_size("root")
    quarter = B // n_mp
    lanes, half = B // n_mp, ROWS // CORE
    tokens = acts.shape[0] * CHIPS * CORE
    swap = ((0, 1), (1, 0))
    info = jnp.stack([core, x, zh, mp, root])

    turned, send = other_half(acts, grads_out, prec_left, prec_right, 1 - core)
    got = lax.ppermute(send, "core", swap)
    (own,) = kernel_call(
        own_kernel,
        "own_half",
        [SMEM, VMEM, VMEM],
        [shape((B, B), F32)],
        work=cost(2 * acts.shape[0] * B * B, 4 * acts.shape[0] * B),
    )(core.reshape(1), turned, grads_out)
    total, left_rows, right_rows = kernel_call(
        join_kernel,
        "join",
        [SMEM] + [VMEM] * 4,
        [shape((B, B)), shape((ROWS, B)), shape((ROWS, B))],
    )(core.reshape(1), own, got, prec_left, prec_right)
    total = lax.all_to_all(total.reshape(X, PART, B), "x", 0, 0)
    got = shifted(left_rows, "zh")
    (total,) = kernel_call(sum_kernel, "sum_x", [VMEM], [shape((PART, B))])(total)
    (left_part,) = kernel_call(
        functools.partial(part_kernel, 2), "left_rows", [SMEM] + [VMEM] * 4, [shape((PART, B))]
    )(info, left_rows, *got)
    left_parts = [left_part] + shifted(left_part, "x")
    old_own = stats_old[0]
    old_low = old_own.astype(BF16)
    olds = [old_low] + shifted(old_low, "mp")
    total = lax.all_to_all(total.reshape(ZH, ROWS, B), "zh", 0, 0)
    grad, pieces = kernel_call(
        functools.partial(pack_kernel, tokens ** -0.5),
        "pack",
        [VMEM],
        [shape((ROWS, B)), shape((CORE, n_mp, n_root, half, lanes))],
        awaited=6,
    )(total, *left_parts[1:], *olds[1:])

    blocks = lax.all_to_all(pieces.reshape(-1, half, lanes), ("core", "mp", "root"), 0, 0)
    (left,) = kernel_call(
        left_kernel,
        "left",
        [SMEM] + [VMEM] * 5,
        [shape((CHIPS, half, lanes))],
        [pltpu.VMEM((lanes, B), BF16)] * 2 + [pltpu.VMEM((B, B), BF16)],
        cost(4 * CHIPS * half * lanes * B, 2 * B * B),
    )(info, grad, *left_parts)
    got = shifted(right_rows, "zh")
    at = (listed % 2) * (n_mp * n_root) + listed // 2
    (chosen,) = kernel_call(
        choose_kernel, "choose", [SMEM, VMEM, VMEM], [shape((CHIPS, 2 * half, lanes))], awaited=3
    )(at, blocks, left, *got)
    parts = lax.all_to_all(chosen, GRID, 0, 0)
    (right_part,) = kernel_call(
        functools.partial(part_kernel, 2), "right_rows", [SMEM] + [VMEM] * 4, [shape((PART, B))]
    )(info, right_rows, *got)
    right_parts = [right_part] + shifted(right_part, "x")
    (mine,) = kernel_call(
        spread_kernel,
        "spread",
        [VMEM],
        [shape((CORE * n_mp, CHIPS, half, lanes))],
        awaited=3,
    )(parts, *right_parts[1:])
    gathered = lax.all_to_all(mine, ("core", "mp"), 0, 0)
    gathered = gathered.reshape((CORE, n_mp) + gathered.shape[1:])

    keep, send = kernel_call(
        update_kernel,
        "update",
        [SMEM] + [VMEM] * 5,
        [shape((half, B))] * 2,
        [pltpu.VMEM((ROWS, B), BF16), pltpu.VMEM((B, B), BF16)],
        cost(2 * ROWS * B * B, 2 * B * B),
    )(info, parts, *right_parts)
    got = lax.ppermute(send, "core", swap)
    update = jnp.where(
        core == 0, jnp.concatenate([keep, got], 1), jnp.concatenate([got, keep], 1)
    )

    new_stats, new_roots = kernel_call(
        refresh_kernel,
        "refresh",
        [SMEM, SMEM] + [VMEM] * 6,
        [shape((quarter, B), F32)] * 2,
        [pltpu.VMEM((B, B), BF16), pltpu.VMEM((B, B), F32), pltpu.VMEM((B, B), BF16)],
        cost(2 * B ** 3 + 10 * quarter * B * B, 2 * B * B * 2),
    )(info, owner, gathered, old_own, *olds)
    return update[None], new_stats[None, None], new_roots[None, None]


def solution(mesh):
    n_dp, n_mp, n_root = mesh.devices.shape
    fine = Mesh(
        mesh.devices.reshape(X, ZH, CORE, n_mp, n_root), ("x", "zh", "core", "mp", "root")
    )
    dp = ("x", "zh", "core")
    in_specs = (
        P(dp, "mp"),
        P(dp, "root"),
        P("mp", "root", dp, None),
        P("mp", "root", dp, None),
        P(dp, "mp", None),
        P(),
        P(),
    )
    out_specs = (P("mp", dp, "root"), P("root", dp, "mp", None), P("root", dp, "mp", None))
    return jax.shard_map(local, mesh=fine, in_specs=in_specs, out_specs=out_specs, check_vma=False)
```

time: 485 us -> 159 us (0.33)
  the two profiles are of different devices: /device:TPU:6 before, /device:TPU:1 now
where the time goes in v1:
time: 159 us; the launch traced here: 158 us
  starting transfers between devices  110 us (69%)
  waiting for transfers between devices  18.6 us (12%)
  Pallas kernels  15.1 us (9%)
  blocking collectives  11.6 us (7%)
    ppermute x15, starting transfers between devices, shifted(): lax.ppermute(value, axis, [(at, (at + step) % size) for at in range(size)])  63.6 us
    ppermute x15, waiting for transfers between devices, shifted(): lax.ppermute(value, axis, [(at, (at + step) % size) for at in range(size)])  12.5 us
    all_to_all x1, blocking collectives, local(): total = lax.all_to_all(total.reshape(X, PART, B), 'x', 0, 0)  11.6 us
    all_to_all x1, starting transfers between devices, local(): total = lax.all_to_all(total.reshape(ZH, ROWS, B), 'zh', 0, 0)  10.8 us
    ppermute x2, starting transfers between devices, local(): got = lax.ppermute(send, 'core', swap)  10.7 us
    all_to_all x1, starting transfers between devices, local(): lax.all_to_all(pieces.reshape(-1, half, lanes), ('core', 'mp', 'root'), 0...  8.84 us
    all_to_all x1, starting transfers between devices, local(): gathered = lax.all_to_all(mine, ('core', 'mp'), 0, 0)  8.3 us
    all_to_all x1, starting transfers between devices, local(): parts = lax.all_to_all(chosen, GRID, 0, 0)  7.44 us
  transfers between devices with their start and end apart: 21, of which 8 were waited for; matrix products, arithmetic and copies ran while one was open for 0% of the time, Pallas kernels for 2%

profile of v1, /device:TPU:1, one launch (start us, length us, event | category | flops | bytes accessed | tf_op | source)
XLA Modules:
  0.0 157.9 jit_solution(2389836028623696460)
XLA Ops:
  0.6 4.8 %other_half.1 = (bf16[512,1024]{1,0:T(8,128)(2,1)}, bf16[544,512]{1,0:T(8,128)(2,1)}) custom-call(s32[1]{0:T(128)} %bitcast.5.index_ref, bf16[1024,512]{1,0:T(8,128)(2,1)} %acts_ref.1, bf16[1024,1024]{1,0:T(8,128)(2,1)} %grads_ref.3, bf16[1,2,16,512]{3,2,1,0:T(8,128)(2,1)} %left_ref.3, bf16[1,2,16,512]{3,2,1,0:T(8,128)(2,1)} %right_ref.3), custom_call_target="tpu_custom_call" | custom-call | flops 536870912 | bytes 2097152 | tf_op jit(solution)/shard_map/other_half/pallas_call | solution.py:69
  5.4 8.8 %collective-permute-start = (bf16[544,512]{1,0:T(8,128)(2,1)}, bf16[544,512]{1,0:T(8,128)(2,1)S(1)}, u32[]{:S(2)}, u32[]{:S(2)}) collective-permute-start(bf16[544,512]{1,0:T(8,128)(2,1)} %get-tuple-element.15), channel_id=1, source_target_pairs={{0,16},{16,0},{1,17},{17,1},{2,18},{18,2},{3,19},{19,3},{4,20},{20... | collective-permute-start | bytes 1671176 | tf_op jit(solution)/shard_map/ppermute | solution.py:262
  14.2 1.2 copy-done.1
  15.4 0.7 own_half.1.own_ref
  16.2 0.0 copy-done.3
  16.2 0.0 copy-done.4
  16.2 0.2 join.1
  16.4 0.0 copy-start.6
  16.4 11.6 %all_to_all.25.parts_ref = bf16[4,128,512]{2,1,0:T(8,128)(2,1)S(1)} all-to-all(bf16[4,128,512]{2,1,0:T(8,128)(2,1)S(1)} %bitcast.17), channel_id=1, replica_groups=mesh['x'=4,'zh'=4,'core'=2,'mp'=4,'root'=4] {'x'}, dimensions={0} | all-to-all | bytes 1048576 | tf_op jit(solution)/shard_map/all_to_all | solution.py:276
  28.0 0.7 sum_x.1
  28.7 10.8 %all-to-all-start.1 = ((bf16[4,32,512]{2,1,0:T(8,128)(2,1)}), bf16[4,32,512]{2,1,0:T(8,128)(2,1)S(1)}, u32[]{:S(2)}, u32[]{:S(2)}) async-start(bf16[4,32,512]{2,1,0:T(8,128)(2,1)} %bitcast.7), calls=%async_computation.1 | async-start | bytes 262144 | tf_op jit(solution)/shard_map/all_to_all | solution.py:286
  39.6 3.2 %collective-permute-start.7 = (bf16[128,512]{1,0:T(8,128)(2,1)S(1)}, bf16[128,512]{1,0:T(8,128)(2,1)S(1)}, u32[]{:S(2)}, u32[]{:S(2)}) collective-permute-start(bf16[128,512]{1,0:T(8,128)(2,1)S(1)} %bitcast_convert_fusion.low_ref), channel_id=1, source_target_pairs={{0,4},{4,8},{8,12},{12,0},{1,5},{5,9},{9,13},{13,1},{2,6},{6,10},{... | collective-permute-start | bytes 393224 | tf_op jit(solution)/shard_map/ppermute | solution.py:112
  42.8 7.3 %collective-permute-start.1 = (bf16[32,512]{1,0:T(8,128)(2,1)S(1)}, bf16[32,512]{1,0:T(8,128)(2,1)S(1)}, u32[]{:S(2)}, u32[]{:S(2)}) collective-permute-start(bf16[32,512]{1,0:T(8,128)(2,1)S(1)} %get-tuple-element.17.one), channel_id=1, source_target_pairs={{0,32},{32,64},{64,96},{96,0},{1,33},{33,65},{65,97},{97,1},{2,34}... | collective-permute-start | bytes 98312 | tf_op jit(solution)/shard_map/ppermute | solution.py:112
  50.1 7.0 %collective-permute-start.2 = (bf16[32,512]{1,0:T(8,128)(2,1)S(1)}, bf16[32,512]{1,0:T(8,128)(2,1)S(1)}, u32[]{:S(2)}, u32[]{:S(2)}) collective-permute-start(bf16[32,512]{1,0:T(8,128)(2,1)S(1)} %get-tuple-element.17.one), channel_id=1, source_target_pairs={{0,64},{32,96},{64,0},{96,32},{1,65},{33,97},{65,1},{97,33},{2,66}... | collective-permute-start | bytes 98312 | tf_op jit(solution)/shard_map/ppermute | solution.py:112
  57.1 7.0 %collective-permute-start.3 = (bf16[32,512]{1,0:T(8,128)(2,1)S(1)}, bf16[32,512]{1,0:T(8,128)(2,1)S(1)}, u32[]{:S(2)}, u32[]{:S(2)}) collective-permute-start(bf16[32,512]{1,0:T(8,128)(2,1)S(1)} %get-tuple-element.17.one), channel_id=1, source_target_pairs={{0,96},{32,0},{64,32},{96,64},{1,97},{33,1},{65,33},{97,65},{2,98}... | collective-permute-start | bytes 98312 | tf_op jit(solution)/shard_map/ppermute | solution.py:112
  64.1 4.5 %collective-permute-start.8 = (bf16[128,512]{1,0:T(8,128)(2,1)S(1)}, bf16[128,512]{1,0:T(8,128)(2,1)S(1)}, u32[]{:S(2)}, u32[]{:S(2)}) collective-permute-start(bf16[128,512]{1,0:T(8,128)(2,1)S(1)} %bitcast_convert_fusion.low_ref), channel_id=1, source_target_pairs={{0,8},{4,12},{8,0},{12,4},{1,9},{5,13},{9,1},{13,5},{2,10},{6,14},... | collective-permute-start | bytes 393224 | tf_op jit(solution)/shard_map/ppermute | solution.py:112
  68.6 0.1 stack.23.info_ref
  68.7 3.0 %collective-permute-start.9 = (bf16[128,512]{1,0:T(8,128)(2,1)S(1)}, bf16[128,512]{1,0:T(8,128)(2,1)S(1)}, u32[]{:S(2)}, u32[]{:S(2)}) collective-permute-start(bf16[128,512]{1,0:T(8,128)(2,1)S(1)} %bitcast_convert_fusion.low_ref), channel_id=1, source_target_pairs={{0,12},{4,0},{8,4},{12,8},{1,13},{5,1},{9,5},{13,9},{2,14},{6,2},{... | collective-permute-start | bytes 393224 | tf_op jit(solution)/shard_map/ppermute | solution.py:112
  71.7 0.6 left_rows.1.own_ref
  72.3 2.2 %collective-permute-start.4 = (bf16[128,512]{1,0:T(8,128)(2,1)S(1)}, bf16[128,512]{1,0:T(8,128)(2,1)S(1)}, u32[]{:S(2)}, u32[]{:S(2)}) collective-permute-start(bf16[128,512]{1,0:T(8,128)(2,1)S(1)} %left_rows.1.own_ref), channel_id=1, source_target_pairs={{0,128},{128,256},{256,384},{384,0},{1,129},{129,257},{257,385},{3... | collective-permute-start | bytes 393224 | tf_op jit(solution)/shard_map/ppermute | solution.py:112
  74.5 3.7 %collective-permute-start.5 = (bf16[128,512]{1,0:T(8,128)(2,1)S(1)}, bf16[128,512]{1,0:T(8,128)(2,1)S(1)}, u32[]{:S(2)}, u32[]{:S(2)}) collective-permute-start(bf16[128,512]{1,0:T(8,128)(2,1)S(1)} %left_rows.1.own_ref), channel_id=1, source_target_pairs={{0,256},{128,384},{256,0},{384,128},{1,257},{129,385},{257,1},{385... | collective-permute-start | bytes 393224 | tf_op jit(solution)/shard_map/ppermute | solution.py:112
  78.2 2.5 %collective-permute-start.6 = (bf16[128,512]{1,0:T(8,128)(2,1)S(1)}, bf16[128,512]{1,0:T(8,128)(2,1)S(1)}, u32[]{:S(2)}, u32[]{:S(2)}) collective-permute-start(bf16[128,512]{1,0:T(8,128)(2,1)S(1)} %left_rows.1.own_ref), channel_id=1, source_target_pairs={{0,384},{128,0},{256,128},{384,256},{1,385},{129,1},{257,129},{385... | collective-permute-start | bytes 393224 | tf_op jit(solution)/shard_map/ppermute | solution.py:112
  80.7 1.5 collective-permute-done.5.refs_1_.two
  82.2 1.7 %collective-permute-done.6.refs_2_.three = bf16[128,512]{1,0:T(8,128)(2,1)S(1)} collective-permute-done((bf16[128,512]{1,0:T(8,128)(2,1)S(1)}, bf16[128,512]{1,0:T(8,128)(2,1)S(1)}, u32[]{:S(2)}, u32[]{:S(2)}) %collective-permute-start.6) | collective-permute-done | bytes 131104 | tf_op jit(solution)/shard_map/ppermute | solution.py:112
  83.9 0.7 pack.1
  84.6 8.8 %all-to-all-start.2 = ((bf16[32,16,128]{2,1,0:T(8,128)(2,1)}), bf16[32,16,128]{2,1,0:T(8,128)(2,1)S(1)}, u32[]{:S(2)}, u32[]{:S(2)}) async-start(bf16[32,16,128]{2,1,0:T(8,128)(2,1)} %bitcast.9), calls=%async_computation.2 | async-start | bytes 262144 | tf_op jit(solution)/shard_map/all_to_all | solution.py:295
  93.4 2.2 %collective-permute-start.10 = (bf16[32,512]{1,0:T(8,128)(2,1)S(1)}, bf16[32,512]{1,0:T(8,128)(2,1)S(1)}, u32[]{:S(2)}, u32[]{:S(2)}) collective-permute-start(bf16[32,512]{1,0:T(8,128)(2,1)S(1)} %get-tuple-element.20.one), channel_id=1, source_target_pairs={{0,32},{32,64},{64,96},{96,0},{1,33},{33,65},{65,97},{97,1},{2,34}... | collective-permute-start | bytes 98312 | tf_op jit(solution)/shard_map/ppermute | solution.py:112
  95.6 8.1 %collective-permute-start.11 = (bf16[32,512]{1,0:T(8,128)(2,1)S(1)}, bf16[32,512]{1,0:T(8,128)(2,1)S(1)}, u32[]{:S(2)}, u32[]{:S(2)}) collective-permute-start(bf16[32,512]{1,0:T(8,128)(2,1)S(1)} %get-tuple-element.20.one), channel_id=1, source_target_pairs={{0,64},{32,96},{64,0},{96,32},{1,65},{33,97},{65,1},{97,33},{2,66}... | collective-permute-start | bytes 98312 | tf_op jit(solution)/shard_map/ppermute | solution.py:112
  103.8 2.2 %collective-permute-start.12 = (bf16[32,512]{1,0:T(8,128)(2,1)S(1)}, bf16[32,512]{1,0:T(8,128)(2,1)S(1)}, u32[]{:S(2)}, u32[]{:S(2)}) collective-permute-start(bf16[32,512]{1,0:T(8,128)(2,1)S(1)} %get-tuple-element.20.one), channel_id=1, source_target_pairs={{0,96},{32,0},{64,32},{96,64},{1,97},{33,1},{65,33},{97,65},{2,98}... | collective-permute-start | bytes 98312 | tf_op jit(solution)/shard_map/ppermute | solution.py:112
  106.0 0.9 left.1.left_ref
  106.9 2.1 %collective-permute-done.11.refs_1_.three = bf16[32,512]{1,0:T(8,128)(2,1)S(1)} collective-permute-done((bf16[32,512]{1,0:T(8,128)(2,1)S(1)}, bf16[32,512]{1,0:T(8,128)(2,1)S(1)}, u32[]{:S(2)}, u32[]{:S(2)}) %collective-permute-start.11) | collective-permute-done | bytes 32800 | tf_op jit(solution)/shard_map/ppermute | solution.py:112
  109.0 3.3 %collective-permute-done.12.refs_2_.four = bf16[32,512]{1,0:T(8,128)(2,1)S(1)} collective-permute-done((bf16[32,512]{1,0:T(8,128)(2,1)S(1)}, bf16[32,512]{1,0:T(8,128)(2,1)S(1)}, u32[]{:S(2)}, u32[]{:S(2)}) %collective-permute-start.12) | collective-permute-done | bytes 32800 | tf_op jit(solution)/shard_map/ppermute | solution.py:112
  112.3 1.2 choose.1
  113.6 7.4 %all-to-all-start.3 = ((bf16[16,32,128]{2,1,0:T(8,128)(2,1)}), bf16[16,32,128]{2,1,0:T(8,128)(2,1)S(1)}, u32[]{:S(2)}, u32[]{:S(2)}) async-start(bf16[16,32,128]{2,1,0:T(8,128)(2,1)} %choose.1), calls=%async_computation.3 | async-start | bytes 262144 | tf_op jit(solution)/shard_map/all_to_all | solution.py:309
  121.0 0.6 right_rows.1.own_ref
  121.6 3.3 %collective-permute-start.13 = (bf16[128,512]{1,0:T(8,128)(2,1)S(1)}, bf16[128,512]{1,0:T(8,128)(2,1)S(1)}, u32[]{:S(2)}, u32[]{:S(2)}) collective-permute-start(bf16[128,512]{1,0:T(8,128)(2,1)S(1)} %right_rows.1.own_ref), channel_id=1, source_target_pairs={{0,128},{128,256},{256,384},{384,0},{1,129},{129,257},{257,385},{3... | collective-permute-start | bytes 393224 | tf_op jit(solution)/shard_map/ppermute | solution.py:112
  124.9 4.3 %collective-permute-start.14 = (bf16[128,512]{1,0:T(8,128)(2,1)S(1)}, bf16[128,512]{1,0:T(8,128)(2,1)S(1)}, u32[]{:S(2)}, u32[]{:S(2)}) collective-permute-start(bf16[128,512]{1,0:T(8,128)(2,1)S(1)} %right_rows.1.own_ref), channel_id=1, source_target_pairs={{0,256},{128,384},{256,0},{384,128},{1,257},{129,385},{257,1},{385... | collective-permute-start | bytes 393224 | tf_op jit(solution)/shard_map/ppermute | solution.py:112
  129.2 3.1 %collective-permute-start.15 = (bf16[128,512]{1,0:T(8,128)(2,1)S(1)}, bf16[128,512]{1,0:T(8,128)(2,1)S(1)}, u32[]{:S(2)}, u32[]{:S(2)}) collective-permute-start(bf16[128,512]{1,0:T(8,128)(2,1)S(1)} %right_rows.1.own_ref), channel_id=1, source_target_pairs={{0,384},{128,0},{256,128},{384,256},{1,385},{129,1},{257,129},{385... | collective-permute-start | bytes 393224 | tf_op jit(solution)/shard_map/ppermute | solution.py:112
  132.3 0.7 collective-permute-done.14.two.refs_1_
  133.0 3.3 %collective-permute-done.15.three.refs_2_ = bf16[128,512]{1,0:T(8,128)(2,1)S(1)} collective-permute-done((bf16[128,512]{1,0:T(8,128)(2,1)S(1)}, bf16[128,512]{1,0:T(8,128)(2,1)S(1)}, u32[]{:S(2)}, u32[]{:S(2)}) %collective-permute-start.15) | collective-permute-done | bytes 131104 | tf_op jit(solution)/shard_map/ppermute | solution.py:112
  136.2 0.9 spread.1
  137.1 8.3 %all-to-all-start.4 = ((bf16[8,16,16,128]{3,2,1,0:T(8,128)(2,1)}), bf16[8,16,16,128]{3,2,1,0:T(8,128)(2,1)S(1)}, u32[]{:S(2)}, u32[]{:S(2)}) async-start(bf16[8,16,16,128]{3,2,1,0:T(8,128)(2,1)} %spread.1), calls=%async_computation.4 | async-start | bytes 1048576 | tf_op jit(solution)/shard_map/all_to_all | solution.py:321
  145.4 0.8 update.1
  146.1 1.9 %collective-permute-start.16 = (bf16[16,512]{1,0:T(8,128)(2,1)S(1)}, bf16[16,512]{1,0:T(8,128)(2,1)S(1)}, u32[]{:S(2)}, u32[]{:S(2)}) collective-permute-start(bf16[16,512]{1,0:T(8,128)(2,1)S(1)} %get-tuple-element.22), channel_id=1, source_target_pairs={{0,16},{16,0},{1,17},{17,1},{2,18},{18,2},{3,19},{19,3},{4,20},{20... | collective-permute-start | bytes 49160 | tf_op jit(solution)/shard_map/ppermute | solution.py:332
  148.1 1.1 collective-permute-done.16
  149.2 0.6 maximum_select_fusion
  149.9 4.9 %all-to-all-done.4 = bf16[8,16,16,128]{3,2,1,0:T(8,128)(2,1)S(1)} async-done(((bf16[8,16,16,128]{3,2,1,0:T(8,128)(2,1)}), bf16[8,16,16,128]{3,2,1,0:T(8,128)(2,1)S(1)}, u32[]{:S(2)}, u32[]{:S(2)}) %all-to-all-start.4) | async-done | bytes 524320 | tf_op jit(solution)/shard_map/all_to_all | solution.py:321
  154.8 3.2 %refresh.1 = (f32[128,512]{1,0:T(8,128)}, f32[128,512]{1,0:T(8,128)}) custom-call(s32[5]{0:T(128)S(1)} %stack.23.info_ref, s32[16]{0:T(128)S(1)} %copy-done.5, bf16[2,4,16,16,128]{4,3,2,1,0:T(8,128)(2,1)S(1)} %bitcast.16, f32[128,512]{1,0:T(8,128)S(1)} %bitcast.18, bf16[128,512]{1,0:T(8,128)(2,1)S(1)} %bitcast_convert_fusion.low_ref, ...), custom_call_target="tpu_custom_call" | custom-call | flops 603979776 | bytes 1048576 | tf_op jit(solution)/shard_map/refresh/pallas_call | solution.py:337
  (25 shorter events, 0.1 us)
Async XLA Ops:
  0.6 13.6 %copy-start = (bf16[1024,1024]{1,0:T(8,128)(2,1)S(1)}, bf16[1024,1024]{1,0:T(8,128)(2,1)}, u32[]{:S(2)}) copy-start(bf16[1024,1024]{1,0:T(8,128)(2,1)} %grads_ref.3) | copy-start | bytes 6291460
  5.4 10.8 %collective-permute-start = (bf16[544,512]{1,0:T(8,128)(2,1)}, bf16[544,512]{1,0:T(8,128)(2,1)S(1)}, u32[]{:S(2)}, u32[]{:S(2)}) collective-permute-start(bf16[544,512]{1,0:T(8,128)(2,1)} %get-tuple-element.15), channel_id=1, source_target_pairs={{0,16},{16,0},{1,17},{17,1},{2,18},{18,2},{3,19},{19,3},{4,20},{20... | collective-permute-start | bytes 1671176 | tf_op jit(solution)/shard_map/ppermute | solution.py:262
  14.2 1.2 copy-start.1
  15.4 0.8 copy-start.3
  15.4 0.8 copy-start.4
  16.2 23.4 %copy-start.2 = (f32[1,128,512]{2,1,0:T(8,128)S(1)}, f32[1,128,512]{2,1,0:T(8,128)}, u32[]{:S(2)}) copy-start(f32[1,128,512]{2,1,0:T(8,128)} %param.11) | copy-start | bytes 786436
  16.4 89.6 %copy-start.6 = (s32[16]{0:T(128)S(1)}, s32[16]{0:T(128)}, u32[]{:S(2)}) copy-start(s32[16]{0:T(128)} %param.12) | copy-start | bytes 196
  28.7 55.2 %all-to-all-start.1 = ((bf16[4,32,512]{2,1,0:T(8,128)(2,1)}), bf16[4,32,512]{2,1,0:T(8,128)(2,1)S(1)}, u32[]{:S(2)}, u32[]{:S(2)}) async-start(bf16[4,32,512]{2,1,0:T(8,128)(2,1)} %bitcast.7), calls=%async_computation.1 | async-start | bytes 262144 | tf_op jit(solution)/shard_map/all_to_all | solution.py:286
  39.6 38.6 %collective-permute-start.7 = (bf16[128,512]{1,0:T(8,128)(2,1)S(1)}, bf16[128,512]{1,0:T(8,128)(2,1)S(1)}, u32[]{:S(2)}, u32[]{:S(2)}) collective-permute-start(bf16[128,512]{1,0:T(8,128)(2,1)S(1)} %bitcast_convert_fusion.low_ref), channel_id=1, source_target_pairs={{0,4},{4,8},{8,12},{12,0},{1,5},{5,9},{9,13},{13,1},{2,6},{6,10},{... | collective-permute-start | bytes 393224 | tf_op jit(solution)/shard_map/ppermute | solution.py:112
  42.8 25.9 %collective-permute-start.1 = (bf16[32,512]{1,0:T(8,128)(2,1)S(1)}, bf16[32,512]{1,0:T(8,128)(2,1)S(1)}, u32[]{:S(2)}, u32[]{:S(2)}) collective-permute-start(bf16[32,512]{1,0:T(8,128)(2,1)S(1)} %get-tuple-element.17.one), channel_id=1, source_target_pairs={{0,32},{32,64},{64,96},{96,0},{1,33},{33,65},{65,97},{97,1},{2,34}... | collective-permute-start | bytes 98312 | tf_op jit(solution)/shard_map/ppermute | solution.py:112
  50.1 21.6 %collective-permute-start.2 = (bf16[32,512]{1,0:T(8,128)(2,1)S(1)}, bf16[32,512]{1,0:T(8,128)(2,1)S(1)}, u32[]{:S(2)}, u32[]{:S(2)}) collective-permute-start(bf16[32,512]{1,0:T(8,128)(2,1)S(1)} %get-tuple-element.17.one), channel_id=1, source_target_pairs={{0,64},{32,96},{64,0},{96,32},{1,65},{33,97},{65,1},{97,33},{2,66}... | collective-permute-start | bytes 98312 | tf_op jit(solution)/shard_map/ppermute | solution.py:112
  57.1 14.6 %collective-permute-start.3 = (bf16[32,512]{1,0:T(8,128)(2,1)S(1)}, bf16[32,512]{1,0:T(8,128)(2,1)S(1)}, u32[]{:S(2)}, u32[]{:S(2)}) collective-permute-start(bf16[32,512]{1,0:T(8,128)(2,1)S(1)} %get-tuple-element.17.one), channel_id=1, source_target_pairs={{0,96},{32,0},{64,32},{96,64},{1,97},{33,1},{65,33},{97,65},{2,98}... | collective-permute-start | bytes 98312 | tf_op jit(solution)/shard_map/ppermute | solution.py:112
  64.1 16.6 %collective-permute-start.8 = (bf16[128,512]{1,0:T(8,128)(2,1)S(1)}, bf16[128,512]{1,0:T(8,128)(2,1)S(1)}, u32[]{:S(2)}, u32[]{:S(2)}) collective-permute-start(bf16[128,512]{1,0:T(8,128)(2,1)S(1)} %bitcast_convert_fusion.low_ref), channel_id=1, source_target_pairs={{0,8},{4,12},{8,0},{12,4},{1,9},{5,13},{9,1},{13,5},{2,10},{6,14},... | collective-permute-start | bytes 393224 | tf_op jit(solution)/shard_map/ppermute | solution.py:112
  68.7 12.0 %collective-permute-start.9 = (bf16[128,512]{1,0:T(8,128)(2,1)S(1)}, bf16[128,512]{1,0:T(8,128)(2,1)S(1)}, u32[]{:S(2)}, u32[]{:S(2)}) collective-permute-start(bf16[128,512]{1,0:T(8,128)(2,1)S(1)} %bitcast_convert_fusion.low_ref), channel_id=1, source_target_pairs={{0,12},{4,0},{8,4},{12,8},{1,13},{5,1},{9,5},{13,9},{2,14},{6,2},{... | collective-permute-start | bytes 393224 | tf_op jit(solution)/shard_map/ppermute | solution.py:112
  72.3 8.5 %collective-permute-start.4 = (bf16[128,512]{1,0:T(8,128)(2,1)S(1)}, bf16[128,512]{1,0:T(8,128)(2,1)S(1)}, u32[]{:S(2)}, u32[]{:S(2)}) collective-permute-start(bf16[128,512]{1,0:T(8,128)(2,1)S(1)} %left_rows.1.own_ref), channel_id=1, source_target_pairs={{0,128},{128,256},{256,384},{384,0},{1,129},{129,257},{257,385},{3... | collective-permute-start | bytes 393224 | tf_op jit(solution)/shard_map/ppermute | solution.py:112
  74.5 7.8 %collective-permute-start.5 = (bf16[128,512]{1,0:T(8,128)(2,1)S(1)}, bf16[128,512]{1,0:T(8,128)(2,1)S(1)}, u32[]{:S(2)}, u32[]{:S(2)}) collective-permute-start(bf16[128,512]{1,0:T(8,128)(2,1)S(1)} %left_rows.1.own_ref), channel_id=1, source_target_pairs={{0,256},{128,384},{256,0},{384,128},{1,257},{129,385},{257,1},{385... | collective-permute-start | bytes 393224 | tf_op jit(solution)/shard_map/ppermute | solution.py:112
  78.2 5.7 %collective-permute-start.6 = (bf16[128,512]{1,0:T(8,128)(2,1)S(1)}, bf16[128,512]{1,0:T(8,128)(2,1)S(1)}, u32[]{:S(2)}, u32[]{:S(2)}) collective-permute-start(bf16[128,512]{1,0:T(8,128)(2,1)S(1)} %left_rows.1.own_ref), channel_id=1, source_target_pairs={{0,384},{128,0},{256,128},{384,256},{1,385},{129,1},{257,129},{385... | collective-permute-start | bytes 393224 | tf_op jit(solution)/shard_map/ppermute | solution.py:112
  84.6 27.8 %all-to-all-start.2 = ((bf16[32,16,128]{2,1,0:T(8,128)(2,1)}), bf16[32,16,128]{2,1,0:T(8,128)(2,1)S(1)}, u32[]{:S(2)}, u32[]{:S(2)}) async-start(bf16[32,16,128]{2,1,0:T(8,128)(2,1)} %bitcast.9), calls=%async_computation.2 | async-start | bytes 262144 | tf_op jit(solution)/shard_map/all_to_all | solution.py:295
  93.4 13.5 %collective-permute-start.10 = (bf16[32,512]{1,0:T(8,128)(2,1)S(1)}, bf16[32,512]{1,0:T(8,128)(2,1)S(1)}, u32[]{:S(2)}, u32[]{:S(2)}) collective-permute-start(bf16[32,512]{1,0:T(8,128)(2,1)S(1)} %get-tuple-element.20.one), channel_id=1, source_target_pairs={{0,32},{32,64},{64,96},{96,0},{1,33},{33,65},{65,97},{97,1},{2,34}... | collective-permute-start | bytes 98312 | tf_op jit(solution)/shard_map/ppermute | solution.py:112
  95.6 13.4 %collective-permute-start.11 = (bf16[32,512]{1,0:T(8,128)(2,1)S(1)}, bf16[32,512]{1,0:T(8,128)(2,1)S(1)}, u32[]{:S(2)}, u32[]{:S(2)}) collective-permute-start(bf16[32,512]{1,0:T(8,128)(2,1)S(1)} %get-tuple-element.20.one), channel_id=1, source_target_pairs={{0,64},{32,96},{64,0},{96,32},{1,65},{33,97},{65,1},{97,33},{2,66}... | collective-permute-start | bytes 98312 | tf_op jit(solution)/shard_map/ppermute | solution.py:112
  103.8 8.6 %collective-permute-start.12 = (bf16[32,512]{1,0:T(8,128)(2,1)S(1)}, bf16[32,512]{1,0:T(8,128)(2,1)S(1)}, u32[]{:S(2)}, u32[]{:S(2)}) collective-permute-start(bf16[32,512]{1,0:T(8,128)(2,1)S(1)} %get-tuple-element.20.one), channel_id=1, source_target_pairs={{0,96},{32,0},{64,32},{96,64},{1,97},{33,1},{65,33},{97,65},{2,98}... | collective-permute-start | bytes 98312 | tf_op jit(solution)/shard_map/ppermute | solution.py:112
  106.0 48.7 %copy-start.5 = (s32[16]{0:T(128)S(1)}, s32[16]{0:T(128)}, u32[]{:S(2)}) copy-start(s32[16]{0:T(128)} %owner_ref.1) | copy-start | bytes 196
  113.6 22.6 %all-to-all-start.3 = ((bf16[16,32,128]{2,1,0:T(8,128)(2,1)}), bf16[16,32,128]{2,1,0:T(8,128)(2,1)S(1)}, u32[]{:S(2)}, u32[]{:S(2)}) async-start(bf16[16,32,128]{2,1,0:T(8,128)(2,1)} %choose.1), calls=%async_computation.3 | async-start | bytes 262144 | tf_op jit(solution)/shard_map/all_to_all | solution.py:309
  121.6 10.7 %collective-permute-start.13 = (bf16[128,512]{1,0:T(8,128)(2,1)S(1)}, bf16[128,512]{1,0:T(8,128)(2,1)S(1)}, u32[]{:S(2)}, u32[]{:S(2)}) collective-permute-start(bf16[128,512]{1,0:T(8,128)(2,1)S(1)} %right_rows.1.own_ref), channel_id=1, source_target_pairs={{0,128},{128,256},{256,384},{384,0},{1,129},{129,257},{257,385},{3... | collective-permute-start | bytes 393224 | tf_op jit(solution)/shard_map/ppermute | solution.py:112
  124.9 8.1 %collective-permute-start.14 = (bf16[128,512]{1,0:T(8,128)(2,1)S(1)}, bf16[128,512]{1,0:T(8,128)(2,1)S(1)}, u32[]{:S(2)}, u32[]{:S(2)}) collective-permute-start(bf16[128,512]{1,0:T(8,128)(2,1)S(1)} %right_rows.1.own_ref), channel_id=1, source_target_pairs={{0,256},{128,384},{256,0},{384,128},{1,257},{129,385},{257,1},{385... | collective-permute-start | bytes 393224 | tf_op jit(solution)/shard_map/ppermute | solution.py:112
  129.2 7.0 %collective-permute-start.15 = (bf16[128,512]{1,0:T(8,128)(2,1)S(1)}, bf16[128,512]{1,0:T(8,128)(2,1)S(1)}, u32[]{:S(2)}, u32[]{:S(2)}) collective-permute-start(bf16[128,512]{1,0:T(8,128)(2,1)S(1)} %right_rows.1.own_ref), channel_id=1, source_target_pairs={{0,384},{128,0},{256,128},{384,256},{1,385},{129,1},{257,129},{385... | collective-permute-start | bytes 393224 | tf_op jit(solution)/shard_map/ppermute | solution.py:112
  137.1 17.7 %all-to-all-start.4 = ((bf16[8,16,16,128]{3,2,1,0:T(8,128)(2,1)}), bf16[8,16,16,128]{3,2,1,0:T(8,128)(2,1)S(1)}, u32[]{:S(2)}, u32[]{:S(2)}) async-start(bf16[8,16,16,128]{3,2,1,0:T(8,128)(2,1)} %spread.1), calls=%async_computation.4 | async-start | bytes 1048576 | tf_op jit(solution)/shard_map/all_to_all | solution.py:321
  146.1 3.1 %collective-permute-start.16 = (bf16[16,512]{1,0:T(8,128)(2,1)S(1)}, bf16[16,512]{1,0:T(8,128)(2,1)S(1)}, u32[]{:S(2)}, u32[]{:S(2)}) collective-permute-start(bf16[16,512]{1,0:T(8,128)(2,1)S(1)} %get-tuple-element.22), channel_id=1, source_target_pairs={{0,16},{16,0},{1,17},{17,1},{2,18},{18,2},{3,19},{19,3},{4,20},{20... | collective-permute-start | bytes 49160 | tf_op jit(solution)/shard_map/ppermute | solution.py:332

commit v2 on v1

--- a/solution.py
+++ b/solution.py
@@ -37,73 +37,88 @@
     return jax.ShapeDtypeStruct(dims, dtype)
 
 
-def accumulate(total, part):
-    @pl.when(pl.program_id(0) == 0)
-    def _():
-        total[...] = part
-
-    @pl.when(pl.program_id(0) > 0)
-    def _():
-        total[...] += part
-
-
-def other_kernel(index_ref, acts_ref, grads_ref, left_ref, right_ref, turned_ref, out_ref, total):
+def other_kernel(index_ref, acts_ref, grads_ref, left_ref, right_ref, turned_ref, out_ref, own_ref, acts_buf, grads_buf, total, sems):
     other = index_ref[0]
-    turned = acts_ref[...].T
-    turned_ref[...] = turned
-    accumulate(total, dot(turned, grads_ref[...]))
-
-    @pl.when(pl.program_id(0) == pl.num_programs(0) - 1)
-    def _():
-        rows = left_ref.shape[2]
-        out_ref[:B] = total[...].astype(BF16)
-        out_ref[B : B + rows] = left_ref[0, other]
-        out_ref[B + rows :] = right_ref[0, other]
+    steps, piece = acts_buf.shape[:2]
+
+    def half(which):
+        return pl.ds(pl.multiple_of(which * B, B), B)
+
+    copies = []
+    for k in range(steps):
+        rows = pl.ds(k * piece, piece)
+        copies.append(
+            (
+                pltpu.make_async_copy(acts_ref.at[rows, :], acts_buf.at[k], sems.at[0, k]),
+                pltpu.make_async_copy(
+                    grads_ref.at[rows, half(other)], grads_buf.at[k], sems.at[1, k]
+                ),
+            )
+        )
+        for copy in copies[-1]:
+            copy.start()
+    last = pltpu.make_async_copy(grads_ref.at[:, half(1 - other)], own_ref, sems.at[2, 0])
+    last.start()
+    rows = left_ref.shape[2]
+    prec = [
+        pltpu.make_async_copy(
+            ref.at[0, other], out_ref.at[pl.ds(B + side * rows, rows), :], sems.at[3, side]
+        )
+        for side, ref in enumerate((left_ref, right_ref))
+    ]
+    for copy in prec:
+        copy.start()
+    for k, (acts_copy, grads_copy) in enumerate(copies):
+        acts_copy.wait()
+        turned = acts_buf[k].T
+        turned_ref[:, k * piece : (k + 1) * piece] = turned
+        grads_copy.wait()
+        part = dot(turned, grads_buf[k])
+        if k == 0:
+            total[...] = part
+        elif k < steps - 1:
+            total[...] += part
+        else:
+            out_ref[:B] = (total[...] + part).astype(BF16)
+    for copy in (last, *prec):
+        copy.wait()
 
 
 def other_half(acts, grads, prec_left, prec_right, index):
     tokens, rows = acts.shape[0], prec_left.shape[2]
-    steps = 4
-    piece = tokens // steps
-    whole = lambda *dims: pl.BlockSpec(dims, lambda k, index: (0,) * len(dims))
+    steps = 2
+    anywhere = pl.BlockSpec(memory_space=pl.ANY)
+    buffer = pltpu.VMEM((steps, tokens // steps, B), BF16)
     return pl.pallas_call(
         other_kernel,
-        grid_spec=pltpu.PrefetchScalarGridSpec(
-            num_scalar_prefetch=1,
-            grid=(steps,),
-            in_specs=[
-                pl.BlockSpec((piece, B), lambda k, index: (k, 0)),
-                pl.BlockSpec((piece, B), lambda k, index: (k, index[0])),
-                whole(*prec_left.shape),
-                whole(*prec_right.shape),
-            ],
-            out_specs=[
-                pl.BlockSpec((B, piece), lambda k, index: (0, k)),
-                whole(B + 2 * rows, B),
-            ],
-            scratch_shapes=[pltpu.VMEM((B, B), F32)],
-        ),
-        out_shape=[shape((B, tokens)), shape((B + 2 * rows, B))],
-        cost_estimate=cost(2 * tokens * B * B, 4 * tokens * B),
+        in_specs=[SMEM] + [anywhere] * 4,
+        out_specs=[VMEM] * 3,
+        out_shape=[shape((B, tokens)), shape((B + 2 * rows, B)), shape((tokens, B))],
+        scratch_shapes=[
+            buffer,
+            buffer,
+            pltpu.VMEM((B, B), F32),
+            pltpu.SemaphoreType.DMA((4, steps)),
+        ],
+        compiler_params=pltpu.CompilerParams(vmem_limit_bytes=51 * 1024 * 1024),
+        cost_estimate=cost(2 * tokens * B * B, 6 * tokens * B),
         name="other_half",
     )(index.reshape(1), acts, grads, prec_left, prec_right)
 
 
-def own_kernel(index_ref, turned_ref, grads_ref, out_ref):
-    at = pl.multiple_of(index_ref[0] * B, B)
-    out_ref[...] = dot(turned_ref[...], grads_ref[:, pl.ds(at, B)])
-
-
-def join_kernel(index_ref, own_ref, got_ref, left_ref, right_ref, out_ref, left_out, right_out):
+def own_kernel(turned_ref, grads_ref, out_ref):
+    out_ref[...] = dot(turned_ref[...], grads_ref[...])
+
+
+def join_kernel(index_ref, own_ref, got_ref, left_ref, right_ref, out_ref, prec_ref):
     core = index_ref[0]
     rows = left_ref.shape[2]
     out_ref[...] = (own_ref[...] + got_ref[:B].astype(F32)).astype(BF16).T
     mine = pl.ds(pl.multiple_of(core * rows, rows), rows)
     theirs = pl.ds(pl.multiple_of((1 - core) * rows, rows), rows)
-    left_out[mine, :] = left_ref[0, core]
-    left_out[theirs, :] = got_ref[B : B + rows]
-    right_out[mine, :] = right_ref[0, core]
-    right_out[theirs, :] = got_ref[B + rows :]
+    for side, ref in enumerate((left_ref, right_ref)):
+        prec_ref[side, mine, :] = ref[0, core]
+        prec_ref[side, theirs, :] = got_ref[B + side * rows : B + (side + 1) * rows]
 
 
 def shifted(value, axis):
@@ -121,8 +136,10 @@
         out_ref[pl.ds(pl.multiple_of(at, rows), rows), :] = part[...]
 
 
-def part_kernel(axis_at, info_ref, one, two, three, four, out_ref):
-    place(out_ref, (one, two, three, four), info_ref[axis_at])
+def part_kernel(info_ref, one, two, three, four, *out_refs):
+    zh = info_ref[2]
+    for side, ref in enumerate(out_refs):
+        place(ref, [part.at[side] for part in (one, two, three, four)], zh)
 
 
 def added(parts_ref):
@@ -132,7 +149,8 @@
     return total
 
 
-def sum_kernel(parts_ref, out_ref):
+def sum_kernel(parts_ref, *refs):
+    out_ref = refs[-1]
     out_ref[...] = added(parts_ref).astype(BF16)
 
 
@@ -258,28 +276,31 @@
     swap = ((0, 1), (1, 0))
     info = jnp.stack([core, x, zh, mp, root])
 
-    turned, send = other_half(acts, grads_out, prec_left, prec_right, 1 - core)
+    turned, send, grads_own = other_half(acts, grads_out, prec_left, prec_right, 1 - core)
     got = lax.ppermute(send, "core", swap)
     (own,) = kernel_call(
         own_kernel,
         "own_half",
-        [SMEM, VMEM, VMEM],
+        [VMEM, VMEM],
         [shape((B, B), F32)],
         work=cost(2 * acts.shape[0] * B * B, 4 * acts.shape[0] * B),
-    )(core.reshape(1), turned, grads_out)
-    total, left_rows, right_rows = kernel_call(
+    )(turned, grads_own)
+    total, prec = kernel_call(
         join_kernel,
         "join",
         [SMEM] + [VMEM] * 4,
-        [shape((B, B)), shape((ROWS, B)), shape((ROWS, B))],
+        [shape((B, B)), shape((2, ROWS, B))],
     )(core.reshape(1), own, got, prec_left, prec_right)
     total = lax.all_to_all(total.reshape(X, PART, B), "x", 0, 0)
-    got = shifted(left_rows, "zh")
-    (total,) = kernel_call(sum_kernel, "sum_x", [VMEM], [shape((PART, B))])(total)
-    (left_part,) = kernel_call(
-        functools.partial(part_kernel, 2), "left_rows", [SMEM] + [VMEM] * 4, [shape((PART, B))]
-    )(info, left_rows, *got)
+    got = shifted(prec, "zh")
+    (total,) = kernel_call(sum_kernel, "sum_x", [VMEM], [shape((PART, B))], awaited=3)(
+        total, *got
+    )
+    left_part, right_part = kernel_call(
+        part_kernel, "prec_rows", [SMEM] + [VMEM] * 4, [shape((PART, B))] * 2
+    )(info, prec, *got)
     left_parts = [left_part] + shifted(left_part, "x")
+    right_parts = [right_part] + shifted(right_part, "x")
     old_own = stats_old[0]
     old_low = old_own.astype(BF16)
     olds = [old_low] + shifted(old_low, "mp")
@@ -289,8 +310,8 @@
         "pack",
         [VMEM],
         [shape((ROWS, B)), shape((CORE, n_mp, n_root, half, lanes))],
-        awaited=6,
-    )(total, *left_parts[1:], *olds[1:])
+        awaited=3,
+    )(total, *left_parts[1:])
 
     blocks = lax.all_to_all(pieces.reshape(-1, half, lanes), ("core", "mp", "root"), 0, 0)
     (left,) = kernel_call(
@@ -301,23 +322,18 @@
         [pltpu.VMEM((lanes, B), BF16)] * 2 + [pltpu.VMEM((B, B), BF16)],
         cost(4 * CHIPS * half * lanes * B, 2 * B * B),
     )(info, grad, *left_parts)
-    got = shifted(right_rows, "zh")
     at = (listed % 2) * (n_mp * n_root) + listed // 2
     (chosen,) = kernel_call(
         choose_kernel, "choose", [SMEM, VMEM, VMEM], [shape((CHIPS, 2 * half, lanes))], awaited=3
-    )(at, blocks, left, *got)
+    )(at, blocks, left, *right_parts[1:])
     parts = lax.all_to_all(chosen, GRID, 0, 0)
-    (right_part,) = kernel_call(
-        functools.partial(part_kernel, 2), "right_rows", [SMEM] + [VMEM] * 4, [shape((PART, B))]
-    )(info, right_rows, *got)
-    right_parts = [right_part] + shifted(right_part, "x")
     (mine,) = kernel_call(
         spread_kernel,
         "spread",
         [VMEM],
         [shape((CORE * n_mp, CHIPS, half, lanes))],
         awaited=3,
-    )(parts, *right_parts[1:])
+    )(parts, *olds[1:])
     gathered = lax.all_to_all(mine, ("core", "mp"), 0, 0)
     gathered = gathered.reshape((CORE, n_mp) + gathered.shape[1:])
 

time: 159 us -> 145 us (0.912)
  blocking collectives: 11.6 us -> 0 us
  starting transfers between devices: 110 us -> 101 us
  waiting for transfers between devices: 18.6 us -> 27.3 us
  Pallas kernels: 15.1 us -> 12.8 us
    ppermute x15 -> x12, starting transfers between devices: 63.6 us -> 50.5 us  [shifted(): lax.ppermute(value, axis, [(at, (at + step) % size) for at in range(size)])]
    all_to_all x1 -> x0, blocking collectives: 11.6 us -> none  [local(): total = lax.all_to_all(total.reshape(X, PART, B), 'x', 0, 0)]
    all_to_all x1, starting transfers between devices: 7.44 us -> 13.3 us  [local(): parts = lax.all_to_all(chosen, GRID, 0, 0)]
    ppermute x15 -> x12, waiting for transfers between devices: 12.5 us -> 17.7 us  [shifted(): lax.ppermute(value, axis, [(at, (at + step) % size) for at in range(size)])]
    all_to_all x0 -> x1, starting transfers between devices: none -> 3.47 us  [local(): total = lax.all_to_all(total.reshape(X, PART, B), 'x', 0, 0)]
    pallas_call x5 -> x4, Pallas kernels: 7.33 us -> 4.28 us  [the longest x1 2.28 us: other_half(): pl.pallas_call(other_kernel, in_specs=[SMEM] + [anywhere] * 4, out_specs=...]
    all_to_all x1, waiting for transfers between devices: 0.01 us -> 2.72 us  [local(): parts = lax.all_to_all(chosen, GRID, 0, 0)]
    all_to_all x1, starting transfers between devices: 10.8 us -> 8.63 us  [local(): total = lax.all_to_all(total.reshape(ZH, ROWS, B), 'zh', 0, 0)]
  transfers between devices with their start and end apart: 21 -> 19, of which waited for: 8 -> 12; matrix products, arithmetic and copies ran while one was open for 0% -> 1% of each run, Pallas kernels for 2% -> 2%
where the time goes in v2:
time: 145 us; the launch traced here: 144 us
  starting transfers between devices  101 us (70%)
  waiting for transfers between devices  27.3 us (19%)
  Pallas kernels  12.8 us (9%)
  local copies, waits for them, and re-layouts  1.61 us (1%)
    ppermute x12, starting transfers between devices, shifted(): lax.ppermute(value, axis, [(at, (at + step) % size) for at in range(size)])  50.5 us
    ppermute x12, waiting for transfers between devices, shifted(): lax.ppermute(value, axis, [(at, (at + step) % size) for at in range(size)])  17.7 us
    all_to_all x1, starting transfers between devices, local(): parts = lax.all_to_all(chosen, GRID, 0, 0)  13.3 us
    ppermute x2, starting transfers between devices, local(): got = lax.ppermute(send, 'core', swap)  10.7 us
    all_to_all x1, starting transfers between devices, local(): total = lax.all_to_all(total.reshape(ZH, ROWS, B), 'zh', 0, 0)  8.63 us
    all_to_all x1, starting transfers between devices, local(): lax.all_to_all(pieces.reshape(-1, half, lanes), ('core', 'mp', 'root'), 0...  7.12 us
    all_to_all x1, starting transfers between devices, local(): gathered = lax.all_to_all(mine, ('core', 'mp'), 0, 0)  6.87 us
    all_to_all x1, waiting for transfers between devices, local(): gathered = lax.all_to_all(mine, ('core', 'mp'), 0, 0)  4.89 us
  transfers between devices with their start and end apart: 19, of which 12 were waited for; matrix products, arithmetic and copies ran while one was open for 1% of the time, Pallas kernels for 2%

profile of v2, /device:TPU:1, one launch (start us, length us, event | category | flops | bytes accessed | tf_op | source)
XLA Modules:
  0.0 144.0 jit_solution(14452956225385199155)
XLA Ops:
  0.6 0.7 copy-done.1
  1.4 0.8 copy-done.2
  2.2 2.3 %other_half.1 = (bf16[512,1024]{1,0:T(8,128)(2,1)S(1)}, bf16[544,512]{1,0:T(8,128)(2,1)S(1)}, bf16[1024,512]{1,0:T(8,128)(2,1)S(1)}) custom-call(s32[1]{0:T(128)} %bitcast.5.index_ref, bf16[1024,512]{1,0:T(8,128)(2,1)} %acts_ref.1, bf16[1024,1024]{1,0:T(8,128)(2,1)} %grads_ref.1, bf16[1,2,16,512]{3,2,1,0:T(8,128)(2,1)S(1)} %copy-done.1, ...), custom_call_target="tpu_custom_call" | custom-call | flops 536870912 | bytes 3145728 | tf_op jit(solution)/shard_map/other_half/pallas_call | solution.py:92
  4.4 8.8 %collective-permute-start = (bf16[544,512]{1,0:T(8,128)(2,1)S(1)}, bf16[544,512]{1,0:T(8,128)(2,1)S(1)}, u32[]{:S(2)}, u32[]{:S(2)}) collective-permute-start(bf16[544,512]{1,0:T(8,128)(2,1)S(1)} %get-tuple-element.18), channel_id=1, source_target_pairs={{0,16},{16,0},{1,17},{17,1},{2,18},{18,2},{3,19},{19,3},{4,20},{20... | collective-permute-start | bytes 1671176 | tf_op jit(solution)/shard_map/ppermute | solution.py:280
  13.2 0.7 own_half.1.own_ref
  14.0 0.9 collective-permute-done.got_ref
  14.8 1.0 join.1
  15.8 3.5 %all-to-all-start = ((bf16[4,128,512]{2,1,0:T(8,128)(2,1)}), bf16[4,128,512]{2,1,0:T(8,128)(2,1)S(1)}, u32[]{:S(2)}, u32[]{:S(2)}) async-start(bf16[4,128,512]{2,1,0:T(8,128)(2,1)} %bitcast.6), calls=%async_computation | async-start | bytes 1048576 | tf_op jit(solution)/shard_map/all_to_all | solution.py:294
  19.3 0.0 copy-start
  19.3 4.1 %collective-permute-start.1 = (bf16[2,32,512]{2,1,0:T(8,128)(2,1)S(1)}, bf16[2,32,512]{2,1,0:T(8,128)(2,1)S(1)}, u32[]{:S(2)}, u32[]{:S(2)}) collective-permute-start(bf16[2,32,512]{2,1,0:T(8,128)(2,1)S(1)} %get-tuple-element.20.one), channel_id=1, source_target_pairs={{0,32},{32,64},{64,96},{96,0},{1,33},{33,65},{65,97},{97,1},{2,34}... | collective-permute-start | bytes 196616 | tf_op jit(solution)/shard_map/ppermute | solution.py:127
  23.4 10.6 %collective-permute-start.2 = (bf16[2,32,512]{2,1,0:T(8,128)(2,1)S(1)}, bf16[2,32,512]{2,1,0:T(8,128)(2,1)S(1)}, u32[]{:S(2)}, u32[]{:S(2)}) collective-permute-start(bf16[2,32,512]{2,1,0:T(8,128)(2,1)S(1)} %get-tuple-element.20.one), channel_id=1, source_target_pairs={{0,64},{32,96},{64,0},{96,32},{1,65},{33,97},{65,1},{97,33},{2,66}... | collective-permute-start | bytes 196616 | tf_op jit(solution)/shard_map/ppermute | solution.py:127
  34.0 5.2 %collective-permute-start.3 = (bf16[2,32,512]{2,1,0:T(8,128)(2,1)S(1)}, bf16[2,32,512]{2,1,0:T(8,128)(2,1)S(1)}, u32[]{:S(2)}, u32[]{:S(2)}) collective-permute-start(bf16[2,32,512]{2,1,0:T(8,128)(2,1)S(1)} %get-tuple-element.20.one), channel_id=1, source_target_pairs={{0,96},{32,0},{64,32},{96,64},{1,97},{33,1},{65,33},{97,65},{2,98}... | collective-permute-start | bytes 196616 | tf_op jit(solution)/shard_map/ppermute | solution.py:127
  39.2 2.0 %collective-permute-done.2.refs_1_.three = bf16[2,32,512]{2,1,0:T(8,128)(2,1)S(1)} collective-permute-done((bf16[2,32,512]{2,1,0:T(8,128)(2,1)S(1)}, bf16[2,32,512]{2,1,0:T(8,128)(2,1)S(1)}, u32[]{:S(2)}, u32[]{:S(2)}) %collective-permute-start.2) | collective-permute-done | bytes 65568 | tf_op jit(solution)/shard_map/ppermute | solution.py:127
  41.2 6.9 %collective-permute-done.3.refs_2_.four = bf16[2,32,512]{2,1,0:T(8,128)(2,1)S(1)} collective-permute-done((bf16[2,32,512]{2,1,0:T(8,128)(2,1)S(1)}, bf16[2,32,512]{2,1,0:T(8,128)(2,1)S(1)}, u32[]{:S(2)}, u32[]{:S(2)}) %collective-permute-start.3) | collective-permute-done | bytes 65568 | tf_op jit(solution)/shard_map/ppermute | solution.py:127
  48.0 0.7 sum_x.1
  48.8 8.6 %all-to-all-start.1 = ((bf16[4,32,512]{2,1,0:T(8,128)(2,1)}), bf16[4,32,512]{2,1,0:T(8,128)(2,1)S(1)}, u32[]{:S(2)}, u32[]{:S(2)}) async-start(bf16[4,32,512]{2,1,0:T(8,128)(2,1)} %bitcast.7), calls=%async_computation.1 | async-start | bytes 262144 | tf_op jit(solution)/shard_map/all_to_all | solution.py:307
  57.4 0.1 stack.23.info_ref
  57.5 0.6 prec_rows.1
  58.1 3.4 %collective-permute-start.4 = (bf16[128,512]{1,0:T(8,128)(2,1)S(1)}, bf16[128,512]{1,0:T(8,128)(2,1)S(1)}, u32[]{:S(2)}, u32[]{:S(2)}) collective-permute-start(bf16[128,512]{1,0:T(8,128)(2,1)S(1)} %get-tuple-element.21.own_ref), channel_id=1, source_target_pairs={{0,128},{128,256},{256,384},{384,0},{1,129},{129,257},{257,385},{3... | collective-permute-start | bytes 393224 | tf_op jit(solution)/shard_map/ppermute | solution.py:127
  61.4 4.3 %collective-permute-start.5 = (bf16[128,512]{1,0:T(8,128)(2,1)S(1)}, bf16[128,512]{1,0:T(8,128)(2,1)S(1)}, u32[]{:S(2)}, u32[]{:S(2)}) collective-permute-start(bf16[128,512]{1,0:T(8,128)(2,1)S(1)} %get-tuple-element.21.own_ref), channel_id=1, source_target_pairs={{0,256},{128,384},{256,0},{384,128},{1,257},{129,385},{257,1},{385... | collective-permute-start | bytes 393224 | tf_op jit(solution)/shard_map/ppermute | solution.py:127
  65.8 3.1 %collective-permute-start.6 = (bf16[128,512]{1,0:T(8,128)(2,1)S(1)}, bf16[128,512]{1,0:T(8,128)(2,1)S(1)}, u32[]{:S(2)}, u32[]{:S(2)}) collective-permute-start(bf16[128,512]{1,0:T(8,128)(2,1)S(1)} %get-tuple-element.21.own_ref), channel_id=1, source_target_pairs={{0,384},{128,0},{256,128},{384,256},{1,385},{129,1},{257,129},{385... | collective-permute-start | bytes 393224 | tf_op jit(solution)/shard_map/ppermute | solution.py:127
  68.9 0.5 collective-permute-done.5.refs_1_.two
  69.4 2.1 %collective-permute-done.6.refs_2_.three = bf16[128,512]{1,0:T(8,128)(2,1)S(1)} collective-permute-done((bf16[128,512]{1,0:T(8,128)(2,1)S(1)}, bf16[128,512]{1,0:T(8,128)(2,1)S(1)}, u32[]{:S(2)}, u32[]{:S(2)}) %collective-permute-start.6) | collective-permute-done | bytes 131104 | tf_op jit(solution)/shard_map/ppermute | solution.py:127
  71.5 0.7 pack.1
  72.2 7.1 %all-to-all-start.2 = ((bf16[32,16,128]{2,1,0:T(8,128)(2,1)}), bf16[32,16,128]{2,1,0:T(8,128)(2,1)S(1)}, u32[]{:S(2)}, u32[]{:S(2)}) async-start(bf16[32,16,128]{2,1,0:T(8,128)(2,1)} %bitcast.8), calls=%async_computation.2 | async-start | bytes 262144 | tf_op jit(solution)/shard_map/all_to_all | solution.py:316
  79.3 2.7 %collective-permute-start.7 = (bf16[128,512]{1,0:T(8,128)(2,1)S(1)}, bf16[128,512]{1,0:T(8,128)(2,1)S(1)}, u32[]{:S(2)}, u32[]{:S(2)}) collective-permute-start(bf16[128,512]{1,0:T(8,128)(2,1)S(1)} %get-tuple-element.24.own_ref), channel_id=1, source_target_pairs={{0,128},{128,256},{256,384},{384,0},{1,129},{129,257},{257,385},{3... | collective-permute-start | bytes 393224 | tf_op jit(solution)/shard_map/ppermute | solution.py:127
  82.0 4.7 %collective-permute-start.8 = (bf16[128,512]{1,0:T(8,128)(2,1)S(1)}, bf16[128,512]{1,0:T(8,128)(2,1)S(1)}, u32[]{:S(2)}, u32[]{:S(2)}) collective-permute-start(bf16[128,512]{1,0:T(8,128)(2,1)S(1)} %get-tuple-element.24.own_ref), channel_id=1, source_target_pairs={{0,256},{128,384},{256,0},{384,128},{1,257},{129,385},{257,1},{385... | collective-permute-start | bytes 393224 | tf_op jit(solution)/shard_map/ppermute | solution.py:127
  86.7 1.9 %collective-permute-start.9 = (bf16[128,512]{1,0:T(8,128)(2,1)S(1)}, bf16[128,512]{1,0:T(8,128)(2,1)S(1)}, u32[]{:S(2)}, u32[]{:S(2)}) collective-permute-start(bf16[128,512]{1,0:T(8,128)(2,1)S(1)} %get-tuple-element.24.own_ref), channel_id=1, source_target_pairs={{0,384},{128,0},{256,128},{384,256},{1,385},{129,1},{257,129},{385... | collective-permute-start | bytes 393224 | tf_op jit(solution)/shard_map/ppermute | solution.py:127
  88.6 0.9 left.1.left_ref
  89.5 0.0 copy-start.3
  89.5 1.4 collective-permute-done.8.refs_1_.two
  91.0 1.9 %collective-permute-done.9.refs_2_.three = bf16[128,512]{1,0:T(8,128)(2,1)S(1)} collective-permute-done((bf16[128,512]{1,0:T(8,128)(2,1)S(1)}, bf16[128,512]{1,0:T(8,128)(2,1)S(1)}, u32[]{:S(2)}, u32[]{:S(2)}) %collective-permute-start.9) | collective-permute-done | bytes 131104 | tf_op jit(solution)/shard_map/ppermute | solution.py:127
  92.8 1.2 choose.1
  94.0 13.3 %all-to-all-start.3 = ((bf16[16,32,128]{2,1,0:T(8,128)(2,1)}), bf16[16,32,128]{2,1,0:T(8,128)(2,1)S(1)}, u32[]{:S(2)}, u32[]{:S(2)}) async-start(bf16[16,32,128]{2,1,0:T(8,128)(2,1)} %choose.1), calls=%async_computation.3 | async-start | bytes 262144 | tf_op jit(solution)/shard_map/all_to_all | solution.py:329
  107.4 3.1 %collective-permute-start.11 = (bf16[128,512]{1,0:T(8,128)(2,1)S(1)}, bf16[128,512]{1,0:T(8,128)(2,1)S(1)}, u32[]{:S(2)}, u32[]{:S(2)}) collective-permute-start(bf16[128,512]{1,0:T(8,128)(2,1)S(1)} %bitcast_convert_fusion.low_ref), channel_id=1, source_target_pairs={{0,4},{4,8},{8,12},{12,0},{1,5},{5,9},{9,13},{13,1},{2,6},{6,10},{... | collective-permute-start | bytes 393224 | tf_op jit(solution)/shard_map/ppermute | solution.py:127
  110.5 4.4 %collective-permute-start.12 = (bf16[128,512]{1,0:T(8,128)(2,1)S(1)}, bf16[128,512]{1,0:T(8,128)(2,1)S(1)}, u32[]{:S(2)}, u32[]{:S(2)}) collective-permute-start(bf16[128,512]{1,0:T(8,128)(2,1)S(1)} %bitcast_convert_fusion.low_ref), channel_id=1, source_target_pairs={{0,8},{4,12},{8,0},{12,4},{1,9},{5,13},{9,1},{13,5},{2,10},{6,14},... | collective-permute-start | bytes 393224 | tf_op jit(solution)/shard_map/ppermute | solution.py:127
  114.9 3.0 %collective-permute-start.13 = (bf16[128,512]{1,0:T(8,128)(2,1)S(1)}, bf16[128,512]{1,0:T(8,128)(2,1)S(1)}, u32[]{:S(2)}, u32[]{:S(2)}) collective-permute-start(bf16[128,512]{1,0:T(8,128)(2,1)S(1)} %bitcast_convert_fusion.low_ref), channel_id=1, source_target_pairs={{0,12},{4,0},{8,4},{12,8},{1,13},{5,1},{9,5},{13,9},{2,14},{6,2},{... | collective-permute-start | bytes 393224 | tf_op jit(solution)/shard_map/ppermute | solution.py:127
  118.0 1.3 collective-permute-done.12.refs_1_.two
  119.3 1.6 %collective-permute-done.13.refs_2_.three = bf16[128,512]{1,0:T(8,128)(2,1)S(1)} collective-permute-done((bf16[128,512]{1,0:T(8,128)(2,1)S(1)}, bf16[128,512]{1,0:T(8,128)(2,1)S(1)}, u32[]{:S(2)}, u32[]{:S(2)}) %collective-permute-start.13) | collective-permute-done | bytes 131104 | tf_op jit(solution)/shard_map/ppermute | solution.py:127
  120.9 2.7 %all-to-all-done.3.parts_ref = bf16[16,32,128]{2,1,0:T(8,128)(2,1)S(1)} async-done(((bf16[16,32,128]{2,1,0:T(8,128)(2,1)}), bf16[16,32,128]{2,1,0:T(8,128)(2,1)S(1)}, u32[]{:S(2)}, u32[]{:S(2)}) %all-to-all-start.3) | async-done | bytes 131104 | tf_op jit(solution)/shard_map/all_to_all | solution.py:329
  123.7 0.9 spread.1
  124.5 6.9 %all-to-all-start.4 = ((bf16[8,16,16,128]{3,2,1,0:T(8,128)(2,1)}), bf16[8,16,16,128]{3,2,1,0:T(8,128)(2,1)S(1)}, u32[]{:S(2)}, u32[]{:S(2)}) async-start(bf16[8,16,16,128]{3,2,1,0:T(8,128)(2,1)} %spread.1), calls=%async_computation.4 | async-start | bytes 1048576 | tf_op jit(solution)/shard_map/all_to_all | solution.py:337
  131.4 0.8 update.1
  132.2 1.9 %collective-permute-start.10 = (bf16[16,512]{1,0:T(8,128)(2,1)S(1)}, bf16[16,512]{1,0:T(8,128)(2,1)S(1)}, u32[]{:S(2)}, u32[]{:S(2)}) collective-permute-start(bf16[16,512]{1,0:T(8,128)(2,1)S(1)} %get-tuple-element.26), channel_id=1, source_target_pairs={{0,16},{16,0},{1,17},{17,1},{2,18},{18,2},{3,19},{19,3},{4,20},{20... | collective-permute-start | bytes 49160 | tf_op jit(solution)/shard_map/ppermute | solution.py:348
  134.1 1.1 collective-permute-done.10
  135.3 0.6 maximum_select_fusion
  135.9 4.9 %all-to-all-done.4 = bf16[8,16,16,128]{3,2,1,0:T(8,128)(2,1)S(1)} async-done(((bf16[8,16,16,128]{3,2,1,0:T(8,128)(2,1)}), bf16[8,16,16,128]{3,2,1,0:T(8,128)(2,1)S(1)}, u32[]{:S(2)}, u32[]{:S(2)}) %all-to-all-start.4) | async-done | bytes 524320 | tf_op jit(solution)/shard_map/all_to_all | solution.py:337
  140.8 3.2 %refresh.1 = (f32[128,512]{1,0:T(8,128)}, f32[128,512]{1,0:T(8,128)}) custom-call(s32[5]{0:T(128)S(1)} %stack.23.info_ref, s32[16]{0:T(128)S(1)} %copy-done.3, bf16[2,4,16,16,128]{4,3,2,1,0:T(8,128)(2,1)S(1)} %bitcast.16, f32[128,512]{1,0:T(8,128)S(1)} %bitcast.17, bf16[128,512]{1,0:T(8,128)(2,1)S(1)} %bitcast_convert_fusion.low_ref, ...), custom_call_target="tpu_custom_call" | custom-call | flops 603979776 | bytes 1048576 | tf_op jit(solution)/shard_map/refresh/pallas_call | solution.py:353
  (15 shorter events, 0.1 us)
Async XLA Ops:
  0.6 0.8 copy-start.1
  1.4 0.8 copy-start.2
  4.4 10.4 %collective-permute-start = (bf16[544,512]{1,0:T(8,128)(2,1)S(1)}, bf16[544,512]{1,0:T(8,128)(2,1)S(1)}, u32[]{:S(2)}, u32[]{:S(2)}) collective-permute-start(bf16[544,512]{1,0:T(8,128)(2,1)S(1)} %get-tuple-element.18), channel_id=1, source_target_pairs={{0,16},{16,0},{1,17},{17,1},{2,18},{18,2},{3,19},{19,3},{4,20},{20... | collective-permute-start | bytes 1671176 | tf_op jit(solution)/shard_map/ppermute | solution.py:280
  14.8 73.8 %copy-start.4 = (s32[16]{0:T(128)S(1)}, s32[16]{0:T(128)}, u32[]{:S(2)}) copy-start(s32[16]{0:T(128)} %param.12) | copy-start | bytes 196
  15.8 32.3 %all-to-all-start = ((bf16[4,128,512]{2,1,0:T(8,128)(2,1)}), bf16[4,128,512]{2,1,0:T(8,128)(2,1)S(1)}, u32[]{:S(2)}, u32[]{:S(2)}) async-start(bf16[4,128,512]{2,1,0:T(8,128)(2,1)} %bitcast.6), calls=%async_computation | async-start | bytes 1048576 | tf_op jit(solution)/shard_map/all_to_all | solution.py:294
  19.3 88.1 %copy-start = (f32[1,128,512]{2,1,0:T(8,128)S(1)}, f32[1,128,512]{2,1,0:T(8,128)}, u32[]{:S(2)}) copy-start(f32[1,128,512]{2,1,0:T(8,128)} %param.11) | copy-start | bytes 786436
  19.3 19.9 %collective-permute-start.1 = (bf16[2,32,512]{2,1,0:T(8,128)(2,1)S(1)}, bf16[2,32,512]{2,1,0:T(8,128)(2,1)S(1)}, u32[]{:S(2)}, u32[]{:S(2)}) collective-permute-start(bf16[2,32,512]{2,1,0:T(8,128)(2,1)S(1)} %get-tuple-element.20.one), channel_id=1, source_target_pairs={{0,32},{32,64},{64,96},{96,0},{1,33},{33,65},{65,97},{97,1},{2,34}... | collective-permute-start | bytes 196616 | tf_op jit(solution)/shard_map/ppermute | solution.py:127
  23.4 17.8 %collective-permute-start.2 = (bf16[2,32,512]{2,1,0:T(8,128)(2,1)S(1)}, bf16[2,32,512]{2,1,0:T(8,128)(2,1)S(1)}, u32[]{:S(2)}, u32[]{:S(2)}) collective-permute-start(bf16[2,32,512]{2,1,0:T(8,128)(2,1)S(1)} %get-tuple-element.20.one), channel_id=1, source_target_pairs={{0,64},{32,96},{64,0},{96,32},{1,65},{33,97},{65,1},{97,33},{2,66}... | collective-permute-start | bytes 196616 | tf_op jit(solution)/shard_map/ppermute | solution.py:127
  34.0 14.0 %collective-permute-start.3 = (bf16[2,32,512]{2,1,0:T(8,128)(2,1)S(1)}, bf16[2,32,512]{2,1,0:T(8,128)(2,1)S(1)}, u32[]{:S(2)}, u32[]{:S(2)}) collective-permute-start(bf16[2,32,512]{2,1,0:T(8,128)(2,1)S(1)} %get-tuple-element.20.one), channel_id=1, source_target_pairs={{0,96},{32,0},{64,32},{96,64},{1,97},{33,1},{65,33},{97,65},{2,98}... | collective-permute-start | bytes 196616 | tf_op jit(solution)/shard_map/ppermute | solution.py:127
  48.8 22.7 %all-to-all-start.1 = ((bf16[4,32,512]{2,1,0:T(8,128)(2,1)}), bf16[4,32,512]{2,1,0:T(8,128)(2,1)S(1)}, u32[]{:S(2)}, u32[]{:S(2)}) async-start(bf16[4,32,512]{2,1,0:T(8,128)(2,1)} %bitcast.7), calls=%async_computation.1 | async-start | bytes 262144 | tf_op jit(solution)/shard_map/all_to_all | solution.py:307
  58.1 10.8 %collective-permute-start.4 = (bf16[128,512]{1,0:T(8,128)(2,1)S(1)}, bf16[128,512]{1,0:T(8,128)(2,1)S(1)}, u32[]{:S(2)}, u32[]{:S(2)}) collective-permute-start(bf16[128,512]{1,0:T(8,128)(2,1)S(1)} %get-tuple-element.21.own_ref), channel_id=1, source_target_pairs={{0,128},{128,256},{256,384},{384,0},{1,129},{129,257},{257,385},{3... | collective-permute-start | bytes 393224 | tf_op jit(solution)/shard_map/ppermute | solution.py:127
  61.4 8.0 %collective-permute-start.5 = (bf16[128,512]{1,0:T(8,128)(2,1)S(1)}, bf16[128,512]{1,0:T(8,128)(2,1)S(1)}, u32[]{:S(2)}, u32[]{:S(2)}) collective-permute-start(bf16[128,512]{1,0:T(8,128)(2,1)S(1)} %get-tuple-element.21.own_ref), channel_id=1, source_target_pairs={{0,256},{128,384},{256,0},{384,128},{1,257},{129,385},{257,1},{385... | collective-permute-start | bytes 393224 | tf_op jit(solution)/shard_map/ppermute | solution.py:127
  65.8 5.7 %collective-permute-start.6 = (bf16[128,512]{1,0:T(8,128)(2,1)S(1)}, bf16[128,512]{1,0:T(8,128)(2,1)S(1)}, u32[]{:S(2)}, u32[]{:S(2)}) collective-permute-start(bf16[128,512]{1,0:T(8,128)(2,1)S(1)} %get-tuple-element.21.own_ref), channel_id=1, source_target_pairs={{0,384},{128,0},{256,128},{384,256},{1,385},{129,1},{257,129},{385... | collective-permute-start | bytes 393224 | tf_op jit(solution)/shard_map/ppermute | solution.py:127
  72.2 20.7 %all-to-all-start.2 = ((bf16[32,16,128]{2,1,0:T(8,128)(2,1)}), bf16[32,16,128]{2,1,0:T(8,128)(2,1)S(1)}, u32[]{:S(2)}, u32[]{:S(2)}) async-start(bf16[32,16,128]{2,1,0:T(8,128)(2,1)} %bitcast.8), calls=%async_computation.2 | async-start | bytes 262144 | tf_op jit(solution)/shard_map/all_to_all | solution.py:316
  79.3 10.3 %collective-permute-start.7 = (bf16[128,512]{1,0:T(8,128)(2,1)S(1)}, bf16[128,512]{1,0:T(8,128)(2,1)S(1)}, u32[]{:S(2)}, u32[]{:S(2)}) collective-permute-start(bf16[128,512]{1,0:T(8,128)(2,1)S(1)} %get-tuple-element.24.own_ref), channel_id=1, source_target_pairs={{0,128},{128,256},{256,384},{384,0},{1,129},{129,257},{257,385},{3... | collective-permute-start | bytes 393224 | tf_op jit(solution)/shard_map/ppermute | solution.py:127
  82.0 9.0 %collective-permute-start.8 = (bf16[128,512]{1,0:T(8,128)(2,1)S(1)}, bf16[128,512]{1,0:T(8,128)(2,1)S(1)}, u32[]{:S(2)}, u32[]{:S(2)}) collective-permute-start(bf16[128,512]{1,0:T(8,128)(2,1)S(1)} %get-tuple-element.24.own_ref), channel_id=1, source_target_pairs={{0,256},{128,384},{256,0},{384,128},{1,257},{129,385},{257,1},{385... | collective-permute-start | bytes 393224 | tf_op jit(solution)/shard_map/ppermute | solution.py:127
  86.7 6.1 %collective-permute-start.9 = (bf16[128,512]{1,0:T(8,128)(2,1)S(1)}, bf16[128,512]{1,0:T(8,128)(2,1)S(1)}, u32[]{:S(2)}, u32[]{:S(2)}) collective-permute-start(bf16[128,512]{1,0:T(8,128)(2,1)S(1)} %get-tuple-element.24.own_ref), channel_id=1, source_target_pairs={{0,384},{128,0},{256,128},{384,256},{1,385},{129,1},{257,129},{385... | collective-permute-start | bytes 393224 | tf_op jit(solution)/shard_map/ppermute | solution.py:127
  89.5 51.3 %copy-start.3 = (s32[16]{0:T(128)S(1)}, s32[16]{0:T(128)}, u32[]{:S(2)}) copy-start(s32[16]{0:T(128)} %owner_ref.1) | copy-start | bytes 196
  94.0 29.6 %all-to-all-start.3 = ((bf16[16,32,128]{2,1,0:T(8,128)(2,1)}), bf16[16,32,128]{2,1,0:T(8,128)(2,1)S(1)}, u32[]{:S(2)}, u32[]{:S(2)}) async-start(bf16[16,32,128]{2,1,0:T(8,128)(2,1)} %choose.1), calls=%async_computation.3 | async-start | bytes 262144 | tf_op jit(solution)/shard_map/all_to_all | solution.py:329
  107.4 10.6 %collective-permute-start.11 = (bf16[128,512]{1,0:T(8,128)(2,1)S(1)}, bf16[128,512]{1,0:T(8,128)(2,1)S(1)}, u32[]{:S(2)}, u32[]{:S(2)}) collective-permute-start(bf16[128,512]{1,0:T(8,128)(2,1)S(1)} %bitcast_convert_fusion.low_ref), channel_id=1, source_target_pairs={{0,4},{4,8},{8,12},{12,0},{1,5},{5,9},{9,13},{13,1},{2,6},{6,10},{... | collective-permute-start | bytes 393224 | tf_op jit(solution)/shard_map/ppermute | solution.py:127
  110.5 8.8 %collective-permute-start.12 = (bf16[128,512]{1,0:T(8,128)(2,1)S(1)}, bf16[128,512]{1,0:T(8,128)(2,1)S(1)}, u32[]{:S(2)}, u32[]{:S(2)}) collective-permute-start(bf16[128,512]{1,0:T(8,128)(2,1)S(1)} %bitcast_convert_fusion.low_ref), channel_id=1, source_target_pairs={{0,8},{4,12},{8,0},{12,4},{1,9},{5,13},{9,1},{13,5},{2,10},{6,14},... | collective-permute-start | bytes 393224 | tf_op jit(solution)/shard_map/ppermute | solution.py:127
  114.9 6.0 %collective-permute-start.13 = (bf16[128,512]{1,0:T(8,128)(2,1)S(1)}, bf16[128,512]{1,0:T(8,128)(2,1)S(1)}, u32[]{:S(2)}, u32[]{:S(2)}) collective-permute-start(bf16[128,512]{1,0:T(8,128)(2,1)S(1)} %bitcast_convert_fusion.low_ref), channel_id=1, source_target_pairs={{0,12},{4,0},{8,4},{12,8},{1,13},{5,1},{9,5},{13,9},{2,14},{6,2},{... | collective-permute-start | bytes 393224 | tf_op jit(solution)/shard_map/ppermute | solution.py:127
  124.5 16.2 %all-to-all-start.4 = ((bf16[8,16,16,128]{3,2,1,0:T(8,128)(2,1)}), bf16[8,16,16,128]{3,2,1,0:T(8,128)(2,1)S(1)}, u32[]{:S(2)}, u32[]{:S(2)}) async-start(bf16[8,16,16,128]{3,2,1,0:T(8,128)(2,1)} %spread.1), calls=%async_computation.4 | async-start | bytes 1048576 | tf_op jit(solution)/shard_map/all_to_all | solution.py:337
  132.2 3.1 %collective-permute-start.10 = (bf16[16,512]{1,0:T(8,128)(2,1)S(1)}, bf16[16,512]{1,0:T(8,128)(2,1)S(1)}, u32[]{:S(2)}, u32[]{:S(2)}) collective-permute-start(bf16[16,512]{1,0:T(8,128)(2,1)S(1)} %get-tuple-element.26), channel_id=1, source_target_pairs={{0,16},{16,0},{1,17},{17,1},{2,18},{18,2},{3,19},{19,3},{4,20},{20... | collective-permute-start | bytes 49160 | tf_op jit(solution)/shard_map/ppermute | solution.py:348

commit v3 on v2

v3 whole, which is shorter than its diff:
```python
import functools

import jax
import jax.numpy as jnp
from jax import lax
from jax.experimental import pallas as pl
from jax.experimental.pallas import tpu as pltpu
from jax.sharding import Mesh, PartitionSpec as P

B = 512
DECAY = 0.6
KAPPA = 1.25 ** 4
X, ZH, CORE = 4, 4, 2
CHIPS = X * ZH
PART = B // X
ROWS = B // CHIPS
F32, BF16 = jnp.float32, jnp.bfloat16
VMEM = pl.BlockSpec(memory_space=pltpu.VMEM)
SMEM = pl.BlockSpec(memory_space=pltpu.SMEM)


def dot(left, right, left_dim=1, right_dim=0):
    dims = (((left_dim,), (right_dim,)), ((), ()))
    return lax.dot_general(left, right, dims, preferred_element_type=F32)


def params():
    return pltpu.CompilerParams(vmem_limit_bytes=32 * 1024 * 1024)


def cost(flops, nbytes):
    return pl.CostEstimate(flops=flops, bytes_accessed=nbytes, transcendentals=0)


def shape(dims, dtype=BF16):
    return jax.ShapeDtypeStruct(dims, dtype)


def other_kernel(index_ref, acts_ref, grads_ref, turned_ref, out_ref, own_ref, acts_buf, grads_buf, total, sems):
    other = index_ref[0]
    steps, piece = acts_buf.shape[:2]

    def half(which):
        return pl.ds(pl.multiple_of(which * B, B), B)

    copies = []
    for k in range(steps):
        rows = pl.ds(k * piece, piece)
        copies.append(
            (
                pltpu.make_async_copy(acts_ref.at[rows, :], acts_buf.at[k], sems.at[0, k]),
                pltpu.make_async_copy(
                    grads_ref.at[rows, half(other)], grads_buf.at[k], sems.at[1, k]
                ),
            )
        )
        for copy in copies[-1]:
            copy.start()
    last = pltpu.make_async_copy(grads_ref.at[:, half(1 - other)], own_ref, sems.at[2, 0])
    last.start()
    for k, (acts_copy, grads_copy) in enumerate(copies):
        acts_copy.wait()
        turned = acts_buf[k].T
        turned_ref[:, k * piece : (k + 1) * piece] = turned
        grads_copy.wait()
        part = dot(turned, grads_buf[k])
        if k == 0:
            total[...] = part
        elif k < steps - 1:
            total[...] += part
        else:
            out_ref[...] = (total[...] + part).astype(BF16)
    last.wait()


def other_half(acts, grads, index):
    tokens, steps = acts.shape[0], 2
    anywhere = pl.BlockSpec(memory_space=pl.ANY)
    buffer = pltpu.VMEM((steps, tokens // steps, B), BF16)
    return pl.pallas_call(
        other_kernel,
        in_specs=[SMEM, anywhere, anywhere],
        out_specs=[VMEM] * 3,
        out_shape=[shape((B, tokens)), shape((B, B)), shape((tokens, B))],
        scratch_shapes=[
            buffer,
            buffer,
            pltpu.VMEM((B, B), F32),
            pltpu.SemaphoreType.DMA((3, steps)),
        ],
        compiler_params=pltpu.CompilerParams(vmem_limit_bytes=51 * 1024 * 1024),
        cost_estimate=cost(2 * tokens * B * B, 6 * tokens * B),
        name="other_half",
    )(index.reshape(1), acts, grads)


def own_kernel(turned_ref, grads_ref, out_ref):
    out_ref[...] = dot(turned_ref[...], grads_ref[...])


def join_kernel(own_ref, got_ref, out_ref):
    out_ref[...] = (own_ref[...] + got_ref[...].astype(F32)).astype(BF16).T


def shift(value, axis, step):
    size = lax.axis_size(axis)
    return lax.ppermute(value, axis, [(at, (at + step) % size) for at in range(size)])


def shifted(value, axis):
    return [shift(value, axis, step) for step in range(1, lax.axis_size(axis))]


def place(out_ref, parts, index):
    rows = parts[0].shape[0]
    for step, part in enumerate(parts):
        at = (index + len(parts) - step) % len(parts) * rows
        out_ref[pl.ds(pl.multiple_of(at, rows), rows), :] = part[...]


def added(parts_ref):
    total = parts_ref[0].astype(F32)
    for part in range(1, parts_ref.shape[0]):
        total = total + parts_ref[part].astype(F32)
    return total


def sum_kernel(info_ref, parts_ref, mine_ref, theirs_ref, *refs):
    keep_ref, left_ref, send_one, send_two = refs[-5:-1]
    right, core = refs[-1], info_ref[0]
    rows = mine_ref.shape[1]
    for side, ref in enumerate((left_ref, right)):
        ref[pl.ds(pl.multiple_of(core * rows, rows), rows), :] = mine_ref[side]
        ref[pl.ds(pl.multiple_of((1 - core) * rows, rows), rows), :] = theirs_ref[side]
    total = added(parts_ref)
    keep_ref[...] = total
    half = PART // 2
    for part, ref in enumerate((send_one, send_two)):
        ref[:half] = total[part * half : (part + 1) * half].astype(BF16)
        ref[half:] = right[part * rows : (part + 1) * rows]


def middle_kernel(keep_ref, sent_one, sent_two, got_one, got_two, out_ref, send_one, send_two):
    half = PART // 2
    for part, (sent, got, ref) in enumerate(
        ((sent_one, got_one, send_one), (sent_two, got_two, send_two))
    ):
        at = slice(part * half, (part + 1) * half)
        total = keep_ref[at] + got[:half].astype(F32)
        out_ref[at] = total
        rows = sent.shape[0] - half
        ref[:half] = total.astype(BF16)
        ref[half : half + rows] = sent[half:]
        ref[half + rows :] = got[half:]


def pack_kernel(scale, info_ref, keep_ref, sent_one, sent_two, got_one, got_two, *refs):
    grad_ref, pieces_ref, right_ref = refs[-3:]
    zh = info_ref[2]
    half, rows = PART // 2, ROWS // 2
    near = zh + 1 - 2 * (zh % 2)
    far = ZH - 1 - zh
    across = far + 1 - 2 * (far % 2)
    for part, (sent, got, mates) in enumerate(
        (
            (sent_one, got_one, (zh, near, far, across)),
            (sent_two, got_two, (zh, far, near, across)),
        )
    ):
        at = slice(part * half, (part + 1) * half)
        grad_ref[at] = ((keep_ref[at] + got[:half].astype(F32)) * scale).astype(BF16)
        for place_at, mate in enumerate(mates):
            source = (sent, got)[place_at // 2]
            start = half + place_at % 2 * rows
            to = pl.multiple_of(mate * ROWS + part * rows, rows)
            right_ref[pl.ds(to, rows), :] = source[start : start + rows]
    cores, n_mp, n_root, rows, lanes = pieces_ref.shape
    for c in range(cores):
        for r in range(n_root):
            at = (c * n_root + r) * rows
            for m in range(n_mp):
                pieces_ref[c, m, r] = grad_ref[at : at + rows, m * lanes : (m + 1) * lanes]


def choose_kernel(info_ref, place_ref, blocks_ref, *refs):
    out_ref = refs[-1]
    for w in range(X):
        out_ref[w] = blocks_ref[place_ref[w * ZH + info_ref[2]]]


def spread_kernel(parts_ref, *refs):
    out_ref = refs[-1]
    for peer in range(out_ref.shape[0]):
        out_ref[peer] = parts_ref[...]


def update_kernel(info_ref, *refs):
    x = info_ref[1]
    sides, (grad, right), outs, (left, total) = refs[:4], refs[4:6], refs[6:10], refs[10:]
    place(left, sides, x)
    total[...] = dot(dot(left[...], grad[...], 1, 1).astype(BF16), right[...])
    for step, ref in enumerate(outs):
        at = pl.multiple_of((x + step) % X * ROWS, ROWS)
        ref[...] = total[pl.ds(at, ROWS), :].astype(ref.dtype)


def halves_kernel(info_ref, own_ref, one, two, three, keep_ref, send_ref):
    core = info_ref[0]
    total = own_ref[...]
    for got in (one, two, three):
        total = total + got[...].astype(F32)
    half = keep_ref.shape[0]
    keep_ref[...] = jnp.where(core == 0, total[:half], total[half:]).astype(BF16)
    send_ref[...] = jnp.where(core == 0, total[half:], total[:half]).astype(BF16)


def refresh_kernel(info_ref, owner_ref, pieces_ref, own_ref, low_ref, one, two, three, stats_ref, roots_ref, block, product, old):
    core, x, zh, mp, root = (info_ref[at] for at in range(5))
    n_mp, n_root = pieces_ref.shape[1:3]
    rows, lanes = pieces_ref.shape[4:]
    quarter = own_ref.shape[0]
    for c in range(CORE):
        for m in range(n_mp):
            for r in range(n_root):
                for w in range(X):
                    at = w * PART + (c * n_root + r) * rows
                    block[at : at + rows, m * lanes : (m + 1) * lanes] = pieces_ref[c, m, r, w]

    place(old, (low_ref, one, two, three), mp)

    @pl.when(core == 0)
    def _():
        value = block[...]
        product[...] = dot(value, value, 0, 0) * ((1.0 - DECAY) / B)

    @pl.when(core != 0)
    def _():
        value = block[...]
        product[...] = dot(value, value, 1, 1) * ((1.0 - DECAY) / B)

    mine = pl.ds(pl.multiple_of(mp * quarter, quarter), quarter)
    stats_rows = DECAY * own_ref[...] + product[mine, :]
    full = DECAY * old[...].astype(F32) + product[...]
    square = jnp.sum(full * full, axis=0, keepdims=True)
    factor = 2.5 / jnp.sqrt(jnp.sum(square, axis=1, keepdims=True))
    block[...] = (full * (factor * 0.2)).astype(BF16)
    e_rows = stats_rows * (factor * 0.2)
    y = e_rows
    for _ in range(5):
        y = y - dot(y.astype(BF16), block[...])
    line = lax.broadcasted_iota(jnp.int32, (quarter, B), 0) + mp * quarter
    unit = jnp.where(line == lax.broadcasted_iota(jnp.int32, (quarter, B), 1), 1.0, 0.0)
    roots_rows = (jnp.sqrt(jnp.sqrt(factor)) * 1.5625) * (unit - e_rows - KAPPA * y)
    owned = owner_ref[x * ZH + zh] == root
    stats_ref[...] = jnp.where(owned, stats_rows, 0.0)
    roots_ref[...] = jnp.where(owned, roots_rows, 0.0)


def kernel_call(kernel, name, in_specs, out_shape, scratch=(), work=None, awaited=0):
    return pl.pallas_call(
        kernel,
        in_specs=in_specs + [pl.BlockSpec(memory_space=pl.ANY)] * awaited,
        out_specs=[VMEM] * len(out_shape),
        out_shape=out_shape,
        scratch_shapes=list(scratch),
        compiler_params=params(),
        cost_estimate=work,
        name=name,
    )


def local(acts, grads_out, prec_left, prec_right, stats_old, listed, owner):
    x, zh, core = (lax.axis_index(name) for name in ("x", "zh", "core"))
    mp, root = lax.axis_index("mp"), lax.axis_index("root")
    n_mp, n_root = lax.axis_size("mp"), lax.axis_size("root")
    quarter = B // n_mp
    lanes, half = B // n_mp, ROWS // CORE
    tokens = acts.shape[0] * CHIPS * CORE
    swap = ((0, 1), (1, 0))
    info = jnp.stack([core, x, zh, mp, root])

    turned, send, grads_own = other_half(acts, grads_out, 1 - core)
    got = lax.ppermute(send, "core", swap)
    (own,) = kernel_call(
        own_kernel,
        "own_half",
        [VMEM, VMEM],
        [shape((B, B), F32)],
        work=cost(2 * acts.shape[0] * B * B, 4 * acts.shape[0] * B),
    )(turned, grads_own)
    (total,) = kernel_call(join_kernel, "join", [VMEM, VMEM], [shape((B, B))])(own, got)
    total = lax.all_to_all(total.reshape(X, PART, B), "x", 0, 0)
    prec = jnp.stack([prec_left[0], prec_right[0]])
    mine = lax.dynamic_index_in_dim(prec, core, 1, keepdims=False)
    theirs = lax.ppermute(
        lax.dynamic_index_in_dim(prec, 1 - core, 1, keepdims=False), "core", swap
    )
    old_own = stats_old[0]
    old_low = old_own.astype(BF16)
    olds = [old_low] + shifted(old_low, "mp")
    keep, left_rows, *sends = kernel_call(
        sum_kernel,
        "sum_x",
        [SMEM] + [VMEM] * 3,
        [shape((PART, B), F32), shape((ROWS, B))] + [shape((PART // 2 + half, B))] * 2,
        [pltpu.VMEM((ROWS, B), BF16)],
        awaited=3,
    )(info, total, mine, theirs, *olds[1:])
    near = [(z, z ^ 1) for z in range(ZH)]
    far = [(z, ZH - 1 - z) for z in range(ZH)]
    got = [lax.ppermute(sends[0], "zh", near), lax.ppermute(sends[1], "zh", far)]
    lefts = [left_rows] + shifted(left_rows, "x")
    keep, *sends = kernel_call(
        middle_kernel,
        "middle",
        [VMEM] * 5,
        [shape((PART, B), F32)] + [shape((PART // 2 + 2 * half, B))] * 2,
    )(keep, *sends, *got)
    got = [lax.ppermute(sends[0], "zh", far), lax.ppermute(sends[1], "zh", near)]
    grad, pieces, right_part = kernel_call(
        functools.partial(pack_kernel, tokens ** -0.5),
        "pack",
        [SMEM] + [VMEM] * 5,
        [shape((PART, B)), shape((CORE, n_mp, n_root, half, lanes)), shape((PART, B))],
        awaited=3,
    )(info, keep, *sends, *got, *lefts[1:])

    blocks = lax.all_to_all(pieces.reshape(-1, half, lanes), ("core", "mp", "root"), 0, 0)

    own, *sends = kernel_call(
        update_kernel,
        "update",
        [SMEM] + [VMEM] * 6,
        [shape((ROWS, B), F32)] + [shape((ROWS, B))] * 3,
        [pltpu.VMEM((PART, B), BF16), pltpu.VMEM((PART, B), F32)],
        cost(2 * PART * B * (PART + B), 6 * PART * B),
    )(info, *lefts, grad, right_part)
    got = [shift(send, "x", step) for step, send in enumerate(sends, 1)]

    at = (listed % 2) * (n_mp * n_root) + listed // 2
    (chosen,) = kernel_call(
        choose_kernel, "choose", [SMEM, SMEM, VMEM], [shape((X, half, lanes))], awaited=3
    )(info, at, blocks, *got)
    parts = lax.all_to_all(chosen, "x", 0, 0)
    (mine,) = kernel_call(
        spread_kernel, "spread", [VMEM], [shape((CORE * n_mp * n_root, X, half, lanes))]
    )(parts)
    gathered = lax.all_to_all(mine, ("core", "mp", "root"), 0, 0)
    gathered = gathered.reshape((CORE, n_mp, n_root) + gathered.shape[1:])
    keep, send = kernel_call(
        halves_kernel, "halves", [SMEM] + [VMEM] * 4, [shape((half, B))] * 2
    )(info, own, *got)
    got = lax.ppermute(send, "core", swap)
    update = jnp.where(
        core == 0, jnp.concatenate([keep, got], 1), jnp.concatenate([got, keep], 1)
    )

    new_stats, new_roots = kernel_call(
        refresh_kernel,
        "refresh",
        [SMEM, SMEM] + [VMEM] * 6,
        [shape((quarter, B), F32)] * 2,
        [pltpu.VMEM((B, B), BF16), pltpu.VMEM((B, B), F32), pltpu.VMEM((B, B), BF16)],
        cost(2 * B ** 3 + 10 * quarter * B * B, 2 * B * B * 2),
    )(info, owner, gathered, old_own, *olds)
    return update[None], new_stats[None, None], new_roots[None, None]


def solution(mesh):
    n_dp, n_mp, n_root = mesh.devices.shape
    fine = Mesh(
        mesh.devices.reshape(X, ZH, CORE, n_mp, n_root), ("x", "zh", "core", "mp", "root")
    )
    dp = ("x", "zh", "core")
    in_specs = (
        P(dp, "mp"),
        P(dp, "root"),
        P("mp", "root", dp, None),
        P("mp", "root", dp, None),
        P(dp, "mp", None),
        P(),
        P(),
    )
    out_specs = (P("mp", dp, "root"), P("root", dp, "mp", None), P("root", dp, "mp", None))
    return jax.shard_map(local, mesh=fine, in_specs=in_specs, out_specs=out_specs, check_vma=False)
```

time: 145 us -> 138 us (0.952)
  starting transfers between devices: 101 us -> 90.9 us
  blocking collectives: 0 us -> 6.56 us
  waiting for transfers between devices: 27.3 us -> 25.5 us
  local copies, waits for them, and re-layouts: 1.61 us -> 0.14 us
    all_to_all x3 -> x1, starting transfers between devices: 28.8 us -> 10.5 us  [local(): gathered = lax.all_to_all(mine, ('core', 'mp', 'root'), 0, 0)]
    all_to_all x0 -> x1, blocking collectives: none -> 6.56 us  [local(): parts = lax.all_to_all(chosen, 'x', 0, 0)]
    ppermute x12 -> x14, starting transfers between devices: 50.5 us -> 56.5 us  [the longest x9 28.8 us: shift(): lax.ppermute(value, axis, [(at, (at + step) % size) for at in range(size)])]
    ppermute x12 -> x14, waiting for transfers between devices: 17.7 us -> 12.8 us  [the longest x1 6.27 us: local(): lax.ppermute(sends[1], 'zh', far)]
    all_to_all x3 -> x1, waiting for transfers between devices: 7.61 us -> 11 us  [local(): gathered = lax.all_to_all(mine, ('core', 'mp', 'root'), 0, 0)]
    all_to_all x1, starting transfers between devices: 7.12 us -> 9.48 us  [local(): lax.all_to_all(pieces.reshape(-1, half, lanes), ('core', 'mp', 'root'), 0...]
    unnamed x10 -> x11, local copies, waits for them, and re-layouts: 1.52 us -> 0.04 us
  transfers between devices with their start and end apart: 19 -> 19, of which waited for: 12 -> 9; matrix products, arithmetic and copies ran while one was open for 1% -> 1% of each run, Pallas kernels for 2% -> 2%
where the time goes in v3:
time: 138 us; the launch traced here: 137 us
  starting transfers between devices  90.9 us (66%)
  waiting for transfers between devices  25.5 us (18%)
  Pallas kernels  12 us (9%)
  blocking collectives  6.56 us (5%)
    ppermute x9, starting transfers between devices, shift(): lax.ppermute(value, axis, [(at, (at + step) % size) for at in range(size)])  28.8 us
    all_to_all x1, waiting for transfers between devices, local(): gathered = lax.all_to_all(mine, ('core', 'mp', 'root'), 0, 0)  11 us
    ppermute x2, starting transfers between devices, local(): got = lax.ppermute(send, 'core', swap)  10.9 us
    all_to_all x1, starting transfers between devices, local(): gathered = lax.all_to_all(mine, ('core', 'mp', 'root'), 0, 0)  10.5 us
    all_to_all x1, starting transfers between devices, local(): lax.all_to_all(pieces.reshape(-1, half, lanes), ('core', 'mp', 'root'), 0...  9.48 us
    ppermute x1, starting transfers between devices, local(): lax.ppermute(sends[1], 'zh', far)  8.82 us
    ppermute x1, starting transfers between devices, local(): lax.ppermute(sends[0], 'zh', far)  8.16 us
    all_to_all x1, blocking collectives, local(): parts = lax.all_to_all(chosen, 'x', 0, 0)  6.56 us
  transfers between devices with their start and end apart: 19, of which 9 were waited for; matrix products, arithmetic and copies ran while one was open for 1% of the time, Pallas kernels for 2%

profile of v3, /device:TPU:1, one launch (start us, length us, event | category | flops | bytes accessed | tf_op | source)
XLA Modules:
  0.0 136.8 jit_solution(18392941654904130796)
XLA Ops:
  0.6 2.3 %other_half.1 = (bf16[512,1024]{1,0:T(8,128)(2,1)S(1)}, bf16[512,512]{1,0:T(8,128)(2,1)S(1)}, bf16[1024,512]{1,0:T(8,128)(2,1)S(1)}) custom-call(s32[1]{0:T(128)} %bitcast.5.index_ref, bf16[1024,512]{1,0:T(8,128)(2,1)} %acts_ref.1, bf16[1024,1024]{1,0:T(8,128)(2,1)} %grads_ref.1), custom_call_target="tpu_custom_call" | custom-call | flops 536870912 | bytes 3145728 | tf_op jit(solution)/shard_map/other_half/pallas_call | solution.py:80
  2.9 8.8 %collective-permute-start = (bf16[512,512]{1,0:T(8,128)(2,1)S(1)}, bf16[512,512]{1,0:T(8,128)(2,1)S(1)}, u32[]{:S(2)}, u32[]{:S(2)}) collective-permute-start(bf16[512,512]{1,0:T(8,128)(2,1)S(1)} %get-tuple-element.26), channel_id=1, source_target_pairs={{0,16},{16,0},{1,17},{17,1},{2,18},{18,2},{3,19},{19,3},{4,20},{20... | collective-permute-start | bytes 1572872 | tf_op jit(solution)/shard_map/ppermute | solution.py:283
  11.7 0.7 own_half.1.own_ref
  12.4 0.0 copy-start
  12.4 0.0 copy-start.2
  12.4 0.0 copy-start.3
  12.4 0.8 collective-permute-done.got_ref
  13.2 1.0 join.1
  14.2 3.5 %all-to-all-start = ((bf16[4,128,512]{2,1,0:T(8,128)(2,1)}), bf16[4,128,512]{2,1,0:T(8,128)(2,1)S(1)}, u32[]{:S(2)}, u32[]{:S(2)}) async-start(bf16[4,128,512]{2,1,0:T(8,128)(2,1)} %bitcast.6), calls=%async_computation | async-start | bytes 1048576 | tf_op jit(solution)/shard_map/all_to_all | solution.py:292
  17.7 0.0 copy-start.4
  17.8 1.9 %collective-permute-start.2 = (bf16[128,512]{1,0:T(8,128)(2,1)S(1)}, bf16[128,512]{1,0:T(8,128)(2,1)S(1)}, u32[]{:S(2)}, u32[]{:S(2)}) collective-permute-start(bf16[128,512]{1,0:T(8,128)(2,1)S(1)} %bitcast_convert_fusion.low_ref), channel_id=1, source_target_pairs={{0,4},{4,8},{8,12},{12,0},{1,5},{5,9},{9,13},{13,1},{2,6},{6,10},{... | collective-permute-start | bytes 393224 | tf_op jit(solution)/shard_map/ppermute | solution.py:107
  19.7 1.9 %collective-permute-start.3 = (bf16[128,512]{1,0:T(8,128)(2,1)S(1)}, bf16[128,512]{1,0:T(8,128)(2,1)S(1)}, u32[]{:S(2)}, u32[]{:S(2)}) collective-permute-start(bf16[128,512]{1,0:T(8,128)(2,1)S(1)} %bitcast_convert_fusion.low_ref), channel_id=1, source_target_pairs={{0,8},{4,12},{8,0},{12,4},{1,9},{5,13},{9,1},{13,5},{2,10},{6,14},... | collective-permute-start | bytes 393224 | tf_op jit(solution)/shard_map/ppermute | solution.py:107
  21.6 4.6 %collective-permute-start.4 = (bf16[128,512]{1,0:T(8,128)(2,1)S(1)}, bf16[128,512]{1,0:T(8,128)(2,1)S(1)}, u32[]{:S(2)}, u32[]{:S(2)}) collective-permute-start(bf16[128,512]{1,0:T(8,128)(2,1)S(1)} %bitcast_convert_fusion.low_ref), channel_id=1, source_target_pairs={{0,12},{4,0},{8,4},{12,8},{1,13},{5,1},{9,5},{13,9},{2,14},{6,2},{... | collective-permute-start | bytes 393224 | tf_op jit(solution)/shard_map/ppermute | solution.py:107
  26.3 2.8 %collective-permute-start.1 = (bf16[2,16,512]{2,1,0:T(8,128)(2,1)S(1)}, bf16[2,16,512]{2,1,0:T(8,128)(2,1)S(1)}, u32[]{:S(2)}, u32[]{:S(2)}) collective-permute-start(bf16[2,16,512]{2,1,0:T(8,128)(2,1)S(1)} %get-tuple-element.45), channel_id=1, source_target_pairs={{0,16},{16,0},{1,17},{17,1},{2,18},{18,2},{3,19},{19,3},{4,20},{20... | collective-permute-start | bytes 98312 | tf_op jit(solution)/shard_map/ppermute | solution.py:295
  29.1 0.1 stack.26.info_ref
  29.2 0.7 collective-permute-done.1.theirs_ref
  30.0 0.8 collective-permute-done.4.refs_2_.three
  30.8 0.0 all-to-all-done.parts_ref
  30.8 0.6 sum_x.1
  31.4 0.0 copy-start.1
  31.4 6.0 %collective-permute-start.8 = (bf16[80,512]{1,0:T(8,128)(2,1)S(1)}, bf16[80,512]{1,0:T(8,128)(2,1)S(1)}, u32[]{:S(2)}, u32[]{:S(2)}) collective-permute-start(bf16[80,512]{1,0:T(8,128)(2,1)S(1)} %get-tuple-element.29.sent_one), channel_id=1, source_target_pairs={{0,32},{32,0},{64,96},{96,64},{1,33},{33,1},{65,97},{97,65},{2,34}... | collective-permute-start | bytes 245768 | tf_op jit(solution)/shard_map/ppermute | solution.py:311
  37.4 8.8 %collective-permute-start.9 = (bf16[80,512]{1,0:T(8,128)(2,1)S(1)}, bf16[80,512]{1,0:T(8,128)(2,1)S(1)}, u32[]{:S(2)}, u32[]{:S(2)}) collective-permute-start(bf16[80,512]{1,0:T(8,128)(2,1)S(1)} %get-tuple-element.30.sent_two), channel_id=1, source_target_pairs={{0,96},{32,64},{64,32},{96,0},{1,97},{33,65},{65,33},{97,1},{2,98}... | collective-permute-start | bytes 245768 | tf_op jit(solution)/shard_map/ppermute | solution.py:311
  46.3 0.5 collective-permute-done.8.got_one
  46.8 6.3 %collective-permute-done.9.got_two = bf16[80,512]{1,0:T(8,128)(2,1)S(1)} collective-permute-done((bf16[80,512]{1,0:T(8,128)(2,1)S(1)}, bf16[80,512]{1,0:T(8,128)(2,1)S(1)}, u32[]{:S(2)}, u32[]{:S(2)}) %collective-permute-start.9) | collective-permute-done | bytes 81952 | tf_op jit(solution)/shard_map/ppermute | solution.py:311
  53.1 8.2 %collective-permute-start.10 = (bf16[96,512]{1,0:T(8,128)(2,1)S(1)}, bf16[96,512]{1,0:T(8,128)(2,1)S(1)}, u32[]{:S(2)}, u32[]{:S(2)}) collective-permute-start(bf16[96,512]{1,0:T(8,128)(2,1)S(1)} %get-tuple-element.32.sent_one), channel_id=1, source_target_pairs={{0,96},{32,64},{64,32},{96,0},{1,97},{33,65},{65,33},{97,1},{2,98}... | collective-permute-start | bytes 294920 | tf_op jit(solution)/shard_map/ppermute | solution.py:319
  61.2 1.9 %collective-permute-start.11 = (bf16[96,512]{1,0:T(8,128)(2,1)S(1)}, bf16[96,512]{1,0:T(8,128)(2,1)S(1)}, u32[]{:S(2)}, u32[]{:S(2)}) collective-permute-start(bf16[96,512]{1,0:T(8,128)(2,1)S(1)} %get-tuple-element.33.sent_two), channel_id=1, source_target_pairs={{0,32},{32,0},{64,96},{96,64},{1,33},{33,1},{65,97},{97,65},{2,34}... | collective-permute-start | bytes 294920 | tf_op jit(solution)/shard_map/ppermute | solution.py:319
  63.2 3.7 %collective-permute-start.5 = (bf16[32,512]{1,0:T(8,128)(2,1)S(1)}, bf16[32,512]{1,0:T(8,128)(2,1)S(1)}, u32[]{:S(2)}, u32[]{:S(2)}) collective-permute-start(bf16[32,512]{1,0:T(8,128)(2,1)S(1)} %get-tuple-element.27.refs_0_), channel_id=1, source_target_pairs={{0,128},{128,256},{256,384},{384,0},{1,129},{129,257},{257,385},{3... | collective-permute-start | bytes 98312 | tf_op jit(solution)/shard_map/ppermute | solution.py:107
  66.8 4.3 %collective-permute-start.6 = (bf16[32,512]{1,0:T(8,128)(2,1)S(1)}, bf16[32,512]{1,0:T(8,128)(2,1)S(1)}, u32[]{:S(2)}, u32[]{:S(2)}) collective-permute-start(bf16[32,512]{1,0:T(8,128)(2,1)S(1)} %get-tuple-element.27.refs_0_), channel_id=1, source_target_pairs={{0,256},{128,384},{256,0},{384,128},{1,257},{129,385},{257,1},{385... | collective-permute-start | bytes 98312 | tf_op jit(solution)/shard_map/ppermute | solution.py:107
  71.1 3.1 %collective-permute-start.7 = (bf16[32,512]{1,0:T(8,128)(2,1)S(1)}, bf16[32,512]{1,0:T(8,128)(2,1)S(1)}, u32[]{:S(2)}, u32[]{:S(2)}) collective-permute-start(bf16[32,512]{1,0:T(8,128)(2,1)S(1)} %get-tuple-element.27.refs_0_), channel_id=1, source_target_pairs={{0,384},{128,0},{256,128},{384,256},{1,385},{129,1},{257,129},{385... | collective-permute-start | bytes 98312 | tf_op jit(solution)/shard_map/ppermute | solution.py:107
  74.2 0.0 collective-permute-done.6.refs_1_.refs_2_
  74.2 1.8 %collective-permute-done.7.refs_2_.refs_3_ = bf16[32,512]{1,0:T(8,128)(2,1)S(1)} collective-permute-done((bf16[32,512]{1,0:T(8,128)(2,1)S(1)}, bf16[32,512]{1,0:T(8,128)(2,1)S(1)}, u32[]{:S(2)}, u32[]{:S(2)}) %collective-permute-start.7) | collective-permute-done | bytes 32800 | tf_op jit(solution)/shard_map/ppermute | solution.py:107
  76.1 1.3 pack.1
  77.4 9.5 %all-to-all-start.1 = ((bf16[32,16,128]{2,1,0:T(8,128)(2,1)}), bf16[32,16,128]{2,1,0:T(8,128)(2,1)S(1)}, u32[]{:S(2)}, u32[]{:S(2)}) async-start(bf16[32,16,128]{2,1,0:T(8,128)(2,1)} %bitcast.12), calls=%async_computation.1 | async-start | bytes 262144 | tf_op jit(solution)/shard_map/all_to_all | solution.py:328
  86.8 0.9 update.1
  87.8 1.9 %collective-permute-start.12 = (bf16[32,512]{1,0:T(8,128)(2,1)S(1)}, bf16[32,512]{1,0:T(8,128)(2,1)S(1)}, u32[]{:S(2)}, u32[]{:S(2)}) collective-permute-start(bf16[32,512]{1,0:T(8,128)(2,1)S(1)} %get-tuple-element.37), channel_id=1, source_target_pairs={{0,128},{128,256},{256,384},{384,0},{1,129},{129,257},{257,385},{3... | collective-permute-start | bytes 98312 | tf_op jit(solution)/shard_map/ppermute | solution.py:107
  89.7 5.5 %collective-permute-start.13 = (bf16[32,512]{1,0:T(8,128)(2,1)S(1)}, bf16[32,512]{1,0:T(8,128)(2,1)S(1)}, u32[]{:S(2)}, u32[]{:S(2)}) collective-permute-start(bf16[32,512]{1,0:T(8,128)(2,1)S(1)} %get-tuple-element.38), channel_id=1, source_target_pairs={{0,256},{128,384},{256,0},{384,128},{1,257},{129,385},{257,1},{385... | collective-permute-start | bytes 98312 | tf_op jit(solution)/shard_map/ppermute | solution.py:107
  95.2 1.9 %collective-permute-start.14 = (bf16[32,512]{1,0:T(8,128)(2,1)S(1)}, bf16[32,512]{1,0:T(8,128)(2,1)S(1)}, u32[]{:S(2)}, u32[]{:S(2)}) collective-permute-start(bf16[32,512]{1,0:T(8,128)(2,1)S(1)} %get-tuple-element.39), channel_id=1, source_target_pairs={{0,384},{128,0},{256,128},{384,256},{1,385},{129,1},{257,129},{385... | collective-permute-start | bytes 98312 | tf_op jit(solution)/shard_map/ppermute | solution.py:107
  97.2 2.7 %collective-permute-done.14.three.refs_2_ = bf16[32,512]{1,0:T(8,128)(2,1)S(1)} collective-permute-done((bf16[32,512]{1,0:T(8,128)(2,1)S(1)}, bf16[32,512]{1,0:T(8,128)(2,1)S(1)}, u32[]{:S(2)}, u32[]{:S(2)}) %collective-permute-start.14) | collective-permute-done | bytes 32800 | tf_op jit(solution)/shard_map/ppermute | solution.py:107
  99.8 0.6 choose.1
  100.4 6.6 %all_to_all.20.parts_ref = bf16[4,16,128]{2,1,0:T(8,128)(2,1)S(1)} all-to-all(bf16[4,16,128]{2,1,0:T(8,128)(2,1)S(1)} %choose.1), channel_id=1, replica_groups=mesh['x'=4,'zh'=4,'core'=2,'mp'=4,'root'=4] {'x'}, dimensions={0} | all-to-all | bytes 32768 | tf_op jit(solution)/shard_map/all_to_all | solution.py:344
  107.0 0.9 spread.1
  107.8 10.5 %all-to-all-start.3 = ((bf16[32,4,16,128]{3,2,1,0:T(8,128)(2,1)}), bf16[32,4,16,128]{3,2,1,0:T(8,128)(2,1)S(1)}, u32[]{:S(2)}, u32[]{:S(2)}) async-start(bf16[32,4,16,128]{3,2,1,0:T(8,128)(2,1)} %spread.1), calls=%async_computation.3 | async-start | bytes 1048576 | tf_op jit(solution)/shard_map/all_to_all | solution.py:348
  118.4 0.6 halves.1
  118.9 2.1 %collective-permute-start.15 = (bf16[16,512]{1,0:T(8,128)(2,1)S(1)}, bf16[16,512]{1,0:T(8,128)(2,1)S(1)}, u32[]{:S(2)}, u32[]{:S(2)}) collective-permute-start(bf16[16,512]{1,0:T(8,128)(2,1)S(1)} %get-tuple-element.41), channel_id=1, source_target_pairs={{0,16},{16,0},{1,17},{17,1},{2,18},{18,2},{3,19},{19,3},{4,20},{20... | collective-permute-start | bytes 49160 | tf_op jit(solution)/shard_map/ppermute | solution.py:353
  121.1 0.9 collective-permute-done.15
  122.0 0.6 maximum_select_fusion
  122.6 11.0 %all-to-all-done.3 = bf16[32,4,16,128]{3,2,1,0:T(8,128)(2,1)S(1)} async-done(((bf16[32,4,16,128]{3,2,1,0:T(8,128)(2,1)}), bf16[32,4,16,128]{3,2,1,0:T(8,128)(2,1)S(1)}, u32[]{:S(2)}, u32[]{:S(2)}) %all-to-all-start.3) | async-done | bytes 524320 | tf_op jit(solution)/shard_map/all_to_all | solution.py:348
  133.6 3.2 %refresh.1 = (f32[128,512]{1,0:T(8,128)}, f32[128,512]{1,0:T(8,128)}) custom-call(s32[5]{0:T(128)S(1)} %stack.26.info_ref, s32[16]{0:T(128)S(1)} %copy-done.1, bf16[2,4,4,4,16,128]{5,4,3,2,1,0:T(8,128)(2,1)S(1)} %bitcast.19, f32[128,512]{1,0:T(8,128)S(1)} %bitcast.20, bf16[128,512]{1,0:T(8,128)(2,1)S(1)} %bitcast_convert_fusion.low_ref, ...), custom_call_target="tpu_custom_call" | custom-call | flops 603979776 | bytes 1048576 | tf_op jit(solution)/shard_map/refresh/pallas_call | solution.py:358
  (19 shorter events, 0.1 us)
Async XLA Ops:
  2.9 10.3 %collective-permute-start = (bf16[512,512]{1,0:T(8,128)(2,1)S(1)}, bf16[512,512]{1,0:T(8,128)(2,1)S(1)}, u32[]{:S(2)}, u32[]{:S(2)}) collective-permute-start(bf16[512,512]{1,0:T(8,128)(2,1)S(1)} %get-tuple-element.26), channel_id=1, source_target_pairs={{0,16},{16,0},{1,17},{17,1},{2,18},{18,2},{3,19},{19,3},{4,20},{20... | collective-permute-start | bytes 1572872 | tf_op jit(solution)/shard_map/ppermute | solution.py:283
  12.4 5.3 %copy-start = (f32[1,128,512]{2,1,0:T(8,128)S(1)}, f32[1,128,512]{2,1,0:T(8,128)}, u32[]{:S(2)}) copy-start(f32[1,128,512]{2,1,0:T(8,128)} %param.11) | copy-start | bytes 786436
  12.4 13.8 %copy-start.2 = (bf16[1,2,16,512]{3,2,1,0:T(8,128)(2,1)S(1)}, bf16[1,2,16,512]{3,2,1,0:T(8,128)(2,1)}, u32[]{:S(2)}) copy-start(bf16[1,2,16,512]{3,2,1,0:T(8,128)(2,1)} %param.9) | copy-start | bytes 98308
  12.4 13.8 %copy-start.3 = (bf16[1,2,16,512]{3,2,1,0:T(8,128)(2,1)S(1)}, bf16[1,2,16,512]{3,2,1,0:T(8,128)(2,1)}, u32[]{:S(2)}) copy-start(bf16[1,2,16,512]{3,2,1,0:T(8,128)(2,1)} %param.10) | copy-start | bytes 98308
  14.2 16.5 %all-to-all-start = ((bf16[4,128,512]{2,1,0:T(8,128)(2,1)}), bf16[4,128,512]{2,1,0:T(8,128)(2,1)S(1)}, u32[]{:S(2)}, u32[]{:S(2)}) async-start(bf16[4,128,512]{2,1,0:T(8,128)(2,1)} %bitcast.6), calls=%async_computation | async-start | bytes 1048576 | tf_op jit(solution)/shard_map/all_to_all | solution.py:292
  17.7 79.4 %copy-start.4 = (s32[16]{0:T(128)S(1)}, s32[16]{0:T(128)}, u32[]{:S(2)}) copy-start(s32[16]{0:T(128)} %param.12) | copy-start | bytes 196
  17.8 12.2 %collective-permute-start.2 = (bf16[128,512]{1,0:T(8,128)(2,1)S(1)}, bf16[128,512]{1,0:T(8,128)(2,1)S(1)}, u32[]{:S(2)}, u32[]{:S(2)}) collective-permute-start(bf16[128,512]{1,0:T(8,128)(2,1)S(1)} %bitcast_convert_fusion.low_ref), channel_id=1, source_target_pairs={{0,4},{4,8},{8,12},{12,0},{1,5},{5,9},{9,13},{13,1},{2,6},{6,10},{... | collective-permute-start | bytes 393224 | tf_op jit(solution)/shard_map/ppermute | solution.py:107
  19.7 10.3 %collective-permute-start.3 = (bf16[128,512]{1,0:T(8,128)(2,1)S(1)}, bf16[128,512]{1,0:T(8,128)(2,1)S(1)}, u32[]{:S(2)}, u32[]{:S(2)}) collective-permute-start(bf16[128,512]{1,0:T(8,128)(2,1)S(1)} %bitcast_convert_fusion.low_ref), channel_id=1, source_target_pairs={{0,8},{4,12},{8,0},{12,4},{1,9},{5,13},{9,1},{13,5},{2,10},{6,14},... | collective-permute-start | bytes 393224 | tf_op jit(solution)/shard_map/ppermute | solution.py:107
  21.6 9.2 %collective-permute-start.4 = (bf16[128,512]{1,0:T(8,128)(2,1)S(1)}, bf16[128,512]{1,0:T(8,128)(2,1)S(1)}, u32[]{:S(2)}, u32[]{:S(2)}) collective-permute-start(bf16[128,512]{1,0:T(8,128)(2,1)S(1)} %bitcast_convert_fusion.low_ref), channel_id=1, source_target_pairs={{0,12},{4,0},{8,4},{12,8},{1,13},{5,1},{9,5},{13,9},{2,14},{6,2},{... | collective-permute-start | bytes 393224 | tf_op jit(solution)/shard_map/ppermute | solution.py:107
  26.3 3.7 %collective-permute-start.1 = (bf16[2,16,512]{2,1,0:T(8,128)(2,1)S(1)}, bf16[2,16,512]{2,1,0:T(8,128)(2,1)S(1)}, u32[]{:S(2)}, u32[]{:S(2)}) collective-permute-start(bf16[2,16,512]{2,1,0:T(8,128)(2,1)S(1)} %get-tuple-element.45), channel_id=1, source_target_pairs={{0,16},{16,0},{1,17},{17,1},{2,18},{18,2},{3,19},{19,3},{4,20},{20... | collective-permute-start | bytes 98312 | tf_op jit(solution)/shard_map/ppermute | solution.py:295
  31.4 102.2 %copy-start.1 = (s32[16]{0:T(128)S(1)}, s32[16]{0:T(128)}, u32[]{:S(2)}) copy-start(s32[16]{0:T(128)} %owner_ref.1) | copy-start | bytes 196
  31.4 15.3 %collective-permute-start.8 = (bf16[80,512]{1,0:T(8,128)(2,1)S(1)}, bf16[80,512]{1,0:T(8,128)(2,1)S(1)}, u32[]{:S(2)}, u32[]{:S(2)}) collective-permute-start(bf16[80,512]{1,0:T(8,128)(2,1)S(1)} %get-tuple-element.29.sent_one), channel_id=1, source_target_pairs={{0,32},{32,0},{64,96},{96,64},{1,33},{33,1},{65,97},{97,65},{2,34}... | collective-permute-start | bytes 245768 | tf_op jit(solution)/shard_map/ppermute | solution.py:311
  37.4 15.6 %collective-permute-start.9 = (bf16[80,512]{1,0:T(8,128)(2,1)S(1)}, bf16[80,512]{1,0:T(8,128)(2,1)S(1)}, u32[]{:S(2)}, u32[]{:S(2)}) collective-permute-start(bf16[80,512]{1,0:T(8,128)(2,1)S(1)} %get-tuple-element.30.sent_two), channel_id=1, source_target_pairs={{0,96},{32,64},{64,32},{96,0},{1,97},{33,65},{65,33},{97,1},{2,98}... | collective-permute-start | bytes 245768 | tf_op jit(solution)/shard_map/ppermute | solution.py:311
  53.1 23.0 %collective-permute-start.10 = (bf16[96,512]{1,0:T(8,128)(2,1)S(1)}, bf16[96,512]{1,0:T(8,128)(2,1)S(1)}, u32[]{:S(2)}, u32[]{:S(2)}) collective-permute-start(bf16[96,512]{1,0:T(8,128)(2,1)S(1)} %get-tuple-element.32.sent_one), channel_id=1, source_target_pairs={{0,96},{32,64},{64,32},{96,0},{1,97},{33,65},{65,33},{97,1},{2,98}... | collective-permute-start | bytes 294920 | tf_op jit(solution)/shard_map/ppermute | solution.py:319
  61.2 14.9 %collective-permute-start.11 = (bf16[96,512]{1,0:T(8,128)(2,1)S(1)}, bf16[96,512]{1,0:T(8,128)(2,1)S(1)}, u32[]{:S(2)}, u32[]{:S(2)}) collective-permute-start(bf16[96,512]{1,0:T(8,128)(2,1)S(1)} %get-tuple-element.33.sent_two), channel_id=1, source_target_pairs={{0,32},{32,0},{64,96},{96,64},{1,33},{33,1},{65,97},{97,65},{2,34}... | collective-permute-start | bytes 294920 | tf_op jit(solution)/shard_map/ppermute | solution.py:319
  63.2 11.1 %collective-permute-start.5 = (bf16[32,512]{1,0:T(8,128)(2,1)S(1)}, bf16[32,512]{1,0:T(8,128)(2,1)S(1)}, u32[]{:S(2)}, u32[]{:S(2)}) collective-permute-start(bf16[32,512]{1,0:T(8,128)(2,1)S(1)} %get-tuple-element.27.refs_0_), channel_id=1, source_target_pairs={{0,128},{128,256},{256,384},{384,0},{1,129},{129,257},{257,385},{3... | collective-permute-start | bytes 98312 | tf_op jit(solution)/shard_map/ppermute | solution.py:107
  66.8 7.4 %collective-permute-start.6 = (bf16[32,512]{1,0:T(8,128)(2,1)S(1)}, bf16[32,512]{1,0:T(8,128)(2,1)S(1)}, u32[]{:S(2)}, u32[]{:S(2)}) collective-permute-start(bf16[32,512]{1,0:T(8,128)(2,1)S(1)} %get-tuple-element.27.refs_0_), channel_id=1, source_target_pairs={{0,256},{128,384},{256,0},{384,128},{1,257},{129,385},{257,1},{385... | collective-permute-start | bytes 98312 | tf_op jit(solution)/shard_map/ppermute | solution.py:107
  71.1 5.0 %collective-permute-start.7 = (bf16[32,512]{1,0:T(8,128)(2,1)S(1)}, bf16[32,512]{1,0:T(8,128)(2,1)S(1)}, u32[]{:S(2)}, u32[]{:S(2)}) collective-permute-start(bf16[32,512]{1,0:T(8,128)(2,1)S(1)} %get-tuple-element.27.refs_0_), channel_id=1, source_target_pairs={{0,384},{128,0},{256,128},{384,256},{1,385},{129,1},{257,129},{385... | collective-permute-start | bytes 98312 | tf_op jit(solution)/shard_map/ppermute | solution.py:107
  77.4 22.5 %all-to-all-start.1 = ((bf16[32,16,128]{2,1,0:T(8,128)(2,1)}), bf16[32,16,128]{2,1,0:T(8,128)(2,1)S(1)}, u32[]{:S(2)}, u32[]{:S(2)}) async-start(bf16[32,16,128]{2,1,0:T(8,128)(2,1)} %bitcast.12), calls=%async_computation.1 | async-start | bytes 262144 | tf_op jit(solution)/shard_map/all_to_all | solution.py:328
  87.8 9.4 %collective-permute-start.12 = (bf16[32,512]{1,0:T(8,128)(2,1)S(1)}, bf16[32,512]{1,0:T(8,128)(2,1)S(1)}, u32[]{:S(2)}, u32[]{:S(2)}) collective-permute-start(bf16[32,512]{1,0:T(8,128)(2,1)S(1)} %get-tuple-element.37), channel_id=1, source_target_pairs={{0,128},{128,256},{256,384},{384,0},{1,129},{129,257},{257,385},{3... | collective-permute-start | bytes 98312 | tf_op jit(solution)/shard_map/ppermute | solution.py:107
  89.7 7.5 %collective-permute-start.13 = (bf16[32,512]{1,0:T(8,128)(2,1)S(1)}, bf16[32,512]{1,0:T(8,128)(2,1)S(1)}, u32[]{:S(2)}, u32[]{:S(2)}) collective-permute-start(bf16[32,512]{1,0:T(8,128)(2,1)S(1)} %get-tuple-element.38), channel_id=1, source_target_pairs={{0,256},{128,384},{256,0},{384,128},{1,257},{129,385},{257,1},{385... | collective-permute-start | bytes 98312 | tf_op jit(solution)/shard_map/ppermute | solution.py:107
  95.2 4.7 %collective-permute-start.14 = (bf16[32,512]{1,0:T(8,128)(2,1)S(1)}, bf16[32,512]{1,0:T(8,128)(2,1)S(1)}, u32[]{:S(2)}, u32[]{:S(2)}) collective-permute-start(bf16[32,512]{1,0:T(8,128)(2,1)S(1)} %get-tuple-element.39), channel_id=1, source_target_pairs={{0,384},{128,0},{256,128},{384,256},{1,385},{129,1},{257,129},{385... | collective-permute-start | bytes 98312 | tf_op jit(solution)/shard_map/ppermute | solution.py:107
  107.8 25.8 %all-to-all-start.3 = ((bf16[32,4,16,128]{3,2,1,0:T(8,128)(2,1)}), bf16[32,4,16,128]{3,2,1,0:T(8,128)(2,1)S(1)}, u32[]{:S(2)}, u32[]{:S(2)}) async-start(bf16[32,4,16,128]{3,2,1,0:T(8,128)(2,1)} %spread.1), calls=%async_computation.3 | async-start | bytes 1048576 | tf_op jit(solution)/shard_map/all_to_all | solution.py:348
  118.9 3.1 %collective-permute-start.15 = (bf16[16,512]{1,0:T(8,128)(2,1)S(1)}, bf16[16,512]{1,0:T(8,128)(2,1)S(1)}, u32[]{:S(2)}, u32[]{:S(2)}) collective-permute-start(bf16[16,512]{1,0:T(8,128)(2,1)S(1)} %get-tuple-element.41), channel_id=1, source_target_pairs={{0,16},{16,0},{1,17},{17,1},{2,18},{18,2},{3,19},{19,3},{4,20},{20... | collective-permute-start | bytes 49160 | tf_op jit(solution)/shard_map/ppermute | solution.py:353

commit v4 on v3

--- a/solution.py
+++ b/solution.py
@@ -140,7 +140,8 @@
         ref[half:] = right[part * rows : (part + 1) * rows]
 
 
-def middle_kernel(keep_ref, sent_one, sent_two, got_one, got_two, out_ref, send_one, send_two):
+def middle_kernel(keep_ref, sent_one, sent_two, got_one, got_two, *refs):
+    out_ref, send_one, send_two = refs[-3:]
     half = PART // 2
     for part, (sent, got, ref) in enumerate(
         ((sent_one, got_one, send_one), (sent_two, got_two, send_two))
@@ -188,20 +189,19 @@
         out_ref[w] = blocks_ref[place_ref[w * ZH + info_ref[2]]]
 
 
-def spread_kernel(parts_ref, *refs):
-    out_ref = refs[-1]
+def spread_kernel(info_ref, parts_ref, total_ref, out_ref, *outs):
+    x = info_ref[1]
     for peer in range(out_ref.shape[0]):
         out_ref[peer] = parts_ref[...]
-
-
-def update_kernel(info_ref, *refs):
-    x = info_ref[1]
-    sides, (grad, right), outs, (left, total) = refs[:4], refs[4:6], refs[6:10], refs[10:]
-    place(left, sides, x)
-    total[...] = dot(dot(left[...], grad[...], 1, 1).astype(BF16), right[...])
     for step, ref in enumerate(outs):
         at = pl.multiple_of((x + step) % X * ROWS, ROWS)
-        ref[...] = total[pl.ds(at, ROWS), :].astype(ref.dtype)
+        ref[...] = total_ref[pl.ds(at, ROWS), :].astype(ref.dtype)
+
+
+def update_kernel(info_ref, own_ref, one, two, three, grad_ref, right_ref, out_ref, left):
+    place(left, (own_ref, one, two, three), info_ref[1])
+    product = dot(left[...], grad_ref[...], 1, 1).astype(BF16)
+    out_ref[...] = dot(product, right_ref[...])
 
 
 def halves_kernel(info_ref, own_ref, one, two, three, keep_ref, send_ref):
@@ -304,8 +304,8 @@
         [SMEM] + [VMEM] * 3,
         [shape((PART, B), F32), shape((ROWS, B))] + [shape((PART // 2 + half, B))] * 2,
         [pltpu.VMEM((ROWS, B), BF16)],
-        awaited=3,
-    )(info, total, mine, theirs, *olds[1:])
+        awaited=1,
+    )(info, total, mine, theirs, olds[1])
     near = [(z, z ^ 1) for z in range(ZH)]
     far = [(z, ZH - 1 - z) for z in range(ZH)]
     got = [lax.ppermute(sends[0], "zh", near), lax.ppermute(sends[1], "zh", far)]
@@ -315,38 +315,43 @@
         "middle",
         [VMEM] * 5,
         [shape((PART, B), F32)] + [shape((PART // 2 + 2 * half, B))] * 2,
-    )(keep, *sends, *got)
+        awaited=3,
+    )(keep, *sends, *got, *lefts[1:])
     got = [lax.ppermute(sends[0], "zh", far), lax.ppermute(sends[1], "zh", near)]
     grad, pieces, right_part = kernel_call(
         functools.partial(pack_kernel, tokens ** -0.5),
         "pack",
         [SMEM] + [VMEM] * 5,
         [shape((PART, B)), shape((CORE, n_mp, n_root, half, lanes)), shape((PART, B))],
-        awaited=3,
-    )(info, keep, *sends, *got, *lefts[1:])
+        awaited=2,
+    )(info, keep, *sends, *got, *olds[2:])
 
     blocks = lax.all_to_all(pieces.reshape(-1, half, lanes), ("core", "mp", "root"), 0, 0)
 
-    own, *sends = kernel_call(
+    (total,) = kernel_call(
         update_kernel,
         "update",
         [SMEM] + [VMEM] * 6,
-        [shape((ROWS, B), F32)] + [shape((ROWS, B))] * 3,
-        [pltpu.VMEM((PART, B), BF16), pltpu.VMEM((PART, B), F32)],
+        [shape((PART, B), F32)],
+        [pltpu.VMEM((PART, B), BF16)],
         cost(2 * PART * B * (PART + B), 6 * PART * B),
     )(info, *lefts, grad, right_part)
-    got = [shift(send, "x", step) for step, send in enumerate(sends, 1)]
 
     at = (listed % 2) * (n_mp * n_root) + listed // 2
     (chosen,) = kernel_call(
-        choose_kernel, "choose", [SMEM, SMEM, VMEM], [shape((X, half, lanes))], awaited=3
-    )(info, at, blocks, *got)
+        choose_kernel, "choose", [SMEM, SMEM, VMEM], [shape((X, half, lanes))], awaited=1
+    )(info, at, blocks, total)
     parts = lax.all_to_all(chosen, "x", 0, 0)
-    (mine,) = kernel_call(
-        spread_kernel, "spread", [VMEM], [shape((CORE * n_mp * n_root, X, half, lanes))]
-    )(parts)
+    mine, own, *sends = kernel_call(
+        spread_kernel,
+        "spread",
+        [SMEM, VMEM, VMEM],
+        [shape((CORE * n_mp * n_root, X, half, lanes)), shape((ROWS, B), F32)]
+        + [shape((ROWS, B))] * 3,
+    )(info, parts, total)
     gathered = lax.all_to_all(mine, ("core", "mp", "root"), 0, 0)
     gathered = gathered.reshape((CORE, n_mp, n_root) + gathered.shape[1:])
+    got = [shift(send, "x", step) for step, send in enumerate(sends, 1)]
     keep, send = kernel_call(
         halves_kernel, "halves", [SMEM] + [VMEM] * 4, [shape((half, B))] * 2
     )(info, own, *got)

time: 138 us -> 126 us (0.913)
  starting transfers between devices: 90.9 us -> 75.8 us
  waiting for transfers between devices: 25.5 us -> 27.2 us
    all_to_all x1, waiting for transfers between devices: 11 us -> 0.01 us  [local(): gathered = lax.all_to_all(mine, ('core', 'mp', 'root'), 0, 0)]
    all_to_all x1, waiting for transfers between devices: 0.01 us -> 7.56 us  [local(): lax.all_to_all(pieces.reshape(-1, half, lanes), ('core', 'mp', 'root'), 0...]
    ppermute x1, waiting for transfers between devices: 0.01 us -> 6.94 us  [local(): lax.ppermute(sends[1], 'zh', near)]
    ppermute x1, waiting for transfers between devices: 6.27 us -> 0.01 us  [local(): lax.ppermute(sends[1], 'zh', far)]
    ppermute x1, starting transfers between devices: 8.16 us -> 1.92 us  [local(): lax.ppermute(sends[0], 'zh', far)]
    all_to_all x1, starting transfers between devices: 10.5 us -> 5.98 us  [local(): gathered = lax.all_to_all(mine, ('core', 'mp', 'root'), 0, 0)]
    ppermute x1, waiting for transfers between devices: 0.01 us -> 4.12 us  [local(): lax.ppermute(sends[0], 'zh', far)]
    all_to_all x1, starting transfers between devices: 9.48 us -> 5.92 us  [local(): lax.all_to_all(pieces.reshape(-1, half, lanes), ('core', 'mp', 'root'), 0...]
where the time goes in v4:
time: 126 us; the launch traced here: 125 us
  starting transfers between devices  75.8 us (60%)
  waiting for transfers between devices  27.2 us (22%)
  Pallas kernels  12.5 us (10%)
  blocking collectives  7.64 us (6%)
    ppermute x9, starting transfers between devices, shift(): lax.ppermute(value, axis, [(at, (at + step) % size) for at in range(size)])  27.2 us
    ppermute x2, starting transfers between devices, local(): got = lax.ppermute(send, 'core', swap)  12.4 us
    ppermute x1, starting transfers between devices, local(): lax.ppermute(sends[1], 'zh', far)  8.82 us
    all_to_all x1, blocking collectives, local(): parts = lax.all_to_all(chosen, 'x', 0, 0)  7.64 us
    all_to_all x1, waiting for transfers between devices, local(): lax.all_to_all(pieces.reshape(-1, half, lanes), ('core', 'mp', 'root'), 0...  7.56 us
    ppermute x1, waiting for transfers between devices, local(): lax.ppermute(sends[1], 'zh', near)  6.94 us
    all_to_all x1, starting transfers between devices, local(): gathered = lax.all_to_all(mine, ('core', 'mp', 'root'), 0, 0)  5.98 us
    all_to_all x1, starting transfers between devices, local(): lax.all_to_all(pieces.reshape(-1, half, lanes), ('core', 'mp', 'root'), 0...  5.92 us
  transfers between devices with their start and end apart: 19, of which 9 were waited for; matrix products, arithmetic and copies ran while one was open for 1% of the time, Pallas kernels for 2%

profile of v4, /device:TPU:1, one launch (start us, length us, event | category | flops | bytes accessed | tf_op | source)
XLA Modules:
  0.0 124.9 jit_solution(6338557972797085994)
XLA Ops:
  0.6 2.3 %other_half.1 = (bf16[512,1024]{1,0:T(8,128)(2,1)S(1)}, bf16[512,512]{1,0:T(8,128)(2,1)S(1)}, bf16[1024,512]{1,0:T(8,128)(2,1)S(1)}) custom-call(s32[1]{0:T(128)} %bitcast.5.index_ref, bf16[1024,512]{1,0:T(8,128)(2,1)} %acts_ref.1, bf16[1024,1024]{1,0:T(8,128)(2,1)} %grads_ref.1), custom_call_target="tpu_custom_call" | custom-call | flops 536870912 | bytes 3145728 | tf_op jit(solution)/shard_map/other_half/pallas_call | solution.py:80
  2.9 8.8 %collective-permute-start = (bf16[512,512]{1,0:T(8,128)(2,1)S(1)}, bf16[512,512]{1,0:T(8,128)(2,1)S(1)}, u32[]{:S(2)}, u32[]{:S(2)}) collective-permute-start(bf16[512,512]{1,0:T(8,128)(2,1)S(1)} %get-tuple-element.27), channel_id=1, source_target_pairs={{0,16},{16,0},{1,17},{17,1},{2,18},{18,2},{3,19},{19,3},{4,20},{20... | collective-permute-start | bytes 1572872 | tf_op jit(solution)/shard_map/ppermute | solution.py:283
  11.7 0.7 own_half.1.own_ref
  12.4 0.0 copy-start
  12.4 0.0 copy-start.2
  12.4 0.0 copy-start.3
  12.4 0.8 collective-permute-done.got_ref
  13.2 1.0 join.1
  14.2 3.6 %all-to-all-start = ((bf16[4,128,512]{2,1,0:T(8,128)(2,1)}), bf16[4,128,512]{2,1,0:T(8,128)(2,1)S(1)}, u32[]{:S(2)}, u32[]{:S(2)}) async-start(bf16[4,128,512]{2,1,0:T(8,128)(2,1)} %bitcast.6), calls=%async_computation | async-start | bytes 1048576 | tf_op jit(solution)/shard_map/all_to_all | solution.py:292
  17.9 1.9 %collective-permute-start.2 = (bf16[128,512]{1,0:T(8,128)(2,1)S(1)}, bf16[128,512]{1,0:T(8,128)(2,1)S(1)}, u32[]{:S(2)}, u32[]{:S(2)}) collective-permute-start(bf16[128,512]{1,0:T(8,128)(2,1)S(1)} %bitcast_convert_fusion.low_ref), channel_id=1, source_target_pairs={{0,4},{4,8},{8,12},{12,0},{1,5},{5,9},{9,13},{13,1},{2,6},{6,10},{... | collective-permute-start | bytes 393224 | tf_op jit(solution)/shard_map/ppermute | solution.py:107
  19.9 2.3 %collective-permute-start.1 = (bf16[2,16,512]{2,1,0:T(8,128)(2,1)S(1)}, bf16[2,16,512]{2,1,0:T(8,128)(2,1)S(1)}, u32[]{:S(2)}, u32[]{:S(2)}) collective-permute-start(bf16[2,16,512]{2,1,0:T(8,128)(2,1)S(1)} %get-tuple-element.47), channel_id=1, source_target_pairs={{0,16},{16,0},{1,17},{17,1},{2,18},{18,2},{3,19},{19,3},{4,20},{20... | collective-permute-start | bytes 98312 | tf_op jit(solution)/shard_map/ppermute | solution.py:295
  22.2 0.1 stack.26.info_ref
  22.3 0.7 collective-permute-done.1.theirs_ref
  23.0 2.7 %collective-permute-done.2.refs_0_.one = bf16[128,512]{1,0:T(8,128)(2,1)S(1)} collective-permute-done((bf16[128,512]{1,0:T(8,128)(2,1)S(1)}, bf16[128,512]{1,0:T(8,128)(2,1)S(1)}, u32[]{:S(2)}, u32[]{:S(2)}) %collective-permute-start.2) | collective-permute-done | bytes 131104 | tf_op jit(solution)/shard_map/ppermute | solution.py:107
  25.7 1.3 %all-to-all-done.parts_ref = bf16[4,128,512]{2,1,0:T(8,128)(2,1)S(1)} async-done(((bf16[4,128,512]{2,1,0:T(8,128)(2,1)}), bf16[4,128,512]{2,1,0:T(8,128)(2,1)S(1)}, u32[]{:S(2)}, u32[]{:S(2)}) %all-to-all-start) | async-done | bytes 524320 | tf_op jit(solution)/shard_map/all_to_all | solution.py:292
  27.0 0.6 sum_x.1
  27.7 3.7 %collective-permute-start.3 = (bf16[80,512]{1,0:T(8,128)(2,1)S(1)}, bf16[80,512]{1,0:T(8,128)(2,1)S(1)}, u32[]{:S(2)}, u32[]{:S(2)}) collective-permute-start(bf16[80,512]{1,0:T(8,128)(2,1)S(1)} %get-tuple-element.29.sent_one), channel_id=1, source_target_pairs={{0,32},{32,0},{64,96},{96,64},{1,33},{33,1},{65,97},{97,65},{2,34}... | collective-permute-start | bytes 245768 | tf_op jit(solution)/shard_map/ppermute | solution.py:311
  31.4 8.8 %collective-permute-start.4 = (bf16[80,512]{1,0:T(8,128)(2,1)S(1)}, bf16[80,512]{1,0:T(8,128)(2,1)S(1)}, u32[]{:S(2)}, u32[]{:S(2)}) collective-permute-start(bf16[80,512]{1,0:T(8,128)(2,1)S(1)} %get-tuple-element.30.sent_two), channel_id=1, source_target_pairs={{0,96},{32,64},{64,32},{96,0},{1,97},{33,65},{65,33},{97,1},{2,98}... | collective-permute-start | bytes 245768 | tf_op jit(solution)/shard_map/ppermute | solution.py:311
  40.2 2.2 %collective-permute-start.5 = (bf16[32,512]{1,0:T(8,128)(2,1)S(1)}, bf16[32,512]{1,0:T(8,128)(2,1)S(1)}, u32[]{:S(2)}, u32[]{:S(2)}) collective-permute-start(bf16[32,512]{1,0:T(8,128)(2,1)S(1)} %get-tuple-element.31.own_ref), channel_id=1, source_target_pairs={{0,128},{128,256},{256,384},{384,0},{1,129},{129,257},{257,385},{3... | collective-permute-start | bytes 98312 | tf_op jit(solution)/shard_map/ppermute | solution.py:107
  42.4 3.9 %collective-permute-start.6 = (bf16[32,512]{1,0:T(8,128)(2,1)S(1)}, bf16[32,512]{1,0:T(8,128)(2,1)S(1)}, u32[]{:S(2)}, u32[]{:S(2)}) collective-permute-start(bf16[32,512]{1,0:T(8,128)(2,1)S(1)} %get-tuple-element.31.own_ref), channel_id=1, source_target_pairs={{0,256},{128,384},{256,0},{384,128},{1,257},{129,385},{257,1},{385... | collective-permute-start | bytes 98312 | tf_op jit(solution)/shard_map/ppermute | solution.py:107
  46.3 3.1 %collective-permute-start.7 = (bf16[32,512]{1,0:T(8,128)(2,1)S(1)}, bf16[32,512]{1,0:T(8,128)(2,1)S(1)}, u32[]{:S(2)}, u32[]{:S(2)}) collective-permute-start(bf16[32,512]{1,0:T(8,128)(2,1)S(1)} %get-tuple-element.31.own_ref), channel_id=1, source_target_pairs={{0,384},{128,0},{256,128},{384,256},{1,385},{129,1},{257,129},{385... | collective-permute-start | bytes 98312 | tf_op jit(solution)/shard_map/ppermute | solution.py:107
  49.4 4.5 %collective-permute-start.10 = (bf16[128,512]{1,0:T(8,128)(2,1)S(1)}, bf16[128,512]{1,0:T(8,128)(2,1)S(1)}, u32[]{:S(2)}, u32[]{:S(2)}) collective-permute-start(bf16[128,512]{1,0:T(8,128)(2,1)S(1)} %bitcast_convert_fusion.low_ref), channel_id=1, source_target_pairs={{0,8},{4,12},{8,0},{12,4},{1,9},{5,13},{9,1},{13,5},{2,10},{6,14},... | collective-permute-start | bytes 393224 | tf_op jit(solution)/shard_map/ppermute | solution.py:107
  53.9 0.0 collective-permute-done.6.refs_1_.two
  53.9 3.0 %collective-permute-start.11 = (bf16[128,512]{1,0:T(8,128)(2,1)S(1)}, bf16[128,512]{1,0:T(8,128)(2,1)S(1)}, u32[]{:S(2)}, u32[]{:S(2)}) collective-permute-start(bf16[128,512]{1,0:T(8,128)(2,1)S(1)} %bitcast_convert_fusion.low_ref), channel_id=1, source_target_pairs={{0,12},{4,0},{8,4},{12,8},{1,13},{5,1},{9,5},{13,9},{2,14},{6,2},{... | collective-permute-start | bytes 393224 | tf_op jit(solution)/shard_map/ppermute | solution.py:107
  56.9 0.0 collective-permute-done.7.refs_2_.three
  56.9 0.0 collective-permute-done.3.got_one
  57.0 0.0 copy-start.1
  57.0 1.9 %collective-permute-start.8 = (bf16[96,512]{1,0:T(8,128)(2,1)S(1)}, bf16[96,512]{1,0:T(8,128)(2,1)S(1)}, u32[]{:S(2)}, u32[]{:S(2)}) collective-permute-start(bf16[96,512]{1,0:T(8,128)(2,1)S(1)} %get-tuple-element.33.sent_one), channel_id=1, source_target_pairs={{0,96},{32,64},{64,32},{96,0},{1,97},{33,65},{65,33},{97,1},{2,98}... | collective-permute-start | bytes 294920 | tf_op jit(solution)/shard_map/ppermute | solution.py:320
  58.9 4.0 %collective-permute-start.9 = (bf16[96,512]{1,0:T(8,128)(2,1)S(1)}, bf16[96,512]{1,0:T(8,128)(2,1)S(1)}, u32[]{:S(2)}, u32[]{:S(2)}) collective-permute-start(bf16[96,512]{1,0:T(8,128)(2,1)S(1)} %get-tuple-element.34.sent_two), channel_id=1, source_target_pairs={{0,32},{32,0},{64,96},{96,64},{1,33},{33,1},{65,97},{97,65},{2,34}... | collective-permute-start | bytes 294920 | tf_op jit(solution)/shard_map/ppermute | solution.py:320
  63.0 4.1 %collective-permute-done.8.got_one = bf16[96,512]{1,0:T(8,128)(2,1)S(1)} collective-permute-done((bf16[96,512]{1,0:T(8,128)(2,1)S(1)}, bf16[96,512]{1,0:T(8,128)(2,1)S(1)}, u32[]{:S(2)}, u32[]{:S(2)}) %collective-permute-start.8) | collective-permute-done | bytes 98336 | tf_op jit(solution)/shard_map/ppermute | solution.py:320
  67.1 6.9 %collective-permute-done.9.got_two = bf16[96,512]{1,0:T(8,128)(2,1)S(1)} collective-permute-done((bf16[96,512]{1,0:T(8,128)(2,1)S(1)}, bf16[96,512]{1,0:T(8,128)(2,1)S(1)}, u32[]{:S(2)}, u32[]{:S(2)}) %collective-permute-start.9) | collective-permute-done | bytes 98336 | tf_op jit(solution)/shard_map/ppermute | solution.py:320
  74.0 1.3 %pack.1 = (bf16[128,512]{1,0:T(8,128)(2,1)S(1)}, bf16[2,4,4,16,128]{4,3,2,1,0:T(8,128)(2,1)}, bf16[128,512]{1,0:T(8,128)(2,1)S(1)}) custom-call(s32[5]{0:T(128)S(1)} %stack.26.info_ref, f32[128,512]{1,0:T(8,128)S(1)} %get-tuple-element.32.keep_ref, bf16[96,512]{1,0:T(8,128)(2,1)S(1)} %get-tuple-element.33.sent_one, ...), custom_call_target="tpu_custom_call" | custom-call | tf_op jit(solution)/shard_map/pack/pallas_call | solution.py:321
  75.3 5.9 %all-to-all-start.1 = ((bf16[32,16,128]{2,1,0:T(8,128)(2,1)}), bf16[32,16,128]{2,1,0:T(8,128)(2,1)S(1)}, u32[]{:S(2)}, u32[]{:S(2)}) async-start(bf16[32,16,128]{2,1,0:T(8,128)(2,1)} %bitcast.10), calls=%async_computation.1 | async-start | bytes 262144 | tf_op jit(solution)/shard_map/all_to_all | solution.py:329
  81.2 0.9 update.1.refs_0_.total_ref
  82.1 7.6 %all-to-all-done.1.blocks_ref = bf16[32,16,128]{2,1,0:T(8,128)(2,1)S(1)} async-done(((bf16[32,16,128]{2,1,0:T(8,128)(2,1)}), bf16[32,16,128]{2,1,0:T(8,128)(2,1)S(1)}, u32[]{:S(2)}, u32[]{:S(2)}) %all-to-all-start.1) | async-done | bytes 131104 | tf_op jit(solution)/shard_map/all_to_all | solution.py:329
  89.7 0.6 choose.1
  90.3 7.6 %all_to_all.20.parts_ref = bf16[4,16,128]{2,1,0:T(8,128)(2,1)S(1)} all-to-all(bf16[4,16,128]{2,1,0:T(8,128)(2,1)S(1)} %choose.1), channel_id=1, replica_groups=mesh['x'=4,'zh'=4,'core'=2,'mp'=4,'root'=4] {'x'}, dimensions={0} | all-to-all | bytes 32768 | tf_op jit(solution)/shard_map/all_to_all | solution.py:344
  97.9 1.4 %spread.1 = (bf16[32,4,16,128]{3,2,1,0:T(8,128)(2,1)}, f32[32,512]{1,0:T(8,128)S(1)}, bf16[32,512]{1,0:T(8,128)(2,1)S(1)}, bf16[32,512]{1,0:T(8,128)(2,1)S(1)}, bf16[32,512]{1,0:T(8,128)(2,1)S(1)}) custom-call(s32[5]{0:T(128)S(1)} %stack.26.info_ref, bf16[4,16,128]{2,1,0:T(8,128)(2,1)S(1)} %all_to_all.20.parts_ref, f32[128,512]{1,0:T(8,128)S(1)} %update.1.refs_0_.total_ref), custom_call_target="tpu_custom_call" | custom-call | tf_op jit(solution)/shard_map/spread/pallas_call | solution.py:345
  99.3 6.0 %all-to-all-start.3 = ((bf16[32,4,16,128]{3,2,1,0:T(8,128)(2,1)}), bf16[32,4,16,128]{3,2,1,0:T(8,128)(2,1)S(1)}, u32[]{:S(2)}, u32[]{:S(2)}) async-start(bf16[32,4,16,128]{3,2,1,0:T(8,128)(2,1)} %get-tuple-element.44), calls=%async_computation.3 | async-start | bytes 1048576 | tf_op jit(solution)/shard_map/all_to_all | solution.py:352
  105.3 2.2 %collective-permute-start.12 = (bf16[32,512]{1,0:T(8,128)(2,1)S(1)}, bf16[32,512]{1,0:T(8,128)(2,1)S(1)}, u32[]{:S(2)}, u32[]{:S(2)}) collective-permute-start(bf16[32,512]{1,0:T(8,128)(2,1)S(1)} %get-tuple-element.39), channel_id=1, source_target_pairs={{0,128},{128,256},{256,384},{384,0},{1,129},{129,257},{257,385},{3... | collective-permute-start | bytes 98312 | tf_op jit(solution)/shard_map/ppermute | solution.py:107
  107.5 3.7 %collective-permute-start.13 = (bf16[32,512]{1,0:T(8,128)(2,1)S(1)}, bf16[32,512]{1,0:T(8,128)(2,1)S(1)}, u32[]{:S(2)}, u32[]{:S(2)}) collective-permute-start(bf16[32,512]{1,0:T(8,128)(2,1)S(1)} %get-tuple-element.40), channel_id=1, source_target_pairs={{0,256},{128,384},{256,0},{384,128},{1,257},{129,385},{257,1},{385... | collective-permute-start | bytes 98312 | tf_op jit(solution)/shard_map/ppermute | solution.py:107
  111.2 2.8 %collective-permute-start.14 = (bf16[32,512]{1,0:T(8,128)(2,1)S(1)}, bf16[32,512]{1,0:T(8,128)(2,1)S(1)}, u32[]{:S(2)}, u32[]{:S(2)}) collective-permute-start(bf16[32,512]{1,0:T(8,128)(2,1)S(1)} %get-tuple-element.41), channel_id=1, source_target_pairs={{0,384},{128,0},{256,128},{384,256},{1,385},{129,1},{257,129},{385... | collective-permute-start | bytes 98312 | tf_op jit(solution)/shard_map/ppermute | solution.py:107
  114.0 2.2 %collective-permute-done.14.three = bf16[32,512]{1,0:T(8,128)(2,1)S(1)} collective-permute-done((bf16[32,512]{1,0:T(8,128)(2,1)S(1)}, bf16[32,512]{1,0:T(8,128)(2,1)S(1)}, u32[]{:S(2)}, u32[]{:S(2)}) %collective-permute-start.14) | collective-permute-done | bytes 32800 | tf_op jit(solution)/shard_map/ppermute | solution.py:107
  116.1 0.6 halves.1
  116.7 3.6 %collective-permute-start.15 = (bf16[16,512]{1,0:T(8,128)(2,1)S(1)}, bf16[16,512]{1,0:T(8,128)(2,1)S(1)}, u32[]{:S(2)}, u32[]{:S(2)}) collective-permute-start(bf16[16,512]{1,0:T(8,128)(2,1)S(1)} %get-tuple-element.43), channel_id=1, source_target_pairs={{0,16},{16,0},{1,17},{17,1},{2,18},{18,2},{3,19},{19,3},{4,20},{20... | collective-permute-start | bytes 49160 | tf_op jit(solution)/shard_map/ppermute | solution.py:358
  120.3 0.8 collective-permute-done.15
  121.1 0.6 maximum_select_fusion
  121.7 3.2 %refresh.1 = (f32[128,512]{1,0:T(8,128)}, f32[128,512]{1,0:T(8,128)}) custom-call(s32[5]{0:T(128)S(1)} %stack.26.info_ref, s32[16]{0:T(128)S(1)} %copy-done.1, bf16[2,4,4,4,16,128]{5,4,3,2,1,0:T(8,128)(2,1)S(1)} %bitcast.19, f32[128,512]{1,0:T(8,128)S(1)} %bitcast.20, bf16[128,512]{1,0:T(8,128)(2,1)S(1)} %bitcast_convert_fusion.low_ref, ...), custom_call_target="tpu_custom_call" | custom-call | flops 603979776 | bytes 1048576 | tf_op jit(solution)/shard_map/refresh/pallas_call | solution.py:363
  (19 shorter events, 0.1 us)
Async XLA Ops:
  2.9 10.3 %collective-permute-start = (bf16[512,512]{1,0:T(8,128)(2,1)S(1)}, bf16[512,512]{1,0:T(8,128)(2,1)S(1)}, u32[]{:S(2)}, u32[]{:S(2)}) collective-permute-start(bf16[512,512]{1,0:T(8,128)(2,1)S(1)} %get-tuple-element.27), channel_id=1, source_target_pairs={{0,16},{16,0},{1,17},{17,1},{2,18},{18,2},{3,19},{19,3},{4,20},{20... | collective-permute-start | bytes 1572872 | tf_op jit(solution)/shard_map/ppermute | solution.py:283
  12.4 5.4 %copy-start = (f32[1,128,512]{2,1,0:T(8,128)S(1)}, f32[1,128,512]{2,1,0:T(8,128)}, u32[]{:S(2)}) copy-start(f32[1,128,512]{2,1,0:T(8,128)} %param.11) | copy-start | bytes 786436
  12.4 7.4 %copy-start.2 = (bf16[1,2,16,512]{3,2,1,0:T(8,128)(2,1)S(1)}, bf16[1,2,16,512]{3,2,1,0:T(8,128)(2,1)}, u32[]{:S(2)}) copy-start(bf16[1,2,16,512]{3,2,1,0:T(8,128)(2,1)} %param.9) | copy-start | bytes 98308
  12.4 7.4 %copy-start.3 = (bf16[1,2,16,512]{3,2,1,0:T(8,128)(2,1)S(1)}, bf16[1,2,16,512]{3,2,1,0:T(8,128)(2,1)}, u32[]{:S(2)}) copy-start(bf16[1,2,16,512]{3,2,1,0:T(8,128)(2,1)} %param.10) | copy-start | bytes 98308
  14.2 67.0 %copy-start.4 = (s32[16]{0:T(128)S(1)}, s32[16]{0:T(128)}, u32[]{:S(2)}) copy-start(s32[16]{0:T(128)} %param.12) | copy-start | bytes 196
  14.2 12.8 %all-to-all-start = ((bf16[4,128,512]{2,1,0:T(8,128)(2,1)}), bf16[4,128,512]{2,1,0:T(8,128)(2,1)S(1)}, u32[]{:S(2)}, u32[]{:S(2)}) async-start(bf16[4,128,512]{2,1,0:T(8,128)(2,1)} %bitcast.6), calls=%async_computation | async-start | bytes 1048576 | tf_op jit(solution)/shard_map/all_to_all | solution.py:292
  17.9 7.8 %collective-permute-start.2 = (bf16[128,512]{1,0:T(8,128)(2,1)S(1)}, bf16[128,512]{1,0:T(8,128)(2,1)S(1)}, u32[]{:S(2)}, u32[]{:S(2)}) collective-permute-start(bf16[128,512]{1,0:T(8,128)(2,1)S(1)} %bitcast_convert_fusion.low_ref), channel_id=1, source_target_pairs={{0,4},{4,8},{8,12},{12,0},{1,5},{5,9},{9,13},{13,1},{2,6},{6,10},{... | collective-permute-start | bytes 393224 | tf_op jit(solution)/shard_map/ppermute | solution.py:107
  19.9 3.1 %collective-permute-start.1 = (bf16[2,16,512]{2,1,0:T(8,128)(2,1)S(1)}, bf16[2,16,512]{2,1,0:T(8,128)(2,1)S(1)}, u32[]{:S(2)}, u32[]{:S(2)}) collective-permute-start(bf16[2,16,512]{2,1,0:T(8,128)(2,1)S(1)} %get-tuple-element.47), channel_id=1, source_target_pairs={{0,16},{16,0},{1,17},{17,1},{2,18},{18,2},{3,19},{19,3},{4,20},{20... | collective-permute-start | bytes 98312 | tf_op jit(solution)/shard_map/ppermute | solution.py:295
  27.7 29.2 %collective-permute-start.3 = (bf16[80,512]{1,0:T(8,128)(2,1)S(1)}, bf16[80,512]{1,0:T(8,128)(2,1)S(1)}, u32[]{:S(2)}, u32[]{:S(2)}) collective-permute-start(bf16[80,512]{1,0:T(8,128)(2,1)S(1)} %get-tuple-element.29.sent_one), channel_id=1, source_target_pairs={{0,32},{32,0},{64,96},{96,64},{1,33},{33,1},{65,97},{97,65},{2,34}... | collective-permute-start | bytes 245768 | tf_op jit(solution)/shard_map/ppermute | solution.py:311
  31.4 25.6 %collective-permute-start.4 = (bf16[80,512]{1,0:T(8,128)(2,1)S(1)}, bf16[80,512]{1,0:T(8,128)(2,1)S(1)}, u32[]{:S(2)}, u32[]{:S(2)}) collective-permute-start(bf16[80,512]{1,0:T(8,128)(2,1)S(1)} %get-tuple-element.30.sent_two), channel_id=1, source_target_pairs={{0,96},{32,64},{64,32},{96,0},{1,97},{33,65},{65,33},{97,1},{2,98}... | collective-permute-start | bytes 245768 | tf_op jit(solution)/shard_map/ppermute | solution.py:311
  40.2 9.2 %collective-permute-start.5 = (bf16[32,512]{1,0:T(8,128)(2,1)S(1)}, bf16[32,512]{1,0:T(8,128)(2,1)S(1)}, u32[]{:S(2)}, u32[]{:S(2)}) collective-permute-start(bf16[32,512]{1,0:T(8,128)(2,1)S(1)} %get-tuple-element.31.own_ref), channel_id=1, source_target_pairs={{0,128},{128,256},{256,384},{384,0},{1,129},{129,257},{257,385},{3... | collective-permute-start | bytes 98312 | tf_op jit(solution)/shard_map/ppermute | solution.py:107
  42.4 11.5 %collective-permute-start.6 = (bf16[32,512]{1,0:T(8,128)(2,1)S(1)}, bf16[32,512]{1,0:T(8,128)(2,1)S(1)}, u32[]{:S(2)}, u32[]{:S(2)}) collective-permute-start(bf16[32,512]{1,0:T(8,128)(2,1)S(1)} %get-tuple-element.31.own_ref), channel_id=1, source_target_pairs={{0,256},{128,384},{256,0},{384,128},{1,257},{129,385},{257,1},{385... | collective-permute-start | bytes 98312 | tf_op jit(solution)/shard_map/ppermute | solution.py:107
  46.3 10.6 %collective-permute-start.7 = (bf16[32,512]{1,0:T(8,128)(2,1)S(1)}, bf16[32,512]{1,0:T(8,128)(2,1)S(1)}, u32[]{:S(2)}, u32[]{:S(2)}) collective-permute-start(bf16[32,512]{1,0:T(8,128)(2,1)S(1)} %get-tuple-element.31.own_ref), channel_id=1, source_target_pairs={{0,384},{128,0},{256,128},{384,256},{1,385},{129,1},{257,129},{385... | collective-permute-start | bytes 98312 | tf_op jit(solution)/shard_map/ppermute | solution.py:107
  49.4 13.5 %collective-permute-start.10 = (bf16[128,512]{1,0:T(8,128)(2,1)S(1)}, bf16[128,512]{1,0:T(8,128)(2,1)S(1)}, u32[]{:S(2)}, u32[]{:S(2)}) collective-permute-start(bf16[128,512]{1,0:T(8,128)(2,1)S(1)} %bitcast_convert_fusion.low_ref), channel_id=1, source_target_pairs={{0,8},{4,12},{8,0},{12,4},{1,9},{5,13},{9,1},{13,5},{2,10},{6,14},... | collective-permute-start | bytes 393224 | tf_op jit(solution)/shard_map/ppermute | solution.py:107
  53.9 9.0 %collective-permute-start.11 = (bf16[128,512]{1,0:T(8,128)(2,1)S(1)}, bf16[128,512]{1,0:T(8,128)(2,1)S(1)}, u32[]{:S(2)}, u32[]{:S(2)}) collective-permute-start(bf16[128,512]{1,0:T(8,128)(2,1)S(1)} %bitcast_convert_fusion.low_ref), channel_id=1, source_target_pairs={{0,12},{4,0},{8,4},{12,8},{1,13},{5,1},{9,5},{13,9},{2,14},{6,2},{... | collective-permute-start | bytes 393224 | tf_op jit(solution)/shard_map/ppermute | solution.py:107
  57.0 64.8 %copy-start.1 = (s32[16]{0:T(128)S(1)}, s32[16]{0:T(128)}, u32[]{:S(2)}) copy-start(s32[16]{0:T(128)} %owner_ref.1) | copy-start | bytes 196
  57.0 10.1 %collective-permute-start.8 = (bf16[96,512]{1,0:T(8,128)(2,1)S(1)}, bf16[96,512]{1,0:T(8,128)(2,1)S(1)}, u32[]{:S(2)}, u32[]{:S(2)}) collective-permute-start(bf16[96,512]{1,0:T(8,128)(2,1)S(1)} %get-tuple-element.33.sent_one), channel_id=1, source_target_pairs={{0,96},{32,64},{64,32},{96,0},{1,97},{33,65},{65,33},{97,1},{2,98}... | collective-permute-start | bytes 294920 | tf_op jit(solution)/shard_map/ppermute | solution.py:320
  58.9 15.1 %collective-permute-start.9 = (bf16[96,512]{1,0:T(8,128)(2,1)S(1)}, bf16[96,512]{1,0:T(8,128)(2,1)S(1)}, u32[]{:S(2)}, u32[]{:S(2)}) collective-permute-start(bf16[96,512]{1,0:T(8,128)(2,1)S(1)} %get-tuple-element.34.sent_two), channel_id=1, source_target_pairs={{0,32},{32,0},{64,96},{96,64},{1,33},{33,1},{65,97},{97,65},{2,34}... | collective-permute-start | bytes 294920 | tf_op jit(solution)/shard_map/ppermute | solution.py:320
  75.3 14.4 %all-to-all-start.1 = ((bf16[32,16,128]{2,1,0:T(8,128)(2,1)}), bf16[32,16,128]{2,1,0:T(8,128)(2,1)S(1)}, u32[]{:S(2)}, u32[]{:S(2)}) async-start(bf16[32,16,128]{2,1,0:T(8,128)(2,1)} %bitcast.10), calls=%async_computation.1 | async-start | bytes 262144 | tf_op jit(solution)/shard_map/all_to_all | solution.py:329
  99.3 22.4 %all-to-all-start.3 = ((bf16[32,4,16,128]{3,2,1,0:T(8,128)(2,1)}), bf16[32,4,16,128]{3,2,1,0:T(8,128)(2,1)S(1)}, u32[]{:S(2)}, u32[]{:S(2)}) async-start(bf16[32,4,16,128]{3,2,1,0:T(8,128)(2,1)} %get-tuple-element.44), calls=%async_computation.3 | async-start | bytes 1048576 | tf_op jit(solution)/shard_map/all_to_all | solution.py:352
  105.3 8.7 %collective-permute-start.12 = (bf16[32,512]{1,0:T(8,128)(2,1)S(1)}, bf16[32,512]{1,0:T(8,128)(2,1)S(1)}, u32[]{:S(2)}, u32[]{:S(2)}) collective-permute-start(bf16[32,512]{1,0:T(8,128)(2,1)S(1)} %get-tuple-element.39), channel_id=1, source_target_pairs={{0,128},{128,256},{256,384},{384,0},{1,129},{129,257},{257,385},{3... | collective-permute-start | bytes 98312 | tf_op jit(solution)/shard_map/ppermute | solution.py:107
  107.5 6.5 %collective-permute-start.13 = (bf16[32,512]{1,0:T(8,128)(2,1)S(1)}, bf16[32,512]{1,0:T(8,128)(2,1)S(1)}, u32[]{:S(2)}, u32[]{:S(2)}) collective-permute-start(bf16[32,512]{1,0:T(8,128)(2,1)S(1)} %get-tuple-element.40), channel_id=1, source_target_pairs={{0,256},{128,384},{256,0},{384,128},{1,257},{129,385},{257,1},{385... | collective-permute-start | bytes 98312 | tf_op jit(solution)/shard_map/ppermute | solution.py:107
  111.2 5.0 %collective-permute-start.14 = (bf16[32,512]{1,0:T(8,128)(2,1)S(1)}, bf16[32,512]{1,0:T(8,128)(2,1)S(1)}, u32[]{:S(2)}, u32[]{:S(2)}) collective-permute-start(bf16[32,512]{1,0:T(8,128)(2,1)S(1)} %get-tuple-element.41), channel_id=1, source_target_pairs={{0,384},{128,0},{256,128},{384,256},{1,385},{129,1},{257,129},{385... | collective-permute-start | bytes 98312 | tf_op jit(solution)/shard_map/ppermute | solution.py:107
  116.7 4.4 %collective-permute-start.15 = (bf16[16,512]{1,0:T(8,128)(2,1)S(1)}, bf16[16,512]{1,0:T(8,128)(2,1)S(1)}, u32[]{:S(2)}, u32[]{:S(2)}) collective-permute-start(bf16[16,512]{1,0:T(8,128)(2,1)S(1)} %get-tuple-element.43), channel_id=1, source_target_pairs={{0,16},{16,0},{1,17},{17,1},{2,18},{18,2},{3,19},{19,3},{4,20},{20... | collective-permute-start | bytes 49160 | tf_op jit(solution)/shard_map/ppermute | solution.py:358

commit v5 on v4

--- a/solution.py
+++ b/solution.py
@@ -183,19 +183,40 @@
                 pieces_ref[c, m, r] = grad_ref[at : at + rows, m * lanes : (m + 1) * lanes]
 
 
-def choose_kernel(info_ref, place_ref, blocks_ref, *refs):
+def cast_kernel(value_ref, *refs):
+    refs[-1][...] = value_ref[...].astype(BF16)
+
+
+def choose_kernel(info_ref, place_ref, blocks_ref, total_ref, *refs):
     out_ref = refs[-1]
+    rows, lanes = out_ref.shape[2:]
     for w in range(X):
-        out_ref[w] = blocks_ref[place_ref[w * ZH + info_ref[2]]]
-
-
-def spread_kernel(info_ref, parts_ref, total_ref, out_ref, *outs):
-    x = info_ref[1]
-    for peer in range(out_ref.shape[0]):
-        out_ref[peer] = parts_ref[...]
-    for step, ref in enumerate(outs):
-        at = pl.multiple_of((x + step) % X * ROWS, ROWS)
-        ref[...] = total_ref[pl.ds(at, ROWS), :].astype(ref.dtype)
+        tile = blocks_ref[place_ref[w * ZH + info_ref[2]]]
+        for c in range(CORE):
+            out_ref[w * CORE + c, 0] = tile
+            at = w * ROWS + c * rows
+            for lane in range(B // lanes):
+                part = total_ref[at : at + rows, lane * lanes : (lane + 1) * lanes]
+                out_ref[w * CORE + c, 1 + lane] = part.astype(BF16)
+
+
+def spread_kernel(info_ref, parts_ref, out_ref):
+    core = info_ref[0]
+    for w in range(X):
+        tile = parts_ref[w * CORE + core, 0]
+        for peer in range(out_ref.shape[0]):
+            out_ref[peer, w] = tile
+
+
+def finish_kernel(parts_ref, out_ref):
+    lanes = parts_ref.shape[3]
+    for c in range(CORE):
+        for lane in range(B // lanes):
+            total = parts_ref[c, 1 + lane].astype(F32)
+            for w in range(1, X):
+                total = total + parts_ref[w * CORE + c, 1 + lane].astype(F32)
+            at = c * B + lane * lanes
+            out_ref[:, at : at + lanes] = total.astype(BF16)
 
 
 def update_kernel(info_ref, own_ref, one, two, three, grad_ref, right_ref, out_ref, left):
@@ -204,28 +225,16 @@
     out_ref[...] = dot(product, right_ref[...])
 
 
-def halves_kernel(info_ref, own_ref, one, two, three, keep_ref, send_ref):
-    core = info_ref[0]
-    total = own_ref[...]
-    for got in (one, two, three):
-        total = total + got[...].astype(F32)
-    half = keep_ref.shape[0]
-    keep_ref[...] = jnp.where(core == 0, total[:half], total[half:]).astype(BF16)
-    send_ref[...] = jnp.where(core == 0, total[half:], total[:half]).astype(BF16)
-
-
-def refresh_kernel(info_ref, owner_ref, pieces_ref, own_ref, low_ref, one, two, three, stats_ref, roots_ref, block, product, old):
+def refresh_kernel(info_ref, owner_ref, mine_ref, theirs_ref, own_ref, low_ref, one, two, three, stats_ref, roots_ref, block, product, old):
     core, x, zh, mp, root = (info_ref[at] for at in range(5))
-    n_mp, n_root = pieces_ref.shape[1:3]
-    rows, lanes = pieces_ref.shape[4:]
+    n_mp, n_root, _, rows, lanes = mine_ref.shape
     quarter = own_ref.shape[0]
-    for c in range(CORE):
-        for m in range(n_mp):
-            for r in range(n_root):
-                for w in range(X):
-                    at = w * PART + (c * n_root + r) * rows
-                    block[at : at + rows, m * lanes : (m + 1) * lanes] = pieces_ref[c, m, r, w]
-
+    for ref, side in ((mine_ref, core), (theirs_ref, 1 - core)):
+        for r in range(n_root):
+            for w in range(X):
+                at = pl.ds(pl.multiple_of(w * PART + (side * n_root + r) * rows, rows), rows)
+                for m in range(n_mp):
+                    block[at, m * lanes : (m + 1) * lanes] = ref[m, r, w]
     place(old, (low_ref, one, two, three), mp)
 
     @pl.when(core == 0)
@@ -295,17 +304,13 @@
     theirs = lax.ppermute(
         lax.dynamic_index_in_dim(prec, 1 - core, 1, keepdims=False), "core", swap
     )
-    old_own = stats_old[0]
-    old_low = old_own.astype(BF16)
-    olds = [old_low] + shifted(old_low, "mp")
     keep, left_rows, *sends = kernel_call(
         sum_kernel,
         "sum_x",
         [SMEM] + [VMEM] * 3,
         [shape((PART, B), F32), shape((ROWS, B))] + [shape((PART // 2 + half, B))] * 2,
         [pltpu.VMEM((ROWS, B), BF16)],
-        awaited=1,
-    )(info, total, mine, theirs, olds[1])
+    )(info, total, mine, theirs)
     near = [(z, z ^ 1) for z in range(ZH)]
     far = [(z, ZH - 1 - z) for z in range(ZH)]
     got = [lax.ppermute(sends[0], "zh", near), lax.ppermute(sends[1], "zh", far)]
@@ -323,8 +328,12 @@
         "pack",
         [SMEM] + [VMEM] * 5,
         [shape((PART, B)), shape((CORE, n_mp, n_root, half, lanes)), shape((PART, B))],
-        awaited=2,
-    )(info, keep, *sends, *got, *olds[2:])
+    )(info, keep, *sends, *got)
+    old_own = stats_old[0]
+    (old_low,) = kernel_call(
+        cast_kernel, "cast", [VMEM], [shape((quarter, B))], awaited=1
+    )(old_own, got[0])
+    olds = [old_low] + shifted(old_low, "mp")
 
     blocks = lax.all_to_all(pieces.reshape(-1, half, lanes), ("core", "mp", "root"), 0, 0)
 
@@ -339,35 +348,29 @@
 
     at = (listed % 2) * (n_mp * n_root) + listed // 2
     (chosen,) = kernel_call(
-        choose_kernel, "choose", [SMEM, SMEM, VMEM], [shape((X, half, lanes))], awaited=1
-    )(info, at, blocks, total)
-    parts = lax.all_to_all(chosen, "x", 0, 0)
-    mine, own, *sends = kernel_call(
-        spread_kernel,
-        "spread",
-        [SMEM, VMEM, VMEM],
-        [shape((CORE * n_mp * n_root, X, half, lanes)), shape((ROWS, B), F32)]
-        + [shape((ROWS, B))] * 3,
-    )(info, parts, total)
-    gathered = lax.all_to_all(mine, ("core", "mp", "root"), 0, 0)
-    gathered = gathered.reshape((CORE, n_mp, n_root) + gathered.shape[1:])
-    got = [shift(send, "x", step) for step, send in enumerate(sends, 1)]
-    keep, send = kernel_call(
-        halves_kernel, "halves", [SMEM] + [VMEM] * 4, [shape((half, B))] * 2
-    )(info, own, *got)
-    got = lax.ppermute(send, "core", swap)
-    update = jnp.where(
-        core == 0, jnp.concatenate([keep, got], 1), jnp.concatenate([got, keep], 1)
-    )
+        choose_kernel,
+        "choose",
+        [SMEM, SMEM, VMEM, VMEM],
+        [shape((X * CORE, 1 + B // lanes, half, lanes))],
+        awaited=3,
+    )(info, at, blocks, total, *olds[1:])
+    parts = lax.all_to_all(chosen, ("x", "core"), 0, 0)
+    (mine,) = kernel_call(
+        spread_kernel, "spread", [SMEM, VMEM], [shape((n_mp * n_root, X, half, lanes))]
+    )(info, parts)
+    mine = lax.all_to_all(mine, ("mp", "root"), 0, 0)
+    theirs = lax.ppermute(mine, "core", swap)
+    gathered = [value.reshape((n_mp, n_root) + value.shape[1:]) for value in (mine, theirs)]
+    (update,) = kernel_call(finish_kernel, "finish", [VMEM], [shape((half, 2 * B))])(parts)
 
     new_stats, new_roots = kernel_call(
         refresh_kernel,
         "refresh",
-        [SMEM, SMEM] + [VMEM] * 6,
+        [SMEM, SMEM] + [VMEM] * 7,
         [shape((quarter, B), F32)] * 2,
         [pltpu.VMEM((B, B), BF16), pltpu.VMEM((B, B), F32), pltpu.VMEM((B, B), BF16)],
         cost(2 * B ** 3 + 10 * quarter * B * B, 2 * B * B * 2),
-    )(info, owner, gathered, old_own, *olds)
+    )(info, owner, *gathered, old_own, *olds)
     return update[None], new_stats[None, None], new_roots[None, None]
 
 

time: 126 us -> 128 us (1.016)
  blocking collectives: 7.64 us -> 26.2 us
  starting transfers between devices: 75.8 us -> 63.9 us
  waiting for transfers between devices: 27.2 us -> 24 us
    all_to_all x1 -> x2, blocking collectives: 7.64 us -> 26.2 us  [the longest x1 15.9 us: local(): mine = lax.all_to_all(mine, ('mp', 'root'), 0, 0)]
    ppermute x9 -> x6, starting transfers between devices: 27.2 us -> 19.1 us  [shift(): lax.ppermute(value, axis, [(at, (at + step) % size) for at in range(size)])]
    all_to_all x1, waiting for transfers between devices: 7.56 us -> 0.01 us  [local(): lax.all_to_all(pieces.reshape(-1, half, lanes), ('core', 'mp', 'root'), 0...]
    all_to_all x1 -> x0, starting transfers between devices: 5.98 us -> none  [local(): gathered = lax.all_to_all(mine, ('core', 'mp', 'root'), 0, 0)]
    all_to_all x1, waiting for transfers between devices: 1.34 us -> 6 us  [local(): total = lax.all_to_all(total.reshape(X, PART, B), 'x', 0, 0)]
    ppermute x0 -> x1, starting transfers between devices: none -> 4.06 us  [local(): theirs = lax.ppermute(mine, 'core', swap)]
    ppermute x2 -> x1, starting transfers between devices: 12.4 us -> 8.79 us  [local(): got = lax.ppermute(send, 'core', swap)]
    ppermute x1, starting transfers between devices: 1.92 us -> 4.03 us  [local(): lax.ppermute(sends[0], 'zh', far)]
  transfers between devices with their start and end apart: 19 -> 15, of which waited for: 9 -> 9; matrix products, arithmetic and copies ran while one was open for 1% -> 0% of each run, Pallas kernels for 2% -> 2%
where the time goes in v5:
time: 128 us; the launch traced here: 127 us
  starting transfers between devices  63.9 us (50%)
  blocking collectives  26.2 us (20%)
  waiting for transfers between devices  24 us (19%)
  Pallas kernels  11.8 us (9%)
    ppermute x6, starting transfers between devices, shift(): lax.ppermute(value, axis, [(at, (at + step) % size) for at in range(size)])  19.1 us
    all_to_all x1, blocking collectives, local(): mine = lax.all_to_all(mine, ('mp', 'root'), 0, 0)  15.9 us
    all_to_all x1, blocking collectives, local(): parts = lax.all_to_all(chosen, ('x', 'core'), 0, 0)  10.3 us
    ppermute x1, starting transfers between devices, local(): lax.ppermute(sends[1], 'zh', far)  8.81 us
    ppermute x1, starting transfers between devices, local(): got = lax.ppermute(send, 'core', swap)  8.79 us
    all_to_all x1, starting transfers between devices, local(): lax.all_to_all(pieces.reshape(-1, half, lanes), ('core', 'mp', 'root'), 0...  7.6 us
    all_to_all x1, waiting for transfers between devices, local(): total = lax.all_to_all(total.reshape(X, PART, B), 'x', 0, 0)  6 us
    ppermute x1, waiting for transfers between devices, local(): lax.ppermute(sends[1], 'zh', near)  5.96 us
  transfers between devices with their start and end apart: 15, of which 9 were waited for; matrix products, arithmetic and copies ran while one was open for 0% of the time, Pallas kernels for 2%

profile of v5, /device:TPU:1, one launch (start us, length us, event | category | flops | bytes accessed | tf_op | source)
XLA Modules:
  0.0 127.0 jit_solution(4646066335292302967)
XLA Ops:
  0.6 2.3 %other_half.1 = (bf16[512,1024]{1,0:T(8,128)(2,1)S(1)}, bf16[512,512]{1,0:T(8,128)(2,1)S(1)}, bf16[1024,512]{1,0:T(8,128)(2,1)S(1)}) custom-call(s32[1]{0:T(128)} %bitcast.5.index_ref, bf16[1024,512]{1,0:T(8,128)(2,1)} %acts_ref.1, bf16[1024,1024]{1,0:T(8,128)(2,1)} %grads_ref.1), custom_call_target="tpu_custom_call" | custom-call | flops 536870912 | bytes 3145728 | tf_op jit(solution)/shard_map/other_half/pallas_call | solution.py:80
  2.9 8.8 %collective-permute-start = (bf16[512,512]{1,0:T(8,128)(2,1)S(1)}, bf16[512,512]{1,0:T(8,128)(2,1)S(1)}, u32[]{:S(2)}, u32[]{:S(2)}) collective-permute-start(bf16[512,512]{1,0:T(8,128)(2,1)S(1)} %get-tuple-element.20), channel_id=1, source_target_pairs={{0,16},{16,0},{1,17},{17,1},{2,18},{18,2},{3,19},{19,3},{4,20},{20... | collective-permute-start | bytes 1572872 | tf_op jit(solution)/shard_map/ppermute | solution.py:292
  11.7 0.7 own_half.1.own_ref
  12.4 0.0 copy-start.2
  12.4 0.0 copy-start.3
  12.4 0.8 collective-permute-done.got_ref
  13.2 1.0 join.1
  14.3 3.6 %all-to-all-start = ((bf16[4,128,512]{2,1,0:T(8,128)(2,1)}), bf16[4,128,512]{2,1,0:T(8,128)(2,1)S(1)}, u32[]{:S(2)}, u32[]{:S(2)}) async-start(bf16[4,128,512]{2,1,0:T(8,128)(2,1)} %bitcast.6), calls=%async_computation | async-start | bytes 1048576 | tf_op jit(solution)/shard_map/all_to_all | solution.py:301
  17.9 0.0 copy-done.2
  17.9 0.0 copy-done.3
  17.9 2.3 %collective-permute-start.1 = (bf16[2,16,512]{2,1,0:T(8,128)(2,1)S(1)}, bf16[2,16,512]{2,1,0:T(8,128)(2,1)S(1)}, u32[]{:S(2)}, u32[]{:S(2)}) collective-permute-start(bf16[2,16,512]{2,1,0:T(8,128)(2,1)S(1)} %get-tuple-element.33), channel_id=1, source_target_pairs={{0,16},{16,0},{1,17},{17,1},{2,18},{18,2},{3,19},{19,3},{4,20},{20... | collective-permute-start | bytes 98312 | tf_op jit(solution)/shard_map/ppermute | solution.py:304
  20.2 0.1 stack.26.info_ref
  20.3 0.7 collective-permute-done.1.theirs_ref
  21.1 6.0 %all-to-all-done.parts_ref = bf16[4,128,512]{2,1,0:T(8,128)(2,1)S(1)} async-done(((bf16[4,128,512]{2,1,0:T(8,128)(2,1)}), bf16[4,128,512]{2,1,0:T(8,128)(2,1)S(1)}, u32[]{:S(2)}, u32[]{:S(2)}) %all-to-all-start) | async-done | bytes 524320 | tf_op jit(solution)/shard_map/all_to_all | solution.py:301
  27.1 0.6 sum_x.1
  27.7 3.7 %collective-permute-start.2 = (bf16[80,512]{1,0:T(8,128)(2,1)S(1)}, bf16[80,512]{1,0:T(8,128)(2,1)S(1)}, u32[]{:S(2)}, u32[]{:S(2)}) collective-permute-start(bf16[80,512]{1,0:T(8,128)(2,1)S(1)} %get-tuple-element.22.sent_one), channel_id=1, source_target_pairs={{0,32},{32,0},{64,96},{96,64},{1,33},{33,1},{65,97},{97,65},{2,34}... | collective-permute-start | bytes 245768 | tf_op jit(solution)/shard_map/ppermute | solution.py:316
  31.4 8.8 %collective-permute-start.3 = (bf16[80,512]{1,0:T(8,128)(2,1)S(1)}, bf16[80,512]{1,0:T(8,128)(2,1)S(1)}, u32[]{:S(2)}, u32[]{:S(2)}) collective-permute-start(bf16[80,512]{1,0:T(8,128)(2,1)S(1)} %get-tuple-element.23.sent_two), channel_id=1, source_target_pairs={{0,96},{32,64},{64,32},{96,0},{1,97},{33,65},{65,33},{97,1},{2,98}... | collective-permute-start | bytes 245768 | tf_op jit(solution)/shard_map/ppermute | solution.py:316
  40.2 2.2 %collective-permute-start.4 = (bf16[32,512]{1,0:T(8,128)(2,1)S(1)}, bf16[32,512]{1,0:T(8,128)(2,1)S(1)}, u32[]{:S(2)}, u32[]{:S(2)}) collective-permute-start(bf16[32,512]{1,0:T(8,128)(2,1)S(1)} %get-tuple-element.24.own_ref), channel_id=1, source_target_pairs={{0,128},{128,256},{256,384},{384,0},{1,129},{129,257},{257,385},{3... | collective-permute-start | bytes 98312 | tf_op jit(solution)/shard_map/ppermute | solution.py:107
  42.4 3.7 %collective-permute-start.5 = (bf16[32,512]{1,0:T(8,128)(2,1)S(1)}, bf16[32,512]{1,0:T(8,128)(2,1)S(1)}, u32[]{:S(2)}, u32[]{:S(2)}) collective-permute-start(bf16[32,512]{1,0:T(8,128)(2,1)S(1)} %get-tuple-element.24.own_ref), channel_id=1, source_target_pairs={{0,256},{128,384},{256,0},{384,128},{1,257},{129,385},{257,1},{385... | collective-permute-start | bytes 98312 | tf_op jit(solution)/shard_map/ppermute | solution.py:107
  46.1 2.5 %collective-permute-start.6 = (bf16[32,512]{1,0:T(8,128)(2,1)S(1)}, bf16[32,512]{1,0:T(8,128)(2,1)S(1)}, u32[]{:S(2)}, u32[]{:S(2)}) collective-permute-start(bf16[32,512]{1,0:T(8,128)(2,1)S(1)} %get-tuple-element.24.own_ref), channel_id=1, source_target_pairs={{0,384},{128,0},{256,128},{384,256},{1,385},{129,1},{257,129},{385... | collective-permute-start | bytes 98312 | tf_op jit(solution)/shard_map/ppermute | solution.py:107
  48.7 0.0 collective-permute-done.4.refs_0_.one
  48.7 0.0 collective-permute-done.5.refs_1_.two
  48.7 2.4 %collective-permute-done.6.refs_2_.three = bf16[32,512]{1,0:T(8,128)(2,1)S(1)} collective-permute-done((bf16[32,512]{1,0:T(8,128)(2,1)S(1)}, bf16[32,512]{1,0:T(8,128)(2,1)S(1)}, u32[]{:S(2)}, u32[]{:S(2)}) %collective-permute-start.6) | collective-permute-done | bytes 32800 | tf_op jit(solution)/shard_map/ppermute | solution.py:107
  51.1 0.0 collective-permute-done.2.got_one
  51.1 0.0 collective-permute-done.3.got_two
  51.1 4.0 %collective-permute-start.7 = (bf16[96,512]{1,0:T(8,128)(2,1)S(1)}, bf16[96,512]{1,0:T(8,128)(2,1)S(1)}, u32[]{:S(2)}, u32[]{:S(2)}) collective-permute-start(bf16[96,512]{1,0:T(8,128)(2,1)S(1)} %get-tuple-element.26.sent_one), channel_id=1, source_target_pairs={{0,96},{32,64},{64,32},{96,0},{1,97},{33,65},{65,33},{97,1},{2,98}... | collective-permute-start | bytes 294920 | tf_op jit(solution)/shard_map/ppermute | solution.py:325
  55.2 1.9 %collective-permute-start.8 = (bf16[96,512]{1,0:T(8,128)(2,1)S(1)}, bf16[96,512]{1,0:T(8,128)(2,1)S(1)}, u32[]{:S(2)}, u32[]{:S(2)}) collective-permute-start(bf16[96,512]{1,0:T(8,128)(2,1)S(1)} %get-tuple-element.27.sent_two), channel_id=1, source_target_pairs={{0,32},{32,0},{64,96},{96,64},{1,33},{33,1},{65,97},{97,65},{2,34}... | collective-permute-start | bytes 294920 | tf_op jit(solution)/shard_map/ppermute | solution.py:325
  57.1 5.6 %collective-permute-done.7.got_one.refs_0_ = bf16[96,512]{1,0:T(8,128)(2,1)S(1)} collective-permute-done((bf16[96,512]{1,0:T(8,128)(2,1)S(1)}, bf16[96,512]{1,0:T(8,128)(2,1)S(1)}, u32[]{:S(2)}, u32[]{:S(2)}) %collective-permute-start.7) | collective-permute-done | bytes 98336 | tf_op jit(solution)/shard_map/ppermute | solution.py:325
  62.7 6.0 %collective-permute-done.8.got_two = bf16[96,512]{1,0:T(8,128)(2,1)S(1)} collective-permute-done((bf16[96,512]{1,0:T(8,128)(2,1)S(1)}, bf16[96,512]{1,0:T(8,128)(2,1)S(1)}, u32[]{:S(2)}, u32[]{:S(2)}) %collective-permute-start.8) | collective-permute-done | bytes 98336 | tf_op jit(solution)/shard_map/ppermute | solution.py:325
  68.7 1.3 pack.1
  70.0 7.6 %all-to-all-start.1 = ((bf16[32,16,128]{2,1,0:T(8,128)(2,1)}), bf16[32,16,128]{2,1,0:T(8,128)(2,1)S(1)}, u32[]{:S(2)}, u32[]{:S(2)}) async-start(bf16[32,16,128]{2,1,0:T(8,128)(2,1)} %bitcast.9), calls=%async_computation.1 | async-start | bytes 262144 | tf_op jit(solution)/shard_map/all_to_all | solution.py:338
  77.6 0.0 copy-done
  77.6 3.3 %collective-permute-start.9 = (bf16[128,512]{1,0:T(8,128)(2,1)S(1)}, bf16[128,512]{1,0:T(8,128)(2,1)S(1)}, u32[]{:S(2)}, u32[]{:S(2)}) collective-permute-start(bf16[128,512]{1,0:T(8,128)(2,1)S(1)} %cast.1.low_ref), channel_id=1, source_target_pairs={{0,4},{4,8},{8,12},{12,0},{1,5},{5,9},{9,13},{13,1},{2,6},{6,10},{... | collective-permute-start | bytes 393224 | tf_op jit(solution)/shard_map/ppermute | solution.py:107
  80.9 4.3 %collective-permute-start.10 = (bf16[128,512]{1,0:T(8,128)(2,1)S(1)}, bf16[128,512]{1,0:T(8,128)(2,1)S(1)}, u32[]{:S(2)}, u32[]{:S(2)}) collective-permute-start(bf16[128,512]{1,0:T(8,128)(2,1)S(1)} %cast.1.low_ref), channel_id=1, source_target_pairs={{0,8},{4,12},{8,0},{12,4},{1,9},{5,13},{9,1},{13,5},{2,10},{6,14},... | collective-permute-start | bytes 393224 | tf_op jit(solution)/shard_map/ppermute | solution.py:107
  85.2 3.1 %collective-permute-start.11 = (bf16[128,512]{1,0:T(8,128)(2,1)S(1)}, bf16[128,512]{1,0:T(8,128)(2,1)S(1)}, u32[]{:S(2)}, u32[]{:S(2)}) collective-permute-start(bf16[128,512]{1,0:T(8,128)(2,1)S(1)} %cast.1.low_ref), channel_id=1, source_target_pairs={{0,12},{4,0},{8,4},{12,8},{1,13},{5,1},{9,5},{13,9},{2,14},{6,2},{... | collective-permute-start | bytes 393224 | tf_op jit(solution)/shard_map/ppermute | solution.py:107
  88.3 0.9 update.1.total_ref
  89.2 0.0 collective-permute-done.9.refs_0_.one
  89.3 0.8 collective-permute-done.10.refs_1_.two
  90.0 1.2 collective-permute-done.11.refs_2_.three
  91.3 0.0 all-to-all-done.1.blocks_ref
  91.3 0.6 choose.1
  91.8 10.3 %all_to_all.20.parts_ref = bf16[8,5,16,128]{3,2,1,0:T(8,128)(2,1)S(1)} all-to-all(bf16[8,5,16,128]{3,2,1,0:T(8,128)(2,1)S(1)} %choose.1), channel_id=1, replica_groups=mesh['x'=4,'zh'=4,'core'=2,'mp'=4,'root'=4] {'x','core'}, dimensions={0} | all-to-all | bytes 327680 | tf_op jit(solution)/shard_map/all_to_all | solution.py:357
  102.1 0.6 spread.1
  102.7 15.9 %all_to_all.21 = bf16[16,4,16,128]{3,2,1,0:T(8,128)(2,1)S(1)} all-to-all(bf16[16,4,16,128]{3,2,1,0:T(8,128)(2,1)S(1)} %spread.1), channel_id=1, replica_groups=mesh['x'=4,'zh'=4,'core'=2,'mp'=4,'root'=4] {'mp','root'}, dimensions={0} | all-to-all | bytes 524288 | tf_op jit(solution)/shard_map/all_to_all | solution.py:361
  118.6 4.1 %collective-permute-start.12 = (bf16[16,4,16,128]{3,2,1,0:T(8,128)(2,1)S(1)}, bf16[16,4,16,128]{3,2,1,0:T(8,128)(2,1)S(1)}, u32[]{:S(2)}, u32[]{:S(2)}) collective-permute-start(bf16[16,4,16,128]{3,2,1,0:T(8,128)(2,1)S(1)} %all_to_all.21), channel_id=1, source_target_pairs={{0,16},{16,0},{1,17},{17,1},{2,18},{18,2},{3,19},{19,3},{4,20},{20... | collective-permute-start | bytes 786440 | tf_op jit(solution)/shard_map/ppermute | solution.py:362
  122.7 0.6 finish.1
  123.3 0.5 collective-permute-done.12
  123.8 3.2 %refresh.1 = (f32[128,512]{1,0:T(8,128)}, f32[128,512]{1,0:T(8,128)}) custom-call(s32[5]{0:T(128)S(1)} %stack.26.info_ref, s32[16]{0:T(128)S(1)} %copy-done.1, bf16[4,4,4,16,128]{4,3,2,1,0:T(8,128)(2,1)S(1)} %bitcast.18, bf16[4,4,4,16,128]{4,3,2,1,0:T(8,128)(2,1)S(1)} %bitcast.21, f32[128,512]{1,0:T(8,128)S(1)} %bitcast.20, ...), custom_call_target="tpu_custom_call" | custom-call | flops 603979776 | bytes 1048576 | tf_op jit(solution)/shard_map/refresh/pallas_call | solution.py:366
  (11 shorter events, 0.1 us)
Async XLA Ops:
  2.9 10.3 %collective-permute-start = (bf16[512,512]{1,0:T(8,128)(2,1)S(1)}, bf16[512,512]{1,0:T(8,128)(2,1)S(1)}, u32[]{:S(2)}, u32[]{:S(2)}) collective-permute-start(bf16[512,512]{1,0:T(8,128)(2,1)S(1)} %get-tuple-element.20), channel_id=1, source_target_pairs={{0,16},{16,0},{1,17},{17,1},{2,18},{18,2},{3,19},{19,3},{4,20},{20... | collective-permute-start | bytes 1572872 | tf_op jit(solution)/shard_map/ppermute | solution.py:292
  12.4 5.4 %copy-start.2 = (bf16[1,2,16,512]{3,2,1,0:T(8,128)(2,1)S(1)}, bf16[1,2,16,512]{3,2,1,0:T(8,128)(2,1)}, u32[]{:S(2)}) copy-start(bf16[1,2,16,512]{3,2,1,0:T(8,128)(2,1)} %param.9) | copy-start | bytes 98308
  12.4 5.5 %copy-start.3 = (bf16[1,2,16,512]{3,2,1,0:T(8,128)(2,1)S(1)}, bf16[1,2,16,512]{3,2,1,0:T(8,128)(2,1)}, u32[]{:S(2)}) copy-start(bf16[1,2,16,512]{3,2,1,0:T(8,128)(2,1)} %param.10) | copy-start | bytes 98308
  14.2 63.3 %copy-start = (f32[1,128,512]{2,1,0:T(8,128)S(1)}, f32[1,128,512]{2,1,0:T(8,128)}, u32[]{:S(2)}) copy-start(f32[1,128,512]{2,1,0:T(8,128)} %param.11) | copy-start | bytes 786436
  14.2 74.1 %copy-start.4 = (s32[16]{0:T(128)S(1)}, s32[16]{0:T(128)}, u32[]{:S(2)}) copy-start(s32[16]{0:T(128)} %param.12) | copy-start | bytes 196
  14.3 12.8 %all-to-all-start = ((bf16[4,128,512]{2,1,0:T(8,128)(2,1)}), bf16[4,128,512]{2,1,0:T(8,128)(2,1)S(1)}, u32[]{:S(2)}, u32[]{:S(2)}) async-start(bf16[4,128,512]{2,1,0:T(8,128)(2,1)} %bitcast.6), calls=%async_computation | async-start | bytes 1048576 | tf_op jit(solution)/shard_map/all_to_all | solution.py:301
  17.9 3.1 %collective-permute-start.1 = (bf16[2,16,512]{2,1,0:T(8,128)(2,1)S(1)}, bf16[2,16,512]{2,1,0:T(8,128)(2,1)S(1)}, u32[]{:S(2)}, u32[]{:S(2)}) collective-permute-start(bf16[2,16,512]{2,1,0:T(8,128)(2,1)S(1)} %get-tuple-element.33), channel_id=1, source_target_pairs={{0,16},{16,0},{1,17},{17,1},{2,18},{18,2},{3,19},{19,3},{4,20},{20... | collective-permute-start | bytes 98312 | tf_op jit(solution)/shard_map/ppermute | solution.py:304
  27.7 23.4 %collective-permute-start.2 = (bf16[80,512]{1,0:T(8,128)(2,1)S(1)}, bf16[80,512]{1,0:T(8,128)(2,1)S(1)}, u32[]{:S(2)}, u32[]{:S(2)}) collective-permute-start(bf16[80,512]{1,0:T(8,128)(2,1)S(1)} %get-tuple-element.22.sent_one), channel_id=1, source_target_pairs={{0,32},{32,0},{64,96},{96,64},{1,33},{33,1},{65,97},{97,65},{2,34}... | collective-permute-start | bytes 245768 | tf_op jit(solution)/shard_map/ppermute | solution.py:316
  31.4 19.7 %collective-permute-start.3 = (bf16[80,512]{1,0:T(8,128)(2,1)S(1)}, bf16[80,512]{1,0:T(8,128)(2,1)S(1)}, u32[]{:S(2)}, u32[]{:S(2)}) collective-permute-start(bf16[80,512]{1,0:T(8,128)(2,1)S(1)} %get-tuple-element.23.sent_two), channel_id=1, source_target_pairs={{0,96},{32,64},{64,32},{96,0},{1,97},{33,65},{65,33},{97,1},{2,98}... | collective-permute-start | bytes 245768 | tf_op jit(solution)/shard_map/ppermute | solution.py:316
  40.2 8.4 %collective-permute-start.4 = (bf16[32,512]{1,0:T(8,128)(2,1)S(1)}, bf16[32,512]{1,0:T(8,128)(2,1)S(1)}, u32[]{:S(2)}, u32[]{:S(2)}) collective-permute-start(bf16[32,512]{1,0:T(8,128)(2,1)S(1)} %get-tuple-element.24.own_ref), channel_id=1, source_target_pairs={{0,128},{128,256},{256,384},{384,0},{1,129},{129,257},{257,385},{3... | collective-permute-start | bytes 98312 | tf_op jit(solution)/shard_map/ppermute | solution.py:107
  42.4 6.3 %collective-permute-start.5 = (bf16[32,512]{1,0:T(8,128)(2,1)S(1)}, bf16[32,512]{1,0:T(8,128)(2,1)S(1)}, u32[]{:S(2)}, u32[]{:S(2)}) collective-permute-start(bf16[32,512]{1,0:T(8,128)(2,1)S(1)} %get-tuple-element.24.own_ref), channel_id=1, source_target_pairs={{0,256},{128,384},{256,0},{384,128},{1,257},{129,385},{257,1},{385... | collective-permute-start | bytes 98312 | tf_op jit(solution)/shard_map/ppermute | solution.py:107
  46.1 5.0 %collective-permute-start.6 = (bf16[32,512]{1,0:T(8,128)(2,1)S(1)}, bf16[32,512]{1,0:T(8,128)(2,1)S(1)}, u32[]{:S(2)}, u32[]{:S(2)}) collective-permute-start(bf16[32,512]{1,0:T(8,128)(2,1)S(1)} %get-tuple-element.24.own_ref), channel_id=1, source_target_pairs={{0,384},{128,0},{256,128},{384,256},{1,385},{129,1},{257,129},{385... | collective-permute-start | bytes 98312 | tf_op jit(solution)/shard_map/ppermute | solution.py:107
  51.1 11.6 %collective-permute-start.7 = (bf16[96,512]{1,0:T(8,128)(2,1)S(1)}, bf16[96,512]{1,0:T(8,128)(2,1)S(1)}, u32[]{:S(2)}, u32[]{:S(2)}) collective-permute-start(bf16[96,512]{1,0:T(8,128)(2,1)S(1)} %get-tuple-element.26.sent_one), channel_id=1, source_target_pairs={{0,96},{32,64},{64,32},{96,0},{1,97},{33,65},{65,33},{97,1},{2,98}... | collective-permute-start | bytes 294920 | tf_op jit(solution)/shard_map/ppermute | solution.py:325
  55.2 13.5 %collective-permute-start.8 = (bf16[96,512]{1,0:T(8,128)(2,1)S(1)}, bf16[96,512]{1,0:T(8,128)(2,1)S(1)}, u32[]{:S(2)}, u32[]{:S(2)}) collective-permute-start(bf16[96,512]{1,0:T(8,128)(2,1)S(1)} %get-tuple-element.27.sent_two), channel_id=1, source_target_pairs={{0,32},{32,0},{64,96},{96,64},{1,33},{33,1},{65,97},{97,65},{2,34}... | collective-permute-start | bytes 294920 | tf_op jit(solution)/shard_map/ppermute | solution.py:325
  68.7 55.1 %copy-start.1 = (s32[16]{0:T(128)S(1)}, s32[16]{0:T(128)}, u32[]{:S(2)}) copy-start(s32[16]{0:T(128)} %owner_ref.1) | copy-start | bytes 196
  70.0 21.3 %all-to-all-start.1 = ((bf16[32,16,128]{2,1,0:T(8,128)(2,1)}), bf16[32,16,128]{2,1,0:T(8,128)(2,1)S(1)}, u32[]{:S(2)}, u32[]{:S(2)}) async-start(bf16[32,16,128]{2,1,0:T(8,128)(2,1)} %bitcast.9), calls=%async_computation.1 | async-start | bytes 262144 | tf_op jit(solution)/shard_map/all_to_all | solution.py:338
  77.6 11.7 %collective-permute-start.9 = (bf16[128,512]{1,0:T(8,128)(2,1)S(1)}, bf16[128,512]{1,0:T(8,128)(2,1)S(1)}, u32[]{:S(2)}, u32[]{:S(2)}) collective-permute-start(bf16[128,512]{1,0:T(8,128)(2,1)S(1)} %cast.1.low_ref), channel_id=1, source_target_pairs={{0,4},{4,8},{8,12},{12,0},{1,5},{5,9},{9,13},{13,1},{2,6},{6,10},{... | collective-permute-start | bytes 393224 | tf_op jit(solution)/shard_map/ppermute | solution.py:107
  80.9 9.1 %collective-permute-start.10 = (bf16[128,512]{1,0:T(8,128)(2,1)S(1)}, bf16[128,512]{1,0:T(8,128)(2,1)S(1)}, u32[]{:S(2)}, u32[]{:S(2)}) collective-permute-start(bf16[128,512]{1,0:T(8,128)(2,1)S(1)} %cast.1.low_ref), channel_id=1, source_target_pairs={{0,8},{4,12},{8,0},{12,4},{1,9},{5,13},{9,1},{13,5},{2,10},{6,14},... | collective-permute-start | bytes 393224 | tf_op jit(solution)/shard_map/ppermute | solution.py:107
  85.2 6.0 %collective-permute-start.11 = (bf16[128,512]{1,0:T(8,128)(2,1)S(1)}, bf16[128,512]{1,0:T(8,128)(2,1)S(1)}, u32[]{:S(2)}, u32[]{:S(2)}) collective-permute-start(bf16[128,512]{1,0:T(8,128)(2,1)S(1)} %cast.1.low_ref), channel_id=1, source_target_pairs={{0,12},{4,0},{8,4},{12,8},{1,13},{5,1},{9,5},{13,9},{2,14},{6,2},{... | collective-permute-start | bytes 393224 | tf_op jit(solution)/shard_map/ppermute | solution.py:107
  118.6 5.2 %collective-permute-start.12 = (bf16[16,4,16,128]{3,2,1,0:T(8,128)(2,1)S(1)}, bf16[16,4,16,128]{3,2,1,0:T(8,128)(2,1)S(1)}, u32[]{:S(2)}, u32[]{:S(2)}) collective-permute-start(bf16[16,4,16,128]{3,2,1,0:T(8,128)(2,1)S(1)} %all_to_all.21), channel_id=1, source_target_pairs={{0,16},{16,0},{1,17},{17,1},{2,18},{18,2},{3,19},{19,3},{4,20},{20... | collective-permute-start | bytes 786440 | tf_op jit(solution)/shard_map/ppermute | solution.py:362

commit v6 on v5

--- a/solution.py
+++ b/solution.py
@@ -175,35 +175,35 @@
             start = half + place_at % 2 * rows
             to = pl.multiple_of(mate * ROWS + part * rows, rows)
             right_ref[pl.ds(to, rows), :] = source[start : start + rows]
-    cores, n_mp, n_root, rows, lanes = pieces_ref.shape
+    n_mp, n_root, cores, rows, lanes = pieces_ref.shape
     for c in range(cores):
         for r in range(n_root):
             at = (c * n_root + r) * rows
             for m in range(n_mp):
-                pieces_ref[c, m, r] = grad_ref[at : at + rows, m * lanes : (m + 1) * lanes]
-
-
-def cast_kernel(value_ref, *refs):
-    refs[-1][...] = value_ref[...].astype(BF16)
-
-
-def choose_kernel(info_ref, place_ref, blocks_ref, total_ref, *refs):
+                pieces_ref[m, r, c] = grad_ref[at : at + rows, m * lanes : (m + 1) * lanes]
+
+
+def copy_kernel(value_ref, *refs):
+    refs[-1][...] = value_ref[...]
+
+
+def choose_kernel(info_ref, listed_ref, blocks_ref, total_ref, *refs):
     out_ref = refs[-1]
     rows, lanes = out_ref.shape[2:]
     for w in range(X):
-        tile = blocks_ref[place_ref[w * ZH + info_ref[2]]]
+        pair = listed_ref[w * ZH + info_ref[2]] // 2
         for c in range(CORE):
-            out_ref[w * CORE + c, 0] = tile
+            out_ref[w * CORE + c, 0] = blocks_ref[pair, c]
             at = w * ROWS + c * rows
             for lane in range(B // lanes):
                 part = total_ref[at : at + rows, lane * lanes : (lane + 1) * lanes]
                 out_ref[w * CORE + c, 1 + lane] = part.astype(BF16)
 
 
-def spread_kernel(info_ref, parts_ref, out_ref):
-    core = info_ref[0]
+def spread_kernel(info_ref, listed_ref, parts_ref, out_ref):
+    holder = listed_ref[info_ref[1] * ZH + info_ref[2]] % 2
     for w in range(X):
-        tile = parts_ref[w * CORE + core, 0]
+        tile = parts_ref[w * CORE + holder, 0]
         for peer in range(out_ref.shape[0]):
             out_ref[peer, w] = tile
 
@@ -304,38 +304,44 @@
     theirs = lax.ppermute(
         lax.dynamic_index_in_dim(prec, 1 - core, 1, keepdims=False), "core", swap
     )
+    old_own = stats_old[0]
+    old_low = old_own.astype(BF16)
+    olds = [old_low] + shifted(old_low, "mp")
     keep, left_rows, *sends = kernel_call(
         sum_kernel,
         "sum_x",
         [SMEM] + [VMEM] * 3,
         [shape((PART, B), F32), shape((ROWS, B))] + [shape((PART // 2 + half, B))] * 2,
         [pltpu.VMEM((ROWS, B), BF16)],
-    )(info, total, mine, theirs)
+        awaited=1,
+    )(info, total, mine, theirs, olds[1])
     near = [(z, z ^ 1) for z in range(ZH)]
     far = [(z, ZH - 1 - z) for z in range(ZH)]
     got = [lax.ppermute(sends[0], "zh", near), lax.ppermute(sends[1], "zh", far)]
-    lefts = [left_rows] + shifted(left_rows, "x")
+    lefts = [left_rows, shift(left_rows, "x", 1)]
     keep, *sends = kernel_call(
         middle_kernel,
         "middle",
         [VMEM] * 5,
         [shape((PART, B), F32)] + [shape((PART // 2 + 2 * half, B))] * 2,
-        awaited=3,
-    )(keep, *sends, *got, *lefts[1:])
+        awaited=1,
+    )(keep, *sends, *got, lefts[1])
     got = [lax.ppermute(sends[0], "zh", far), lax.ppermute(sends[1], "zh", near)]
+    (left_later,) = kernel_call(
+        copy_kernel, "left_rows", [VMEM], [shape((ROWS, B))], awaited=1
+    )(left_rows, got[0])
+    lefts += [shift(left_later, "x", step) for step in range(2, X)]
     grad, pieces, right_part = kernel_call(
         functools.partial(pack_kernel, tokens ** -0.5),
         "pack",
         [SMEM] + [VMEM] * 5,
-        [shape((PART, B)), shape((CORE, n_mp, n_root, half, lanes)), shape((PART, B))],
-    )(info, keep, *sends, *got)
-    old_own = stats_old[0]
-    (old_low,) = kernel_call(
-        cast_kernel, "cast", [VMEM], [shape((quarter, B))], awaited=1
-    )(old_own, got[0])
-    olds = [old_low] + shifted(old_low, "mp")
-
-    blocks = lax.all_to_all(pieces.reshape(-1, half, lanes), ("core", "mp", "root"), 0, 0)
+        [shape((PART, B)), shape((n_mp, n_root, CORE, half, lanes)), shape((PART, B))],
+        awaited=2,
+    )(info, keep, *sends, *got, *lefts[2:])
+
+
+    pieces = pieces.reshape((n_mp * n_root,) + pieces.shape[2:])
+    blocks = lax.all_to_all(pieces, ("mp", "root"), 0, 0)
 
     (total,) = kernel_call(
         update_kernel,
@@ -346,18 +352,17 @@
         cost(2 * PART * B * (PART + B), 6 * PART * B),
     )(info, *lefts, grad, right_part)
 
-    at = (listed % 2) * (n_mp * n_root) + listed // 2
     (chosen,) = kernel_call(
         choose_kernel,
         "choose",
         [SMEM, SMEM, VMEM, VMEM],
         [shape((X * CORE, 1 + B // lanes, half, lanes))],
-        awaited=3,
-    )(info, at, blocks, total, *olds[1:])
+        awaited=1,
+    )(info, listed, blocks, total, olds[2])
     parts = lax.all_to_all(chosen, ("x", "core"), 0, 0)
     (mine,) = kernel_call(
-        spread_kernel, "spread", [SMEM, VMEM], [shape((n_mp * n_root, X, half, lanes))]
-    )(info, parts)
+        spread_kernel, "spread", [SMEM, SMEM, VMEM], [shape((n_mp * n_root, X, half, lanes))]
+    )(info, listed, parts)
     mine = lax.all_to_all(mine, ("mp", "root"), 0, 0)
     theirs = lax.ppermute(mine, "core", swap)
     gathered = [value.reshape((n_mp, n_root) + value.shape[1:]) for value in (mine, theirs)]

time: 128 us -> 132 us (1.031)
  starting transfers between devices: 63.9 us -> 67.7 us
  blocking collectives: 26.2 us -> 29.1 us
  waiting for transfers between devices: 24 us -> 21.3 us
    ppermute x6, waiting for transfers between devices: 4.4 us -> 14 us  [shift(): lax.ppermute(value, axis, [(at, (at + step) % size) for at in range(size)])]
    ppermute x1, waiting for transfers between devices: 5.96 us -> 0.01 us  [local(): lax.ppermute(sends[1], 'zh', near)]
    all_to_all x1, waiting for transfers between devices: 6 us -> 1.33 us  [local(): total = lax.all_to_all(total.reshape(X, PART, B), 'x', 0, 0)]
    ppermute x1, starting transfers between devices: 4.03 us -> 8.16 us  [local(): lax.ppermute(sends[0], 'zh', far)]
    all_to_all x1, blocking collectives: 10.3 us -> 12.8 us  [local(): parts = lax.all_to_all(chosen, ('x', 'core'), 0, 0)]
    ppermute x1, waiting for transfers between devices: 5.64 us -> 3.54 us  [local(): lax.ppermute(sends[0], 'zh', far)]
  transfers between devices with their start and end apart: 15 -> 15, of which waited for: 9 -> 10; matrix products, arithmetic and copies ran while one was open for 0% -> 0% of each run, Pallas kernels for 2% -> 2%
where the time goes in v6:
time: 132 us; the launch traced here: 131 us
  starting transfers between devices  67.7 us (51%)
  blocking collectives  29.1 us (22%)
  waiting for transfers between devices  21.3 us (16%)
  Pallas kernels  11.8 us (9%)
    ppermute x6, starting transfers between devices, shift(): lax.ppermute(value, axis, [(at, (at + step) % size) for at in range(size)])  17.8 us
    all_to_all x1, blocking collectives, local(): mine = lax.all_to_all(mine, ('mp', 'root'), 0, 0)  16.3 us
    ppermute x6, waiting for transfers between devices, shift(): lax.ppermute(value, axis, [(at, (at + step) % size) for at in range(size)])  14 us
    all_to_all x1, blocking collectives, local(): parts = lax.all_to_all(chosen, ('x', 'core'), 0, 0)  12.8 us
    ppermute x1, starting transfers between devices, local(): lax.ppermute(sends[1], 'zh', far)  8.81 us
    ppermute x1, starting transfers between devices, local(): got = lax.ppermute(send, 'core', swap)  8.79 us
    all_to_all x1, starting transfers between devices, local(): blocks = lax.all_to_all(pieces, ('mp', 'root'), 0, 0)  8.71 us
    ppermute x1, starting transfers between devices, local(): lax.ppermute(sends[0], 'zh', far)  8.16 us
  transfers between devices with their start and end apart: 15, of which 10 were waited for; matrix products, arithmetic and copies ran while one was open for 0% of the time, Pallas kernels for 2%

profile of v6, /device:TPU:1, one launch (start us, length us, event | category | flops | bytes accessed | tf_op | source)
XLA Modules:
  0.0 131.1 jit_solution(8797341382527187401)
XLA Ops:
  0.6 2.3 %other_half.1 = (bf16[512,1024]{1,0:T(8,128)(2,1)S(1)}, bf16[512,512]{1,0:T(8,128)(2,1)S(1)}, bf16[1024,512]{1,0:T(8,128)(2,1)S(1)}) custom-call(s32[1]{0:T(128)} %bitcast.5.index_ref, bf16[1024,512]{1,0:T(8,128)(2,1)} %acts_ref.1, bf16[1024,1024]{1,0:T(8,128)(2,1)} %grads_ref.1), custom_call_target="tpu_custom_call" | custom-call | flops 536870912 | bytes 3145728 | tf_op jit(solution)/shard_map/other_half/pallas_call | solution.py:80
  2.9 8.8 %collective-permute-start = (bf16[512,512]{1,0:T(8,128)(2,1)S(1)}, bf16[512,512]{1,0:T(8,128)(2,1)S(1)}, u32[]{:S(2)}, u32[]{:S(2)}) collective-permute-start(bf16[512,512]{1,0:T(8,128)(2,1)S(1)} %get-tuple-element.20), channel_id=1, source_target_pairs={{0,16},{16,0},{1,17},{17,1},{2,18},{18,2},{3,19},{19,3},{4,20},{20... | collective-permute-start | bytes 1572872 | tf_op jit(solution)/shard_map/ppermute | solution.py:292
  11.7 0.7 own_half.1.own_ref
  12.4 0.0 copy-start
  12.4 0.0 copy-start.3
  12.4 0.0 copy-start.4
  12.4 0.8 collective-permute-done.got_ref
  13.2 1.0 join.1
  14.2 3.5 %all-to-all-start = ((bf16[4,128,512]{2,1,0:T(8,128)(2,1)}), bf16[4,128,512]{2,1,0:T(8,128)(2,1)S(1)}, u32[]{:S(2)}, u32[]{:S(2)}) async-start(bf16[4,128,512]{2,1,0:T(8,128)(2,1)} %bitcast.6), calls=%async_computation | async-start | bytes 1048576 | tf_op jit(solution)/shard_map/all_to_all | solution.py:301
  17.7 0.0 copy-start.1
  17.8 1.9 %collective-permute-start.2 = (bf16[128,512]{1,0:T(8,128)(2,1)S(1)}, bf16[128,512]{1,0:T(8,128)(2,1)S(1)}, u32[]{:S(2)}, u32[]{:S(2)}) collective-permute-start(bf16[128,512]{1,0:T(8,128)(2,1)S(1)} %bitcast_convert_fusion.low_ref), channel_id=1, source_target_pairs={{0,4},{4,8},{8,12},{12,0},{1,5},{5,9},{9,13},{13,1},{2,6},{6,10},{... | collective-permute-start | bytes 393224 | tf_op jit(solution)/shard_map/ppermute | solution.py:107
  19.8 2.3 %collective-permute-start.1 = (bf16[2,16,512]{2,1,0:T(8,128)(2,1)S(1)}, bf16[2,16,512]{2,1,0:T(8,128)(2,1)S(1)}, u32[]{:S(2)}, u32[]{:S(2)}) collective-permute-start(bf16[2,16,512]{2,1,0:T(8,128)(2,1)S(1)} %get-tuple-element.33), channel_id=1, source_target_pairs={{0,16},{16,0},{1,17},{17,1},{2,18},{18,2},{3,19},{19,3},{4,20},{20... | collective-permute-start | bytes 98312 | tf_op jit(solution)/shard_map/ppermute | solution.py:304
  22.1 0.1 stack.26.info_ref
  22.2 0.7 collective-permute-done.1.theirs_ref
  22.9 2.7 %collective-permute-done.2.refs_0_.one = bf16[128,512]{1,0:T(8,128)(2,1)S(1)} collective-permute-done((bf16[128,512]{1,0:T(8,128)(2,1)S(1)}, bf16[128,512]{1,0:T(8,128)(2,1)S(1)}, u32[]{:S(2)}, u32[]{:S(2)}) %collective-permute-start.2) | collective-permute-done | bytes 131104 | tf_op jit(solution)/shard_map/ppermute | solution.py:107
  25.6 1.3 %all-to-all-done.parts_ref = bf16[4,128,512]{2,1,0:T(8,128)(2,1)S(1)} async-done(((bf16[4,128,512]{2,1,0:T(8,128)(2,1)}), bf16[4,128,512]{2,1,0:T(8,128)(2,1)S(1)}, u32[]{:S(2)}, u32[]{:S(2)}) %all-to-all-start) | async-done | bytes 524320 | tf_op jit(solution)/shard_map/all_to_all | solution.py:301
  26.9 0.6 sum_x.1
  27.6 3.7 %collective-permute-start.3 = (bf16[80,512]{1,0:T(8,128)(2,1)S(1)}, bf16[80,512]{1,0:T(8,128)(2,1)S(1)}, u32[]{:S(2)}, u32[]{:S(2)}) collective-permute-start(bf16[80,512]{1,0:T(8,128)(2,1)S(1)} %get-tuple-element.22.sent_one), channel_id=1, source_target_pairs={{0,32},{32,0},{64,96},{96,64},{1,33},{33,1},{65,97},{97,65},{2,34}... | collective-permute-start | bytes 245768 | tf_op jit(solution)/shard_map/ppermute | solution.py:320
  31.3 8.8 %collective-permute-start.4 = (bf16[80,512]{1,0:T(8,128)(2,1)S(1)}, bf16[80,512]{1,0:T(8,128)(2,1)S(1)}, u32[]{:S(2)}, u32[]{:S(2)}) collective-permute-start(bf16[80,512]{1,0:T(8,128)(2,1)S(1)} %get-tuple-element.23.sent_two), channel_id=1, source_target_pairs={{0,96},{32,64},{64,32},{96,0},{1,97},{33,65},{65,33},{97,1},{2,98}... | collective-permute-start | bytes 245768 | tf_op jit(solution)/shard_map/ppermute | solution.py:320
  40.1 2.2 %collective-permute-start.5 = (bf16[32,512]{1,0:T(8,128)(2,1)S(1)}, bf16[32,512]{1,0:T(8,128)(2,1)S(1)}, u32[]{:S(2)}, u32[]{:S(2)}) collective-permute-start(bf16[32,512]{1,0:T(8,128)(2,1)S(1)} %get-tuple-element.24.value_ref.own_ref), channel_id=1, source_target_pairs={{0,128},{128,256},{256,384},{384,0},{1,129},{129,257},{257,385},{3... | collective-permute-start | bytes 98312 | tf_op jit(solution)/shard_map/ppermute | solution.py:107
  42.3 3.7 %collective-permute-done.5.refs_0_.one = bf16[32,512]{1,0:T(8,128)(2,1)S(1)} collective-permute-done((bf16[32,512]{1,0:T(8,128)(2,1)S(1)}, bf16[32,512]{1,0:T(8,128)(2,1)S(1)}, u32[]{:S(2)}, u32[]{:S(2)}) %collective-permute-start.5) | collective-permute-done | bytes 32800 | tf_op jit(solution)/shard_map/ppermute | solution.py:107
  46.0 0.0 collective-permute-done.3.got_one
  46.0 0.9 collective-permute-done.4.got_two
  46.9 0.0 copy-start.2
  46.9 8.2 %collective-permute-start.6 = (bf16[96,512]{1,0:T(8,128)(2,1)S(1)}, bf16[96,512]{1,0:T(8,128)(2,1)S(1)}, u32[]{:S(2)}, u32[]{:S(2)}) collective-permute-start(bf16[96,512]{1,0:T(8,128)(2,1)S(1)} %get-tuple-element.26.sent_one), channel_id=1, source_target_pairs={{0,96},{32,64},{64,32},{96,0},{1,97},{33,65},{65,33},{97,1},{2,98}... | collective-permute-start | bytes 294920 | tf_op jit(solution)/shard_map/ppermute | solution.py:329
  55.0 1.9 %collective-permute-start.7 = (bf16[96,512]{1,0:T(8,128)(2,1)S(1)}, bf16[96,512]{1,0:T(8,128)(2,1)S(1)}, u32[]{:S(2)}, u32[]{:S(2)}) collective-permute-start(bf16[96,512]{1,0:T(8,128)(2,1)S(1)} %get-tuple-element.27.sent_two), channel_id=1, source_target_pairs={{0,32},{32,0},{64,96},{96,64},{1,33},{33,1},{65,97},{97,65},{2,34}... | collective-permute-start | bytes 294920 | tf_op jit(solution)/shard_map/ppermute | solution.py:329
  57.0 3.5 %collective-permute-done.6.refs_0_.got_one = bf16[96,512]{1,0:T(8,128)(2,1)S(1)} collective-permute-done((bf16[96,512]{1,0:T(8,128)(2,1)S(1)}, bf16[96,512]{1,0:T(8,128)(2,1)S(1)}, u32[]{:S(2)}, u32[]{:S(2)}) %collective-permute-start.6) | collective-permute-done | bytes 98336 | tf_op jit(solution)/shard_map/ppermute | solution.py:329
  60.5 3.0 %collective-permute-start.8 = (bf16[32,512]{1,0:T(8,128)(2,1)S(1)}, bf16[32,512]{1,0:T(8,128)(2,1)S(1)}, u32[]{:S(2)}, u32[]{:S(2)}) collective-permute-start(bf16[32,512]{1,0:T(8,128)(2,1)S(1)} %left_rows.1), channel_id=1, source_target_pairs={{0,256},{128,384},{256,0},{384,128},{1,257},{129,385},{257,1},{385... | collective-permute-start | bytes 98312 | tf_op jit(solution)/shard_map/ppermute | solution.py:107
  63.5 3.5 %collective-permute-start.9 = (bf16[32,512]{1,0:T(8,128)(2,1)S(1)}, bf16[32,512]{1,0:T(8,128)(2,1)S(1)}, u32[]{:S(2)}, u32[]{:S(2)}) collective-permute-start(bf16[32,512]{1,0:T(8,128)(2,1)S(1)} %left_rows.1), channel_id=1, source_target_pairs={{0,384},{128,0},{256,128},{384,256},{1,385},{129,1},{257,129},{385... | collective-permute-start | bytes 98312 | tf_op jit(solution)/shard_map/ppermute | solution.py:107
  67.0 0.0 collective-permute-done.7.got_two
  67.0 0.0 collective-permute-done.8.refs_0_.two
  67.0 1.4 %collective-permute-done.9.refs_1_.three = bf16[32,512]{1,0:T(8,128)(2,1)S(1)} collective-permute-done((bf16[32,512]{1,0:T(8,128)(2,1)S(1)}, bf16[32,512]{1,0:T(8,128)(2,1)S(1)}, u32[]{:S(2)}, u32[]{:S(2)}) %collective-permute-start.9) | collective-permute-done | bytes 32800 | tf_op jit(solution)/shard_map/ppermute | solution.py:107
  68.4 1.3 pack.1
  69.7 8.7 %all-to-all-start.1 = ((bf16[16,2,16,128]{3,2,1,0:T(8,128)(2,1)}), bf16[16,2,16,128]{3,2,1,0:T(8,128)(2,1)S(1)}, u32[]{:S(2)}, u32[]{:S(2)}) async-start(bf16[16,2,16,128]{3,2,1,0:T(8,128)(2,1)} %bitcast.10), calls=%async_computation.1 | async-start | bytes 262144 | tf_op jit(solution)/shard_map/all_to_all | solution.py:344
  78.4 4.8 %collective-permute-start.10 = (bf16[128,512]{1,0:T(8,128)(2,1)S(1)}, bf16[128,512]{1,0:T(8,128)(2,1)S(1)}, u32[]{:S(2)}, u32[]{:S(2)}) collective-permute-start(bf16[128,512]{1,0:T(8,128)(2,1)S(1)} %bitcast_convert_fusion.low_ref), channel_id=1, source_target_pairs={{0,8},{4,12},{8,0},{12,4},{1,9},{5,13},{9,1},{13,5},{2,10},{6,14},... | collective-permute-start | bytes 393224 | tf_op jit(solution)/shard_map/ppermute | solution.py:107
  83.2 0.9 update.1.total_ref
  84.1 2.4 %collective-permute-done.10.refs_0_.two = bf16[128,512]{1,0:T(8,128)(2,1)S(1)} collective-permute-done((bf16[128,512]{1,0:T(8,128)(2,1)S(1)}, bf16[128,512]{1,0:T(8,128)(2,1)S(1)}, u32[]{:S(2)}, u32[]{:S(2)}) %collective-permute-start.10) | collective-permute-done | bytes 131104 | tf_op jit(solution)/shard_map/ppermute | solution.py:107
  86.5 0.0 all-to-all-done.1.blocks_ref
  86.5 0.6 choose.1
  87.0 12.8 %all_to_all.20.parts_ref = bf16[8,5,16,128]{3,2,1,0:T(8,128)(2,1)S(1)} all-to-all(bf16[8,5,16,128]{3,2,1,0:T(8,128)(2,1)S(1)} %choose.1), channel_id=1, replica_groups=mesh['x'=4,'zh'=4,'core'=2,'mp'=4,'root'=4] {'x','core'}, dimensions={0} | all-to-all | bytes 327680 | tf_op jit(solution)/shard_map/all_to_all | solution.py:362
  99.8 0.6 spread.1
  100.4 16.3 %all_to_all.21 = bf16[16,4,16,128]{3,2,1,0:T(8,128)(2,1)S(1)} all-to-all(bf16[16,4,16,128]{3,2,1,0:T(8,128)(2,1)S(1)} %spread.1), channel_id=1, replica_groups=mesh['x'=4,'zh'=4,'core'=2,'mp'=4,'root'=4] {'mp','root'}, dimensions={0} | all-to-all | bytes 524288 | tf_op jit(solution)/shard_map/all_to_all | solution.py:366
  116.8 4.1 %collective-permute-start.11 = (bf16[16,4,16,128]{3,2,1,0:T(8,128)(2,1)S(1)}, bf16[16,4,16,128]{3,2,1,0:T(8,128)(2,1)S(1)}, u32[]{:S(2)}, u32[]{:S(2)}) collective-permute-start(bf16[16,4,16,128]{3,2,1,0:T(8,128)(2,1)S(1)} %all_to_all.21), channel_id=1, source_target_pairs={{0,16},{16,0},{1,17},{17,1},{2,18},{18,2},{3,19},{19,3},{4,20},{20... | collective-permute-start | bytes 786440 | tf_op jit(solution)/shard_map/ppermute | solution.py:367
  120.9 2.5 %collective-permute-start.12 = (bf16[128,512]{1,0:T(8,128)(2,1)S(1)}, bf16[128,512]{1,0:T(8,128)(2,1)S(1)}, u32[]{:S(2)}, u32[]{:S(2)}) collective-permute-start(bf16[128,512]{1,0:T(8,128)(2,1)S(1)} %bitcast_convert_fusion.low_ref), channel_id=1, source_target_pairs={{0,12},{4,0},{8,4},{12,8},{1,13},{5,1},{9,5},{13,9},{2,14},{6,2},{... | collective-permute-start | bytes 393224 | tf_op jit(solution)/shard_map/ppermute | solution.py:107
  123.4 0.6 finish.1
  124.0 3.9 %collective-permute-done.12.three = bf16[128,512]{1,0:T(8,128)(2,1)S(1)} collective-permute-done((bf16[128,512]{1,0:T(8,128)(2,1)S(1)}, bf16[128,512]{1,0:T(8,128)(2,1)S(1)}, u32[]{:S(2)}, u32[]{:S(2)}) %collective-permute-start.12) | collective-permute-done | bytes 131104 | tf_op jit(solution)/shard_map/ppermute | solution.py:107
  127.9 0.0 collective-permute-done.11
  127.9 3.2 %refresh.1 = (f32[128,512]{1,0:T(8,128)}, f32[128,512]{1,0:T(8,128)}) custom-call(s32[5]{0:T(128)S(1)} %stack.26.info_ref, s32[16]{0:T(128)S(1)} %copy-done.2, bf16[4,4,4,16,128]{4,3,2,1,0:T(8,128)(2,1)S(1)} %bitcast.20, bf16[4,4,4,16,128]{4,3,2,1,0:T(8,128)(2,1)S(1)} %bitcast.21, f32[128,512]{1,0:T(8,128)S(1)} %bitcast.19, ...), custom_call_target="tpu_custom_call" | custom-call | flops 603979776 | bytes 1048576 | tf_op jit(solution)/shard_map/refresh/pallas_call | solution.py:371
  (11 shorter events, 0.1 us)
Async XLA Ops:
  2.9 10.3 %collective-permute-start = (bf16[512,512]{1,0:T(8,128)(2,1)S(1)}, bf16[512,512]{1,0:T(8,128)(2,1)S(1)}, u32[]{:S(2)}, u32[]{:S(2)}) collective-permute-start(bf16[512,512]{1,0:T(8,128)(2,1)S(1)} %get-tuple-element.20), channel_id=1, source_target_pairs={{0,16},{16,0},{1,17},{17,1},{2,18},{18,2},{3,19},{19,3},{4,20},{20... | collective-permute-start | bytes 1572872 | tf_op jit(solution)/shard_map/ppermute | solution.py:292
  12.4 5.3 %copy-start = (f32[1,128,512]{2,1,0:T(8,128)S(1)}, f32[1,128,512]{2,1,0:T(8,128)}, u32[]{:S(2)}) copy-start(f32[1,128,512]{2,1,0:T(8,128)} %param.11) | copy-start | bytes 786436
  12.4 7.3 %copy-start.3 = (bf16[1,2,16,512]{3,2,1,0:T(8,128)(2,1)S(1)}, bf16[1,2,16,512]{3,2,1,0:T(8,128)(2,1)}, u32[]{:S(2)}) copy-start(bf16[1,2,16,512]{3,2,1,0:T(8,128)(2,1)} %param.9) | copy-start | bytes 98308
  12.4 7.3 %copy-start.4 = (bf16[1,2,16,512]{3,2,1,0:T(8,128)(2,1)S(1)}, bf16[1,2,16,512]{3,2,1,0:T(8,128)(2,1)}, u32[]{:S(2)}) copy-start(bf16[1,2,16,512]{3,2,1,0:T(8,128)(2,1)} %param.10) | copy-start | bytes 98308
  14.2 12.7 %all-to-all-start = ((bf16[4,128,512]{2,1,0:T(8,128)(2,1)}), bf16[4,128,512]{2,1,0:T(8,128)(2,1)S(1)}, u32[]{:S(2)}, u32[]{:S(2)}) async-start(bf16[4,128,512]{2,1,0:T(8,128)(2,1)} %bitcast.6), calls=%async_computation | async-start | bytes 1048576 | tf_op jit(solution)/shard_map/all_to_all | solution.py:301
  17.7 68.7 %copy-start.1 = (s32[16]{0:T(128)S(1)}, s32[16]{0:T(128)}, u32[]{:S(2)}) copy-start(s32[16]{0:T(128)} %listed_ref.3) | copy-start | bytes 196
  17.8 7.8 %collective-permute-start.2 = (bf16[128,512]{1,0:T(8,128)(2,1)S(1)}, bf16[128,512]{1,0:T(8,128)(2,1)S(1)}, u32[]{:S(2)}, u32[]{:S(2)}) collective-permute-start(bf16[128,512]{1,0:T(8,128)(2,1)S(1)} %bitcast_convert_fusion.low_ref), channel_id=1, source_target_pairs={{0,4},{4,8},{8,12},{12,0},{1,5},{5,9},{9,13},{13,1},{2,6},{6,10},{... | collective-permute-start | bytes 393224 | tf_op jit(solution)/shard_map/ppermute | solution.py:107
  19.8 3.1 %collective-permute-start.1 = (bf16[2,16,512]{2,1,0:T(8,128)(2,1)S(1)}, bf16[2,16,512]{2,1,0:T(8,128)(2,1)S(1)}, u32[]{:S(2)}, u32[]{:S(2)}) collective-permute-start(bf16[2,16,512]{2,1,0:T(8,128)(2,1)S(1)} %get-tuple-element.33), channel_id=1, source_target_pairs={{0,16},{16,0},{1,17},{17,1},{2,18},{18,2},{3,19},{19,3},{4,20},{20... | collective-permute-start | bytes 98312 | tf_op jit(solution)/shard_map/ppermute | solution.py:304
  27.6 18.4 %collective-permute-start.3 = (bf16[80,512]{1,0:T(8,128)(2,1)S(1)}, bf16[80,512]{1,0:T(8,128)(2,1)S(1)}, u32[]{:S(2)}, u32[]{:S(2)}) collective-permute-start(bf16[80,512]{1,0:T(8,128)(2,1)S(1)} %get-tuple-element.22.sent_one), channel_id=1, source_target_pairs={{0,32},{32,0},{64,96},{96,64},{1,33},{33,1},{65,97},{97,65},{2,34}... | collective-permute-start | bytes 245768 | tf_op jit(solution)/shard_map/ppermute | solution.py:320
  31.3 15.6 %collective-permute-start.4 = (bf16[80,512]{1,0:T(8,128)(2,1)S(1)}, bf16[80,512]{1,0:T(8,128)(2,1)S(1)}, u32[]{:S(2)}, u32[]{:S(2)}) collective-permute-start(bf16[80,512]{1,0:T(8,128)(2,1)S(1)} %get-tuple-element.23.sent_two), channel_id=1, source_target_pairs={{0,96},{32,64},{64,32},{96,0},{1,97},{33,65},{65,33},{97,1},{2,98}... | collective-permute-start | bytes 245768 | tf_op jit(solution)/shard_map/ppermute | solution.py:320
  40.1 5.9 %collective-permute-start.5 = (bf16[32,512]{1,0:T(8,128)(2,1)S(1)}, bf16[32,512]{1,0:T(8,128)(2,1)S(1)}, u32[]{:S(2)}, u32[]{:S(2)}) collective-permute-start(bf16[32,512]{1,0:T(8,128)(2,1)S(1)} %get-tuple-element.24.value_ref.own_ref), channel_id=1, source_target_pairs={{0,128},{128,256},{256,384},{384,0},{1,129},{129,257},{257,385},{3... | collective-permute-start | bytes 98312 | tf_op jit(solution)/shard_map/ppermute | solution.py:107
  46.9 81.0 %copy-start.2 = (s32[16]{0:T(128)S(1)}, s32[16]{0:T(128)}, u32[]{:S(2)}) copy-start(s32[16]{0:T(128)} %owner_ref.1) | copy-start | bytes 196
  46.9 13.6 %collective-permute-start.6 = (bf16[96,512]{1,0:T(8,128)(2,1)S(1)}, bf16[96,512]{1,0:T(8,128)(2,1)S(1)}, u32[]{:S(2)}, u32[]{:S(2)}) collective-permute-start(bf16[96,512]{1,0:T(8,128)(2,1)S(1)} %get-tuple-element.26.sent_one), channel_id=1, source_target_pairs={{0,96},{32,64},{64,32},{96,0},{1,97},{33,65},{65,33},{97,1},{2,98}... | collective-permute-start | bytes 294920 | tf_op jit(solution)/shard_map/ppermute | solution.py:329
  55.0 12.0 %collective-permute-start.7 = (bf16[96,512]{1,0:T(8,128)(2,1)S(1)}, bf16[96,512]{1,0:T(8,128)(2,1)S(1)}, u32[]{:S(2)}, u32[]{:S(2)}) collective-permute-start(bf16[96,512]{1,0:T(8,128)(2,1)S(1)} %get-tuple-element.27.sent_two), channel_id=1, source_target_pairs={{0,32},{32,0},{64,96},{96,64},{1,33},{33,1},{65,97},{97,65},{2,34}... | collective-permute-start | bytes 294920 | tf_op jit(solution)/shard_map/ppermute | solution.py:329
  60.5 6.5 %collective-permute-start.8 = (bf16[32,512]{1,0:T(8,128)(2,1)S(1)}, bf16[32,512]{1,0:T(8,128)(2,1)S(1)}, u32[]{:S(2)}, u32[]{:S(2)}) collective-permute-start(bf16[32,512]{1,0:T(8,128)(2,1)S(1)} %left_rows.1), channel_id=1, source_target_pairs={{0,256},{128,384},{256,0},{384,128},{1,257},{129,385},{257,1},{385... | collective-permute-start | bytes 98312 | tf_op jit(solution)/shard_map/ppermute | solution.py:107
  63.5 5.0 %collective-permute-start.9 = (bf16[32,512]{1,0:T(8,128)(2,1)S(1)}, bf16[32,512]{1,0:T(8,128)(2,1)S(1)}, u32[]{:S(2)}, u32[]{:S(2)}) collective-permute-start(bf16[32,512]{1,0:T(8,128)(2,1)S(1)} %left_rows.1), channel_id=1, source_target_pairs={{0,384},{128,0},{256,128},{384,256},{1,385},{129,1},{257,129},{385... | collective-permute-start | bytes 98312 | tf_op jit(solution)/shard_map/ppermute | solution.py:107
  69.7 16.8 %all-to-all-start.1 = ((bf16[16,2,16,128]{3,2,1,0:T(8,128)(2,1)}), bf16[16,2,16,128]{3,2,1,0:T(8,128)(2,1)S(1)}, u32[]{:S(2)}, u32[]{:S(2)}) async-start(bf16[16,2,16,128]{3,2,1,0:T(8,128)(2,1)} %bitcast.10), calls=%async_computation.1 | async-start | bytes 262144 | tf_op jit(solution)/shard_map/all_to_all | solution.py:344
  78.4 8.0 %collective-permute-start.10 = (bf16[128,512]{1,0:T(8,128)(2,1)S(1)}, bf16[128,512]{1,0:T(8,128)(2,1)S(1)}, u32[]{:S(2)}, u32[]{:S(2)}) collective-permute-start(bf16[128,512]{1,0:T(8,128)(2,1)S(1)} %bitcast_convert_fusion.low_ref), channel_id=1, source_target_pairs={{0,8},{4,12},{8,0},{12,4},{1,9},{5,13},{9,1},{13,5},{2,10},{6,14},... | collective-permute-start | bytes 393224 | tf_op jit(solution)/shard_map/ppermute | solution.py:107
  116.8 11.1 %collective-permute-start.11 = (bf16[16,4,16,128]{3,2,1,0:T(8,128)(2,1)S(1)}, bf16[16,4,16,128]{3,2,1,0:T(8,128)(2,1)S(1)}, u32[]{:S(2)}, u32[]{:S(2)}) collective-permute-start(bf16[16,4,16,128]{3,2,1,0:T(8,128)(2,1)S(1)} %all_to_all.21), channel_id=1, source_target_pairs={{0,16},{16,0},{1,17},{17,1},{2,18},{18,2},{3,19},{19,3},{4,20},{20... | collective-permute-start | bytes 786440 | tf_op jit(solution)/shard_map/ppermute | solution.py:367
  120.9 7.0 %collective-permute-start.12 = (bf16[128,512]{1,0:T(8,128)(2,1)S(1)}, bf16[128,512]{1,0:T(8,128)(2,1)S(1)}, u32[]{:S(2)}, u32[]{:S(2)}) collective-permute-start(bf16[128,512]{1,0:T(8,128)(2,1)S(1)} %bitcast_convert_fusion.low_ref), channel_id=1, source_target_pairs={{0,12},{4,0},{8,4},{12,8},{1,13},{5,1},{9,5},{13,9},{2,14},{6,2},{... | collective-permute-start | bytes 393224 | tf_op jit(solution)/shard_map/ppermute | solution.py:107

commit v7 on v6

--- a/solution.py
+++ b/solution.py
@@ -98,8 +98,20 @@
     out_ref[...] = dot(turned_ref[...], grads_ref[...])
 
 
-def join_kernel(own_ref, got_ref, out_ref):
-    out_ref[...] = (own_ref[...] + got_ref[...].astype(F32)).astype(BF16).T
+def join_kernel(index_ref, own_ref, got_ref, mine_ref, theirs_ref, out_ref, right_ref):
+    core = index_ref[0]
+    rows = mine_ref.shape[1]
+    total = (own_ref[...] + got_ref[...].astype(F32)).astype(BF16).T
+    mine = pl.ds(pl.multiple_of(core * rows, rows), rows)
+    theirs = pl.ds(pl.multiple_of((1 - core) * rows, rows), rows)
+    right_ref[mine, :] = mine_ref[1]
+    right_ref[theirs, :] = theirs_ref[1]
+    mine = pl.ds(pl.multiple_of(PART + core * rows, rows), rows)
+    theirs = pl.ds(pl.multiple_of(PART + (1 - core) * rows, rows), rows)
+    for w in range(X):
+        out_ref[w, :PART] = total[w * PART : (w + 1) * PART]
+        out_ref[w, mine, :] = mine_ref[0]
+        out_ref[w, theirs, :] = theirs_ref[0]
 
 
 def shift(value, axis, step):
@@ -118,26 +130,21 @@
         out_ref[pl.ds(pl.multiple_of(at, rows), rows), :] = part[...]
 
 
-def added(parts_ref):
-    total = parts_ref[0].astype(F32)
-    for part in range(1, parts_ref.shape[0]):
-        total = total + parts_ref[part].astype(F32)
-    return total
-
-
-def sum_kernel(info_ref, parts_ref, mine_ref, theirs_ref, *refs):
-    keep_ref, left_ref, send_one, send_two = refs[-5:-1]
-    right, core = refs[-1], info_ref[0]
-    rows = mine_ref.shape[1]
-    for side, ref in enumerate((left_ref, right)):
-        ref[pl.ds(pl.multiple_of(core * rows, rows), rows), :] = mine_ref[side]
-        ref[pl.ds(pl.multiple_of((1 - core) * rows, rows), rows), :] = theirs_ref[side]
-    total = added(parts_ref)
+def sum_kernel(parts_ref, *refs):
+    keep_ref, left_ref, pieces_ref = refs[-3:]
+    total = parts_ref[0, :PART].astype(F32)
+    for w in range(X):
+        left_ref[w * ROWS : (w + 1) * ROWS] = parts_ref[w, PART:]
+        if w:
+            total = total + parts_ref[w, :PART].astype(F32)
     keep_ref[...] = total
-    half = PART // 2
-    for part, ref in enumerate((send_one, send_two)):
-        ref[:half] = total[part * half : (part + 1) * half].astype(BF16)
-        ref[half:] = right[part * rows : (part + 1) * rows]
+    n_mp, n_root, cores, rows, lanes = pieces_ref.shape
+    for c in range(cores):
+        for r in range(n_root):
+            at = (c * n_root + r) * rows
+            for m in range(n_mp):
+                piece = total[at : at + rows, m * lanes : (m + 1) * lanes]
+                pieces_ref[m, r, c] = piece.astype(BF16)
 
 
 def middle_kernel(keep_ref, sent_one, sent_two, got_one, got_two, *refs):
@@ -155,8 +162,31 @@
         ref[half + rows :] = got[half:]
 
 
-def pack_kernel(scale, info_ref, keep_ref, sent_one, sent_two, got_one, got_two, *refs):
-    grad_ref, pieces_ref, right_ref = refs[-3:]
+def choose_kernel(listed_ref, blocks_ref, keep_ref, right_ref, out_ref, send_one, send_two):
+    for j in range(CHIPS):
+        pair = listed_ref[j] // 2
+        for c in range(CORE):
+            out_ref[j * CORE + c] = blocks_ref[pair, c]
+    half, rows = PART // 2, ROWS // 2
+    for part, ref in enumerate((send_one, send_two)):
+        ref[:half] = keep_ref[part * half : (part + 1) * half].astype(BF16)
+        ref[half:] = right_ref[part * rows : (part + 1) * rows]
+
+
+def spread_kernel(scale, info_ref, listed_ref, parts_ref, *refs):
+    out_ref = refs[-1]
+    holder = listed_ref[info_ref[1] * ZH + info_ref[2]] % 2
+    for w in range(X):
+        total = parts_ref[w * ZH * CORE + holder].astype(F32)
+        for z in range(1, ZH):
+            total = total + parts_ref[(w * ZH + z) * CORE + holder].astype(F32)
+        tile = (total * scale).astype(BF16)
+        for peer in range(out_ref.shape[0]):
+            out_ref[peer, w] = tile
+
+
+def update_kernel(scale, info_ref, keep_ref, sent_one, sent_two, got_one, got_two, *refs):
+    left, out_ref, grad, right, total = refs
     zh = info_ref[2]
     half, rows = PART // 2, ROWS // 2
     near = zh + 1 - 2 * (zh % 2)
@@ -169,72 +199,42 @@
         )
     ):
         at = slice(part * half, (part + 1) * half)
-        grad_ref[at] = ((keep_ref[at] + got[:half].astype(F32)) * scale).astype(BF16)
+        grad[at] = ((keep_ref[at] + got[:half].astype(F32)) * scale).astype(BF16)
         for place_at, mate in enumerate(mates):
             source = (sent, got)[place_at // 2]
             start = half + place_at % 2 * rows
             to = pl.multiple_of(mate * ROWS + part * rows, rows)
-            right_ref[pl.ds(to, rows), :] = source[start : start + rows]
-    n_mp, n_root, cores, rows, lanes = pieces_ref.shape
-    for c in range(cores):
-        for r in range(n_root):
-            at = (c * n_root + r) * rows
-            for m in range(n_mp):
-                pieces_ref[m, r, c] = grad_ref[at : at + rows, m * lanes : (m + 1) * lanes]
-
-
-def copy_kernel(value_ref, *refs):
-    refs[-1][...] = value_ref[...]
-
-
-def choose_kernel(info_ref, listed_ref, blocks_ref, total_ref, *refs):
-    out_ref = refs[-1]
+            right[pl.ds(to, rows), :] = source[start : start + rows]
+    product = dot(left[...], grad[...], 1, 1).astype(BF16)
+    total[...] = dot(product, right[...])
     rows, lanes = out_ref.shape[2:]
-    for w in range(X):
-        pair = listed_ref[w * ZH + info_ref[2]] // 2
-        for c in range(CORE):
-            out_ref[w * CORE + c, 0] = blocks_ref[pair, c]
-            at = w * ROWS + c * rows
-            for lane in range(B // lanes):
-                part = total_ref[at : at + rows, lane * lanes : (lane + 1) * lanes]
-                out_ref[w * CORE + c, 1 + lane] = part.astype(BF16)
-
-
-def spread_kernel(info_ref, listed_ref, parts_ref, out_ref):
-    holder = listed_ref[info_ref[1] * ZH + info_ref[2]] % 2
-    for w in range(X):
-        tile = parts_ref[w * CORE + holder, 0]
-        for peer in range(out_ref.shape[0]):
-            out_ref[peer, w] = tile
+    for peer in range(X * CORE):
+        for lane in range(B // lanes):
+            part = total[peer * rows : (peer + 1) * rows, lane * lanes : (lane + 1) * lanes]
+            out_ref[peer, lane] = part.astype(BF16)
 
 
 def finish_kernel(parts_ref, out_ref):
     lanes = parts_ref.shape[3]
     for c in range(CORE):
         for lane in range(B // lanes):
-            total = parts_ref[c, 1 + lane].astype(F32)
+            total = parts_ref[c, lane].astype(F32)
             for w in range(1, X):
-                total = total + parts_ref[w * CORE + c, 1 + lane].astype(F32)
+                total = total + parts_ref[w * CORE + c, lane].astype(F32)
             at = c * B + lane * lanes
             out_ref[:, at : at + lanes] = total.astype(BF16)
 
 
-def update_kernel(info_ref, own_ref, one, two, three, grad_ref, right_ref, out_ref, left):
-    place(left, (own_ref, one, two, three), info_ref[1])
-    product = dot(left[...], grad_ref[...], 1, 1).astype(BF16)
-    out_ref[...] = dot(product, right_ref[...])
-
-
-def refresh_kernel(info_ref, owner_ref, mine_ref, theirs_ref, own_ref, low_ref, one, two, three, stats_ref, roots_ref, block, product, old):
+def refresh_kernel(info_ref, owner_ref, pieces_ref, own_ref, low_ref, one, two, three, stats_ref, roots_ref, block, product, old):
     core, x, zh, mp, root = (info_ref[at] for at in range(5))
-    n_mp, n_root, _, rows, lanes = mine_ref.shape
+    _, n_mp, n_root, _, rows, lanes = pieces_ref.shape
     quarter = own_ref.shape[0]
-    for ref, side in ((mine_ref, core), (theirs_ref, 1 - core)):
+    for c in range(CORE):
         for r in range(n_root):
             for w in range(X):
-                at = pl.ds(pl.multiple_of(w * PART + (side * n_root + r) * rows, rows), rows)
+                at = w * PART + (c * n_root + r) * rows
                 for m in range(n_mp):
-                    block[at, m * lanes : (m + 1) * lanes] = ref[m, r, w]
+                    block[at : at + rows, m * lanes : (m + 1) * lanes] = pieces_ref[c, m, r, w]
     place(old, (low_ref, one, two, three), mp)
 
     @pl.when(core == 0)
@@ -290,6 +290,11 @@
 
     turned, send, grads_own = other_half(acts, grads_out, 1 - core)
     got = lax.ppermute(send, "core", swap)
+    prec = jnp.stack([prec_left[0], prec_right[0]])
+    mine = lax.dynamic_index_in_dim(prec, core, 1, keepdims=False)
+    theirs = lax.ppermute(
+        lax.dynamic_index_in_dim(prec, 1 - core, 1, keepdims=False), "core", swap
+    )
     (own,) = kernel_call(
         own_kernel,
         "own_half",
@@ -297,85 +302,72 @@
         [shape((B, B), F32)],
         work=cost(2 * acts.shape[0] * B * B, 4 * acts.shape[0] * B),
     )(turned, grads_own)
-    (total,) = kernel_call(join_kernel, "join", [VMEM, VMEM], [shape((B, B))])(own, got)
-    total = lax.all_to_all(total.reshape(X, PART, B), "x", 0, 0)
-    prec = jnp.stack([prec_left[0], prec_right[0]])
-    mine = lax.dynamic_index_in_dim(prec, core, 1, keepdims=False)
-    theirs = lax.ppermute(
-        lax.dynamic_index_in_dim(prec, 1 - core, 1, keepdims=False), "core", swap
-    )
+    total, right_rows = kernel_call(
+        join_kernel,
+        "join",
+        [SMEM] + [VMEM] * 4,
+        [shape((X, PART + ROWS, B)), shape((ROWS, B))],
+    )(core.reshape(1), own, got, mine, theirs)
+    total = lax.all_to_all(total, "x", 0, 0)
     old_own = stats_old[0]
     old_low = old_own.astype(BF16)
     olds = [old_low] + shifted(old_low, "mp")
-    keep, left_rows, *sends = kernel_call(
+    keep, left_part, pieces = kernel_call(
         sum_kernel,
         "sum_x",
+        [VMEM],
+        [shape((PART, B), F32), shape((PART, B)), shape((n_mp, n_root, CORE, half, lanes))],
+        awaited=3,
+    )(total, *olds[1:])
+
+    pieces = pieces.reshape((n_mp * n_root,) + pieces.shape[2:])
+    blocks = lax.all_to_all(pieces, ("mp", "root"), 0, 0)
+    chosen, *sends = kernel_call(
+        choose_kernel,
+        "choose",
         [SMEM] + [VMEM] * 3,
-        [shape((PART, B), F32), shape((ROWS, B))] + [shape((PART // 2 + half, B))] * 2,
-        [pltpu.VMEM((ROWS, B), BF16)],
-        awaited=1,
-    )(info, total, mine, theirs, olds[1])
+        [shape((CHIPS * CORE, half, lanes))] + [shape((PART // 2 + half, B))] * 2,
+    )(listed, blocks, keep, right_rows)
+    parts = lax.all_to_all(chosen, ("x", "zh", "core"), 0, 0)
     near = [(z, z ^ 1) for z in range(ZH)]
     far = [(z, ZH - 1 - z) for z in range(ZH)]
     got = [lax.ppermute(sends[0], "zh", near), lax.ppermute(sends[1], "zh", far)]
-    lefts = [left_rows, shift(left_rows, "x", 1)]
+    (spread,) = kernel_call(
+        functools.partial(spread_kernel, tokens ** -0.5),
+        "spread",
+        [SMEM, SMEM, VMEM],
+        [shape((CORE * n_mp * n_root, X, half, lanes))],
+    )(info, listed, parts)
+    gathered = lax.all_to_all(spread, ("core", "mp", "root"), 0, 0)
+    gathered = gathered.reshape((CORE, n_mp, n_root) + gathered.shape[1:])
+
     keep, *sends = kernel_call(
         middle_kernel,
         "middle",
         [VMEM] * 5,
         [shape((PART, B), F32)] + [shape((PART // 2 + 2 * half, B))] * 2,
         awaited=1,
-    )(keep, *sends, *got, lefts[1])
+    )(keep, *sends, *got, spread)
     got = [lax.ppermute(sends[0], "zh", far), lax.ppermute(sends[1], "zh", near)]
-    (left_later,) = kernel_call(
-        copy_kernel, "left_rows", [VMEM], [shape((ROWS, B))], awaited=1
-    )(left_rows, got[0])
-    lefts += [shift(left_later, "x", step) for step in range(2, X)]
-    grad, pieces, right_part = kernel_call(
-        functools.partial(pack_kernel, tokens ** -0.5),
-        "pack",
-        [SMEM] + [VMEM] * 5,
-        [shape((PART, B)), shape((n_mp, n_root, CORE, half, lanes)), shape((PART, B))],
-        awaited=2,
-    )(info, keep, *sends, *got, *lefts[2:])
-
-
-    pieces = pieces.reshape((n_mp * n_root,) + pieces.shape[2:])
-    blocks = lax.all_to_all(pieces, ("mp", "root"), 0, 0)
-
-    (total,) = kernel_call(
-        update_kernel,
+    (send,) = kernel_call(
+        functools.partial(update_kernel, tokens ** -0.5),
         "update",
         [SMEM] + [VMEM] * 6,
-        [shape((PART, B), F32)],
-        [pltpu.VMEM((PART, B), BF16)],
+        [shape((X * CORE, B // lanes, half, lanes))],
+        [pltpu.VMEM((PART, B), BF16)] * 2 + [pltpu.VMEM((PART, B), F32)],
         cost(2 * PART * B * (PART + B), 6 * PART * B),
-    )(info, *lefts, grad, right_part)
-
-    (chosen,) = kernel_call(
-        choose_kernel,
-        "choose",
-        [SMEM, SMEM, VMEM, VMEM],
-        [shape((X * CORE, 1 + B // lanes, half, lanes))],
-        awaited=1,
-    )(info, listed, blocks, total, olds[2])
-    parts = lax.all_to_all(chosen, ("x", "core"), 0, 0)
-    (mine,) = kernel_call(
-        spread_kernel, "spread", [SMEM, SMEM, VMEM], [shape((n_mp * n_root, X, half, lanes))]
-    )(info, listed, parts)
-    mine = lax.all_to_all(mine, ("mp", "root"), 0, 0)
-    theirs = lax.ppermute(mine, "core", swap)
-    gathered = [value.reshape((n_mp, n_root) + value.shape[1:]) for value in (mine, theirs)]
-    (update,) = kernel_call(finish_kernel, "finish", [VMEM], [shape((half, 2 * B))])(parts)
+    )(info, keep, *sends, *got, left_part)
+    got = lax.all_to_all(send, ("x", "core"), 0, 0)
+    (update,) = kernel_call(finish_kernel, "finish", [VMEM], [shape((half, 2 * B))])(got)
 
     new_stats, new_roots = kernel_call(
         refresh_kernel,
         "refresh",
-        [SMEM, SMEM] + [VMEM] * 7,
+        [SMEM, SMEM] + [VMEM] * 6,
         [shape((quarter, B), F32)] * 2,
         [pltpu.VMEM((B, B), BF16), pltpu.VMEM((B, B), F32), pltpu.VMEM((B, B), BF16)],
         cost(2 * B ** 3 + 10 * quarter * B * B, 2 * B * B * 2),
-    )(info, owner, *gathered, old_own, *olds)
+    )(info, owner, gathered, old_own, *olds)
     return update[None], new_stats[None, None], new_roots[None, None]
 
 

time: 132 us -> 141 us (1.068)
  starting transfers between devices: 67.7 us -> 76.2 us
  waiting for transfers between devices: 21.3 us -> 29.8 us
  blocking collectives: 29.1 us -> 21.6 us
    all_to_all x2 -> x3, starting transfers between devices: 12.2 us -> 32.1 us  [the longest x1 18 us: local(): parts = lax.all_to_all(chosen, ('x', 'zh', 'core'), 0, 0)]
    all_to_all x2 -> x3, waiting for transfers between devices: 1.33 us -> 18 us  [the longest x1 14.6 us: local(): gathered = lax.all_to_all(spread, ('core', 'mp', 'root'), 0, 0)]
    ppermute x6 -> x3, starting transfers between devices: 17.8 us -> 8.41 us  [shift(): lax.ppermute(value, axis, [(at, (at + step) % size) for at in range(size)])]
    ppermute x6 -> x3, waiting for transfers between devices: 14 us -> 4.6 us  [shift(): lax.ppermute(value, axis, [(at, (at + step) % size) for at in range(size)])]
    all_to_all x2, blocking collectives: 29.1 us -> 21.6 us  [the longest x1 11.4 us: local(): blocks = lax.all_to_all(pieces, ('mp', 'root'), 0, 0)]
    ppermute x1 -> x0, starting transfers between devices: 4.06 us -> none  [local(): theirs = lax.ppermute(mine, 'core', swap)]
    ppermute x1, starting transfers between devices: 3.69 us -> 7.2 us  [local(): lax.ppermute(sends[0], 'zh', near)]
    ppermute x1, waiting for transfers between devices: 0.01 us -> 2.57 us  [local(): lax.ppermute(sends[1], 'zh', near)]
  transfers between devices with their start and end apart: 15 -> 12, of which waited for: 10 -> 7; matrix products, arithmetic and copies ran while one was open for 0% -> 0% of each run, Pallas kernels for 2% -> 2%
where the time goes in v7:
time: 141 us; the launch traced here: 140 us
  starting transfers between devices  76.2 us (54%)
  waiting for transfers between devices  29.8 us (21%)
  blocking collectives  21.6 us (15%)
  Pallas kernels  11.6 us (8%)
    all_to_all x1, starting transfers between devices, local(): parts = lax.all_to_all(chosen, ('x', 'zh', 'core'), 0, 0)  18 us
    all_to_all x1, waiting for transfers between devices, local(): gathered = lax.all_to_all(spread, ('core', 'mp', 'root'), 0, 0)  14.6 us
    all_to_all x1, blocking collectives, local(): blocks = lax.all_to_all(pieces, ('mp', 'root'), 0, 0)  11.4 us
    all_to_all x1, starting transfers between devices, local(): gathered = lax.all_to_all(spread, ('core', 'mp', 'root'), 0, 0)  10.6 us
    all_to_all x1, blocking collectives, local(): got = lax.all_to_all(send, ('x', 'core'), 0, 0)  10.2 us
    ppermute x1, starting transfers between devices, local(): got = lax.ppermute(send, 'core', swap)  8.78 us
    ppermute x3, starting transfers between devices, shift(): lax.ppermute(value, axis, [(at, (at + step) % size) for at in range(size)])  8.41 us
    ppermute x1, starting transfers between devices, local(): lax.ppermute(sends[0], 'zh', near)  7.2 us
  transfers between devices with their start and end apart: 12, of which 7 were waited for; matrix products, arithmetic and copies ran while one was open for 0% of the time, Pallas kernels for 2%

profile of v7, /device:TPU:1, one launch (start us, length us, event | category | flops | bytes accessed | tf_op | source)
XLA Modules:
  0.0 140.2 jit_solution(17931143352573422815)
XLA Ops:
  0.6 0.0 copy-start.3
  0.6 0.0 copy-start.4
  0.7 2.3 %other_half.1 = (bf16[512,1024]{1,0:T(8,128)(2,1)S(1)}, bf16[512,512]{1,0:T(8,128)(2,1)S(1)}, bf16[1024,512]{1,0:T(8,128)(2,1)S(1)}) custom-call(s32[1]{0:T(128)} %bitcast.5.index_ref, bf16[1024,512]{1,0:T(8,128)(2,1)} %acts_ref.1, bf16[1024,1024]{1,0:T(8,128)(2,1)} %grads_ref.1), custom_call_target="tpu_custom_call" | custom-call | flops 536870912 | bytes 3145728 | tf_op jit(solution)/shard_map/other_half/pallas_call | solution.py:80
  2.9 8.8 %collective-permute-start = (bf16[512,512]{1,0:T(8,128)(2,1)S(1)}, bf16[512,512]{1,0:T(8,128)(2,1)S(1)}, u32[]{:S(2)}, u32[]{:S(2)}) collective-permute-start(bf16[512,512]{1,0:T(8,128)(2,1)S(1)} %get-tuple-element.21), channel_id=1, source_target_pairs={{0,16},{16,0},{1,17},{17,1},{2,18},{18,2},{3,19},{19,3},{4,20},{20... | collective-permute-start | bytes 1572872 | tf_op jit(solution)/shard_map/ppermute | solution.py:292
  11.7 0.0 copy-done.3
  11.7 0.0 copy-done.4
  11.8 1.9 %collective-permute-start.1 = (bf16[2,16,512]{2,1,0:T(8,128)(2,1)S(1)}, bf16[2,16,512]{2,1,0:T(8,128)(2,1)S(1)}, u32[]{:S(2)}, u32[]{:S(2)}) collective-permute-start(bf16[2,16,512]{2,1,0:T(8,128)(2,1)S(1)} %get-tuple-element.35), channel_id=1, source_target_pairs={{0,16},{16,0},{1,17},{17,1},{2,18},{18,2},{3,19},{19,3},{4,20},{20... | collective-permute-start | bytes 98312 | tf_op jit(solution)/shard_map/ppermute | solution.py:295
  13.7 0.7 own_half.1.own_ref
  14.4 0.0 copy-start
  14.4 0.5 collective-permute-done.1.theirs_ref
  14.9 0.0 collective-permute-done.got_ref
  14.9 0.0 copy-start.1
  14.9 1.1 join.1
  16.0 3.5 %all-to-all-start = ((bf16[4,160,512]{2,1,0:T(8,128)(2,1)}), bf16[4,160,512]{2,1,0:T(8,128)(2,1)S(1)}, u32[]{:S(2)}, u32[]{:S(2)}) async-start(bf16[4,160,512]{2,1,0:T(8,128)(2,1)} %get-tuple-element.22), calls=%async_computation | async-start | bytes 1310720 | tf_op jit(solution)/shard_map/all_to_all | solution.py:311
  19.5 0.0 copy-done
  19.5 1.9 %collective-permute-start.2 = (bf16[128,512]{1,0:T(8,128)(2,1)S(1)}, bf16[128,512]{1,0:T(8,128)(2,1)S(1)}, u32[]{:S(2)}, u32[]{:S(2)}) collective-permute-start(bf16[128,512]{1,0:T(8,128)(2,1)S(1)} %bitcast_convert_fusion.low_ref), channel_id=1, source_target_pairs={{0,4},{4,8},{8,12},{12,0},{1,5},{5,9},{9,13},{13,1},{2,6},{6,10},{... | collective-permute-start | bytes 393224 | tf_op jit(solution)/shard_map/ppermute | solution.py:119
  21.4 1.9 %collective-permute-start.3 = (bf16[128,512]{1,0:T(8,128)(2,1)S(1)}, bf16[128,512]{1,0:T(8,128)(2,1)S(1)}, u32[]{:S(2)}, u32[]{:S(2)}) collective-permute-start(bf16[128,512]{1,0:T(8,128)(2,1)S(1)} %bitcast_convert_fusion.low_ref), channel_id=1, source_target_pairs={{0,8},{4,12},{8,0},{12,4},{1,9},{5,13},{9,1},{13,5},{2,10},{6,14},... | collective-permute-start | bytes 393224 | tf_op jit(solution)/shard_map/ppermute | solution.py:119
  23.4 4.6 %collective-permute-start.4 = (bf16[128,512]{1,0:T(8,128)(2,1)S(1)}, bf16[128,512]{1,0:T(8,128)(2,1)S(1)}, u32[]{:S(2)}, u32[]{:S(2)}) collective-permute-start(bf16[128,512]{1,0:T(8,128)(2,1)S(1)} %bitcast_convert_fusion.low_ref), channel_id=1, source_target_pairs={{0,12},{4,0},{8,4},{12,8},{1,13},{5,1},{9,5},{13,9},{2,14},{6,2},{... | collective-permute-start | bytes 393224 | tf_op jit(solution)/shard_map/ppermute | solution.py:119
  28.0 0.0 collective-permute-done.2.refs_0_.one
  28.0 1.9 %collective-permute-done.3.refs_1_.two = bf16[128,512]{1,0:T(8,128)(2,1)S(1)} collective-permute-done((bf16[128,512]{1,0:T(8,128)(2,1)S(1)}, bf16[128,512]{1,0:T(8,128)(2,1)S(1)}, u32[]{:S(2)}, u32[]{:S(2)}) %collective-permute-start.3) | collective-permute-done | bytes 131104 | tf_op jit(solution)/shard_map/ppermute | solution.py:119
  29.8 2.7 %collective-permute-done.4.refs_2_.three = bf16[128,512]{1,0:T(8,128)(2,1)S(1)} collective-permute-done((bf16[128,512]{1,0:T(8,128)(2,1)S(1)}, bf16[128,512]{1,0:T(8,128)(2,1)S(1)}, u32[]{:S(2)}, u32[]{:S(2)}) %collective-permute-start.4) | collective-permute-done | bytes 131104 | tf_op jit(solution)/shard_map/ppermute | solution.py:119
  32.6 0.0 all-to-all-done.parts_ref
  32.6 0.1 sum_x.1
  32.6 11.4 %all_to_all.25.blocks_ref = bf16[16,2,16,128]{3,2,1,0:T(8,128)(2,1)S(1)} all-to-all(bf16[16,2,16,128]{3,2,1,0:T(8,128)(2,1)S(1)} %bitcast.19), channel_id=1, replica_groups=mesh['x'=4,'zh'=4,'core'=2,'mp'=4,'root'=4] {'mp','root'}, dimensions={0} | all-to-all | bytes 262144 | tf_op jit(solution)/shard_map/all_to_all | solution.py:324
  44.1 0.0 copy-done.1
  44.1 1.3 choose.1
  45.4 18.0 %all-to-all-start.2 = ((bf16[32,16,128]{2,1,0:T(8,128)(2,1)}), bf16[32,16,128]{2,1,0:T(8,128)(2,1)S(1)}, u32[]{:S(2)}, u32[]{:S(2)}) async-start(bf16[32,16,128]{2,1,0:T(8,128)(2,1)} %get-tuple-element.28), calls=%async_computation.2 | async-start | bytes 262144 | tf_op jit(solution)/shard_map/all_to_all | solution.py:331
  63.4 7.2 %collective-permute-start.5 = (bf16[80,512]{1,0:T(8,128)(2,1)S(1)}, bf16[80,512]{1,0:T(8,128)(2,1)S(1)}, u32[]{:S(2)}, u32[]{:S(2)}) collective-permute-start(bf16[80,512]{1,0:T(8,128)(2,1)S(1)} %get-tuple-element.26.sent_one), channel_id=1, source_target_pairs={{0,32},{32,0},{64,96},{96,64},{1,33},{33,1},{65,97},{97,65},{2,34}... | collective-permute-start | bytes 245768 | tf_op jit(solution)/shard_map/ppermute | solution.py:334
  70.6 7.0 %collective-permute-start.6 = (bf16[80,512]{1,0:T(8,128)(2,1)S(1)}, bf16[80,512]{1,0:T(8,128)(2,1)S(1)}, u32[]{:S(2)}, u32[]{:S(2)}) collective-permute-start(bf16[80,512]{1,0:T(8,128)(2,1)S(1)} %get-tuple-element.27.sent_two), channel_id=1, source_target_pairs={{0,96},{32,64},{64,32},{96,0},{1,97},{33,65},{65,33},{97,1},{2,98}... | collective-permute-start | bytes 245768 | tf_op jit(solution)/shard_map/ppermute | solution.py:334
  77.6 0.0 copy-start.2
  77.6 0.1 stack.26.info_ref
  77.7 3.4 %all-to-all-done.2.parts_ref = bf16[32,16,128]{2,1,0:T(8,128)(2,1)S(1)} async-done(((bf16[32,16,128]{2,1,0:T(8,128)(2,1)}), bf16[32,16,128]{2,1,0:T(8,128)(2,1)S(1)}, u32[]{:S(2)}, u32[]{:S(2)}) %all-to-all-start.2) | async-done | bytes 131104 | tf_op jit(solution)/shard_map/all_to_all | solution.py:331
  81.0 1.4 %spread.1.refs_0_ = bf16[32,4,16,128]{3,2,1,0:T(8,128)(2,1)} custom-call(s32[5]{0:T(128)S(1)} %stack.26.info_ref, s32[16]{0:T(128)S(1)} %copy-done.1, bf16[32,16,128]{2,1,0:T(8,128)(2,1)S(1)} %all-to-all-done.2.parts_ref), custom_call_target="tpu_custom_call" | custom-call | tf_op jit(solution)/shard_map/spread/pallas_call | solution.py:335
  82.5 0.0 collective-permute-done.5.got_one
  82.5 0.0 collective-permute-done.6.got_two
  82.5 7.0 %collective-permute-start.7 = (bf16[96,512]{1,0:T(8,128)(2,1)S(1)}, bf16[96,512]{1,0:T(8,128)(2,1)S(1)}, u32[]{:S(2)}, u32[]{:S(2)}) collective-permute-start(bf16[96,512]{1,0:T(8,128)(2,1)S(1)} %get-tuple-element.30.sent_one), channel_id=1, source_target_pairs={{0,96},{32,64},{64,32},{96,0},{1,97},{33,65},{65,33},{97,1},{2,98}... | collective-permute-start | bytes 294920 | tf_op jit(solution)/shard_map/ppermute | solution.py:351
  89.5 3.8 %collective-permute-start.8 = (bf16[96,512]{1,0:T(8,128)(2,1)S(1)}, bf16[96,512]{1,0:T(8,128)(2,1)S(1)}, u32[]{:S(2)}, u32[]{:S(2)}) collective-permute-start(bf16[96,512]{1,0:T(8,128)(2,1)S(1)} %get-tuple-element.31.sent_two), channel_id=1, source_target_pairs={{0,32},{32,0},{64,96},{96,64},{1,33},{33,1},{65,97},{97,65},{2,34}... | collective-permute-start | bytes 294920 | tf_op jit(solution)/shard_map/ppermute | solution.py:351
  93.3 4.2 %collective-permute-done.7.got_one = bf16[96,512]{1,0:T(8,128)(2,1)S(1)} collective-permute-done((bf16[96,512]{1,0:T(8,128)(2,1)S(1)}, bf16[96,512]{1,0:T(8,128)(2,1)S(1)}, u32[]{:S(2)}, u32[]{:S(2)}) %collective-permute-start.7) | collective-permute-done | bytes 98336 | tf_op jit(solution)/shard_map/ppermute | solution.py:351
  97.5 2.6 %collective-permute-done.8.got_two = bf16[96,512]{1,0:T(8,128)(2,1)S(1)} collective-permute-done((bf16[96,512]{1,0:T(8,128)(2,1)S(1)}, bf16[96,512]{1,0:T(8,128)(2,1)S(1)}, u32[]{:S(2)}, u32[]{:S(2)}) %collective-permute-start.8) | collective-permute-done | bytes 98336 | tf_op jit(solution)/shard_map/ppermute | solution.py:351
  100.1 0.9 update.1
  101.0 10.2 %all_to_all.26.parts_ref = bf16[8,4,16,128]{3,2,1,0:T(8,128)(2,1)S(1)} all-to-all(bf16[8,4,16,128]{3,2,1,0:T(8,128)(2,1)S(1)} %update.1), channel_id=1, replica_groups=mesh['x'=4,'zh'=4,'core'=2,'mp'=4,'root'=4] {'x','core'}, dimensions={0} | all-to-all | bytes 262144 | tf_op jit(solution)/shard_map/all_to_all | solution.py:360
  111.2 10.6 %all-to-all-start.4 = ((bf16[32,4,16,128]{3,2,1,0:T(8,128)(2,1)}), bf16[32,4,16,128]{3,2,1,0:T(8,128)(2,1)S(1)}, u32[]{:S(2)}, u32[]{:S(2)}) async-start(bf16[32,4,16,128]{3,2,1,0:T(8,128)(2,1)} %spread.1.refs_0_), calls=%async_computation.4 | async-start | bytes 1048576 | tf_op jit(solution)/shard_map/all_to_all | solution.py:341
  121.8 0.6 finish.1
  122.4 14.6 %all-to-all-done.4 = bf16[32,4,16,128]{3,2,1,0:T(8,128)(2,1)S(1)} async-done(((bf16[32,4,16,128]{3,2,1,0:T(8,128)(2,1)}), bf16[32,4,16,128]{3,2,1,0:T(8,128)(2,1)S(1)}, u32[]{:S(2)}, u32[]{:S(2)}) %all-to-all-start.4) | async-done | bytes 524320 | tf_op jit(solution)/shard_map/all_to_all | solution.py:341
  137.0 0.0 copy-done.2
  137.0 3.2 %refresh.1 = (f32[128,512]{1,0:T(8,128)}, f32[128,512]{1,0:T(8,128)}) custom-call(s32[5]{0:T(128)S(1)} %stack.26.info_ref, s32[16]{0:T(128)S(1)} %copy-done.2, bf16[2,4,4,4,16,128]{5,4,3,2,1,0:T(8,128)(2,1)S(1)} %bitcast.17, f32[128,512]{1,0:T(8,128)S(1)} %bitcast.18, bf16[128,512]{1,0:T(8,128)(2,1)S(1)} %bitcast_convert_fusion.low_ref, ...), custom_call_target="tpu_custom_call" | custom-call | flops 603979776 | bytes 1048576 | tf_op jit(solution)/shard_map/refresh/pallas_call | solution.py:363
  (5 shorter events, 0.1 us)
Async XLA Ops:
  0.6 11.1 %copy-start.3 = (bf16[1,2,16,512]{3,2,1,0:T(8,128)(2,1)S(1)}, bf16[1,2,16,512]{3,2,1,0:T(8,128)(2,1)}, u32[]{:S(2)}) copy-start(bf16[1,2,16,512]{3,2,1,0:T(8,128)(2,1)} %param.9) | copy-start | bytes 98308
  0.6 11.1 %copy-start.4 = (bf16[1,2,16,512]{3,2,1,0:T(8,128)(2,1)S(1)}, bf16[1,2,16,512]{3,2,1,0:T(8,128)(2,1)}, u32[]{:S(2)}) copy-start(bf16[1,2,16,512]{3,2,1,0:T(8,128)(2,1)} %param.10) | copy-start | bytes 98308
  2.9 12.0 %collective-permute-start = (bf16[512,512]{1,0:T(8,128)(2,1)S(1)}, bf16[512,512]{1,0:T(8,128)(2,1)S(1)}, u32[]{:S(2)}, u32[]{:S(2)}) collective-permute-start(bf16[512,512]{1,0:T(8,128)(2,1)S(1)} %get-tuple-element.21), channel_id=1, source_target_pairs={{0,16},{16,0},{1,17},{17,1},{2,18},{18,2},{3,19},{19,3},{4,20},{20... | collective-permute-start | bytes 1572872 | tf_op jit(solution)/shard_map/ppermute | solution.py:292
  11.8 3.1 %collective-permute-start.1 = (bf16[2,16,512]{2,1,0:T(8,128)(2,1)S(1)}, bf16[2,16,512]{2,1,0:T(8,128)(2,1)S(1)}, u32[]{:S(2)}, u32[]{:S(2)}) collective-permute-start(bf16[2,16,512]{2,1,0:T(8,128)(2,1)S(1)} %get-tuple-element.35), channel_id=1, source_target_pairs={{0,16},{16,0},{1,17},{17,1},{2,18},{18,2},{3,19},{19,3},{4,20},{20... | collective-permute-start | bytes 98312 | tf_op jit(solution)/shard_map/ppermute | solution.py:295
  14.4 5.0 %copy-start = (f32[1,128,512]{2,1,0:T(8,128)S(1)}, f32[1,128,512]{2,1,0:T(8,128)}, u32[]{:S(2)}) copy-start(f32[1,128,512]{2,1,0:T(8,128)} %param.11) | copy-start | bytes 786436
  14.9 29.2 %copy-start.1 = (s32[16]{0:T(128)S(1)}, s32[16]{0:T(128)}, u32[]{:S(2)}) copy-start(s32[16]{0:T(128)} %listed_ref.3) | copy-start | bytes 196
  16.0 16.6 %all-to-all-start = ((bf16[4,160,512]{2,1,0:T(8,128)(2,1)}), bf16[4,160,512]{2,1,0:T(8,128)(2,1)S(1)}, u32[]{:S(2)}, u32[]{:S(2)}) async-start(bf16[4,160,512]{2,1,0:T(8,128)(2,1)} %get-tuple-element.22), calls=%async_computation | async-start | bytes 1310720 | tf_op jit(solution)/shard_map/all_to_all | solution.py:311
  19.5 8.4 %collective-permute-start.2 = (bf16[128,512]{1,0:T(8,128)(2,1)S(1)}, bf16[128,512]{1,0:T(8,128)(2,1)S(1)}, u32[]{:S(2)}, u32[]{:S(2)}) collective-permute-start(bf16[128,512]{1,0:T(8,128)(2,1)S(1)} %bitcast_convert_fusion.low_ref), channel_id=1, source_target_pairs={{0,4},{4,8},{8,12},{12,0},{1,5},{5,9},{9,13},{13,1},{2,6},{6,10},{... | collective-permute-start | bytes 393224 | tf_op jit(solution)/shard_map/ppermute | solution.py:119
  21.4 8.4 %collective-permute-start.3 = (bf16[128,512]{1,0:T(8,128)(2,1)S(1)}, bf16[128,512]{1,0:T(8,128)(2,1)S(1)}, u32[]{:S(2)}, u32[]{:S(2)}) collective-permute-start(bf16[128,512]{1,0:T(8,128)(2,1)S(1)} %bitcast_convert_fusion.low_ref), channel_id=1, source_target_pairs={{0,8},{4,12},{8,0},{12,4},{1,9},{5,13},{9,1},{13,5},{2,10},{6,14},... | collective-permute-start | bytes 393224 | tf_op jit(solution)/shard_map/ppermute | solution.py:119
  23.4 9.2 %collective-permute-start.4 = (bf16[128,512]{1,0:T(8,128)(2,1)S(1)}, bf16[128,512]{1,0:T(8,128)(2,1)S(1)}, u32[]{:S(2)}, u32[]{:S(2)}) collective-permute-start(bf16[128,512]{1,0:T(8,128)(2,1)S(1)} %bitcast_convert_fusion.low_ref), channel_id=1, source_target_pairs={{0,12},{4,0},{8,4},{12,8},{1,13},{5,1},{9,5},{13,9},{2,14},{6,2},{... | collective-permute-start | bytes 393224 | tf_op jit(solution)/shard_map/ppermute | solution.py:119
  45.4 35.7 %all-to-all-start.2 = ((bf16[32,16,128]{2,1,0:T(8,128)(2,1)}), bf16[32,16,128]{2,1,0:T(8,128)(2,1)S(1)}, u32[]{:S(2)}, u32[]{:S(2)}) async-start(bf16[32,16,128]{2,1,0:T(8,128)(2,1)} %get-tuple-element.28), calls=%async_computation.2 | async-start | bytes 262144 | tf_op jit(solution)/shard_map/all_to_all | solution.py:331
  63.4 19.1 %collective-permute-start.5 = (bf16[80,512]{1,0:T(8,128)(2,1)S(1)}, bf16[80,512]{1,0:T(8,128)(2,1)S(1)}, u32[]{:S(2)}, u32[]{:S(2)}) collective-permute-start(bf16[80,512]{1,0:T(8,128)(2,1)S(1)} %get-tuple-element.26.sent_one), channel_id=1, source_target_pairs={{0,32},{32,0},{64,96},{96,64},{1,33},{33,1},{65,97},{97,65},{2,34}... | collective-permute-start | bytes 245768 | tf_op jit(solution)/shard_map/ppermute | solution.py:334
  70.6 11.9 %collective-permute-start.6 = (bf16[80,512]{1,0:T(8,128)(2,1)S(1)}, bf16[80,512]{1,0:T(8,128)(2,1)S(1)}, u32[]{:S(2)}, u32[]{:S(2)}) collective-permute-start(bf16[80,512]{1,0:T(8,128)(2,1)S(1)} %get-tuple-element.27.sent_two), channel_id=1, source_target_pairs={{0,96},{32,64},{64,32},{96,0},{1,97},{33,65},{65,33},{97,1},{2,98}... | collective-permute-start | bytes 245768 | tf_op jit(solution)/shard_map/ppermute | solution.py:334
  77.6 59.5 %copy-start.2 = (s32[16]{0:T(128)S(1)}, s32[16]{0:T(128)}, u32[]{:S(2)}) copy-start(s32[16]{0:T(128)} %owner_ref.1) | copy-start | bytes 196
  82.5 15.0 %collective-permute-start.7 = (bf16[96,512]{1,0:T(8,128)(2,1)S(1)}, bf16[96,512]{1,0:T(8,128)(2,1)S(1)}, u32[]{:S(2)}, u32[]{:S(2)}) collective-permute-start(bf16[96,512]{1,0:T(8,128)(2,1)S(1)} %get-tuple-element.30.sent_one), channel_id=1, source_target_pairs={{0,96},{32,64},{64,32},{96,0},{1,97},{33,65},{65,33},{97,1},{2,98}... | collective-permute-start | bytes 294920 | tf_op jit(solution)/shard_map/ppermute | solution.py:351
  89.5 10.5 %collective-permute-start.8 = (bf16[96,512]{1,0:T(8,128)(2,1)S(1)}, bf16[96,512]{1,0:T(8,128)(2,1)S(1)}, u32[]{:S(2)}, u32[]{:S(2)}) collective-permute-start(bf16[96,512]{1,0:T(8,128)(2,1)S(1)} %get-tuple-element.31.sent_two), channel_id=1, source_target_pairs={{0,32},{32,0},{64,96},{96,64},{1,33},{33,1},{65,97},{97,65},{2,34}... | collective-permute-start | bytes 294920 | tf_op jit(solution)/shard_map/ppermute | solution.py:351
  111.2 25.9 %all-to-all-start.4 = ((bf16[32,4,16,128]{3,2,1,0:T(8,128)(2,1)}), bf16[32,4,16,128]{3,2,1,0:T(8,128)(2,1)S(1)}, u32[]{:S(2)}, u32[]{:S(2)}) async-start(bf16[32,4,16,128]{3,2,1,0:T(8,128)(2,1)} %spread.1.refs_0_), calls=%async_computation.4 | async-start | bytes 1048576 | tf_op jit(solution)/shard_map/all_to_all | solution.py:341

commit v8 on v7

--- a/solution.py
+++ b/solution.py
@@ -138,13 +138,13 @@
         if w:
             total = total + parts_ref[w, :PART].astype(F32)
     keep_ref[...] = total
-    n_mp, n_root, cores, rows, lanes = pieces_ref.shape
+    cores, n_mp, n_root, rows, lanes = pieces_ref.shape
     for c in range(cores):
         for r in range(n_root):
             at = (c * n_root + r) * rows
             for m in range(n_mp):
                 piece = total[at : at + rows, m * lanes : (m + 1) * lanes]
-                pieces_ref[m, r, c] = piece.astype(BF16)
+                pieces_ref[c, m, r] = piece.astype(BF16)
 
 
 def middle_kernel(keep_ref, sent_one, sent_two, got_one, got_two, *refs):
@@ -162,31 +162,28 @@
         ref[half + rows :] = got[half:]
 
 
-def choose_kernel(listed_ref, blocks_ref, keep_ref, right_ref, out_ref, send_one, send_two):
+def choose_kernel(place_ref, blocks_ref, keep_ref, right_ref, *refs):
+    out_ref, send_one, send_two = refs[-3:]
     for j in range(CHIPS):
-        pair = listed_ref[j] // 2
-        for c in range(CORE):
-            out_ref[j * CORE + c] = blocks_ref[pair, c]
+        out_ref[j] = blocks_ref[place_ref[j]]
     half, rows = PART // 2, ROWS // 2
     for part, ref in enumerate((send_one, send_two)):
         ref[:half] = keep_ref[part * half : (part + 1) * half].astype(BF16)
         ref[half:] = right_ref[part * rows : (part + 1) * rows]
 
 
-def spread_kernel(scale, info_ref, listed_ref, parts_ref, *refs):
-    out_ref = refs[-1]
-    holder = listed_ref[info_ref[1] * ZH + info_ref[2]] % 2
+def spread_kernel(scale, parts_ref, out_ref):
     for w in range(X):
-        total = parts_ref[w * ZH * CORE + holder].astype(F32)
+        total = parts_ref[w * ZH].astype(F32)
         for z in range(1, ZH):
-            total = total + parts_ref[(w * ZH + z) * CORE + holder].astype(F32)
+            total = total + parts_ref[w * ZH + z].astype(F32)
         tile = (total * scale).astype(BF16)
         for peer in range(out_ref.shape[0]):
             out_ref[peer, w] = tile
 
 
 def update_kernel(scale, info_ref, keep_ref, sent_one, sent_two, got_one, got_two, *refs):
-    left, out_ref, grad, right, total = refs
+    left, (out_ref, grad, right, total) = refs[0], refs[-4:]
     zh = info_ref[2]
     half, rows = PART // 2, ROWS // 2
     near = zh + 1 - 2 * (zh % 2)
@@ -316,28 +313,30 @@
         sum_kernel,
         "sum_x",
         [VMEM],
-        [shape((PART, B), F32), shape((PART, B)), shape((n_mp, n_root, CORE, half, lanes))],
-        awaited=3,
-    )(total, *olds[1:])
-
-    pieces = pieces.reshape((n_mp * n_root,) + pieces.shape[2:])
-    blocks = lax.all_to_all(pieces, ("mp", "root"), 0, 0)
+        [shape((PART, B), F32), shape((PART, B)), shape((CORE, n_mp, n_root, half, lanes))],
+        awaited=2,
+    )(total, *olds[1:3])
+
+    pieces = pieces.reshape((-1,) + pieces.shape[3:])
+    blocks = lax.all_to_all(pieces, ("core", "mp", "root"), 0, 0)
+    at = (listed % 2) * (n_mp * n_root) + listed // 2
     chosen, *sends = kernel_call(
         choose_kernel,
         "choose",
         [SMEM] + [VMEM] * 3,
-        [shape((CHIPS * CORE, half, lanes))] + [shape((PART // 2 + half, B))] * 2,
-    )(listed, blocks, keep, right_rows)
-    parts = lax.all_to_all(chosen, ("x", "zh", "core"), 0, 0)
+        [shape((CHIPS, half, lanes))] + [shape((PART // 2 + half, B))] * 2,
+        awaited=1,
+    )(at, blocks, keep, right_rows, olds[3])
+    parts = lax.all_to_all(chosen, ("x", "zh"), 0, 0)
     near = [(z, z ^ 1) for z in range(ZH)]
     far = [(z, ZH - 1 - z) for z in range(ZH)]
     got = [lax.ppermute(sends[0], "zh", near), lax.ppermute(sends[1], "zh", far)]
     (spread,) = kernel_call(
         functools.partial(spread_kernel, tokens ** -0.5),
         "spread",
-        [SMEM, SMEM, VMEM],
+        [VMEM],
         [shape((CORE * n_mp * n_root, X, half, lanes))],
-    )(info, listed, parts)
+    )(parts)
     gathered = lax.all_to_all(spread, ("core", "mp", "root"), 0, 0)
     gathered = gathered.reshape((CORE, n_mp, n_root) + gathered.shape[1:])
 
@@ -356,7 +355,8 @@
         [shape((X * CORE, B // lanes, half, lanes))],
         [pltpu.VMEM((PART, B), BF16)] * 2 + [pltpu.VMEM((PART, B), F32)],
         cost(2 * PART * B * (PART + B), 6 * PART * B),
-    )(info, keep, *sends, *got, left_part)
+        awaited=1,
+    )(info, keep, *sends, *got, left_part, gathered)
     got = lax.all_to_all(send, ("x", "core"), 0, 0)
     (update,) = kernel_call(finish_kernel, "finish", [VMEM], [shape((half, 2 * B))])(got)
 

time: 141 us -> 133 us (0.943)
  the two profiles are of different devices: /device:TPU:1 before, /device:TPU:72 now
where the time goes in v8:
time: 133 us; the launch traced here: 132 us
  starting transfers between devices  52.9 us (40%)
  waiting for transfers between devices  35.8 us (27%)
  blocking collectives  30.7 us (23%)
  Pallas kernels  11.6 us (9%)
    all_to_all x1, blocking collectives, local(): parts = lax.all_to_all(chosen, ('x', 'zh'), 0, 0)  30.7 us
    ppermute x1, waiting for transfers between devices, local(): lax.ppermute(sends[0], 'zh', near)  13.9 us
    ppermute x3, waiting for transfers between devices, shift(): lax.ppermute(value, axis, [(at, (at + step) % size) for at in range(size)])  11.2 us
    ppermute x3, starting transfers between devices, shift(): lax.ppermute(value, axis, [(at, (at + step) % size) for at in range(size)])  8.81 us
    all_to_all x1, starting transfers between devices, local(): blocks = lax.all_to_all(pieces, ('core', 'mp', 'root'), 0, 0)  7.93 us
    ppermute x1, starting transfers between devices, local(): lax.ppermute(sends[0], 'zh', far)  7.63 us
    all_to_all x1, starting transfers between devices, local(): gathered = lax.all_to_all(spread, ('core', 'mp', 'root'), 0, 0)  7.56 us
    all_to_all x1, starting transfers between devices, local(): total = lax.all_to_all(total, 'x', 0, 0)  4.29 us
  transfers between devices with their start and end apart: 13, of which 8 were waited for; matrix products, arithmetic and copies ran while one was open for 0% of the time, Pallas kernels for 3%

profile of v8, /device:TPU:72, one launch (start us, length us, event | category | flops | bytes accessed | tf_op | source)
XLA Modules:
  0.0 132.1 jit_solution(12679399053721214304)
XLA Ops:
  0.6 0.0 copy-start.2
  0.6 0.0 copy-start.3
  0.7 2.3 %other_half.1 = (bf16[512,1024]{1,0:T(8,128)(2,1)S(1)}, bf16[512,512]{1,0:T(8,128)(2,1)S(1)}, bf16[1024,512]{1,0:T(8,128)(2,1)S(1)}) custom-call(s32[1]{0:T(128)} %bitcast.5.index_ref, bf16[1024,512]{1,0:T(8,128)(2,1)} %acts_ref.1, bf16[1024,1024]{1,0:T(8,128)(2,1)} %grads_ref.1), custom_call_target="tpu_custom_call" | custom-call | flops 536870912 | bytes 3145728 | tf_op jit(solution)/shard_map/other_half/pallas_call | solution.py:80
  2.9 1.9 %collective-permute-start = (bf16[512,512]{1,0:T(8,128)(2,1)S(1)}, bf16[512,512]{1,0:T(8,128)(2,1)S(1)}, u32[]{:S(2)}, u32[]{:S(2)}) collective-permute-start(bf16[512,512]{1,0:T(8,128)(2,1)S(1)} %get-tuple-element.21), channel_id=1, source_target_pairs={{0,16},{16,0},{1,17},{17,1},{2,18},{18,2},{3,19},{19,3},{4,20},{20... | collective-permute-start | bytes 1572872 | tf_op jit(solution)/shard_map/ppermute | solution.py:289
  4.9 0.0 copy-done.2
  4.9 0.0 copy-done.3
  4.9 2.4 %collective-permute-start.1 = (bf16[2,16,512]{2,1,0:T(8,128)(2,1)S(1)}, bf16[2,16,512]{2,1,0:T(8,128)(2,1)S(1)}, u32[]{:S(2)}, u32[]{:S(2)}) collective-permute-start(bf16[2,16,512]{2,1,0:T(8,128)(2,1)S(1)} %get-tuple-element.35), channel_id=1, source_target_pairs={{0,16},{16,0},{1,17},{17,1},{2,18},{18,2},{3,19},{19,3},{4,20},{20... | collective-permute-start | bytes 98312 | tf_op jit(solution)/shard_map/ppermute | solution.py:292
  7.3 0.7 own_half.1.own_ref
  8.0 0.0 copy-start
  8.1 0.1 collective-permute-done.1.theirs_ref
  8.2 0.0 collective-permute-done.got_ref
  8.2 0.0 copy-start.4
  8.2 1.1 join.1
  9.3 4.3 %all-to-all-start = ((bf16[4,160,512]{2,1,0:T(8,128)(2,1)}), bf16[4,160,512]{2,1,0:T(8,128)(2,1)S(1)}, u32[]{:S(2)}, u32[]{:S(2)}) async-start(bf16[4,160,512]{2,1,0:T(8,128)(2,1)} %get-tuple-element.22), calls=%async_computation | async-start | bytes 1310720 | tf_op jit(solution)/shard_map/all_to_all | solution.py:308
  13.6 0.0 copy-done
  13.6 3.5 %collective-permute-start.2 = (bf16[128,512]{1,0:T(8,128)(2,1)S(1)}, bf16[128,512]{1,0:T(8,128)(2,1)S(1)}, u32[]{:S(2)}, u32[]{:S(2)}) collective-permute-start(bf16[128,512]{1,0:T(8,128)(2,1)S(1)} %bitcast_convert_fusion.low_ref), channel_id=1, source_target_pairs={{0,4},{4,8},{8,12},{12,0},{1,5},{5,9},{9,13},{13,1},{2,6},{6,10},{... | collective-permute-start | bytes 393224 | tf_op jit(solution)/shard_map/ppermute | solution.py:119
  17.1 2.9 %collective-permute-start.3 = (bf16[128,512]{1,0:T(8,128)(2,1)S(1)}, bf16[128,512]{1,0:T(8,128)(2,1)S(1)}, u32[]{:S(2)}, u32[]{:S(2)}) collective-permute-start(bf16[128,512]{1,0:T(8,128)(2,1)S(1)} %bitcast_convert_fusion.low_ref), channel_id=1, source_target_pairs={{0,8},{4,12},{8,0},{12,4},{1,9},{5,13},{9,1},{13,5},{2,10},{6,14},... | collective-permute-start | bytes 393224 | tf_op jit(solution)/shard_map/ppermute | solution.py:119
  19.9 1.0 collective-permute-done.2.refs_0_.one
  20.9 4.7 %collective-permute-done.3.refs_1_.two = bf16[128,512]{1,0:T(8,128)(2,1)S(1)} collective-permute-done((bf16[128,512]{1,0:T(8,128)(2,1)S(1)}, bf16[128,512]{1,0:T(8,128)(2,1)S(1)}, u32[]{:S(2)}, u32[]{:S(2)}) %collective-permute-start.3) | collective-permute-done | bytes 131104 | tf_op jit(solution)/shard_map/ppermute | solution.py:119
  25.7 0.0 all-to-all-done.parts_ref
  25.7 0.7 sum_x.1
  26.4 7.9 %all-to-all-start.1 = ((bf16[32,16,128]{2,1,0:T(8,128)(2,1)}), bf16[32,16,128]{2,1,0:T(8,128)(2,1)S(1)}, u32[]{:S(2)}, u32[]{:S(2)}) async-start(bf16[32,16,128]{2,1,0:T(8,128)(2,1)} %bitcast.9), calls=%async_computation.1 | async-start | bytes 262144 | tf_op jit(solution)/shard_map/all_to_all | solution.py:321
  34.3 2.5 %collective-permute-start.4 = (bf16[128,512]{1,0:T(8,128)(2,1)S(1)}, bf16[128,512]{1,0:T(8,128)(2,1)S(1)}, u32[]{:S(2)}, u32[]{:S(2)}) collective-permute-start(bf16[128,512]{1,0:T(8,128)(2,1)S(1)} %bitcast_convert_fusion.low_ref), channel_id=1, source_target_pairs={{0,12},{4,0},{8,4},{12,8},{1,13},{5,1},{9,5},{13,9},{2,14},{6,2},{... | collective-permute-start | bytes 393224 | tf_op jit(solution)/shard_map/ppermute | solution.py:119
  36.8 0.0 copy-done.4
  36.8 5.5 %collective-permute-done.4.refs_0_.three = bf16[128,512]{1,0:T(8,128)(2,1)S(1)} collective-permute-done((bf16[128,512]{1,0:T(8,128)(2,1)S(1)}, bf16[128,512]{1,0:T(8,128)(2,1)S(1)}, u32[]{:S(2)}, u32[]{:S(2)}) %collective-permute-start.4) | collective-permute-done | bytes 131104 | tf_op jit(solution)/shard_map/ppermute | solution.py:119
  42.3 0.0 all-to-all-done.1.blocks_ref
  42.3 0.6 choose.1
  42.9 30.7 %all_to_all.25.parts_ref = bf16[16,16,128]{2,1,0:T(8,128)(2,1)S(1)} all-to-all(bf16[16,16,128]{2,1,0:T(8,128)(2,1)S(1)} %get-tuple-element.28), channel_id=1, replica_groups=mesh['x'=4,'zh'=4,'core'=2,'mp'=4,'root'=4] {'x','zh'}, dimensions={0} | all-to-all | bytes 131072 | tf_op jit(solution)/shard_map/all_to_all | solution.py:330
  73.6 0.9 spread.1.refs_0_
  74.5 0.0 copy-start.1
  74.5 7.6 %all-to-all-start.3 = ((bf16[32,4,16,128]{3,2,1,0:T(8,128)(2,1)}), bf16[32,4,16,128]{3,2,1,0:T(8,128)(2,1)S(1)}, u32[]{:S(2)}, u32[]{:S(2)}) async-start(bf16[32,4,16,128]{3,2,1,0:T(8,128)(2,1)} %spread.1.refs_0_), calls=%async_computation.3 | async-start | bytes 1048576 | tf_op jit(solution)/shard_map/all_to_all | solution.py:340
  82.0 2.6 %collective-permute-start.5 = (bf16[80,512]{1,0:T(8,128)(2,1)S(1)}, bf16[80,512]{1,0:T(8,128)(2,1)S(1)}, u32[]{:S(2)}, u32[]{:S(2)}) collective-permute-start(bf16[80,512]{1,0:T(8,128)(2,1)S(1)} %get-tuple-element.26.sent_one), channel_id=1, source_target_pairs={{0,32},{32,0},{64,96},{96,64},{1,33},{33,1},{65,97},{97,65},{2,34}... | collective-permute-start | bytes 245768 | tf_op jit(solution)/shard_map/ppermute | solution.py:333
  84.6 3.2 %collective-permute-start.6 = (bf16[80,512]{1,0:T(8,128)(2,1)S(1)}, bf16[80,512]{1,0:T(8,128)(2,1)S(1)}, u32[]{:S(2)}, u32[]{:S(2)}) collective-permute-start(bf16[80,512]{1,0:T(8,128)(2,1)S(1)} %get-tuple-element.27.sent_two), channel_id=1, source_target_pairs={{0,96},{32,64},{64,32},{96,0},{1,97},{33,65},{65,33},{97,1},{2,98}... | collective-permute-start | bytes 245768 | tf_op jit(solution)/shard_map/ppermute | solution.py:333
  87.8 13.9 %collective-permute-done.5.got_one = bf16[80,512]{1,0:T(8,128)(2,1)S(1)} collective-permute-done((bf16[80,512]{1,0:T(8,128)(2,1)S(1)}, bf16[80,512]{1,0:T(8,128)(2,1)S(1)}, u32[]{:S(2)}, u32[]{:S(2)}) %collective-permute-start.5) | collective-permute-done | bytes 81952 | tf_op jit(solution)/shard_map/ppermute | solution.py:333
  101.7 0.0 collective-permute-done.6.got_two
  101.7 7.6 %collective-permute-start.7 = (bf16[96,512]{1,0:T(8,128)(2,1)S(1)}, bf16[96,512]{1,0:T(8,128)(2,1)S(1)}, u32[]{:S(2)}, u32[]{:S(2)}) collective-permute-start(bf16[96,512]{1,0:T(8,128)(2,1)S(1)} %get-tuple-element.30.sent_one), channel_id=1, source_target_pairs={{0,96},{32,64},{64,32},{96,0},{1,97},{33,65},{65,33},{97,1},{2,98}... | collective-permute-start | bytes 294920 | tf_op jit(solution)/shard_map/ppermute | solution.py:350
  109.4 3.2 %collective-permute-start.8 = (bf16[96,512]{1,0:T(8,128)(2,1)S(1)}, bf16[96,512]{1,0:T(8,128)(2,1)S(1)}, u32[]{:S(2)}, u32[]{:S(2)}) collective-permute-start(bf16[96,512]{1,0:T(8,128)(2,1)S(1)} %get-tuple-element.31.sent_two), channel_id=1, source_target_pairs={{0,32},{32,0},{64,96},{96,64},{1,33},{33,1},{65,97},{97,65},{2,34}... | collective-permute-start | bytes 294920 | tf_op jit(solution)/shard_map/ppermute | solution.py:350
  112.6 0.1 stack.26.info_ref
  112.7 3.6 %collective-permute-done.7.got_one = bf16[96,512]{1,0:T(8,128)(2,1)S(1)} collective-permute-done((bf16[96,512]{1,0:T(8,128)(2,1)S(1)}, bf16[96,512]{1,0:T(8,128)(2,1)S(1)}, u32[]{:S(2)}, u32[]{:S(2)}) %collective-permute-start.7) | collective-permute-done | bytes 98336 | tf_op jit(solution)/shard_map/ppermute | solution.py:350
  116.3 4.1 %collective-permute-done.8.got_two = bf16[96,512]{1,0:T(8,128)(2,1)S(1)} collective-permute-done((bf16[96,512]{1,0:T(8,128)(2,1)S(1)}, bf16[96,512]{1,0:T(8,128)(2,1)S(1)}, u32[]{:S(2)}, u32[]{:S(2)}) %collective-permute-start.8) | collective-permute-done | bytes 98336 | tf_op jit(solution)/shard_map/ppermute | solution.py:350
  120.4 0.0 all-to-all-done.3
  120.4 1.6 %update.1 = bf16[8,4,16,128]{3,2,1,0:T(8,128)(2,1)} custom-call(s32[5]{0:T(128)S(1)} %stack.26.info_ref, f32[128,512]{1,0:T(8,128)S(1)} %get-tuple-element.29.keep_ref, bf16[96,512]{1,0:T(8,128)(2,1)S(1)} %get-tuple-element.30.sent_one, bf16[96,512]{1,0:T(8,128)(2,1)S(1)} %get-tuple-element.31.sent_two, bf16[96,512]{1,0:T(8,128)(2,1)S(1)} %collective-permute-done.7.got_one, ...), custom_call_target="tpu_custom_call" | custom-call | flops 83886080 | bytes 393216 | tf_op jit(solution)/shard_map/update/pallas_call | solution.py:351
  122.0 3.4 %all-to-all-start.4 = ((bf16[8,4,16,128]{3,2,1,0:T(8,128)(2,1)}), bf16[8,4,16,128]{3,2,1,0:T(8,128)(2,1)S(1)}, u32[]{:S(2)}, u32[]{:S(2)}) async-start(bf16[8,4,16,128]{3,2,1,0:T(8,128)(2,1)} %update.1), calls=%async_computation.4 | async-start | bytes 262144 | tf_op jit(solution)/shard_map/all_to_all | solution.py:360
  125.4 0.0 copy-done.1
  125.4 3.2 %refresh.1 = (f32[128,512]{1,0:T(8,128)}, f32[128,512]{1,0:T(8,128)}) custom-call(s32[5]{0:T(128)S(1)} %stack.26.info_ref, s32[16]{0:T(128)S(1)} %copy-done.1, bf16[2,4,4,4,16,128]{5,4,3,2,1,0:T(8,128)(2,1)S(1)} %bitcast.18, f32[128,512]{1,0:T(8,128)S(1)} %bitcast.19, bf16[128,512]{1,0:T(8,128)(2,1)S(1)} %bitcast_convert_fusion.low_ref, ...), custom_call_target="tpu_custom_call" | custom-call | flops 603979776 | bytes 1048576 | tf_op jit(solution)/shard_map/refresh/pallas_call | solution.py:363
  128.6 2.9 %all-to-all-done.4.parts_ref = bf16[8,4,16,128]{3,2,1,0:T(8,128)(2,1)S(1)} async-done(((bf16[8,4,16,128]{3,2,1,0:T(8,128)(2,1)}), bf16[8,4,16,128]{3,2,1,0:T(8,128)(2,1)S(1)}, u32[]{:S(2)}, u32[]{:S(2)}) %all-to-all-start.4) | async-done | bytes 131104 | tf_op jit(solution)/shard_map/all_to_all | solution.py:360
  131.4 0.6 finish.1
  (6 shorter events, 0.1 us)
Async XLA Ops:
  0.6 4.2 %copy-start.2 = (bf16[1,2,16,512]{3,2,1,0:T(8,128)(2,1)S(1)}, bf16[1,2,16,512]{3,2,1,0:T(8,128)(2,1)}, u32[]{:S(2)}) copy-start(bf16[1,2,16,512]{3,2,1,0:T(8,128)(2,1)} %param.9) | copy-start | bytes 98308
  0.6 4.2 %copy-start.3 = (bf16[1,2,16,512]{3,2,1,0:T(8,128)(2,1)S(1)}, bf16[1,2,16,512]{3,2,1,0:T(8,128)(2,1)}, u32[]{:S(2)}) copy-start(bf16[1,2,16,512]{3,2,1,0:T(8,128)(2,1)} %param.10) | copy-start | bytes 98308
  2.9 5.3 %collective-permute-start = (bf16[512,512]{1,0:T(8,128)(2,1)S(1)}, bf16[512,512]{1,0:T(8,128)(2,1)S(1)}, u32[]{:S(2)}, u32[]{:S(2)}) collective-permute-start(bf16[512,512]{1,0:T(8,128)(2,1)S(1)} %get-tuple-element.21), channel_id=1, source_target_pairs={{0,16},{16,0},{1,17},{17,1},{2,18},{18,2},{3,19},{19,3},{4,20},{20... | collective-permute-start | bytes 1572872 | tf_op jit(solution)/shard_map/ppermute | solution.py:289
  4.9 3.3 %collective-permute-start.1 = (bf16[2,16,512]{2,1,0:T(8,128)(2,1)S(1)}, bf16[2,16,512]{2,1,0:T(8,128)(2,1)S(1)}, u32[]{:S(2)}, u32[]{:S(2)}) collective-permute-start(bf16[2,16,512]{2,1,0:T(8,128)(2,1)S(1)} %get-tuple-element.35), channel_id=1, source_target_pairs={{0,16},{16,0},{1,17},{17,1},{2,18},{18,2},{3,19},{19,3},{4,20},{20... | collective-permute-start | bytes 98312 | tf_op jit(solution)/shard_map/ppermute | solution.py:292
  8.0 5.5 %copy-start = (f32[1,128,512]{2,1,0:T(8,128)S(1)}, f32[1,128,512]{2,1,0:T(8,128)}, u32[]{:S(2)}) copy-start(f32[1,128,512]{2,1,0:T(8,128)} %param.11) | copy-start | bytes 786436
  8.2 28.6 %copy-start.4 = (s32[16]{0:T(128)S(1)}, s32[16]{0:T(128)}, u32[]{:S(2)}) copy-start(s32[16]{0:T(128)} %param.12) | copy-start | bytes 196
  9.3 16.4 %all-to-all-start = ((bf16[4,160,512]{2,1,0:T(8,128)(2,1)}), bf16[4,160,512]{2,1,0:T(8,128)(2,1)S(1)}, u32[]{:S(2)}, u32[]{:S(2)}) async-start(bf16[4,160,512]{2,1,0:T(8,128)(2,1)} %get-tuple-element.22), calls=%async_computation | async-start | bytes 1310720 | tf_op jit(solution)/shard_map/all_to_all | solution.py:308
  13.6 7.4 %collective-permute-start.2 = (bf16[128,512]{1,0:T(8,128)(2,1)S(1)}, bf16[128,512]{1,0:T(8,128)(2,1)S(1)}, u32[]{:S(2)}, u32[]{:S(2)}) collective-permute-start(bf16[128,512]{1,0:T(8,128)(2,1)S(1)} %bitcast_convert_fusion.low_ref), channel_id=1, source_target_pairs={{0,4},{4,8},{8,12},{12,0},{1,5},{5,9},{9,13},{13,1},{2,6},{6,10},{... | collective-permute-start | bytes 393224 | tf_op jit(solution)/shard_map/ppermute | solution.py:119
  17.1 8.6 %collective-permute-start.3 = (bf16[128,512]{1,0:T(8,128)(2,1)S(1)}, bf16[128,512]{1,0:T(8,128)(2,1)S(1)}, u32[]{:S(2)}, u32[]{:S(2)}) collective-permute-start(bf16[128,512]{1,0:T(8,128)(2,1)S(1)} %bitcast_convert_fusion.low_ref), channel_id=1, source_target_pairs={{0,8},{4,12},{8,0},{12,4},{1,9},{5,13},{9,1},{13,5},{2,10},{6,14},... | collective-permute-start | bytes 393224 | tf_op jit(solution)/shard_map/ppermute | solution.py:119
  26.4 15.9 %all-to-all-start.1 = ((bf16[32,16,128]{2,1,0:T(8,128)(2,1)}), bf16[32,16,128]{2,1,0:T(8,128)(2,1)S(1)}, u32[]{:S(2)}, u32[]{:S(2)}) async-start(bf16[32,16,128]{2,1,0:T(8,128)(2,1)} %bitcast.9), calls=%async_computation.1 | async-start | bytes 262144 | tf_op jit(solution)/shard_map/all_to_all | solution.py:321
  34.3 8.0 %collective-permute-start.4 = (bf16[128,512]{1,0:T(8,128)(2,1)S(1)}, bf16[128,512]{1,0:T(8,128)(2,1)S(1)}, u32[]{:S(2)}, u32[]{:S(2)}) collective-permute-start(bf16[128,512]{1,0:T(8,128)(2,1)S(1)} %bitcast_convert_fusion.low_ref), channel_id=1, source_target_pairs={{0,12},{4,0},{8,4},{12,8},{1,13},{5,1},{9,5},{13,9},{2,14},{6,2},{... | collective-permute-start | bytes 393224 | tf_op jit(solution)/shard_map/ppermute | solution.py:119
  74.5 50.9 %copy-start.1 = (s32[16]{0:T(128)S(1)}, s32[16]{0:T(128)}, u32[]{:S(2)}) copy-start(s32[16]{0:T(128)} %owner_ref.1) | copy-start | bytes 196
  74.5 46.0 %all-to-all-start.3 = ((bf16[32,4,16,128]{3,2,1,0:T(8,128)(2,1)}), bf16[32,4,16,128]{3,2,1,0:T(8,128)(2,1)S(1)}, u32[]{:S(2)}, u32[]{:S(2)}) async-start(bf16[32,4,16,128]{3,2,1,0:T(8,128)(2,1)} %spread.1.refs_0_), calls=%async_computation.3 | async-start | bytes 1048576 | tf_op jit(solution)/shard_map/all_to_all | solution.py:340
  82.0 19.7 %collective-permute-start.5 = (bf16[80,512]{1,0:T(8,128)(2,1)S(1)}, bf16[80,512]{1,0:T(8,128)(2,1)S(1)}, u32[]{:S(2)}, u32[]{:S(2)}) collective-permute-start(bf16[80,512]{1,0:T(8,128)(2,1)S(1)} %get-tuple-element.26.sent_one), channel_id=1, source_target_pairs={{0,32},{32,0},{64,96},{96,64},{1,33},{33,1},{65,97},{97,65},{2,34}... | collective-permute-start | bytes 245768 | tf_op jit(solution)/shard_map/ppermute | solution.py:333
  84.6 17.1 %collective-permute-start.6 = (bf16[80,512]{1,0:T(8,128)(2,1)S(1)}, bf16[80,512]{1,0:T(8,128)(2,1)S(1)}, u32[]{:S(2)}, u32[]{:S(2)}) collective-permute-start(bf16[80,512]{1,0:T(8,128)(2,1)S(1)} %get-tuple-element.27.sent_two), channel_id=1, source_target_pairs={{0,96},{32,64},{64,32},{96,0},{1,97},{33,65},{65,33},{97,1},{2,98}... | collective-permute-start | bytes 245768 | tf_op jit(solution)/shard_map/ppermute | solution.py:333
  101.7 14.6 %collective-permute-start.7 = (bf16[96,512]{1,0:T(8,128)(2,1)S(1)}, bf16[96,512]{1,0:T(8,128)(2,1)S(1)}, u32[]{:S(2)}, u32[]{:S(2)}) collective-permute-start(bf16[96,512]{1,0:T(8,128)(2,1)S(1)} %get-tuple-element.30.sent_one), channel_id=1, source_target_pairs={{0,96},{32,64},{64,32},{96,0},{1,97},{33,65},{65,33},{97,1},{2,98}... | collective-permute-start | bytes 294920 | tf_op jit(solution)/shard_map/ppermute | solution.py:350
  109.4 11.0 %collective-permute-start.8 = (bf16[96,512]{1,0:T(8,128)(2,1)S(1)}, bf16[96,512]{1,0:T(8,128)(2,1)S(1)}, u32[]{:S(2)}, u32[]{:S(2)}) collective-permute-start(bf16[96,512]{1,0:T(8,128)(2,1)S(1)} %get-tuple-element.31.sent_two), channel_id=1, source_target_pairs={{0,32},{32,0},{64,96},{96,64},{1,33},{33,1},{65,97},{97,65},{2,34}... | collective-permute-start | bytes 294920 | tf_op jit(solution)/shard_map/ppermute | solution.py:350
  122.0 9.4 %all-to-all-start.4 = ((bf16[8,4,16,128]{3,2,1,0:T(8,128)(2,1)}), bf16[8,4,16,128]{3,2,1,0:T(8,128)(2,1)S(1)}, u32[]{:S(2)}, u32[]{:S(2)}) async-start(bf16[8,4,16,128]{3,2,1,0:T(8,128)(2,1)} %update.1), calls=%async_computation.4 | async-start | bytes 262144 | tf_op jit(solution)/shard_map/all_to_all | solution.py:360

commit v9 on v6

--- a/solution.py
+++ b/solution.py
@@ -98,8 +98,20 @@
     out_ref[...] = dot(turned_ref[...], grads_ref[...])
 
 
-def join_kernel(own_ref, got_ref, out_ref):
-    out_ref[...] = (own_ref[...] + got_ref[...].astype(F32)).astype(BF16).T
+def join_kernel(index_ref, own_ref, got_ref, mine_ref, theirs_ref, out_ref, right_ref):
+    core = index_ref[0]
+    rows = mine_ref.shape[1]
+    total = (own_ref[...] + got_ref[...].astype(F32)).astype(BF16).T
+    mine = pl.ds(pl.multiple_of(core * rows, rows), rows)
+    theirs = pl.ds(pl.multiple_of((1 - core) * rows, rows), rows)
+    right_ref[mine, :] = mine_ref[1]
+    right_ref[theirs, :] = theirs_ref[1]
+    mine = pl.ds(pl.multiple_of(PART + core * rows, rows), rows)
+    theirs = pl.ds(pl.multiple_of(PART + (1 - core) * rows, rows), rows)
+    for w in range(X):
+        out_ref[w, :PART] = total[w * PART : (w + 1) * PART]
+        out_ref[w, mine, :] = mine_ref[0]
+        out_ref[w, theirs, :] = theirs_ref[0]
 
 
 def shift(value, axis, step):
@@ -118,73 +130,46 @@
         out_ref[pl.ds(pl.multiple_of(at, rows), rows), :] = part[...]
 
 
-def added(parts_ref):
-    total = parts_ref[0].astype(F32)
-    for part in range(1, parts_ref.shape[0]):
-        total = total + parts_ref[part].astype(F32)
-    return total
-
-
-def sum_kernel(info_ref, parts_ref, mine_ref, theirs_ref, *refs):
-    keep_ref, left_ref, send_one, send_two = refs[-5:-1]
-    right, core = refs[-1], info_ref[0]
-    rows = mine_ref.shape[1]
-    for side, ref in enumerate((left_ref, right)):
-        ref[pl.ds(pl.multiple_of(core * rows, rows), rows), :] = mine_ref[side]
-        ref[pl.ds(pl.multiple_of((1 - core) * rows, rows), rows), :] = theirs_ref[side]
-    total = added(parts_ref)
+def sum_kernel(parts_ref, right_ref, *refs):
+    keep_ref, left_ref, send_ref = refs[-3:]
+    total = parts_ref[0, :PART].astype(F32)
+    for w in range(X):
+        left_ref[w * ROWS : (w + 1) * ROWS] = parts_ref[w, PART:]
+        if w:
+            total = total + parts_ref[w, :PART].astype(F32)
     keep_ref[...] = total
-    half = PART // 2
-    for part, ref in enumerate((send_one, send_two)):
-        ref[:half] = total[part * half : (part + 1) * half].astype(BF16)
-        ref[half:] = right[part * rows : (part + 1) * rows]
-
-
-def middle_kernel(keep_ref, sent_one, sent_two, got_one, got_two, *refs):
-    out_ref, send_one, send_two = refs[-3:]
-    half = PART // 2
-    for part, (sent, got, ref) in enumerate(
-        ((sent_one, got_one, send_one), (sent_two, got_two, send_two))
-    ):
-        at = slice(part * half, (part + 1) * half)
-        total = keep_ref[at] + got[:half].astype(F32)
-        out_ref[at] = total
-        rows = sent.shape[0] - half
-        ref[:half] = total.astype(BF16)
-        ref[half : half + rows] = sent[half:]
-        ref[half + rows :] = got[half:]
-
-
-def pack_kernel(scale, info_ref, keep_ref, sent_one, sent_two, got_one, got_two, *refs):
-    grad_ref, pieces_ref, right_ref = refs[-3:]
-    zh = info_ref[2]
-    half, rows = PART // 2, ROWS // 2
+    send_ref[:PART] = total.astype(BF16)
+    send_ref[PART:] = right_ref[...]
+
+
+def middle_kernel(keep_ref, right_ref, got_ref, out_ref, send_ref):
+    total = keep_ref[...] + got_ref[:PART].astype(F32)
+    out_ref[...] = total
+    send_ref[:PART] = total.astype(BF16)
+    send_ref[PART : PART + ROWS] = right_ref[...]
+    send_ref[PART + ROWS :] = got_ref[PART:]
+
+
+def pack_kernel(scale, info_ref, keep_ref, sent_ref, got_ref, grad_ref, pieces_ref, right_ref):
+    core, zh = info_ref[0], info_ref[2]
+    grad = ((keep_ref[...] + got_ref[:PART].astype(F32)) * scale).astype(BF16)
+    grad_ref[...] = grad
     near = zh + 1 - 2 * (zh % 2)
     far = ZH - 1 - zh
     across = far + 1 - 2 * (far % 2)
-    for part, (sent, got, mates) in enumerate(
-        (
-            (sent_one, got_one, (zh, near, far, across)),
-            (sent_two, got_two, (zh, far, near, across)),
-        )
-    ):
-        at = slice(part * half, (part + 1) * half)
-        grad_ref[at] = ((keep_ref[at] + got[:half].astype(F32)) * scale).astype(BF16)
-        for place_at, mate in enumerate(mates):
-            source = (sent, got)[place_at // 2]
-            start = half + place_at % 2 * rows
-            to = pl.multiple_of(mate * ROWS + part * rows, rows)
-            right_ref[pl.ds(to, rows), :] = source[start : start + rows]
+    first = jnp.where(core == 0, near, far)
+    second = jnp.where(core == 0, far, near)
+    for place_at, mate in enumerate((zh, first, second, across)):
+        source = (sent_ref, got_ref)[place_at // 2]
+        start = PART + place_at % 2 * ROWS
+        to = pl.multiple_of(mate * ROWS, ROWS)
+        right_ref[pl.ds(to, ROWS), :] = source[start : start + ROWS]
     n_mp, n_root, cores, rows, lanes = pieces_ref.shape
     for c in range(cores):
         for r in range(n_root):
             at = (c * n_root + r) * rows
             for m in range(n_mp):
-                pieces_ref[m, r, c] = grad_ref[at : at + rows, m * lanes : (m + 1) * lanes]
-
-
-def copy_kernel(value_ref, *refs):
-    refs[-1][...] = value_ref[...]
+                pieces_ref[m, r, c] = grad[at : at + rows, m * lanes : (m + 1) * lanes]
 
 
 def choose_kernel(info_ref, listed_ref, blocks_ref, total_ref, *refs):
@@ -219,9 +204,8 @@
             out_ref[:, at : at + lanes] = total.astype(BF16)
 
 
-def update_kernel(info_ref, own_ref, one, two, three, grad_ref, right_ref, out_ref, left):
-    place(left, (own_ref, one, two, three), info_ref[1])
-    product = dot(left[...], grad_ref[...], 1, 1).astype(BF16)
+def update_kernel(left_ref, grad_ref, right_ref, out_ref):
+    product = dot(left_ref[...], grad_ref[...], 1, 1).astype(BF16)
     out_ref[...] = dot(product, right_ref[...])
 
 
@@ -290,6 +274,11 @@
 
     turned, send, grads_own = other_half(acts, grads_out, 1 - core)
     got = lax.ppermute(send, "core", swap)
+    prec = jnp.stack([prec_left[0], prec_right[0]])
+    mine = lax.dynamic_index_in_dim(prec, core, 1, keepdims=False)
+    theirs = lax.ppermute(
+        lax.dynamic_index_in_dim(prec, 1 - core, 1, keepdims=False), "core", swap
+    )
     (own,) = kernel_call(
         own_kernel,
         "own_half",
@@ -297,48 +286,46 @@
         [shape((B, B), F32)],
         work=cost(2 * acts.shape[0] * B * B, 4 * acts.shape[0] * B),
     )(turned, grads_own)
-    (total,) = kernel_call(join_kernel, "join", [VMEM, VMEM], [shape((B, B))])(own, got)
-    total = lax.all_to_all(total.reshape(X, PART, B), "x", 0, 0)
-    prec = jnp.stack([prec_left[0], prec_right[0]])
-    mine = lax.dynamic_index_in_dim(prec, core, 1, keepdims=False)
-    theirs = lax.ppermute(
-        lax.dynamic_index_in_dim(prec, 1 - core, 1, keepdims=False), "core", swap
-    )
+    total, right_rows = kernel_call(
+        join_kernel,
+        "join",
+        [SMEM] + [VMEM] * 4,
+        [shape((X, PART + ROWS, B)), shape((ROWS, B))],
+    )(core.reshape(1), own, got, mine, theirs)
+    total = lax.all_to_all(total, "x", 0, 0)
     old_own = stats_old[0]
     old_low = old_own.astype(BF16)
     olds = [old_low] + shifted(old_low, "mp")
-    keep, left_rows, *sends = kernel_call(
+    keep, left_part, send = kernel_call(
         sum_kernel,
         "sum_x",
-        [SMEM] + [VMEM] * 3,
-        [shape((PART, B), F32), shape((ROWS, B))] + [shape((PART // 2 + half, B))] * 2,
-        [pltpu.VMEM((ROWS, B), BF16)],
-        awaited=1,
-    )(info, total, mine, theirs, olds[1])
-    near = [(z, z ^ 1) for z in range(ZH)]
-    far = [(z, ZH - 1 - z) for z in range(ZH)]
-    got = [lax.ppermute(sends[0], "zh", near), lax.ppermute(sends[1], "zh", far)]
-    lefts = [left_rows, shift(left_rows, "x", 1)]
-    keep, *sends = kernel_call(
+        [VMEM, VMEM],
+        [shape((PART, B), F32), shape((PART, B)), shape((PART + ROWS, B))],
+        awaited=2,
+    )(total, right_rows, *olds[1:3])
+
+    near_far = [
+        [
+            (z * CORE + c, ((z ^ 1) if c == step else ZH - 1 - z) * CORE + c)
+            for z in range(ZH)
+            for c in range(CORE)
+        ]
+        for step in range(2)
+    ]
+    got = lax.ppermute(send, ("zh", "core"), near_far[0])
+    keep, send = kernel_call(
         middle_kernel,
         "middle",
-        [VMEM] * 5,
-        [shape((PART, B), F32)] + [shape((PART // 2 + 2 * half, B))] * 2,
-        awaited=1,
-    )(keep, *sends, *got, lefts[1])
-    got = [lax.ppermute(sends[0], "zh", far), lax.ppermute(sends[1], "zh", near)]
-    (left_later,) = kernel_call(
-        copy_kernel, "left_rows", [VMEM], [shape((ROWS, B))], awaited=1
-    )(left_rows, got[0])
-    lefts += [shift(left_later, "x", step) for step in range(2, X)]
+        [VMEM] * 3,
+        [shape((PART, B), F32), shape((PART + 2 * ROWS, B))],
+    )(keep, right_rows, got)
+    got = lax.ppermute(send, ("zh", "core"), near_far[1])
     grad, pieces, right_part = kernel_call(
         functools.partial(pack_kernel, tokens ** -0.5),
         "pack",
-        [SMEM] + [VMEM] * 5,
+        [SMEM] + [VMEM] * 3,
         [shape((PART, B)), shape((n_mp, n_root, CORE, half, lanes)), shape((PART, B))],
-        awaited=2,
-    )(info, keep, *sends, *got, *lefts[2:])
-
+    )(info, keep, send, got)
 
     pieces = pieces.reshape((n_mp * n_root,) + pieces.shape[2:])
     blocks = lax.all_to_all(pieces, ("mp", "root"), 0, 0)
@@ -346,11 +333,10 @@
     (total,) = kernel_call(
         update_kernel,
         "update",
-        [SMEM] + [VMEM] * 6,
+        [VMEM] * 3,
         [shape((PART, B), F32)],
-        [pltpu.VMEM((PART, B), BF16)],
-        cost(2 * PART * B * (PART + B), 6 * PART * B),
-    )(info, *lefts, grad, right_part)
+        work=cost(2 * PART * B * (PART + B), 6 * PART * B),
+    )(left_part, grad, right_part)
 
     (chosen,) = kernel_call(
         choose_kernel,
@@ -358,7 +344,7 @@
         [SMEM, SMEM, VMEM, VMEM],
         [shape((X * CORE, 1 + B // lanes, half, lanes))],
         awaited=1,
-    )(info, listed, blocks, total, olds[2])
+    )(info, listed, blocks, total, olds[3])
     parts = lax.all_to_all(chosen, ("x", "core"), 0, 0)
     (mine,) = kernel_call(
         spread_kernel, "spread", [SMEM, SMEM, VMEM], [shape((n_mp * n_root, X, half, lanes))]

time: 132 us -> 116 us (0.88)
  starting transfers between devices: 67.7 us -> 49.5 us
  blocking collectives: 29.1 us -> 31.2 us
  waiting for transfers between devices: 21.3 us -> 23.1 us
    ppermute x6 -> x3, starting transfers between devices: 17.8 us -> 8.32 us  [shift(): lax.ppermute(value, axis, [(at, (at + step) % size) for at in range(size)])]
    ppermute x4 -> x2, waiting for transfers between devices: 4.41 us -> 12.8 us  [the longest x1 7.28 us: local(): got = lax.ppermute(send, ('zh', 'core'), near_far[1])]
    ppermute x4 -> x2, starting transfers between devices: 22.6 us -> 16.4 us  [the longest x1 8.81 us: local(): got = lax.ppermute(send, ('zh', 'core'), near_far[0])]
    ppermute x6 -> x3, waiting for transfers between devices: 14 us -> 8.15 us  [shift(): lax.ppermute(value, axis, [(at, (at + step) % size) for at in range(size)])]
    all_to_all x1, starting transfers between devices: 8.71 us -> 6.36 us  [local(): blocks = lax.all_to_all(pieces, ('mp', 'root'), 0, 0)]
    all_to_all x1, blocking collectives: 12.8 us -> 15.1 us  [local(): parts = lax.all_to_all(chosen, ('x', 'core'), 0, 0)]
  transfers between devices with their start and end apart: 15 -> 10, of which waited for: 10 -> 9; matrix products, arithmetic and copies ran while one was open for 0% -> 0% of each run, Pallas kernels for 2% -> 1%
where the time goes in v9:
time: 116 us
  starting transfers between devices  49.5 us (43%)
  blocking collectives  31.2 us (27%)
  waiting for transfers between devices  23.1 us (20%)
  Pallas kernels  10.8 us (9%)
    all_to_all x1, blocking collectives, local(): mine = lax.all_to_all(mine, ('mp', 'root'), 0, 0)  16.1 us
    all_to_all x1, blocking collectives, local(): parts = lax.all_to_all(chosen, ('x', 'core'), 0, 0)  15.1 us
    ppermute x1, starting transfers between devices, local(): got = lax.ppermute(send, ('zh', 'core'), near_far[0])  8.81 us
    ppermute x1, starting transfers between devices, local(): got = lax.ppermute(send, 'core', swap)  8.78 us
    ppermute x3, starting transfers between devices, shift(): lax.ppermute(value, axis, [(at, (at + step) % size) for at in range(size)])  8.32 us
    ppermute x3, waiting for transfers between devices, shift(): lax.ppermute(value, axis, [(at, (at + step) % size) for at in range(size)])  8.15 us
    ppermute x1, starting transfers between devices, local(): got = lax.ppermute(send, ('zh', 'core'), near_far[1])  7.61 us
    ppermute x1, waiting for transfers between devices, local(): got = lax.ppermute(send, ('zh', 'core'), near_far[1])  7.28 us
  transfers between devices with their start and end apart: 10, of which 9 were waited for; matrix products, arithmetic and copies ran while one was open for 0% of the time, Pallas kernels for 1%

profile of v9, /device:TPU:1, one launch (start us, length us, event | category | flops | bytes accessed | tf_op | source)
XLA Modules:
  0.0 115.6 jit_solution(7874145963457428510)
XLA Ops:
  0.6 0.0 copy-start.3
  0.6 0.0 copy-start.4
  0.7 2.3 %other_half.1 = (bf16[512,1024]{1,0:T(8,128)(2,1)S(1)}, bf16[512,512]{1,0:T(8,128)(2,1)S(1)}, bf16[1024,512]{1,0:T(8,128)(2,1)S(1)}) custom-call(s32[1]{0:T(128)} %bitcast.5.index_ref, bf16[1024,512]{1,0:T(8,128)(2,1)} %acts_ref.1, bf16[1024,1024]{1,0:T(8,128)(2,1)} %grads_ref.1), custom_call_target="tpu_custom_call" | custom-call | flops 536870912 | bytes 3145728 | tf_op jit(solution)/shard_map/other_half/pallas_call | solution.py:80
  2.9 8.8 %collective-permute-start = (bf16[512,512]{1,0:T(8,128)(2,1)S(1)}, bf16[512,512]{1,0:T(8,128)(2,1)S(1)}, u32[]{:S(2)}, u32[]{:S(2)}) collective-permute-start(bf16[512,512]{1,0:T(8,128)(2,1)S(1)} %get-tuple-element.20), channel_id=1, source_target_pairs={{0,16},{16,0},{1,17},{17,1},{2,18},{18,2},{3,19},{19,3},{4,20},{20... | collective-permute-start | bytes 1572872 | tf_op jit(solution)/shard_map/ppermute | solution.py:276
  11.7 0.0 copy-done.3
  11.7 0.0 copy-done.4
  11.8 1.9 %collective-permute-start.1 = (bf16[2,16,512]{2,1,0:T(8,128)(2,1)S(1)}, bf16[2,16,512]{2,1,0:T(8,128)(2,1)S(1)}, u32[]{:S(2)}, u32[]{:S(2)}) collective-permute-start(bf16[2,16,512]{2,1,0:T(8,128)(2,1)S(1)} %get-tuple-element.33), channel_id=1, source_target_pairs={{0,16},{16,0},{1,17},{17,1},{2,18},{18,2},{3,19},{19,3},{4,20},{20... | collective-permute-start | bytes 98312 | tf_op jit(solution)/shard_map/ppermute | solution.py:279
  13.7 0.7 own_half.1.own_ref
  14.4 0.0 copy-start
  14.4 0.5 collective-permute-done.1.theirs_ref
  14.9 0.0 collective-permute-done.got_ref
  14.9 1.1 join.1
  16.0 0.0 copy-start.1
  16.0 3.6 %all-to-all-start = ((bf16[4,160,512]{2,1,0:T(8,128)(2,1)}), bf16[4,160,512]{2,1,0:T(8,128)(2,1)S(1)}, u32[]{:S(2)}, u32[]{:S(2)}) async-start(bf16[4,160,512]{2,1,0:T(8,128)(2,1)} %get-tuple-element.21), calls=%async_computation | async-start | bytes 1310720 | tf_op jit(solution)/shard_map/all_to_all | solution.py:295
  19.6 0.0 copy-done
  19.7 1.9 %collective-permute-start.2 = (bf16[128,512]{1,0:T(8,128)(2,1)S(1)}, bf16[128,512]{1,0:T(8,128)(2,1)S(1)}, u32[]{:S(2)}, u32[]{:S(2)}) collective-permute-start(bf16[128,512]{1,0:T(8,128)(2,1)S(1)} %bitcast_convert_fusion.low_ref), channel_id=1, source_target_pairs={{0,4},{4,8},{8,12},{12,0},{1,5},{5,9},{9,13},{13,1},{2,6},{6,10},{... | collective-permute-start | bytes 393224 | tf_op jit(solution)/shard_map/ppermute | solution.py:119
  21.6 1.9 %collective-permute-start.3 = (bf16[128,512]{1,0:T(8,128)(2,1)S(1)}, bf16[128,512]{1,0:T(8,128)(2,1)S(1)}, u32[]{:S(2)}, u32[]{:S(2)}) collective-permute-start(bf16[128,512]{1,0:T(8,128)(2,1)S(1)} %bitcast_convert_fusion.low_ref), channel_id=1, source_target_pairs={{0,8},{4,12},{8,0},{12,4},{1,9},{5,13},{9,1},{13,5},{2,10},{6,14},... | collective-permute-start | bytes 393224 | tf_op jit(solution)/shard_map/ppermute | solution.py:119
  23.5 4.2 %collective-permute-done.2.refs_0_.one = bf16[128,512]{1,0:T(8,128)(2,1)S(1)} collective-permute-done((bf16[128,512]{1,0:T(8,128)(2,1)S(1)}, bf16[128,512]{1,0:T(8,128)(2,1)S(1)}, u32[]{:S(2)}, u32[]{:S(2)}) %collective-permute-start.2) | collective-permute-done | bytes 131104 | tf_op jit(solution)/shard_map/ppermute | solution.py:119
  27.7 2.3 %collective-permute-done.3.refs_1_.two = bf16[128,512]{1,0:T(8,128)(2,1)S(1)} collective-permute-done((bf16[128,512]{1,0:T(8,128)(2,1)S(1)}, bf16[128,512]{1,0:T(8,128)(2,1)S(1)}, u32[]{:S(2)}, u32[]{:S(2)}) %collective-permute-start.3) | collective-permute-done | bytes 131104 | tf_op jit(solution)/shard_map/ppermute | solution.py:119
  30.0 0.5 all-to-all-done.parts_ref
  30.5 0.1 sum_x.1
  30.5 8.8 %collective-permute-start.4 = (bf16[160,512]{1,0:T(8,128)(2,1)S(1)}, bf16[160,512]{1,0:T(8,128)(2,1)S(1)}, u32[]{:S(2)}, u32[]{:S(2)}) collective-permute-start(bf16[160,512]{1,0:T(8,128)(2,1)S(1)} %get-tuple-element.24), channel_id=1, source_target_pairs={{0,32},{16,112},{32,0},{48,80},{64,96},{80,48},{96,64},{112,16},{1... | collective-permute-start | bytes 491528 | tf_op jit(solution)/shard_map/ppermute | solution.py:315
  39.4 5.5 %collective-permute-done.4.got_ref = bf16[160,512]{1,0:T(8,128)(2,1)S(1)} collective-permute-done((bf16[160,512]{1,0:T(8,128)(2,1)S(1)}, bf16[160,512]{1,0:T(8,128)(2,1)S(1)}, u32[]{:S(2)}, u32[]{:S(2)}) %collective-permute-start.4) | collective-permute-done | bytes 163872 | tf_op jit(solution)/shard_map/ppermute | solution.py:315
  44.9 0.0 copy-start.2
  44.9 7.6 %collective-permute-start.5 = (bf16[192,512]{1,0:T(8,128)(2,1)S(1)}, bf16[192,512]{1,0:T(8,128)(2,1)S(1)}, u32[]{:S(2)}, u32[]{:S(2)}) collective-permute-start(bf16[192,512]{1,0:T(8,128)(2,1)S(1)} %get-tuple-element.26.sent_ref), channel_id=1, source_target_pairs={{0,96},{16,48},{32,64},{48,16},{64,32},{80,112},{96,0},{112,80},{1... | collective-permute-start | bytes 589832 | tf_op jit(solution)/shard_map/ppermute | solution.py:322
  52.6 0.1 stack.26.info_ref
  52.7 7.3 %collective-permute-done.5.got_ref = bf16[192,512]{1,0:T(8,128)(2,1)S(1)} collective-permute-done((bf16[192,512]{1,0:T(8,128)(2,1)S(1)}, bf16[192,512]{1,0:T(8,128)(2,1)S(1)}, u32[]{:S(2)}, u32[]{:S(2)}) %collective-permute-start.5) | collective-permute-done | bytes 196640 | tf_op jit(solution)/shard_map/ppermute | solution.py:322
  59.9 1.2 %pack.1 = (bf16[128,512]{1,0:T(8,128)(2,1)S(1)}, bf16[4,4,2,16,128]{4,3,2,1,0:T(8,128)(2,1)}, bf16[128,512]{1,0:T(8,128)(2,1)S(1)}) custom-call(s32[5]{0:T(128)S(1)} %stack.26.info_ref, f32[128,512]{1,0:T(8,128)S(1)} %get-tuple-element.25.keep_ref, bf16[192,512]{1,0:T(8,128)(2,1)S(1)} %get-tuple-element.26.sent_ref, ...), custom_call_target="tpu_custom_call" | custom-call | tf_op jit(solution)/shard_map/pack/pallas_call | solution.py:323
  61.2 6.4 %all-to-all-start.1 = ((bf16[16,2,16,128]{3,2,1,0:T(8,128)(2,1)}), bf16[16,2,16,128]{3,2,1,0:T(8,128)(2,1)S(1)}, u32[]{:S(2)}, u32[]{:S(2)}) async-start(bf16[16,2,16,128]{3,2,1,0:T(8,128)(2,1)} %bitcast.9), calls=%async_computation.1 | async-start | bytes 262144 | tf_op jit(solution)/shard_map/all_to_all | solution.py:331
  67.5 4.5 %collective-permute-start.6 = (bf16[128,512]{1,0:T(8,128)(2,1)S(1)}, bf16[128,512]{1,0:T(8,128)(2,1)S(1)}, u32[]{:S(2)}, u32[]{:S(2)}) collective-permute-start(bf16[128,512]{1,0:T(8,128)(2,1)S(1)} %bitcast_convert_fusion.low_ref), channel_id=1, source_target_pairs={{0,12},{4,0},{8,4},{12,8},{1,13},{5,1},{9,5},{13,9},{2,14},{6,2},{... | collective-permute-start | bytes 393224 | tf_op jit(solution)/shard_map/ppermute | solution.py:119
  72.0 0.4 update.1.total_ref
  72.4 1.7 %collective-permute-done.6.refs_0_.three = bf16[128,512]{1,0:T(8,128)(2,1)S(1)} collective-permute-done((bf16[128,512]{1,0:T(8,128)(2,1)S(1)}, bf16[128,512]{1,0:T(8,128)(2,1)S(1)}, u32[]{:S(2)}, u32[]{:S(2)}) %collective-permute-start.6) | collective-permute-done | bytes 131104 | tf_op jit(solution)/shard_map/ppermute | solution.py:119
  74.1 0.7 all-to-all-done.1.blocks_ref
  74.8 0.0 copy-done.1
  74.8 0.6 choose.1
  75.4 15.1 %all_to_all.20.parts_ref = bf16[8,5,16,128]{3,2,1,0:T(8,128)(2,1)S(1)} all-to-all(bf16[8,5,16,128]{3,2,1,0:T(8,128)(2,1)S(1)} %choose.1), channel_id=1, replica_groups=mesh['x'=4,'zh'=4,'core'=2,'mp'=4,'root'=4] {'x','core'}, dimensions={0} | all-to-all | bytes 327680 | tf_op jit(solution)/shard_map/all_to_all | solution.py:348
  90.5 0.6 spread.1
  91.1 16.1 %all_to_all.21 = bf16[16,4,16,128]{3,2,1,0:T(8,128)(2,1)S(1)} all-to-all(bf16[16,4,16,128]{3,2,1,0:T(8,128)(2,1)S(1)} %spread.1), channel_id=1, replica_groups=mesh['x'=4,'zh'=4,'core'=2,'mp'=4,'root'=4] {'mp','root'}, dimensions={0} | all-to-all | bytes 524288 | tf_op jit(solution)/shard_map/all_to_all | solution.py:352
  107.2 4.1 %collective-permute-start.7 = (bf16[16,4,16,128]{3,2,1,0:T(8,128)(2,1)S(1)}, bf16[16,4,16,128]{3,2,1,0:T(8,128)(2,1)S(1)}, u32[]{:S(2)}, u32[]{:S(2)}) collective-permute-start(bf16[16,4,16,128]{3,2,1,0:T(8,128)(2,1)S(1)} %all_to_all.21), channel_id=1, source_target_pairs={{0,16},{16,0},{1,17},{17,1},{2,18},{18,2},{3,19},{19,3},{4,20},{20... | collective-permute-start | bytes 786440 | tf_op jit(solution)/shard_map/ppermute | solution.py:353
  111.3 0.6 finish.1
  111.9 0.5 collective-permute-done.7
  112.4 0.0 copy-done.2
  112.4 3.2 %refresh.1 = (f32[128,512]{1,0:T(8,128)}, f32[128,512]{1,0:T(8,128)}) custom-call(s32[5]{0:T(128)S(1)} %stack.26.info_ref, s32[16]{0:T(128)S(1)} %copy-done.2, bf16[4,4,4,16,128]{4,3,2,1,0:T(8,128)(2,1)S(1)} %bitcast.19, bf16[4,4,4,16,128]{4,3,2,1,0:T(8,128)(2,1)S(1)} %bitcast.20, f32[128,512]{1,0:T(8,128)S(1)} %bitcast.18, ...), custom_call_target="tpu_custom_call" | custom-call | flops 603979776 | bytes 1048576 | tf_op jit(solution)/shard_map/refresh/pallas_call | solution.py:357
  (5 shorter events, 0.1 us)
Async XLA Ops:
  0.6 11.1 %copy-start.3 = (bf16[1,2,16,512]{3,2,1,0:T(8,128)(2,1)S(1)}, bf16[1,2,16,512]{3,2,1,0:T(8,128)(2,1)}, u32[]{:S(2)}) copy-start(bf16[1,2,16,512]{3,2,1,0:T(8,128)(2,1)} %param.9) | copy-start | bytes 98308
  0.6 11.1 %copy-start.4 = (bf16[1,2,16,512]{3,2,1,0:T(8,128)(2,1)S(1)}, bf16[1,2,16,512]{3,2,1,0:T(8,128)(2,1)}, u32[]{:S(2)}) copy-start(bf16[1,2,16,512]{3,2,1,0:T(8,128)(2,1)} %param.10) | copy-start | bytes 98308
  2.9 12.0 %collective-permute-start = (bf16[512,512]{1,0:T(8,128)(2,1)S(1)}, bf16[512,512]{1,0:T(8,128)(2,1)S(1)}, u32[]{:S(2)}, u32[]{:S(2)}) collective-permute-start(bf16[512,512]{1,0:T(8,128)(2,1)S(1)} %get-tuple-element.20), channel_id=1, source_target_pairs={{0,16},{16,0},{1,17},{17,1},{2,18},{18,2},{3,19},{19,3},{4,20},{20... | collective-permute-start | bytes 1572872 | tf_op jit(solution)/shard_map/ppermute | solution.py:276
  11.8 3.1 %collective-permute-start.1 = (bf16[2,16,512]{2,1,0:T(8,128)(2,1)S(1)}, bf16[2,16,512]{2,1,0:T(8,128)(2,1)S(1)}, u32[]{:S(2)}, u32[]{:S(2)}) collective-permute-start(bf16[2,16,512]{2,1,0:T(8,128)(2,1)S(1)} %get-tuple-element.33), channel_id=1, source_target_pairs={{0,16},{16,0},{1,17},{17,1},{2,18},{18,2},{3,19},{19,3},{4,20},{20... | collective-permute-start | bytes 98312 | tf_op jit(solution)/shard_map/ppermute | solution.py:279
  14.4 5.2 %copy-start = (f32[1,128,512]{2,1,0:T(8,128)S(1)}, f32[1,128,512]{2,1,0:T(8,128)}, u32[]{:S(2)}) copy-start(f32[1,128,512]{2,1,0:T(8,128)} %param.11) | copy-start | bytes 786436
  16.0 58.8 %copy-start.1 = (s32[16]{0:T(128)S(1)}, s32[16]{0:T(128)}, u32[]{:S(2)}) copy-start(s32[16]{0:T(128)} %listed_ref.3) | copy-start | bytes 196
  16.0 14.5 %all-to-all-start = ((bf16[4,160,512]{2,1,0:T(8,128)(2,1)}), bf16[4,160,512]{2,1,0:T(8,128)(2,1)S(1)}, u32[]{:S(2)}, u32[]{:S(2)}) async-start(bf16[4,160,512]{2,1,0:T(8,128)(2,1)} %get-tuple-element.21), calls=%async_computation | async-start | bytes 1310720 | tf_op jit(solution)/shard_map/all_to_all | solution.py:295
  19.7 8.1 %collective-permute-start.2 = (bf16[128,512]{1,0:T(8,128)(2,1)S(1)}, bf16[128,512]{1,0:T(8,128)(2,1)S(1)}, u32[]{:S(2)}, u32[]{:S(2)}) collective-permute-start(bf16[128,512]{1,0:T(8,128)(2,1)S(1)} %bitcast_convert_fusion.low_ref), channel_id=1, source_target_pairs={{0,4},{4,8},{8,12},{12,0},{1,5},{5,9},{9,13},{13,1},{2,6},{6,10},{... | collective-permute-start | bytes 393224 | tf_op jit(solution)/shard_map/ppermute | solution.py:119
  21.6 8.4 %collective-permute-start.3 = (bf16[128,512]{1,0:T(8,128)(2,1)S(1)}, bf16[128,512]{1,0:T(8,128)(2,1)S(1)}, u32[]{:S(2)}, u32[]{:S(2)}) collective-permute-start(bf16[128,512]{1,0:T(8,128)(2,1)S(1)} %bitcast_convert_fusion.low_ref), channel_id=1, source_target_pairs={{0,8},{4,12},{8,0},{12,4},{1,9},{5,13},{9,1},{13,5},{2,10},{6,14},... | collective-permute-start | bytes 393224 | tf_op jit(solution)/shard_map/ppermute | solution.py:119
  30.5 14.4 %collective-permute-start.4 = (bf16[160,512]{1,0:T(8,128)(2,1)S(1)}, bf16[160,512]{1,0:T(8,128)(2,1)S(1)}, u32[]{:S(2)}, u32[]{:S(2)}) collective-permute-start(bf16[160,512]{1,0:T(8,128)(2,1)S(1)} %get-tuple-element.24), channel_id=1, source_target_pairs={{0,32},{16,112},{32,0},{48,80},{64,96},{80,48},{96,64},{112,16},{1... | collective-permute-start | bytes 491528 | tf_op jit(solution)/shard_map/ppermute | solution.py:315
  44.9 67.5 %copy-start.2 = (s32[16]{0:T(128)S(1)}, s32[16]{0:T(128)}, u32[]{:S(2)}) copy-start(s32[16]{0:T(128)} %owner_ref.1) | copy-start | bytes 196
  44.9 15.0 %collective-permute-start.5 = (bf16[192,512]{1,0:T(8,128)(2,1)S(1)}, bf16[192,512]{1,0:T(8,128)(2,1)S(1)}, u32[]{:S(2)}, u32[]{:S(2)}) collective-permute-start(bf16[192,512]{1,0:T(8,128)(2,1)S(1)} %get-tuple-element.26.sent_ref), channel_id=1, source_target_pairs={{0,96},{16,48},{32,64},{48,16},{64,32},{80,112},{96,0},{112,80},{1... | collective-permute-start | bytes 589832 | tf_op jit(solution)/shard_map/ppermute | solution.py:322
  61.2 13.6 %all-to-all-start.1 = ((bf16[16,2,16,128]{3,2,1,0:T(8,128)(2,1)}), bf16[16,2,16,128]{3,2,1,0:T(8,128)(2,1)S(1)}, u32[]{:S(2)}, u32[]{:S(2)}) async-start(bf16[16,2,16,128]{3,2,1,0:T(8,128)(2,1)} %bitcast.9), calls=%async_computation.1 | async-start | bytes 262144 | tf_op jit(solution)/shard_map/all_to_all | solution.py:331
  67.5 6.5 %collective-permute-start.6 = (bf16[128,512]{1,0:T(8,128)(2,1)S(1)}, bf16[128,512]{1,0:T(8,128)(2,1)S(1)}, u32[]{:S(2)}, u32[]{:S(2)}) collective-permute-start(bf16[128,512]{1,0:T(8,128)(2,1)S(1)} %bitcast_convert_fusion.low_ref), channel_id=1, source_target_pairs={{0,12},{4,0},{8,4},{12,8},{1,13},{5,1},{9,5},{13,9},{2,14},{6,2},{... | collective-permute-start | bytes 393224 | tf_op jit(solution)/shard_map/ppermute | solution.py:119
  107.2 5.2 %collective-permute-start.7 = (bf16[16,4,16,128]{3,2,1,0:T(8,128)(2,1)S(1)}, bf16[16,4,16,128]{3,2,1,0:T(8,128)(2,1)S(1)}, u32[]{:S(2)}, u32[]{:S(2)}) collective-permute-start(bf16[16,4,16,128]{3,2,1,0:T(8,128)(2,1)S(1)} %all_to_all.21), channel_id=1, source_target_pairs={{0,16},{16,0},{1,17},{17,1},{2,18},{18,2},{3,19},{19,3},{4,20},{20... | collective-permute-start | bytes 786440 | tf_op jit(solution)/shard_map/ppermute | solution.py:353

commit v10 on v9

--- a/solution.py
+++ b/solution.py
@@ -98,20 +98,13 @@
     out_ref[...] = dot(turned_ref[...], grads_ref[...])
 
 
-def join_kernel(index_ref, own_ref, got_ref, mine_ref, theirs_ref, out_ref, right_ref):
-    core = index_ref[0]
-    rows = mine_ref.shape[1]
+def join_kernel(own_ref, got_ref, prec_ref, out_ref):
     total = (own_ref[...] + got_ref[...].astype(F32)).astype(BF16).T
-    mine = pl.ds(pl.multiple_of(core * rows, rows), rows)
-    theirs = pl.ds(pl.multiple_of((1 - core) * rows, rows), rows)
-    right_ref[mine, :] = mine_ref[1]
-    right_ref[theirs, :] = theirs_ref[1]
-    mine = pl.ds(pl.multiple_of(PART + core * rows, rows), rows)
-    theirs = pl.ds(pl.multiple_of(PART + (1 - core) * rows, rows), rows)
+    rows = prec_ref.shape[2]
     for w in range(X):
         out_ref[w, :PART] = total[w * PART : (w + 1) * PART]
-        out_ref[w, mine, :] = mine_ref[0]
-        out_ref[w, theirs, :] = theirs_ref[0]
+        for c in range(CORE):
+            out_ref[w, PART + c * rows : PART + (c + 1) * rows] = prec_ref[0, c]
 
 
 def shift(value, axis, step):
@@ -130,27 +123,37 @@
         out_ref[pl.ds(pl.multiple_of(at, rows), rows), :] = part[...]
 
 
-def sum_kernel(parts_ref, right_ref, *refs):
-    keep_ref, left_ref, send_ref = refs[-3:]
+def sum_kernel(info_ref, parts_ref, mine_ref, theirs_ref, old_ref, *refs):
+    keep_ref, right_ref, left_ref, left_send, old_low, send_ref = refs
+    core = info_ref[0]
+    rows = mine_ref.shape[0]
+    right_ref[pl.ds(pl.multiple_of(core * rows, rows), rows), :] = mine_ref[...]
+    right_ref[pl.ds(pl.multiple_of((1 - core) * rows, rows), rows), :] = theirs_ref[...]
     total = parts_ref[0, :PART].astype(F32)
     for w in range(X):
-        left_ref[w * ROWS : (w + 1) * ROWS] = parts_ref[w, PART:]
+        for ref, c in ((left_ref, core), (left_send, 1 - core)):
+            at = pl.multiple_of(PART + c * rows, rows)
+            ref[w * rows : (w + 1) * rows] = parts_ref[w, pl.ds(at, rows), :]
         if w:
             total = total + parts_ref[w, :PART].astype(F32)
     keep_ref[...] = total
     send_ref[:PART] = total.astype(BF16)
     send_ref[PART:] = right_ref[...]
-
-
-def middle_kernel(keep_ref, right_ref, got_ref, out_ref, send_ref):
+    old_low[...] = old_ref[...].astype(BF16)
+
+
+def middle_kernel(keep_ref, right_ref, got_ref, old_ref, *refs):
+    out_ref, send_ref, old_low = refs[-3:]
     total = keep_ref[...] + got_ref[:PART].astype(F32)
     out_ref[...] = total
     send_ref[:PART] = total.astype(BF16)
     send_ref[PART : PART + ROWS] = right_ref[...]
     send_ref[PART + ROWS :] = got_ref[PART:]
-
-
-def pack_kernel(scale, info_ref, keep_ref, sent_ref, got_ref, grad_ref, pieces_ref, right_ref):
+    old_low[...] = old_ref[...].astype(BF16)
+
+
+def pack_kernel(scale, info_ref, keep_ref, sent_ref, got_ref, *refs):
+    grad_ref, pieces_ref, right_ref = refs[-3:]
     core, zh = info_ref[0], info_ref[2]
     grad = ((keep_ref[...] + got_ref[:PART].astype(F32)) * scale).astype(BF16)
     grad_ref[...] = grad
@@ -204,8 +207,13 @@
             out_ref[:, at : at + lanes] = total.astype(BF16)
 
 
-def update_kernel(left_ref, grad_ref, right_ref, out_ref):
-    product = dot(left_ref[...], grad_ref[...], 1, 1).astype(BF16)
+def update_kernel(info_ref, mine_ref, theirs_ref, grad_ref, right_ref, out_ref, left):
+    rows = ROWS // CORE
+    for ref, c in ((mine_ref, info_ref[0]), (theirs_ref, 1 - info_ref[0])):
+        for w in range(X):
+            at = pl.multiple_of(w * ROWS + c * rows, rows)
+            left[pl.ds(at, rows), :] = ref[w * rows : (w + 1) * rows]
+    product = dot(left[...], grad_ref[...], 1, 1).astype(BF16)
     out_ref[...] = dot(product, right_ref[...])
 
 
@@ -274,11 +282,6 @@
 
     turned, send, grads_own = other_half(acts, grads_out, 1 - core)
     got = lax.ppermute(send, "core", swap)
-    prec = jnp.stack([prec_left[0], prec_right[0]])
-    mine = lax.dynamic_index_in_dim(prec, core, 1, keepdims=False)
-    theirs = lax.ppermute(
-        lax.dynamic_index_in_dim(prec, 1 - core, 1, keepdims=False), "core", swap
-    )
     (own,) = kernel_call(
         own_kernel,
         "own_half",
@@ -286,23 +289,23 @@
         [shape((B, B), F32)],
         work=cost(2 * acts.shape[0] * B * B, 4 * acts.shape[0] * B),
     )(turned, grads_own)
-    total, right_rows = kernel_call(
-        join_kernel,
-        "join",
-        [SMEM] + [VMEM] * 4,
-        [shape((X, PART + ROWS, B)), shape((ROWS, B))],
-    )(core.reshape(1), own, got, mine, theirs)
+    (total,) = kernel_call(
+        join_kernel, "join", [VMEM] * 3, [shape((X, PART + ROWS, B))]
+    )(own, got, prec_left)
     total = lax.all_to_all(total, "x", 0, 0)
+    mine = lax.dynamic_index_in_dim(prec_right[0], core, 0, keepdims=False)
+    theirs = lax.ppermute(
+        lax.dynamic_index_in_dim(prec_right[0], 1 - core, 0, keepdims=False), "core", swap
+    )
     old_own = stats_old[0]
-    old_low = old_own.astype(BF16)
-    olds = [old_low] + shifted(old_low, "mp")
-    keep, left_part, send = kernel_call(
+    keep, right_rows, left_mine, left_send, old_low, send = kernel_call(
         sum_kernel,
         "sum_x",
-        [VMEM, VMEM],
-        [shape((PART, B), F32), shape((PART, B)), shape((PART + ROWS, B))],
-        awaited=2,
-    )(total, right_rows, *olds[1:3])
+        [SMEM] + [VMEM] * 4,
+        [shape((PART, B), F32), shape((ROWS, B))]
+        + [shape((PART // CORE, B))] * 2
+        + [shape((quarter, B)), shape((PART + ROWS, B))],
+    )(info, total, mine, theirs, old_own)
 
     near_far = [
         [
@@ -313,19 +316,24 @@
         for step in range(2)
     ]
     got = lax.ppermute(send, ("zh", "core"), near_far[0])
-    keep, send = kernel_call(
+    left_theirs = lax.ppermute(left_send, "core", swap)
+    olds = [old_low, shift(old_low, "mp", 1)]
+    keep, send, old_later = kernel_call(
         middle_kernel,
         "middle",
-        [VMEM] * 3,
-        [shape((PART, B), F32), shape((PART + 2 * ROWS, B))],
-    )(keep, right_rows, got)
+        [VMEM] * 4,
+        [shape((PART, B), F32), shape((PART + 2 * ROWS, B)), shape((quarter, B))],
+        awaited=2,
+    )(keep, right_rows, got, old_own, left_theirs, olds[1])
     got = lax.ppermute(send, ("zh", "core"), near_far[1])
+    olds += [shift(old_later, "mp", step) for step in range(2, n_mp)]
     grad, pieces, right_part = kernel_call(
         functools.partial(pack_kernel, tokens ** -0.5),
         "pack",
         [SMEM] + [VMEM] * 3,
         [shape((PART, B)), shape((n_mp, n_root, CORE, half, lanes)), shape((PART, B))],
-    )(info, keep, send, got)
+        awaited=2,
+    )(info, keep, send, got, *olds[2:])
 
     pieces = pieces.reshape((n_mp * n_root,) + pieces.shape[2:])
     blocks = lax.all_to_all(pieces, ("mp", "root"), 0, 0)
@@ -333,18 +341,18 @@
     (total,) = kernel_call(
         update_kernel,
         "update",
-        [VMEM] * 3,
+        [SMEM] + [VMEM] * 4,
         [shape((PART, B), F32)],
-        work=cost(2 * PART * B * (PART + B), 6 * PART * B),
-    )(left_part, grad, right_part)
+        [pltpu.VMEM((PART, B), BF16)],
+        cost(2 * PART * B * (PART + B), 6 * PART * B),
+    )(info, left_mine, left_theirs, grad, right_part)
 
     (chosen,) = kernel_call(
         choose_kernel,
         "choose",
         [SMEM, SMEM, VMEM, VMEM],
         [shape((X * CORE, 1 + B // lanes, half, lanes))],
-        awaited=1,
-    )(info, listed, blocks, total, olds[3])
+    )(info, listed, blocks, total)
     parts = lax.all_to_all(chosen, ("x", "core"), 0, 0)
     (mine,) = kernel_call(
         spread_kernel, "spread", [SMEM, SMEM, VMEM], [shape((n_mp * n_root, X, half, lanes))]

time: 116 us -> 112 us (0.966)
  blocking collectives: 31.2 us -> 28.1 us
  waiting for transfers between devices: 23.1 us -> 21.7 us
    ppermute x1, waiting for transfers between devices: 7.28 us -> 0.01 us  [local(): got = lax.ppermute(send, ('zh', 'core'), near_far[1])]
    all_to_all x1, waiting for transfers between devices: 0.48 us -> 7.45 us  [local(): total = lax.all_to_all(total, 'x', 0, 0)]
    all_to_all x1, waiting for transfers between devices: 0.71 us -> 6.34 us  [local(): blocks = lax.all_to_all(pieces, ('mp', 'root'), 0, 0)]
    ppermute x1, waiting for transfers between devices: 5.54 us -> 0.01 us  [local(): got = lax.ppermute(send, ('zh', 'core'), near_far[0])]
    all_to_all x1, blocking collectives: 16.1 us -> 12.3 us  [local(): mine = lax.all_to_all(mine, ('mp', 'root'), 0, 0)]
    ppermute x3, waiting for transfers between devices: 8.15 us -> 4.66 us  [shift(): lax.ppermute(value, axis, [(at, (at + step) % size) for at in range(size)])]
    all_to_all x1, starting transfers between devices: 6.36 us -> 3.77 us  [local(): blocks = lax.all_to_all(pieces, ('mp', 'root'), 0, 0)]
    ppermute x3, starting transfers between devices: 8.32 us -> 10.7 us  [shift(): lax.ppermute(value, axis, [(at, (at + step) % size) for at in range(size)])]
  transfers between devices with their start and end apart: 10 -> 11, of which waited for: 9 -> 8; matrix products, arithmetic and copies ran while one was open for 0% -> 0% of each run, Pallas kernels for 1% -> 2%
where the time goes in v10:
time: 112 us; the launch traced here: 111 us
  starting transfers between devices  48.5 us (43%)
  blocking collectives  28.1 us (25%)
  waiting for transfers between devices  21.7 us (19%)
  Pallas kernels  11.9 us (11%)
    all_to_all x1, blocking collectives, local(): parts = lax.all_to_all(chosen, ('x', 'core'), 0, 0)  15.8 us
    all_to_all x1, blocking collectives, local(): mine = lax.all_to_all(mine, ('mp', 'root'), 0, 0)  12.3 us
    ppermute x3, starting transfers between devices, shift(): lax.ppermute(value, axis, [(at, (at + step) % size) for at in range(size)])  10.7 us
    ppermute x1, starting transfers between devices, local(): got = lax.ppermute(send, 'core', swap)  8.79 us
    all_to_all x1, waiting for transfers between devices, local(): total = lax.all_to_all(total, 'x', 0, 0)  7.45 us
    ppermute x1, starting transfers between devices, local(): got = lax.ppermute(send, ('zh', 'core'), near_far[0])  7.32 us
    all_to_all x1, waiting for transfers between devices, local(): blocks = lax.all_to_all(pieces, ('mp', 'root'), 0, 0)  6.34 us
    ppermute x1, starting transfers between devices, local(): got = lax.ppermute(send, ('zh', 'core'), near_far[1])  6.15 us
  transfers between devices with their start and end apart: 11, of which 8 were waited for; matrix products, arithmetic and copies ran while one was open for 0% of the time, Pallas kernels for 2%

profile of v10, /device:TPU:1, one launch (start us, length us, event | category | flops | bytes accessed | tf_op | source)
XLA Modules:
  0.0 111.1 jit_solution(11230139324884200378)
XLA Ops:
  0.6 2.3 %other_half.1 = (bf16[512,1024]{1,0:T(8,128)(2,1)S(1)}, bf16[512,512]{1,0:T(8,128)(2,1)S(1)}, bf16[1024,512]{1,0:T(8,128)(2,1)S(1)}) custom-call(s32[1]{0:T(128)} %bitcast.5.index_ref, bf16[1024,512]{1,0:T(8,128)(2,1)} %acts_ref.1, bf16[1024,1024]{1,0:T(8,128)(2,1)} %grads_ref.1), custom_call_target="tpu_custom_call" | custom-call | flops 536870912 | bytes 3145728 | tf_op jit(solution)/shard_map/other_half/pallas_call | solution.py:80
  2.9 0.0 copy-start.1
  2.9 8.8 %collective-permute-start = (bf16[512,512]{1,0:T(8,128)(2,1)S(1)}, bf16[512,512]{1,0:T(8,128)(2,1)S(1)}, u32[]{:S(2)}, u32[]{:S(2)}) collective-permute-start(bf16[512,512]{1,0:T(8,128)(2,1)S(1)} %get-tuple-element.22), channel_id=1, source_target_pairs={{0,16},{16,0},{1,17},{17,1},{2,18},{18,2},{3,19},{19,3},{4,20},{20... | collective-permute-start | bytes 1572872 | tf_op jit(solution)/shard_map/ppermute | solution.py:284
  11.7 0.7 own_half.1.own_ref
  12.4 0.0 copy-start.4
  12.4 0.0 copy-start
  12.5 0.8 collective-permute-done.got_ref
  13.2 0.0 copy-done.1
  13.2 1.1 join.1
  14.3 3.5 %all-to-all-start = ((bf16[4,160,512]{2,1,0:T(8,128)(2,1)}), bf16[4,160,512]{2,1,0:T(8,128)(2,1)S(1)}, u32[]{:S(2)}, u32[]{:S(2)}) async-start(bf16[4,160,512]{2,1,0:T(8,128)(2,1)} %join.1), calls=%async_computation | async-start | bytes 1310720 | tf_op jit(solution)/shard_map/all_to_all | solution.py:295
  17.8 0.0 copy-start.2
  17.8 0.0 copy-done.4
  17.9 2.3 %collective-permute-start.1 = (bf16[16,512]{1,0:T(8,128)(2,1)S(1)}, bf16[16,512]{1,0:T(8,128)(2,1)S(1)}, u32[]{:S(2)}, u32[]{:S(2)}) collective-permute-start(bf16[16,512]{1,0:T(8,128)(2,1)S(1)} %get-tuple-element.37), channel_id=1, source_target_pairs={{0,16},{16,0},{1,17},{17,1},{2,18},{18,2},{3,19},{19,3},{4,20},{20... | collective-permute-start | bytes 49160 | tf_op jit(solution)/shard_map/ppermute | solution.py:297
  20.1 0.1 stack.23.info_ref
  20.2 0.7 collective-permute-done.1.theirs_ref
  21.0 7.4 %all-to-all-done.parts_ref = bf16[4,160,512]{2,1,0:T(8,128)(2,1)S(1)} async-done(((bf16[4,160,512]{2,1,0:T(8,128)(2,1)}), bf16[4,160,512]{2,1,0:T(8,128)(2,1)S(1)}, u32[]{:S(2)}, u32[]{:S(2)}) %all-to-all-start) | async-done | bytes 655392 | tf_op jit(solution)/shard_map/all_to_all | solution.py:295
  28.4 0.0 copy-done
  28.4 0.7 sum_x.1
  29.1 7.3 %collective-permute-start.2 = (bf16[160,512]{1,0:T(8,128)(2,1)S(1)}, bf16[160,512]{1,0:T(8,128)(2,1)S(1)}, u32[]{:S(2)}, u32[]{:S(2)}) collective-permute-start(bf16[160,512]{1,0:T(8,128)(2,1)S(1)} %get-tuple-element.25), channel_id=1, source_target_pairs={{0,32},{16,112},{32,0},{48,80},{64,96},{80,48},{96,64},{112,16},{1... | collective-permute-start | bytes 491528 | tf_op jit(solution)/shard_map/ppermute | solution.py:318
  36.4 3.2 %collective-permute-start.4 = (bf16[128,512]{1,0:T(8,128)(2,1)S(1)}, bf16[128,512]{1,0:T(8,128)(2,1)S(1)}, u32[]{:S(2)}, u32[]{:S(2)}) collective-permute-start(bf16[128,512]{1,0:T(8,128)(2,1)S(1)} %get-tuple-element.27.low_ref), channel_id=1, source_target_pairs={{0,4},{4,8},{8,12},{12,0},{1,5},{5,9},{9,13},{13,1},{2,6},{6,10},{... | collective-permute-start | bytes 393224 | tf_op jit(solution)/shard_map/ppermute | solution.py:112
  39.6 1.9 %collective-permute-start.3 = (bf16[64,512]{1,0:T(8,128)(2,1)S(1)}, bf16[64,512]{1,0:T(8,128)(2,1)S(1)}, u32[]{:S(2)}, u32[]{:S(2)}) collective-permute-start(bf16[64,512]{1,0:T(8,128)(2,1)S(1)} %get-tuple-element.26), channel_id=1, source_target_pairs={{0,16},{16,0},{1,17},{17,1},{2,18},{18,2},{3,19},{19,3},{4,20},{20... | collective-permute-start | bytes 196616 | tf_op jit(solution)/shard_map/ppermute | solution.py:319
  41.5 1.2 %collective-permute-done.3.refs_0_.theirs_ref = bf16[64,512]{1,0:T(8,128)(2,1)S(1)} collective-permute-done((bf16[64,512]{1,0:T(8,128)(2,1)S(1)}, bf16[64,512]{1,0:T(8,128)(2,1)S(1)}, u32[]{:S(2)}, u32[]{:S(2)}) %collective-permute-start.3) | collective-permute-done | bytes 65568 | tf_op jit(solution)/shard_map/ppermute | solution.py:319
  42.7 0.6 collective-permute-done.4.refs_1_.one
  43.4 0.0 collective-permute-done.2.got_ref
  43.4 0.0 copy-start.3
  43.4 6.1 %collective-permute-start.5 = (bf16[192,512]{1,0:T(8,128)(2,1)S(1)}, bf16[192,512]{1,0:T(8,128)(2,1)S(1)}, u32[]{:S(2)}, u32[]{:S(2)}) collective-permute-start(bf16[192,512]{1,0:T(8,128)(2,1)S(1)} %get-tuple-element.29.sent_ref), channel_id=1, source_target_pairs={{0,96},{16,48},{32,64},{48,16},{64,32},{80,112},{96,0},{112,80},{1... | collective-permute-start | bytes 589832 | tf_op jit(solution)/shard_map/ppermute | solution.py:328
  49.6 4.8 %collective-permute-start.6 = (bf16[128,512]{1,0:T(8,128)(2,1)S(1)}, bf16[128,512]{1,0:T(8,128)(2,1)S(1)}, u32[]{:S(2)}, u32[]{:S(2)}) collective-permute-start(bf16[128,512]{1,0:T(8,128)(2,1)S(1)} %get-tuple-element.30), channel_id=1, source_target_pairs={{0,8},{4,12},{8,0},{12,4},{1,9},{5,13},{9,1},{13,5},{2,10},{6,14},... | collective-permute-start | bytes 393224 | tf_op jit(solution)/shard_map/ppermute | solution.py:112
  54.4 2.7 %collective-permute-start.7 = (bf16[128,512]{1,0:T(8,128)(2,1)S(1)}, bf16[128,512]{1,0:T(8,128)(2,1)S(1)}, u32[]{:S(2)}, u32[]{:S(2)}) collective-permute-start(bf16[128,512]{1,0:T(8,128)(2,1)S(1)} %get-tuple-element.30), channel_id=1, source_target_pairs={{0,12},{4,0},{8,4},{12,8},{1,13},{5,1},{9,5},{13,9},{2,14},{6,2},{... | collective-permute-start | bytes 393224 | tf_op jit(solution)/shard_map/ppermute | solution.py:112
  57.1 0.0 collective-permute-done.6.refs_0_.two
  57.1 4.0 %collective-permute-done.7.refs_1_.three = bf16[128,512]{1,0:T(8,128)(2,1)S(1)} collective-permute-done((bf16[128,512]{1,0:T(8,128)(2,1)S(1)}, bf16[128,512]{1,0:T(8,128)(2,1)S(1)}, u32[]{:S(2)}, u32[]{:S(2)}) %collective-permute-start.7) | collective-permute-done | bytes 131104 | tf_op jit(solution)/shard_map/ppermute | solution.py:112
  61.2 0.0 collective-permute-done.5.got_ref
  61.2 1.2 %pack.1 = (bf16[128,512]{1,0:T(8,128)(2,1)S(1)}, bf16[4,4,2,16,128]{4,3,2,1,0:T(8,128)(2,1)}, bf16[128,512]{1,0:T(8,128)(2,1)S(1)}) custom-call(s32[5]{0:T(128)S(1)} %stack.23.info_ref, f32[128,512]{1,0:T(8,128)S(1)} %get-tuple-element.28.keep_ref, bf16[192,512]{1,0:T(8,128)(2,1)S(1)} %get-tuple-element.29.sent_ref, ...), custom_call_target="tpu_custom_call" | custom-call | tf_op jit(solution)/shard_map/pack/pallas_call | solution.py:330
  62.4 3.8 %all-to-all-start.1 = ((bf16[16,2,16,128]{3,2,1,0:T(8,128)(2,1)}), bf16[16,2,16,128]{3,2,1,0:T(8,128)(2,1)S(1)}, u32[]{:S(2)}, u32[]{:S(2)}) async-start(bf16[16,2,16,128]{3,2,1,0:T(8,128)(2,1)} %bitcast.9), calls=%async_computation.1 | async-start | bytes 262144 | tf_op jit(solution)/shard_map/all_to_all | solution.py:339
  66.2 0.9 update.1.total_ref
  67.1 6.3 %all-to-all-done.1.blocks_ref = bf16[16,2,16,128]{3,2,1,0:T(8,128)(2,1)S(1)} async-done(((bf16[16,2,16,128]{3,2,1,0:T(8,128)(2,1)}), bf16[16,2,16,128]{3,2,1,0:T(8,128)(2,1)S(1)}, u32[]{:S(2)}, u32[]{:S(2)}) %all-to-all-start.1) | async-done | bytes 131104 | tf_op jit(solution)/shard_map/all_to_all | solution.py:339
  73.4 0.0 copy-done.2
  73.4 0.6 choose.1
  74.0 15.8 %all_to_all.20.parts_ref = bf16[8,5,16,128]{3,2,1,0:T(8,128)(2,1)S(1)} all-to-all(bf16[8,5,16,128]{3,2,1,0:T(8,128)(2,1)S(1)} %choose.1), channel_id=1, replica_groups=mesh['x'=4,'zh'=4,'core'=2,'mp'=4,'root'=4] {'x','core'}, dimensions={0} | all-to-all | bytes 327680 | tf_op jit(solution)/shard_map/all_to_all | solution.py:356
  89.8 0.6 spread.1
  90.4 12.3 %all_to_all.21 = bf16[16,4,16,128]{3,2,1,0:T(8,128)(2,1)S(1)} all-to-all(bf16[16,4,16,128]{3,2,1,0:T(8,128)(2,1)S(1)} %spread.1), channel_id=1, replica_groups=mesh['x'=4,'zh'=4,'core'=2,'mp'=4,'root'=4] {'mp','root'}, dimensions={0} | all-to-all | bytes 524288 | tf_op jit(solution)/shard_map/all_to_all | solution.py:360
  102.7 4.1 %collective-permute-start.8 = (bf16[16,4,16,128]{3,2,1,0:T(8,128)(2,1)S(1)}, bf16[16,4,16,128]{3,2,1,0:T(8,128)(2,1)S(1)}, u32[]{:S(2)}, u32[]{:S(2)}) collective-permute-start(bf16[16,4,16,128]{3,2,1,0:T(8,128)(2,1)S(1)} %all_to_all.21), channel_id=1, source_target_pairs={{0,16},{16,0},{1,17},{17,1},{2,18},{18,2},{3,19},{19,3},{4,20},{20... | collective-permute-start | bytes 786440 | tf_op jit(solution)/shard_map/ppermute | solution.py:361
  106.8 0.6 finish.1
  107.4 0.5 collective-permute-done.8
  107.9 0.0 copy-done.3
  107.9 3.2 %refresh.1 = (f32[128,512]{1,0:T(8,128)}, f32[128,512]{1,0:T(8,128)}) custom-call(s32[5]{0:T(128)S(1)} %stack.23.info_ref, s32[16]{0:T(128)S(1)} %copy-done.3, bf16[4,4,4,16,128]{4,3,2,1,0:T(8,128)(2,1)S(1)} %bitcast.20, bf16[4,4,4,16,128]{4,3,2,1,0:T(8,128)(2,1)S(1)} %bitcast.21, f32[128,512]{1,0:T(8,128)S(1)} %bitcast.19, ...), custom_call_target="tpu_custom_call" | custom-call | flops 603979776 | bytes 1048576 | tf_op jit(solution)/shard_map/refresh/pallas_call | solution.py:365
  (2 shorter events, 0.1 us)
Async XLA Ops:
  2.9 10.3 %copy-start.1 = (bf16[1,2,16,512]{3,2,1,0:T(8,128)(2,1)S(1)}, bf16[1,2,16,512]{3,2,1,0:T(8,128)(2,1)}, u32[]{:S(2)}) copy-start(bf16[1,2,16,512]{3,2,1,0:T(8,128)(2,1)} %prec_ref.1) | copy-start | bytes 98308
  2.9 10.3 %collective-permute-start = (bf16[512,512]{1,0:T(8,128)(2,1)S(1)}, bf16[512,512]{1,0:T(8,128)(2,1)S(1)}, u32[]{:S(2)}, u32[]{:S(2)}) collective-permute-start(bf16[512,512]{1,0:T(8,128)(2,1)S(1)} %get-tuple-element.22), channel_id=1, source_target_pairs={{0,16},{16,0},{1,17},{17,1},{2,18},{18,2},{3,19},{19,3},{4,20},{20... | collective-permute-start | bytes 1572872 | tf_op jit(solution)/shard_map/ppermute | solution.py:284
  12.4 5.4 %copy-start.4 = (bf16[1,2,16,512]{3,2,1,0:T(8,128)(2,1)S(1)}, bf16[1,2,16,512]{3,2,1,0:T(8,128)(2,1)}, u32[]{:S(2)}) copy-start(bf16[1,2,16,512]{3,2,1,0:T(8,128)(2,1)} %param.10) | copy-start | bytes 98308
  12.4 16.0 %copy-start = (f32[1,128,512]{2,1,0:T(8,128)S(1)}, f32[1,128,512]{2,1,0:T(8,128)}, u32[]{:S(2)}) copy-start(f32[1,128,512]{2,1,0:T(8,128)} %param.11) | copy-start | bytes 786436
  14.3 14.1 %all-to-all-start = ((bf16[4,160,512]{2,1,0:T(8,128)(2,1)}), bf16[4,160,512]{2,1,0:T(8,128)(2,1)S(1)}, u32[]{:S(2)}, u32[]{:S(2)}) async-start(bf16[4,160,512]{2,1,0:T(8,128)(2,1)} %join.1), calls=%async_computation | async-start | bytes 1310720 | tf_op jit(solution)/shard_map/all_to_all | solution.py:295
  17.8 55.6 %copy-start.2 = (s32[16]{0:T(128)S(1)}, s32[16]{0:T(128)}, u32[]{:S(2)}) copy-start(s32[16]{0:T(128)} %listed_ref.3) | copy-start | bytes 196
  17.9 3.1 %collective-permute-start.1 = (bf16[16,512]{1,0:T(8,128)(2,1)S(1)}, bf16[16,512]{1,0:T(8,128)(2,1)S(1)}, u32[]{:S(2)}, u32[]{:S(2)}) collective-permute-start(bf16[16,512]{1,0:T(8,128)(2,1)S(1)} %get-tuple-element.37), channel_id=1, source_target_pairs={{0,16},{16,0},{1,17},{17,1},{2,18},{18,2},{3,19},{19,3},{4,20},{20... | collective-permute-start | bytes 49160 | tf_op jit(solution)/shard_map/ppermute | solution.py:297
  29.1 14.3 %collective-permute-start.2 = (bf16[160,512]{1,0:T(8,128)(2,1)S(1)}, bf16[160,512]{1,0:T(8,128)(2,1)S(1)}, u32[]{:S(2)}, u32[]{:S(2)}) collective-permute-start(bf16[160,512]{1,0:T(8,128)(2,1)S(1)} %get-tuple-element.25), channel_id=1, source_target_pairs={{0,32},{16,112},{32,0},{48,80},{64,96},{80,48},{96,64},{112,16},{1... | collective-permute-start | bytes 491528 | tf_op jit(solution)/shard_map/ppermute | solution.py:318
  36.4 7.0 %collective-permute-start.4 = (bf16[128,512]{1,0:T(8,128)(2,1)S(1)}, bf16[128,512]{1,0:T(8,128)(2,1)S(1)}, u32[]{:S(2)}, u32[]{:S(2)}) collective-permute-start(bf16[128,512]{1,0:T(8,128)(2,1)S(1)} %get-tuple-element.27.low_ref), channel_id=1, source_target_pairs={{0,4},{4,8},{8,12},{12,0},{1,5},{5,9},{9,13},{13,1},{2,6},{6,10},{... | collective-permute-start | bytes 393224 | tf_op jit(solution)/shard_map/ppermute | solution.py:112
  39.6 3.1 %collective-permute-start.3 = (bf16[64,512]{1,0:T(8,128)(2,1)S(1)}, bf16[64,512]{1,0:T(8,128)(2,1)S(1)}, u32[]{:S(2)}, u32[]{:S(2)}) collective-permute-start(bf16[64,512]{1,0:T(8,128)(2,1)S(1)} %get-tuple-element.26), channel_id=1, source_target_pairs={{0,16},{16,0},{1,17},{17,1},{2,18},{18,2},{3,19},{19,3},{4,20},{20... | collective-permute-start | bytes 196616 | tf_op jit(solution)/shard_map/ppermute | solution.py:319
  43.4 64.5 %copy-start.3 = (s32[16]{0:T(128)S(1)}, s32[16]{0:T(128)}, u32[]{:S(2)}) copy-start(s32[16]{0:T(128)} %owner_ref.1) | copy-start | bytes 196
  43.4 17.7 %collective-permute-start.5 = (bf16[192,512]{1,0:T(8,128)(2,1)S(1)}, bf16[192,512]{1,0:T(8,128)(2,1)S(1)}, u32[]{:S(2)}, u32[]{:S(2)}) collective-permute-start(bf16[192,512]{1,0:T(8,128)(2,1)S(1)} %get-tuple-element.29.sent_ref), channel_id=1, source_target_pairs={{0,96},{16,48},{32,64},{48,16},{64,32},{80,112},{96,0},{112,80},{1... | collective-permute-start | bytes 589832 | tf_op jit(solution)/shard_map/ppermute | solution.py:328
  49.6 7.5 %collective-permute-start.6 = (bf16[128,512]{1,0:T(8,128)(2,1)S(1)}, bf16[128,512]{1,0:T(8,128)(2,1)S(1)}, u32[]{:S(2)}, u32[]{:S(2)}) collective-permute-start(bf16[128,512]{1,0:T(8,128)(2,1)S(1)} %get-tuple-element.30), channel_id=1, source_target_pairs={{0,8},{4,12},{8,0},{12,4},{1,9},{5,13},{9,1},{13,5},{2,10},{6,14},... | collective-permute-start | bytes 393224 | tf_op jit(solution)/shard_map/ppermute | solution.py:112
  54.4 6.7 %collective-permute-start.7 = (bf16[128,512]{1,0:T(8,128)(2,1)S(1)}, bf16[128,512]{1,0:T(8,128)(2,1)S(1)}, u32[]{:S(2)}, u32[]{:S(2)}) collective-permute-start(bf16[128,512]{1,0:T(8,128)(2,1)S(1)} %get-tuple-element.30), channel_id=1, source_target_pairs={{0,12},{4,0},{8,4},{12,8},{1,13},{5,1},{9,5},{13,9},{2,14},{6,2},{... | collective-permute-start | bytes 393224 | tf_op jit(solution)/shard_map/ppermute | solution.py:112
  62.4 11.0 %all-to-all-start.1 = ((bf16[16,2,16,128]{3,2,1,0:T(8,128)(2,1)}), bf16[16,2,16,128]{3,2,1,0:T(8,128)(2,1)S(1)}, u32[]{:S(2)}, u32[]{:S(2)}) async-start(bf16[16,2,16,128]{3,2,1,0:T(8,128)(2,1)} %bitcast.9), calls=%async_computation.1 | async-start | bytes 262144 | tf_op jit(solution)/shard_map/all_to_all | solution.py:339
  102.7 5.2 %collective-permute-start.8 = (bf16[16,4,16,128]{3,2,1,0:T(8,128)(2,1)S(1)}, bf16[16,4,16,128]{3,2,1,0:T(8,128)(2,1)S(1)}, u32[]{:S(2)}, u32[]{:S(2)}) collective-permute-start(bf16[16,4,16,128]{3,2,1,0:T(8,128)(2,1)S(1)} %all_to_all.21), channel_id=1, source_target_pairs={{0,16},{16,0},{1,17},{17,1},{2,18},{18,2},{3,19},{19,3},{4,20},{20... | collective-permute-start | bytes 786440 | tf_op jit(solution)/shard_map/ppermute | solution.py:361

commit v11 on v10

--- a/solution.py
+++ b/solution.py
@@ -98,13 +98,14 @@
     out_ref[...] = dot(turned_ref[...], grads_ref[...])
 
 
-def join_kernel(own_ref, got_ref, prec_ref, out_ref):
+def join_kernel(own_ref, got_ref, prec_ref, right_ref, out_ref, right_out):
     total = (own_ref[...] + got_ref[...].astype(F32)).astype(BF16).T
     rows = prec_ref.shape[2]
     for w in range(X):
         out_ref[w, :PART] = total[w * PART : (w + 1) * PART]
         for c in range(CORE):
             out_ref[w, PART + c * rows : PART + (c + 1) * rows] = prec_ref[0, c]
+    right_out[...] = right_ref[0]
 
 
 def shift(value, axis, step):
@@ -123,12 +124,10 @@
         out_ref[pl.ds(pl.multiple_of(at, rows), rows), :] = part[...]
 
 
-def sum_kernel(info_ref, parts_ref, mine_ref, theirs_ref, old_ref, *refs):
-    keep_ref, right_ref, left_ref, left_send, old_low, send_ref = refs
+def sum_kernel(info_ref, parts_ref, old_ref, *refs):
+    keep_ref, left_ref, left_send, old_low, send_ref = refs[-5:]
     core = info_ref[0]
-    rows = mine_ref.shape[0]
-    right_ref[pl.ds(pl.multiple_of(core * rows, rows), rows), :] = mine_ref[...]
-    right_ref[pl.ds(pl.multiple_of((1 - core) * rows, rows), rows), :] = theirs_ref[...]
+    rows = left_ref.shape[0] // X
     total = parts_ref[0, :PART].astype(F32)
     for w in range(X):
         for ref, c in ((left_ref, core), (left_send, 1 - core)):
@@ -137,36 +136,37 @@
         if w:
             total = total + parts_ref[w, :PART].astype(F32)
     keep_ref[...] = total
-    send_ref[:PART] = total.astype(BF16)
-    send_ref[PART:] = right_ref[...]
+    send_ref[...] = total.astype(BF16)
     old_low[...] = old_ref[...].astype(BF16)
 
 
-def middle_kernel(keep_ref, right_ref, got_ref, old_ref, *refs):
-    out_ref, send_ref, old_low = refs[-3:]
-    total = keep_ref[...] + got_ref[:PART].astype(F32)
-    out_ref[...] = total
-    send_ref[:PART] = total.astype(BF16)
-    send_ref[PART : PART + ROWS] = right_ref[...]
-    send_ref[PART + ROWS :] = got_ref[PART:]
-    old_low[...] = old_ref[...].astype(BF16)
-
-
-def pack_kernel(scale, info_ref, keep_ref, sent_ref, got_ref, *refs):
-    grad_ref, pieces_ref, right_ref = refs[-3:]
+def halves_kernel(info_ref, own_ref, one, two, left_ref, keep_ref, send_ref):
     core, zh = info_ref[0], info_ref[2]
-    grad = ((keep_ref[...] + got_ref[:PART].astype(F32)) * scale).astype(BF16)
-    grad_ref[...] = grad
+    rows = own_ref.shape[2]
     near = zh + 1 - 2 * (zh % 2)
     far = ZH - 1 - zh
     across = far + 1 - 2 * (far % 2)
     first = jnp.where(core == 0, near, far)
     second = jnp.where(core == 0, far, near)
-    for place_at, mate in enumerate((zh, first, second, across)):
-        source = (sent_ref, got_ref)[place_at // 2]
-        start = PART + place_at % 2 * ROWS
-        to = pl.multiple_of(mate * ROWS, ROWS)
-        right_ref[pl.ds(to, ROWS), :] = source[start : start + ROWS]
+    sources = (own_ref.at[0], one, two.at[0], two.at[1])
+    send_ref[: ZH * rows] = left_ref[...]
+    for mate, source in zip((zh, first, second, across), sources):
+        keep_ref[pl.ds(pl.multiple_of(mate * rows, rows), rows), :] = source[core]
+        at = pl.multiple_of((ZH + mate) * rows, rows)
+        send_ref[pl.ds(at, rows), :] = source[1 - core]
+
+
+def middle_kernel(keep_ref, got_ref, old_ref, *refs):
+    out_ref, send_ref, old_low = refs[-3:]
+    total = keep_ref[...] + got_ref[...].astype(F32)
+    out_ref[...] = total
+    send_ref[...] = total.astype(BF16)
+    old_low[...] = old_ref[...].astype(BF16)
+
+
+def pack_kernel(scale, keep_ref, got_ref, *refs):
+    pieces_ref = refs[-1]
+    grad = ((keep_ref[...] + got_ref[...].astype(F32)) * scale).astype(BF16)
     n_mp, n_root, cores, rows, lanes = pieces_ref.shape
     for c in range(cores):
         for r in range(n_root):
@@ -207,14 +207,17 @@
             out_ref[:, at : at + lanes] = total.astype(BF16)
 
 
-def update_kernel(info_ref, mine_ref, theirs_ref, grad_ref, right_ref, out_ref, left):
-    rows = ROWS // CORE
-    for ref, c in ((mine_ref, info_ref[0]), (theirs_ref, 1 - info_ref[0])):
-        for w in range(X):
-            at = pl.multiple_of(w * ROWS + c * rows, rows)
-            left[pl.ds(at, rows), :] = ref[w * rows : (w + 1) * rows]
-    product = dot(left[...], grad_ref[...], 1, 1).astype(BF16)
-    out_ref[...] = dot(product, right_ref[...])
+def update_kernel(scale, info_ref, keep_ref, got_ref, left_ref, right_ref, theirs_ref, out_ref, left, right):
+    grad = ((keep_ref[...] + got_ref[...].astype(F32)) * scale).astype(BF16)
+    core, rows, side = info_ref[0], ROWS // CORE, PART // CORE
+    for ref, mine, start in ((left, left_ref, 0), (right, right_ref, side)):
+        for w in range(PART // ROWS):
+            at = pl.multiple_of(w * ROWS + core * rows, rows)
+            ref[pl.ds(at, rows), :] = mine[w * rows : (w + 1) * rows]
+            at = pl.multiple_of(w * ROWS + (1 - core) * rows, rows)
+            ref[pl.ds(at, rows), :] = theirs_ref[start + w * rows : start + (w + 1) * rows]
+    product = dot(left[...], grad, 1, 1).astype(BF16)
+    out_ref[...] = dot(product, right[...])
 
 
 def refresh_kernel(info_ref, owner_ref, mine_ref, theirs_ref, own_ref, low_ref, one, two, three, stats_ref, roots_ref, block, product, old):
@@ -289,24 +292,13 @@
         [shape((B, B), F32)],
         work=cost(2 * acts.shape[0] * B * B, 4 * acts.shape[0] * B),
     )(turned, grads_own)
-    (total,) = kernel_call(
-        join_kernel, "join", [VMEM] * 3, [shape((X, PART + ROWS, B))]
-    )(own, got, prec_left)
+    total, right_own = kernel_call(
+        join_kernel,
+        "join",
+        [VMEM] * 4,
+        [shape((X, PART + ROWS, B)), shape((CORE, half, B))],
+    )(own, got, prec_left, prec_right)
     total = lax.all_to_all(total, "x", 0, 0)
-    mine = lax.dynamic_index_in_dim(prec_right[0], core, 0, keepdims=False)
-    theirs = lax.ppermute(
-        lax.dynamic_index_in_dim(prec_right[0], 1 - core, 0, keepdims=False), "core", swap
-    )
-    old_own = stats_old[0]
-    keep, right_rows, left_mine, left_send, old_low, send = kernel_call(
-        sum_kernel,
-        "sum_x",
-        [SMEM] + [VMEM] * 4,
-        [shape((PART, B), F32), shape((ROWS, B))]
-        + [shape((PART // CORE, B))] * 2
-        + [shape((quarter, B)), shape((PART + ROWS, B))],
-    )(info, total, mine, theirs, old_own)
-
     near_far = [
         [
             (z * CORE + c, ((z ^ 1) if c == step else ZH - 1 - z) * CORE + c)
@@ -315,44 +307,63 @@
         ]
         for step in range(2)
     ]
+    right_one = lax.ppermute(right_own, ("zh", "core"), near_far[0])
+    right_two = lax.ppermute(jnp.stack([right_own, right_one]), ("zh", "core"), near_far[1])
+    old_own = stats_old[0]
+    keep, left_mine, left_send, old_low, send = kernel_call(
+        sum_kernel,
+        "sum_x",
+        [SMEM] + [VMEM] * 2,
+        [shape((PART, B), F32)]
+        + [shape((PART // CORE, B))] * 2
+        + [shape((quarter, B)), shape((PART, B))],
+        awaited=1,
+    )(info, total, old_own, right_one)
     got = lax.ppermute(send, ("zh", "core"), near_far[0])
-    left_theirs = lax.ppermute(left_send, "core", swap)
+    right_mine, prec_send = kernel_call(
+        halves_kernel,
+        "halves",
+        [SMEM] + [VMEM] * 4,
+        [shape((PART // CORE, B)), shape((PART, B))],
+    )(info, prec_right, right_one, right_two, left_send)
+    theirs = lax.ppermute(prec_send, "core", swap)
     olds = [old_low, shift(old_low, "mp", 1)]
     keep, send, old_later = kernel_call(
         middle_kernel,
         "middle",
-        [VMEM] * 4,
-        [shape((PART, B), F32), shape((PART + 2 * ROWS, B)), shape((quarter, B))],
+        [VMEM] * 3,
+        [shape((PART, B), F32), shape((PART, B)), shape((quarter, B))],
         awaited=2,
-    )(keep, right_rows, got, old_own, left_theirs, olds[1])
+    )(keep, got, old_own, theirs, olds[1])
     got = lax.ppermute(send, ("zh", "core"), near_far[1])
     olds += [shift(old_later, "mp", step) for step in range(2, n_mp)]
-    grad, pieces, right_part = kernel_call(
+    (pieces,) = kernel_call(
         functools.partial(pack_kernel, tokens ** -0.5),
         "pack",
-        [SMEM] + [VMEM] * 3,
-        [shape((PART, B)), shape((n_mp, n_root, CORE, half, lanes)), shape((PART, B))],
-        awaited=2,
-    )(info, keep, send, got, *olds[2:])
+        [VMEM] * 2,
+        [shape((n_mp, n_root, CORE, half, lanes))],
+        awaited=1,
+    )(keep, got, olds[2])
 
     pieces = pieces.reshape((n_mp * n_root,) + pieces.shape[2:])
     blocks = lax.all_to_all(pieces, ("mp", "root"), 0, 0)
 
     (total,) = kernel_call(
-        update_kernel,
+        functools.partial(update_kernel, tokens ** -0.5),
         "update",
-        [SMEM] + [VMEM] * 4,
+        [SMEM] + [VMEM] * 5,
         [shape((PART, B), F32)],
-        [pltpu.VMEM((PART, B), BF16)],
+        [pltpu.VMEM((PART, B), BF16)] * 2,
         cost(2 * PART * B * (PART + B), 6 * PART * B),
-    )(info, left_mine, left_theirs, grad, right_part)
+    )(info, keep, got, left_mine, right_mine, theirs)
 
     (chosen,) = kernel_call(
         choose_kernel,
         "choose",
         [SMEM, SMEM, VMEM, VMEM],
         [shape((X * CORE, 1 + B // lanes, half, lanes))],
-    )(info, listed, blocks, total)
+        awaited=1,
+    )(info, listed, blocks, total, olds[3])
     parts = lax.all_to_all(chosen, ("x", "core"), 0, 0)
     (mine,) = kernel_call(
         spread_kernel, "spread", [SMEM, SMEM, VMEM], [shape((n_mp * n_root, X, half, lanes))]

time: 112 us -> 124 us (1.11)
  starting transfers between devices: 48.5 us -> 62.5 us
  waiting for transfers between devices: 21.7 us -> 18.4 us
  blocking collectives: 28.1 us -> 29.7 us
    ppermute x2 -> x3, starting transfers between devices: 4.2 us -> 15.5 us  [the longest x1 7.71 us: local(): right_one = lax.ppermute(right_own, ('zh', 'core'), near_far[0])]
    all_to_all x1, waiting for transfers between devices: 7.45 us -> 0.01 us  [local(): total = lax.all_to_all(total, 'x', 0, 0)]
    all_to_all x1, waiting for transfers between devices: 6.34 us -> 0.61 us  [local(): blocks = lax.all_to_all(pieces, ('mp', 'root'), 0, 0)]
    ppermute x1, waiting for transfers between devices: 0.01 us -> 4.88 us  [local(): got = lax.ppermute(send, ('zh', 'core'), near_far[1])]
    ppermute x2 -> x3, waiting for transfers between devices: 1.94 us -> 6.57 us  [the longest x1 5.28 us: local(): lax.ppermute(jnp.stack([right_own, right_one]), ('zh', 'core'), near_far[1])]
    all_to_all x1, blocking collectives: 12.3 us -> 16.1 us  [local(): mine = lax.all_to_all(mine, ('mp', 'root'), 0, 0)]
    ppermute x1, starting transfers between devices: 6.15 us -> 3.28 us  [local(): got = lax.ppermute(send, ('zh', 'core'), near_far[1])]
    ppermute x1, waiting for transfers between devices: 0.01 us -> 2.69 us  [local(): got = lax.ppermute(send, ('zh', 'core'), near_far[0])]
  transfers between devices with their start and end apart: 11 -> 12, of which waited for: 8 -> 9; matrix products, arithmetic and copies ran while one was open for 0% -> 0% of each run, Pallas kernels for 2% -> 2%
where the time goes in v11:
time: 124 us; the launch traced here: 123 us
  starting transfers between devices  62.5 us (50%)
  blocking collectives  29.7 us (24%)
  waiting for transfers between devices  18.4 us (15%)
  Pallas kernels  11.9 us (10%)
    all_to_all x1, blocking collectives, local(): mine = lax.all_to_all(mine, ('mp', 'root'), 0, 0)  16.1 us
    all_to_all x1, blocking collectives, local(): parts = lax.all_to_all(chosen, ('x', 'core'), 0, 0)  13.6 us
    ppermute x3, starting transfers between devices, shift(): lax.ppermute(value, axis, [(at, (at + step) % size) for at in range(size)])  12.4 us
    ppermute x1, starting transfers between devices, local(): got = lax.ppermute(send, ('zh', 'core'), near_far[0])  9.35 us
    ppermute x1, starting transfers between devices, local(): got = lax.ppermute(send, 'core', swap)  8.8 us
    ppermute x1, starting transfers between devices, local(): right_one = lax.ppermute(right_own, ('zh', 'core'), near_far[0])  7.71 us
    all_to_all x1, starting transfers between devices, local(): blocks = lax.all_to_all(pieces, ('mp', 'root'), 0, 0)  5.65 us
    ppermute x1, waiting for transfers between devices, local(): lax.ppermute(jnp.stack([right_own, right_one]), ('zh', 'core'), near_far[1])  5.28 us
  transfers between devices with their start and end apart: 12, of which 9 were waited for; matrix products, arithmetic and copies ran while one was open for 0% of the time, Pallas kernels for 2%

profile of v11, /device:TPU:1, one launch (start us, length us, event | category | flops | bytes accessed | tf_op | source)
XLA Modules:
  0.0 123.4 jit_solution(7430163952338654288)
XLA Ops:
  0.6 2.3 %other_half.1 = (bf16[512,1024]{1,0:T(8,128)(2,1)S(1)}, bf16[512,512]{1,0:T(8,128)(2,1)S(1)}, bf16[1024,512]{1,0:T(8,128)(2,1)S(1)}) custom-call(s32[1]{0:T(128)} %bitcast.5.index_ref, bf16[1024,512]{1,0:T(8,128)(2,1)} %acts_ref.1, bf16[1024,1024]{1,0:T(8,128)(2,1)} %grads_ref.1), custom_call_target="tpu_custom_call" | custom-call | flops 536870912 | bytes 3145728 | tf_op jit(solution)/shard_map/other_half/pallas_call | solution.py:80
  2.9 0.0 copy-start.1
  2.9 0.0 copy-start.2
  2.9 8.8 %collective-permute-start = (bf16[512,512]{1,0:T(8,128)(2,1)S(1)}, bf16[512,512]{1,0:T(8,128)(2,1)S(1)}, u32[]{:S(2)}, u32[]{:S(2)}) collective-permute-start(bf16[512,512]{1,0:T(8,128)(2,1)S(1)} %get-tuple-element.22), channel_id=1, source_target_pairs={{0,16},{16,0},{1,17},{17,1},{2,18},{18,2},{3,19},{19,3},{4,20},{20... | collective-permute-start | bytes 1572872 | tf_op jit(solution)/shard_map/ppermute | solution.py:287
  11.7 0.7 own_half.1.own_ref
  12.4 0.0 copy-start
  12.5 0.8 collective-permute-done.got_ref
  13.2 0.0 copy-done.1
  13.3 0.0 copy-done.2
  13.3 1.1 join.1
  14.3 3.5 %all-to-all-start = ((bf16[4,160,512]{2,1,0:T(8,128)(2,1)}), bf16[4,160,512]{2,1,0:T(8,128)(2,1)S(1)}, u32[]{:S(2)}, u32[]{:S(2)}) async-start(bf16[4,160,512]{2,1,0:T(8,128)(2,1)} %get-tuple-element.23), calls=%async_computation | async-start | bytes 1310720 | tf_op jit(solution)/shard_map/all_to_all | solution.py:301
  17.8 0.0 copy-start.3
  17.8 7.7 %collective-permute-start.1 = (bf16[2,16,512]{2,1,0:T(8,128)(2,1)S(1)}, bf16[2,16,512]{2,1,0:T(8,128)(2,1)S(1)}, u32[]{:S(2)}, u32[]{:S(2)}) collective-permute-start(bf16[2,16,512]{2,1,0:T(8,128)(2,1)S(1)} %get-tuple-element.24), channel_id=1, source_target_pairs={{0,32},{16,112},{32,0},{48,80},{64,96},{80,48},{96,64},{112,16},{1... | collective-permute-start | bytes 98312 | tf_op jit(solution)/shard_map/ppermute | solution.py:310
  25.6 1.3 %collective-permute-done.1.refs_0_.one = bf16[2,16,512]{2,1,0:T(8,128)(2,1)S(1)} collective-permute-done((bf16[2,16,512]{2,1,0:T(8,128)(2,1)S(1)}, bf16[2,16,512]{2,1,0:T(8,128)(2,1)S(1)}, u32[]{:S(2)}, u32[]{:S(2)}) %collective-permute-start.1) | collective-permute-done | bytes 32800 | tf_op jit(solution)/shard_map/ppermute | solution.py:310
  26.9 5.2 %collective-permute-start.3 = (bf16[2,2,16,512]{3,2,1,0:T(8,128)(2,1)S(1)}, bf16[2,2,16,512]{3,2,1,0:T(8,128)(2,1)S(1)}, u32[]{:S(2)}, u32[]{:S(2)}) collective-permute-start(bf16[2,2,16,512]{3,2,1,0:T(8,128)(2,1)S(1)} %pad_maximum_fusion), channel_id=1, source_target_pairs={{0,96},{16,48},{32,64},{48,16},{64,32},{80,112},{96,0},{112,80},{1... | collective-permute-start | bytes 196616 | tf_op jit(solution)/shard_map/ppermute | solution.py:311
  32.0 0.1 stack.32.info_ref
  32.1 0.0 all-to-all-done.parts_ref
  32.1 0.0 copy-done
  32.1 0.6 sum_x.1
  32.8 5.3 %collective-permute-done.3.two = bf16[2,2,16,512]{3,2,1,0:T(8,128)(2,1)S(1)} collective-permute-done((bf16[2,2,16,512]{3,2,1,0:T(8,128)(2,1)S(1)}, bf16[2,2,16,512]{3,2,1,0:T(8,128)(2,1)S(1)}, u32[]{:S(2)}, u32[]{:S(2)}) %collective-permute-start.3) | collective-permute-done | bytes 65568 | tf_op jit(solution)/shard_map/ppermute | solution.py:311
  38.0 0.6 halves.1
  38.6 2.6 %collective-permute-start.4 = (bf16[128,512]{1,0:T(8,128)(2,1)S(1)}, bf16[128,512]{1,0:T(8,128)(2,1)S(1)}, u32[]{:S(2)}, u32[]{:S(2)}) collective-permute-start(bf16[128,512]{1,0:T(8,128)(2,1)S(1)} %get-tuple-element.28), channel_id=1, source_target_pairs={{0,16},{16,0},{1,17},{17,1},{2,18},{18,2},{3,19},{19,3},{4,20},{20... | collective-permute-start | bytes 393224 | tf_op jit(solution)/shard_map/ppermute | solution.py:329
  41.2 9.3 %collective-permute-start.2 = (bf16[128,512]{1,0:T(8,128)(2,1)S(1)}, bf16[128,512]{1,0:T(8,128)(2,1)S(1)}, u32[]{:S(2)}, u32[]{:S(2)}) collective-permute-start(bf16[128,512]{1,0:T(8,128)(2,1)S(1)} %get-tuple-element.26), channel_id=1, source_target_pairs={{0,32},{16,112},{32,0},{48,80},{64,96},{80,48},{96,64},{112,16},{1... | collective-permute-start | bytes 393224 | tf_op jit(solution)/shard_map/ppermute | solution.py:322
  50.6 3.2 %collective-permute-start.5 = (bf16[128,512]{1,0:T(8,128)(2,1)S(1)}, bf16[128,512]{1,0:T(8,128)(2,1)S(1)}, u32[]{:S(2)}, u32[]{:S(2)}) collective-permute-start(bf16[128,512]{1,0:T(8,128)(2,1)S(1)} %get-tuple-element.29.low_ref), channel_id=1, source_target_pairs={{0,4},{4,8},{8,12},{12,0},{1,5},{5,9},{9,13},{13,1},{2,6},{6,10},{... | collective-permute-start | bytes 393224 | tf_op jit(solution)/shard_map/ppermute | solution.py:113
  53.8 0.0 collective-permute-done.4.refs_0_.theirs_ref
  53.8 2.7 %collective-permute-done.2.got_ref = bf16[128,512]{1,0:T(8,128)(2,1)S(1)} collective-permute-done((bf16[128,512]{1,0:T(8,128)(2,1)S(1)}, bf16[128,512]{1,0:T(8,128)(2,1)S(1)}, u32[]{:S(2)}, u32[]{:S(2)}) %collective-permute-start.2) | collective-permute-done | bytes 131104 | tf_op jit(solution)/shard_map/ppermute | solution.py:322
  56.5 1.1 collective-permute-done.5.refs_1_.one
  57.6 0.0 copy-start.4
  57.6 3.3 %collective-permute-start.6 = (bf16[128,512]{1,0:T(8,128)(2,1)S(1)}, bf16[128,512]{1,0:T(8,128)(2,1)S(1)}, u32[]{:S(2)}, u32[]{:S(2)}) collective-permute-start(bf16[128,512]{1,0:T(8,128)(2,1)S(1)} %get-tuple-element.31), channel_id=1, source_target_pairs={{0,96},{16,48},{32,64},{48,16},{64,32},{80,112},{96,0},{112,80},{1... | collective-permute-start | bytes 393224 | tf_op jit(solution)/shard_map/ppermute | solution.py:338
  60.9 4.7 %collective-permute-start.7 = (bf16[128,512]{1,0:T(8,128)(2,1)S(1)}, bf16[128,512]{1,0:T(8,128)(2,1)S(1)}, u32[]{:S(2)}, u32[]{:S(2)}) collective-permute-start(bf16[128,512]{1,0:T(8,128)(2,1)S(1)} %get-tuple-element.32), channel_id=1, source_target_pairs={{0,8},{4,12},{8,0},{12,4},{1,9},{5,13},{9,1},{13,5},{2,10},{6,14},... | collective-permute-start | bytes 393224 | tf_op jit(solution)/shard_map/ppermute | solution.py:113
  65.6 4.9 %collective-permute-done.6.got_ref = bf16[128,512]{1,0:T(8,128)(2,1)S(1)} collective-permute-done((bf16[128,512]{1,0:T(8,128)(2,1)S(1)}, bf16[128,512]{1,0:T(8,128)(2,1)S(1)}, u32[]{:S(2)}, u32[]{:S(2)}) %collective-permute-start.6) | collective-permute-done | bytes 131104 | tf_op jit(solution)/shard_map/ppermute | solution.py:338
  70.5 0.0 collective-permute-done.7.refs_0_.two
  70.5 0.7 pack.1
  71.2 5.6 %all-to-all-start.1 = ((bf16[16,2,16,128]{3,2,1,0:T(8,128)(2,1)}), bf16[16,2,16,128]{3,2,1,0:T(8,128)(2,1)S(1)}, u32[]{:S(2)}, u32[]{:S(2)}) async-start(bf16[16,2,16,128]{3,2,1,0:T(8,128)(2,1)} %bitcast.9), calls=%async_computation.1 | async-start | bytes 262144 | tf_op jit(solution)/shard_map/all_to_all | solution.py:349
  76.9 4.5 %collective-permute-start.8 = (bf16[128,512]{1,0:T(8,128)(2,1)S(1)}, bf16[128,512]{1,0:T(8,128)(2,1)S(1)}, u32[]{:S(2)}, u32[]{:S(2)}) collective-permute-start(bf16[128,512]{1,0:T(8,128)(2,1)S(1)} %get-tuple-element.32), channel_id=1, source_target_pairs={{0,12},{4,0},{8,4},{12,8},{1,13},{5,1},{9,5},{13,9},{2,14},{6,2},{... | collective-permute-start | bytes 393224 | tf_op jit(solution)/shard_map/ppermute | solution.py:113
  81.3 0.9 update.1.total_ref
  82.3 1.2 %collective-permute-done.8.refs_0_.three = bf16[128,512]{1,0:T(8,128)(2,1)S(1)} collective-permute-done((bf16[128,512]{1,0:T(8,128)(2,1)S(1)}, bf16[128,512]{1,0:T(8,128)(2,1)S(1)}, u32[]{:S(2)}, u32[]{:S(2)}) %collective-permute-start.8) | collective-permute-done | bytes 131104 | tf_op jit(solution)/shard_map/ppermute | solution.py:113
  83.5 0.6 all-to-all-done.1.blocks_ref
  84.1 0.0 copy-done.3
  84.1 0.6 choose.1
  84.7 13.6 %all_to_all.20.parts_ref = bf16[8,5,16,128]{3,2,1,0:T(8,128)(2,1)S(1)} all-to-all(bf16[8,5,16,128]{3,2,1,0:T(8,128)(2,1)S(1)} %choose.1), channel_id=1, replica_groups=mesh['x'=4,'zh'=4,'core'=2,'mp'=4,'root'=4] {'x','core'}, dimensions={0} | all-to-all | bytes 327680 | tf_op jit(solution)/shard_map/all_to_all | solution.py:367
  98.3 0.6 spread.1
  98.9 16.1 %all_to_all.21 = bf16[16,4,16,128]{3,2,1,0:T(8,128)(2,1)S(1)} all-to-all(bf16[16,4,16,128]{3,2,1,0:T(8,128)(2,1)S(1)} %spread.1), channel_id=1, replica_groups=mesh['x'=4,'zh'=4,'core'=2,'mp'=4,'root'=4] {'mp','root'}, dimensions={0} | all-to-all | bytes 524288 | tf_op jit(solution)/shard_map/all_to_all | solution.py:371
  115.0 4.1 %collective-permute-start.9 = (bf16[16,4,16,128]{3,2,1,0:T(8,128)(2,1)S(1)}, bf16[16,4,16,128]{3,2,1,0:T(8,128)(2,1)S(1)}, u32[]{:S(2)}, u32[]{:S(2)}) collective-permute-start(bf16[16,4,16,128]{3,2,1,0:T(8,128)(2,1)S(1)} %all_to_all.21), channel_id=1, source_target_pairs={{0,16},{16,0},{1,17},{17,1},{2,18},{18,2},{3,19},{19,3},{4,20},{20... | collective-permute-start | bytes 786440 | tf_op jit(solution)/shard_map/ppermute | solution.py:372
  119.0 0.6 finish.1
  119.7 0.5 collective-permute-done.9
  120.2 0.0 copy-done.4
  120.2 3.2 %refresh.1 = (f32[128,512]{1,0:T(8,128)}, f32[128,512]{1,0:T(8,128)}) custom-call(s32[5]{0:T(128)S(1)} %stack.32.info_ref, s32[16]{0:T(128)S(1)} %copy-done.4, bf16[4,4,4,16,128]{4,3,2,1,0:T(8,128)(2,1)S(1)} %bitcast.19, bf16[4,4,4,16,128]{4,3,2,1,0:T(8,128)(2,1)S(1)} %bitcast.21, f32[128,512]{1,0:T(8,128)S(1)} %bitcast.17, ...), custom_call_target="tpu_custom_call" | custom-call | flops 603979776 | bytes 1048576 | tf_op jit(solution)/shard_map/refresh/pallas_call | solution.py:376
  (2 shorter events, 0.1 us)
Async XLA Ops:
  2.9 10.3 %copy-start.1 = (bf16[1,2,16,512]{3,2,1,0:T(8,128)(2,1)S(1)}, bf16[1,2,16,512]{3,2,1,0:T(8,128)(2,1)}, u32[]{:S(2)}) copy-start(bf16[1,2,16,512]{3,2,1,0:T(8,128)(2,1)} %own_ref.1) | copy-start | bytes 98308
  2.9 10.3 %copy-start.2 = (bf16[1,2,16,512]{3,2,1,0:T(8,128)(2,1)S(1)}, bf16[1,2,16,512]{3,2,1,0:T(8,128)(2,1)}, u32[]{:S(2)}) copy-start(bf16[1,2,16,512]{3,2,1,0:T(8,128)(2,1)} %prec_ref.1) | copy-start | bytes 98308
  2.9 10.3 %collective-permute-start = (bf16[512,512]{1,0:T(8,128)(2,1)S(1)}, bf16[512,512]{1,0:T(8,128)(2,1)S(1)}, u32[]{:S(2)}, u32[]{:S(2)}) collective-permute-start(bf16[512,512]{1,0:T(8,128)(2,1)S(1)} %get-tuple-element.22), channel_id=1, source_target_pairs={{0,16},{16,0},{1,17},{17,1},{2,18},{18,2},{3,19},{19,3},{4,20},{20... | collective-permute-start | bytes 1572872 | tf_op jit(solution)/shard_map/ppermute | solution.py:287
  12.4 19.7 %copy-start = (f32[1,128,512]{2,1,0:T(8,128)S(1)}, f32[1,128,512]{2,1,0:T(8,128)}, u32[]{:S(2)}) copy-start(f32[1,128,512]{2,1,0:T(8,128)} %param.11) | copy-start | bytes 786436
  14.3 17.8 %all-to-all-start = ((bf16[4,160,512]{2,1,0:T(8,128)(2,1)}), bf16[4,160,512]{2,1,0:T(8,128)(2,1)S(1)}, u32[]{:S(2)}, u32[]{:S(2)}) async-start(bf16[4,160,512]{2,1,0:T(8,128)(2,1)} %get-tuple-element.23), calls=%async_computation | async-start | bytes 1310720 | tf_op jit(solution)/shard_map/all_to_all | solution.py:301
  17.8 66.3 %copy-start.3 = (s32[16]{0:T(128)S(1)}, s32[16]{0:T(128)}, u32[]{:S(2)}) copy-start(s32[16]{0:T(128)} %listed_ref.3) | copy-start | bytes 196
  17.8 9.0 %collective-permute-start.1 = (bf16[2,16,512]{2,1,0:T(8,128)(2,1)S(1)}, bf16[2,16,512]{2,1,0:T(8,128)(2,1)S(1)}, u32[]{:S(2)}, u32[]{:S(2)}) collective-permute-start(bf16[2,16,512]{2,1,0:T(8,128)(2,1)S(1)} %get-tuple-element.24), channel_id=1, source_target_pairs={{0,32},{16,112},{32,0},{48,80},{64,96},{80,48},{96,64},{112,16},{1... | collective-permute-start | bytes 98312 | tf_op jit(solution)/shard_map/ppermute | solution.py:310
  26.9 11.2 %collective-permute-start.3 = (bf16[2,2,16,512]{3,2,1,0:T(8,128)(2,1)S(1)}, bf16[2,2,16,512]{3,2,1,0:T(8,128)(2,1)S(1)}, u32[]{:S(2)}, u32[]{:S(2)}) collective-permute-start(bf16[2,2,16,512]{3,2,1,0:T(8,128)(2,1)S(1)} %pad_maximum_fusion), channel_id=1, source_target_pairs={{0,96},{16,48},{32,64},{48,16},{64,32},{80,112},{96,0},{112,80},{1... | collective-permute-start | bytes 196616 | tf_op jit(solution)/shard_map/ppermute | solution.py:311
  38.6 15.2 %collective-permute-start.4 = (bf16[128,512]{1,0:T(8,128)(2,1)S(1)}, bf16[128,512]{1,0:T(8,128)(2,1)S(1)}, u32[]{:S(2)}, u32[]{:S(2)}) collective-permute-start(bf16[128,512]{1,0:T(8,128)(2,1)S(1)} %get-tuple-element.28), channel_id=1, source_target_pairs={{0,16},{16,0},{1,17},{17,1},{2,18},{18,2},{3,19},{19,3},{4,20},{20... | collective-permute-start | bytes 393224 | tf_op jit(solution)/shard_map/ppermute | solution.py:329
  41.2 15.3 %collective-permute-start.2 = (bf16[128,512]{1,0:T(8,128)(2,1)S(1)}, bf16[128,512]{1,0:T(8,128)(2,1)S(1)}, u32[]{:S(2)}, u32[]{:S(2)}) collective-permute-start(bf16[128,512]{1,0:T(8,128)(2,1)S(1)} %get-tuple-element.26), channel_id=1, source_target_pairs={{0,32},{16,112},{32,0},{48,80},{64,96},{80,48},{96,64},{112,16},{1... | collective-permute-start | bytes 393224 | tf_op jit(solution)/shard_map/ppermute | solution.py:322
  50.6 7.0 %collective-permute-start.5 = (bf16[128,512]{1,0:T(8,128)(2,1)S(1)}, bf16[128,512]{1,0:T(8,128)(2,1)S(1)}, u32[]{:S(2)}, u32[]{:S(2)}) collective-permute-start(bf16[128,512]{1,0:T(8,128)(2,1)S(1)} %get-tuple-element.29.low_ref), channel_id=1, source_target_pairs={{0,4},{4,8},{8,12},{12,0},{1,5},{5,9},{9,13},{13,1},{2,6},{6,10},{... | collective-permute-start | bytes 393224 | tf_op jit(solution)/shard_map/ppermute | solution.py:113
  57.6 62.6 %copy-start.4 = (s32[16]{0:T(128)S(1)}, s32[16]{0:T(128)}, u32[]{:S(2)}) copy-start(s32[16]{0:T(128)} %owner_ref.1) | copy-start | bytes 196
  57.6 12.9 %collective-permute-start.6 = (bf16[128,512]{1,0:T(8,128)(2,1)S(1)}, bf16[128,512]{1,0:T(8,128)(2,1)S(1)}, u32[]{:S(2)}, u32[]{:S(2)}) collective-permute-start(bf16[128,512]{1,0:T(8,128)(2,1)S(1)} %get-tuple-element.31), channel_id=1, source_target_pairs={{0,96},{16,48},{32,64},{48,16},{64,32},{80,112},{96,0},{112,80},{1... | collective-permute-start | bytes 393224 | tf_op jit(solution)/shard_map/ppermute | solution.py:338
  60.9 9.6 %collective-permute-start.7 = (bf16[128,512]{1,0:T(8,128)(2,1)S(1)}, bf16[128,512]{1,0:T(8,128)(2,1)S(1)}, u32[]{:S(2)}, u32[]{:S(2)}) collective-permute-start(bf16[128,512]{1,0:T(8,128)(2,1)S(1)} %get-tuple-element.32), channel_id=1, source_target_pairs={{0,8},{4,12},{8,0},{12,4},{1,9},{5,13},{9,1},{13,5},{2,10},{6,14},... | collective-permute-start | bytes 393224 | tf_op jit(solution)/shard_map/ppermute | solution.py:113
  71.2 12.9 %all-to-all-start.1 = ((bf16[16,2,16,128]{3,2,1,0:T(8,128)(2,1)}), bf16[16,2,16,128]{3,2,1,0:T(8,128)(2,1)S(1)}, u32[]{:S(2)}, u32[]{:S(2)}) async-start(bf16[16,2,16,128]{3,2,1,0:T(8,128)(2,1)} %bitcast.9), calls=%async_computation.1 | async-start | bytes 262144 | tf_op jit(solution)/shard_map/all_to_all | solution.py:349
  76.9 6.6 %collective-permute-start.8 = (bf16[128,512]{1,0:T(8,128)(2,1)S(1)}, bf16[128,512]{1,0:T(8,128)(2,1)S(1)}, u32[]{:S(2)}, u32[]{:S(2)}) collective-permute-start(bf16[128,512]{1,0:T(8,128)(2,1)S(1)} %get-tuple-element.32), channel_id=1, source_target_pairs={{0,12},{4,0},{8,4},{12,8},{1,13},{5,1},{9,5},{13,9},{2,14},{6,2},{... | collective-permute-start | bytes 393224 | tf_op jit(solution)/shard_map/ppermute | solution.py:113
  115.0 5.2 %collective-permute-start.9 = (bf16[16,4,16,128]{3,2,1,0:T(8,128)(2,1)S(1)}, bf16[16,4,16,128]{3,2,1,0:T(8,128)(2,1)S(1)}, u32[]{:S(2)}, u32[]{:S(2)}) collective-permute-start(bf16[16,4,16,128]{3,2,1,0:T(8,128)(2,1)S(1)} %all_to_all.21), channel_id=1, source_target_pairs={{0,16},{16,0},{1,17},{17,1},{2,18},{18,2},{3,19},{19,3},{4,20},{20... | collective-permute-start | bytes 786440 | tf_op jit(solution)/shard_map/ppermute | solution.py:372

commit v12 on v10

--- a/solution.py
+++ b/solution.py
@@ -152,21 +152,8 @@
     old_low[...] = old_ref[...].astype(BF16)
 
 
-def pack_kernel(scale, info_ref, keep_ref, sent_ref, got_ref, *refs):
-    grad_ref, pieces_ref, right_ref = refs[-3:]
-    core, zh = info_ref[0], info_ref[2]
+def pack_kernel(scale, keep_ref, got_ref, pieces_ref):
     grad = ((keep_ref[...] + got_ref[:PART].astype(F32)) * scale).astype(BF16)
-    grad_ref[...] = grad
-    near = zh + 1 - 2 * (zh % 2)
-    far = ZH - 1 - zh
-    across = far + 1 - 2 * (far % 2)
-    first = jnp.where(core == 0, near, far)
-    second = jnp.where(core == 0, far, near)
-    for place_at, mate in enumerate((zh, first, second, across)):
-        source = (sent_ref, got_ref)[place_at // 2]
-        start = PART + place_at % 2 * ROWS
-        to = pl.multiple_of(mate * ROWS, ROWS)
-        right_ref[pl.ds(to, ROWS), :] = source[start : start + ROWS]
     n_mp, n_root, cores, rows, lanes = pieces_ref.shape
     for c in range(cores):
         for r in range(n_root):
@@ -188,7 +175,8 @@
                 out_ref[w * CORE + c, 1 + lane] = part.astype(BF16)
 
 
-def spread_kernel(info_ref, listed_ref, parts_ref, out_ref):
+def spread_kernel(info_ref, listed_ref, parts_ref, *refs):
+    out_ref = refs[-1]
     holder = listed_ref[info_ref[1] * ZH + info_ref[2]] % 2
     for w in range(X):
         tile = parts_ref[w * CORE + holder, 0]
@@ -207,14 +195,26 @@
             out_ref[:, at : at + lanes] = total.astype(BF16)
 
 
-def update_kernel(info_ref, mine_ref, theirs_ref, grad_ref, right_ref, out_ref, left):
+def update_kernel(scale, info_ref, keep_ref, sent_ref, got_ref, mine_ref, theirs_ref, out_ref, left, right):
+    core, zh = info_ref[0], info_ref[2]
     rows = ROWS // CORE
-    for ref, c in ((mine_ref, info_ref[0]), (theirs_ref, 1 - info_ref[0])):
+    for ref, c in ((mine_ref, core), (theirs_ref, 1 - core)):
         for w in range(X):
             at = pl.multiple_of(w * ROWS + c * rows, rows)
             left[pl.ds(at, rows), :] = ref[w * rows : (w + 1) * rows]
-    product = dot(left[...], grad_ref[...], 1, 1).astype(BF16)
-    out_ref[...] = dot(product, right_ref[...])
+    near = zh + 1 - 2 * (zh % 2)
+    far = ZH - 1 - zh
+    across = far + 1 - 2 * (far % 2)
+    first = jnp.where(core == 0, near, far)
+    second = jnp.where(core == 0, far, near)
+    for place_at, mate in enumerate((zh, first, second, across)):
+        source = (sent_ref, got_ref)[place_at // 2]
+        start = PART + place_at % 2 * ROWS
+        to = pl.multiple_of(mate * ROWS, ROWS)
+        right[pl.ds(to, ROWS), :] = source[start : start + ROWS]
+    grad = ((keep_ref[...] + got_ref[:PART].astype(F32)) * scale).astype(BF16)
+    product = dot(left[...], grad, 1, 1).astype(BF16)
+    out_ref[...] = dot(product, right[...])
 
 
 def refresh_kernel(info_ref, owner_ref, mine_ref, theirs_ref, own_ref, low_ref, one, two, three, stats_ref, roots_ref, block, product, old):
@@ -327,36 +327,40 @@
     )(keep, right_rows, got, old_own, left_theirs, olds[1])
     got = lax.ppermute(send, ("zh", "core"), near_far[1])
     olds += [shift(old_later, "mp", step) for step in range(2, n_mp)]
-    grad, pieces, right_part = kernel_call(
+    (pieces,) = kernel_call(
         functools.partial(pack_kernel, tokens ** -0.5),
         "pack",
-        [SMEM] + [VMEM] * 3,
-        [shape((PART, B)), shape((n_mp, n_root, CORE, half, lanes)), shape((PART, B))],
-        awaited=2,
-    )(info, keep, send, got, *olds[2:])
+        [VMEM] * 2,
+        [shape((n_mp, n_root, CORE, half, lanes))],
+    )(keep, got)
 
     pieces = pieces.reshape((n_mp * n_root,) + pieces.shape[2:])
     blocks = lax.all_to_all(pieces, ("mp", "root"), 0, 0)
 
     (total,) = kernel_call(
-        update_kernel,
+        functools.partial(update_kernel, tokens ** -0.5),
         "update",
-        [SMEM] + [VMEM] * 4,
+        [SMEM] + [VMEM] * 5,
         [shape((PART, B), F32)],
-        [pltpu.VMEM((PART, B), BF16)],
+        [pltpu.VMEM((PART, B), BF16)] * 2,
         cost(2 * PART * B * (PART + B), 6 * PART * B),
-    )(info, left_mine, left_theirs, grad, right_part)
+    )(info, keep, send, got, left_mine, left_theirs)
 
     (chosen,) = kernel_call(
         choose_kernel,
         "choose",
         [SMEM, SMEM, VMEM, VMEM],
         [shape((X * CORE, 1 + B // lanes, half, lanes))],
-    )(info, listed, blocks, total)
+        awaited=1,
+    )(info, listed, blocks, total, olds[2])
     parts = lax.all_to_all(chosen, ("x", "core"), 0, 0)
     (mine,) = kernel_call(
-        spread_kernel, "spread", [SMEM, SMEM, VMEM], [shape((n_mp * n_root, X, half, lanes))]
-    )(info, listed, parts)
+        spread_kernel,
+        "spread",
+        [SMEM, SMEM, VMEM],
+        [shape((n_mp * n_root, X, half, lanes))],
+        awaited=1,
+    )(info, listed, parts, olds[3])
     mine = lax.all_to_all(mine, ("mp", "root"), 0, 0)
     theirs = lax.ppermute(mine, "core", swap)
     gathered = [value.reshape((n_mp, n_root) + value.shape[1:]) for value in (mine, theirs)]

time: 112 us -> 117 us (1.045)
  blocking collectives: 28.1 us -> 17 us
  starting transfers between devices: 48.5 us -> 59.5 us
  waiting for transfers between devices: 21.7 us -> 26.5 us
    all_to_all x1 -> x0, blocking collectives: 15.8 us -> none  [local(): parts = lax.all_to_all(chosen, ('x', 'core'), 0, 0)]
    ppermute x1, waiting for transfers between devices: 0.01 us -> 10.6 us  [local(): got = lax.ppermute(send, ('zh', 'core'), near_far[1])]
    all_to_all x0 -> x1, starting transfers between devices: none -> 8.62 us  [local(): parts = lax.all_to_all(chosen, ('x', 'core'), 0, 0)]
    all_to_all x1, waiting for transfers between devices: 6.34 us -> 0.01 us  [local(): blocks = lax.all_to_all(pieces, ('mp', 'root'), 0, 0)]
    all_to_all x1, blocking collectives: 12.3 us -> 17 us  [local(): mine = lax.all_to_all(mine, ('mp', 'root'), 0, 0)]
    ppermute x3, starting transfers between devices: 10.7 us -> 12.4 us  [shift(): lax.ppermute(value, axis, [(at, (at + step) % size) for at in range(size)])]
  transfers between devices with their start and end apart: 11 -> 12, of which waited for: 8 -> 9; matrix products, arithmetic and copies ran while one was open for 0% -> 0% of each run, Pallas kernels for 2% -> 2%
where the time goes in v12:
time: 117 us; the launch traced here: 116 us
  starting transfers between devices  59.5 us (51%)
  waiting for transfers between devices  26.5 us (23%)
  blocking collectives  17 us (15%)
  Pallas kernels  12 us (10%)
    all_to_all x1, blocking collectives, local(): mine = lax.all_to_all(mine, ('mp', 'root'), 0, 0)  17 us
    ppermute x3, starting transfers between devices, shift(): lax.ppermute(value, axis, [(at, (at + step) % size) for at in range(size)])  12.4 us
    ppermute x1, waiting for transfers between devices, local(): got = lax.ppermute(send, ('zh', 'core'), near_far[1])  10.6 us
    ppermute x1, starting transfers between devices, local(): got = lax.ppermute(send, 'core', swap)  8.79 us
    all_to_all x1, starting transfers between devices, local(): parts = lax.all_to_all(chosen, ('x', 'core'), 0, 0)  8.62 us
    all_to_all x1, waiting for transfers between devices, local(): total = lax.all_to_all(total, 'x', 0, 0)  7.45 us
    ppermute x1, starting transfers between devices, local(): got = lax.ppermute(send, ('zh', 'core'), near_far[0])  7.32 us
    ppermute x1, starting transfers between devices, local(): got = lax.ppermute(send, ('zh', 'core'), near_far[1])  6.15 us
  transfers between devices with their start and end apart: 12, of which 9 were waited for; matrix products, arithmetic and copies ran while one was open for 0% of the time, Pallas kernels for 2%

profile of v12, /device:TPU:1, one launch (start us, length us, event | category | flops | bytes accessed | tf_op | source)
XLA Modules:
  0.0 115.9 jit_solution(17841452358055061426)
XLA Ops:
  0.6 2.3 %other_half.1 = (bf16[512,1024]{1,0:T(8,128)(2,1)S(1)}, bf16[512,512]{1,0:T(8,128)(2,1)S(1)}, bf16[1024,512]{1,0:T(8,128)(2,1)S(1)}) custom-call(s32[1]{0:T(128)} %bitcast.5.index_ref, bf16[1024,512]{1,0:T(8,128)(2,1)} %acts_ref.1, bf16[1024,1024]{1,0:T(8,128)(2,1)} %grads_ref.1), custom_call_target="tpu_custom_call" | custom-call | flops 536870912 | bytes 3145728 | tf_op jit(solution)/shard_map/other_half/pallas_call | solution.py:80
  2.9 0.0 copy-start.1
  2.9 8.8 %collective-permute-start = (bf16[512,512]{1,0:T(8,128)(2,1)S(1)}, bf16[512,512]{1,0:T(8,128)(2,1)S(1)}, u32[]{:S(2)}, u32[]{:S(2)}) collective-permute-start(bf16[512,512]{1,0:T(8,128)(2,1)S(1)} %get-tuple-element.19), channel_id=1, source_target_pairs={{0,16},{16,0},{1,17},{17,1},{2,18},{18,2},{3,19},{19,3},{4,20},{20... | collective-permute-start | bytes 1572872 | tf_op jit(solution)/shard_map/ppermute | solution.py:284
  11.7 0.7 own_half.1.own_ref
  12.4 0.0 copy-start.4
  12.4 0.0 copy-start
  12.5 0.8 collective-permute-done.got_ref
  13.2 0.0 copy-done.1
  13.2 1.1 join.1
  14.3 3.5 %all-to-all-start = ((bf16[4,160,512]{2,1,0:T(8,128)(2,1)}), bf16[4,160,512]{2,1,0:T(8,128)(2,1)S(1)}, u32[]{:S(2)}, u32[]{:S(2)}) async-start(bf16[4,160,512]{2,1,0:T(8,128)(2,1)} %join.1), calls=%async_computation | async-start | bytes 1310720 | tf_op jit(solution)/shard_map/all_to_all | solution.py:295
  17.8 0.0 copy-start.2
  17.8 0.0 copy-done.4
  17.8 2.3 %collective-permute-start.1 = (bf16[16,512]{1,0:T(8,128)(2,1)S(1)}, bf16[16,512]{1,0:T(8,128)(2,1)S(1)}, u32[]{:S(2)}, u32[]{:S(2)}) collective-permute-start(bf16[16,512]{1,0:T(8,128)(2,1)S(1)} %get-tuple-element.31), channel_id=1, source_target_pairs={{0,16},{16,0},{1,17},{17,1},{2,18},{18,2},{3,19},{19,3},{4,20},{20... | collective-permute-start | bytes 49160 | tf_op jit(solution)/shard_map/ppermute | solution.py:297
  20.1 0.1 stack.23.info_ref
  20.2 0.7 collective-permute-done.1.theirs_ref
  21.0 7.4 %all-to-all-done.parts_ref = bf16[4,160,512]{2,1,0:T(8,128)(2,1)S(1)} async-done(((bf16[4,160,512]{2,1,0:T(8,128)(2,1)}), bf16[4,160,512]{2,1,0:T(8,128)(2,1)S(1)}, u32[]{:S(2)}, u32[]{:S(2)}) %all-to-all-start) | async-done | bytes 655392 | tf_op jit(solution)/shard_map/all_to_all | solution.py:295
  28.4 0.0 copy-done
  28.4 0.7 sum_x.1
  29.1 7.3 %collective-permute-start.2 = (bf16[160,512]{1,0:T(8,128)(2,1)S(1)}, bf16[160,512]{1,0:T(8,128)(2,1)S(1)}, u32[]{:S(2)}, u32[]{:S(2)}) collective-permute-start(bf16[160,512]{1,0:T(8,128)(2,1)S(1)} %get-tuple-element.22), channel_id=1, source_target_pairs={{0,32},{16,112},{32,0},{48,80},{64,96},{80,48},{96,64},{112,16},{1... | collective-permute-start | bytes 491528 | tf_op jit(solution)/shard_map/ppermute | solution.py:318
  36.4 3.2 %collective-permute-start.4 = (bf16[128,512]{1,0:T(8,128)(2,1)S(1)}, bf16[128,512]{1,0:T(8,128)(2,1)S(1)}, u32[]{:S(2)}, u32[]{:S(2)}) collective-permute-start(bf16[128,512]{1,0:T(8,128)(2,1)S(1)} %get-tuple-element.24.low_ref), channel_id=1, source_target_pairs={{0,4},{4,8},{8,12},{12,0},{1,5},{5,9},{9,13},{13,1},{2,6},{6,10},{... | collective-permute-start | bytes 393224 | tf_op jit(solution)/shard_map/ppermute | solution.py:112
  39.6 1.9 %collective-permute-start.3 = (bf16[64,512]{1,0:T(8,128)(2,1)S(1)}, bf16[64,512]{1,0:T(8,128)(2,1)S(1)}, u32[]{:S(2)}, u32[]{:S(2)}) collective-permute-start(bf16[64,512]{1,0:T(8,128)(2,1)S(1)} %get-tuple-element.23), channel_id=1, source_target_pairs={{0,16},{16,0},{1,17},{17,1},{2,18},{18,2},{3,19},{19,3},{4,20},{20... | collective-permute-start | bytes 196616 | tf_op jit(solution)/shard_map/ppermute | solution.py:319
  41.5 1.2 %collective-permute-done.3.refs_0_.theirs_ref = bf16[64,512]{1,0:T(8,128)(2,1)S(1)} collective-permute-done((bf16[64,512]{1,0:T(8,128)(2,1)S(1)}, bf16[64,512]{1,0:T(8,128)(2,1)S(1)}, u32[]{:S(2)}, u32[]{:S(2)}) %collective-permute-start.3) | collective-permute-done | bytes 65568 | tf_op jit(solution)/shard_map/ppermute | solution.py:319
  42.7 0.6 collective-permute-done.4.refs_1_.one
  43.4 0.0 collective-permute-done.2.got_ref
  43.4 6.1 %collective-permute-start.5 = (bf16[192,512]{1,0:T(8,128)(2,1)S(1)}, bf16[192,512]{1,0:T(8,128)(2,1)S(1)}, u32[]{:S(2)}, u32[]{:S(2)}) collective-permute-start(bf16[192,512]{1,0:T(8,128)(2,1)S(1)} %get-tuple-element.26.sent_ref), channel_id=1, source_target_pairs={{0,96},{16,48},{32,64},{48,16},{64,32},{80,112},{96,0},{112,80},{1... | collective-permute-start | bytes 589832 | tf_op jit(solution)/shard_map/ppermute | solution.py:328
  49.6 10.6 %collective-permute-done.5.got_ref = bf16[192,512]{1,0:T(8,128)(2,1)S(1)} collective-permute-done((bf16[192,512]{1,0:T(8,128)(2,1)S(1)}, bf16[192,512]{1,0:T(8,128)(2,1)S(1)}, u32[]{:S(2)}, u32[]{:S(2)}) %collective-permute-start.5) | collective-permute-done | bytes 196640 | tf_op jit(solution)/shard_map/ppermute | solution.py:328
  60.2 0.0 copy-start.3
  60.2 0.7 pack.1
  60.9 4.5 %all-to-all-start.1 = ((bf16[16,2,16,128]{3,2,1,0:T(8,128)(2,1)}), bf16[16,2,16,128]{3,2,1,0:T(8,128)(2,1)S(1)}, u32[]{:S(2)}, u32[]{:S(2)}) async-start(bf16[16,2,16,128]{3,2,1,0:T(8,128)(2,1)} %bitcast.9), calls=%async_computation.1 | async-start | bytes 262144 | tf_op jit(solution)/shard_map/all_to_all | solution.py:338
  65.4 4.8 %collective-permute-start.6 = (bf16[128,512]{1,0:T(8,128)(2,1)S(1)}, bf16[128,512]{1,0:T(8,128)(2,1)S(1)}, u32[]{:S(2)}, u32[]{:S(2)}) collective-permute-start(bf16[128,512]{1,0:T(8,128)(2,1)S(1)} %get-tuple-element.28), channel_id=1, source_target_pairs={{0,8},{4,12},{8,0},{12,4},{1,9},{5,13},{9,1},{13,5},{2,10},{6,14},... | collective-permute-start | bytes 393224 | tf_op jit(solution)/shard_map/ppermute | solution.py:112
  70.2 0.9 update.1.total_ref
  71.1 1.9 %collective-permute-done.6.refs_0_.two = bf16[128,512]{1,0:T(8,128)(2,1)S(1)} collective-permute-done((bf16[128,512]{1,0:T(8,128)(2,1)S(1)}, bf16[128,512]{1,0:T(8,128)(2,1)S(1)}, u32[]{:S(2)}, u32[]{:S(2)}) %collective-permute-start.6) | collective-permute-done | bytes 131104 | tf_op jit(solution)/shard_map/ppermute | solution.py:112
  72.9 0.0 all-to-all-done.1.blocks_ref
  72.9 0.0 copy-done.2
  72.9 1.2 %choose.1 = bf16[8,5,16,128]{3,2,1,0:T(8,128)(2,1)} custom-call(s32[5]{0:T(128)S(1)} %stack.23.info_ref, s32[16]{0:T(128)S(1)} %copy-done.2, bf16[16,2,16,128]{3,2,1,0:T(8,128)(2,1)S(1)} %all-to-all-done.1.blocks_ref, f32[128,512]{1,0:T(8,128)S(1)} %update.1.total_ref, bf16[128,512]{1,0:T(8,128)(2,1)S(1)} %collective-permute-done.6.refs_0_.two), custom_call_target="tpu_custom_call" | custom-call | tf_op jit(solution)/shard_map/choose/pallas_call | solution.py:349
  74.2 8.6 %all-to-all-start.2 = ((bf16[8,5,16,128]{3,2,1,0:T(8,128)(2,1)}), bf16[8,5,16,128]{3,2,1,0:T(8,128)(2,1)S(1)}, u32[]{:S(2)}, u32[]{:S(2)}) async-start(bf16[8,5,16,128]{3,2,1,0:T(8,128)(2,1)} %choose.1), calls=%async_computation.2 | async-start | bytes 327680 | tf_op jit(solution)/shard_map/all_to_all | solution.py:356
  82.8 4.4 %collective-permute-start.7 = (bf16[128,512]{1,0:T(8,128)(2,1)S(1)}, bf16[128,512]{1,0:T(8,128)(2,1)S(1)}, u32[]{:S(2)}, u32[]{:S(2)}) collective-permute-start(bf16[128,512]{1,0:T(8,128)(2,1)S(1)} %get-tuple-element.28), channel_id=1, source_target_pairs={{0,12},{4,0},{8,4},{12,8},{1,13},{5,1},{9,5},{13,9},{2,14},{6,2},{... | collective-permute-start | bytes 393224 | tf_op jit(solution)/shard_map/ppermute | solution.py:112
  87.2 2.7 %collective-permute-done.7.refs_0_.three = bf16[128,512]{1,0:T(8,128)(2,1)S(1)} collective-permute-done((bf16[128,512]{1,0:T(8,128)(2,1)S(1)}, bf16[128,512]{1,0:T(8,128)(2,1)S(1)}, u32[]{:S(2)}, u32[]{:S(2)}) %collective-permute-start.7) | collective-permute-done | bytes 131104 | tf_op jit(solution)/shard_map/ppermute | solution.py:112
  90.0 0.0 all-to-all-done.2.parts_ref
  90.0 0.6 spread.1
  90.6 17.0 %all_to_all.20 = bf16[16,4,16,128]{3,2,1,0:T(8,128)(2,1)S(1)} all-to-all(bf16[16,4,16,128]{3,2,1,0:T(8,128)(2,1)S(1)} %spread.1), channel_id=1, replica_groups=mesh['x'=4,'zh'=4,'core'=2,'mp'=4,'root'=4] {'mp','root'}, dimensions={0} | all-to-all | bytes 524288 | tf_op jit(solution)/shard_map/all_to_all | solution.py:364
  107.5 4.1 %collective-permute-start.8 = (bf16[16,4,16,128]{3,2,1,0:T(8,128)(2,1)S(1)}, bf16[16,4,16,128]{3,2,1,0:T(8,128)(2,1)S(1)}, u32[]{:S(2)}, u32[]{:S(2)}) collective-permute-start(bf16[16,4,16,128]{3,2,1,0:T(8,128)(2,1)S(1)} %all_to_all.20), channel_id=1, source_target_pairs={{0,16},{16,0},{1,17},{17,1},{2,18},{18,2},{3,19},{19,3},{4,20},{20... | collective-permute-start | bytes 786440 | tf_op jit(solution)/shard_map/ppermute | solution.py:365
  111.6 0.6 finish.1
  112.2 0.5 collective-permute-done.8
  112.7 0.0 copy-done.3
  112.7 3.2 %refresh.1 = (f32[128,512]{1,0:T(8,128)}, f32[128,512]{1,0:T(8,128)}) custom-call(s32[5]{0:T(128)S(1)} %stack.23.info_ref, s32[16]{0:T(128)S(1)} %copy-done.3, bf16[4,4,4,16,128]{4,3,2,1,0:T(8,128)(2,1)S(1)} %bitcast.20, bf16[4,4,4,16,128]{4,3,2,1,0:T(8,128)(2,1)S(1)} %bitcast.21, f32[128,512]{1,0:T(8,128)S(1)} %bitcast.19, ...), custom_call_target="tpu_custom_call" | custom-call | flops 603979776 | bytes 1048576 | tf_op jit(solution)/shard_map/refresh/pallas_call | solution.py:369
  (2 shorter events, 0.1 us)
Async XLA Ops:
  2.9 10.3 %copy-start.1 = (bf16[1,2,16,512]{3,2,1,0:T(8,128)(2,1)S(1)}, bf16[1,2,16,512]{3,2,1,0:T(8,128)(2,1)}, u32[]{:S(2)}) copy-start(bf16[1,2,16,512]{3,2,1,0:T(8,128)(2,1)} %prec_ref.1) | copy-start | bytes 98308
  2.9 10.3 %collective-permute-start = (bf16[512,512]{1,0:T(8,128)(2,1)S(1)}, bf16[512,512]{1,0:T(8,128)(2,1)S(1)}, u32[]{:S(2)}, u32[]{:S(2)}) collective-permute-start(bf16[512,512]{1,0:T(8,128)(2,1)S(1)} %get-tuple-element.19), channel_id=1, source_target_pairs={{0,16},{16,0},{1,17},{17,1},{2,18},{18,2},{3,19},{19,3},{4,20},{20... | collective-permute-start | bytes 1572872 | tf_op jit(solution)/shard_map/ppermute | solution.py:284
  12.4 5.4 %copy-start.4 = (bf16[1,2,16,512]{3,2,1,0:T(8,128)(2,1)S(1)}, bf16[1,2,16,512]{3,2,1,0:T(8,128)(2,1)}, u32[]{:S(2)}) copy-start(bf16[1,2,16,512]{3,2,1,0:T(8,128)(2,1)} %param.10) | copy-start | bytes 98308
  12.4 16.0 %copy-start = (f32[1,128,512]{2,1,0:T(8,128)S(1)}, f32[1,128,512]{2,1,0:T(8,128)}, u32[]{:S(2)}) copy-start(f32[1,128,512]{2,1,0:T(8,128)} %param.11) | copy-start | bytes 786436
  14.3 14.1 %all-to-all-start = ((bf16[4,160,512]{2,1,0:T(8,128)(2,1)}), bf16[4,160,512]{2,1,0:T(8,128)(2,1)S(1)}, u32[]{:S(2)}, u32[]{:S(2)}) async-start(bf16[4,160,512]{2,1,0:T(8,128)(2,1)} %join.1), calls=%async_computation | async-start | bytes 1310720 | tf_op jit(solution)/shard_map/all_to_all | solution.py:295
  17.8 55.1 %copy-start.2 = (s32[16]{0:T(128)S(1)}, s32[16]{0:T(128)}, u32[]{:S(2)}) copy-start(s32[16]{0:T(128)} %listed_ref.3) | copy-start | bytes 196
  17.8 3.1 %collective-permute-start.1 = (bf16[16,512]{1,0:T(8,128)(2,1)S(1)}, bf16[16,512]{1,0:T(8,128)(2,1)S(1)}, u32[]{:S(2)}, u32[]{:S(2)}) collective-permute-start(bf16[16,512]{1,0:T(8,128)(2,1)S(1)} %get-tuple-element.31), channel_id=1, source_target_pairs={{0,16},{16,0},{1,17},{17,1},{2,18},{18,2},{3,19},{19,3},{4,20},{20... | collective-permute-start | bytes 49160 | tf_op jit(solution)/shard_map/ppermute | solution.py:297
  29.1 14.3 %collective-permute-start.2 = (bf16[160,512]{1,0:T(8,128)(2,1)S(1)}, bf16[160,512]{1,0:T(8,128)(2,1)S(1)}, u32[]{:S(2)}, u32[]{:S(2)}) collective-permute-start(bf16[160,512]{1,0:T(8,128)(2,1)S(1)} %get-tuple-element.22), channel_id=1, source_target_pairs={{0,32},{16,112},{32,0},{48,80},{64,96},{80,48},{96,64},{112,16},{1... | collective-permute-start | bytes 491528 | tf_op jit(solution)/shard_map/ppermute | solution.py:318
  36.4 7.0 %collective-permute-start.4 = (bf16[128,512]{1,0:T(8,128)(2,1)S(1)}, bf16[128,512]{1,0:T(8,128)(2,1)S(1)}, u32[]{:S(2)}, u32[]{:S(2)}) collective-permute-start(bf16[128,512]{1,0:T(8,128)(2,1)S(1)} %get-tuple-element.24.low_ref), channel_id=1, source_target_pairs={{0,4},{4,8},{8,12},{12,0},{1,5},{5,9},{9,13},{13,1},{2,6},{6,10},{... | collective-permute-start | bytes 393224 | tf_op jit(solution)/shard_map/ppermute | solution.py:112
  39.6 3.1 %collective-permute-start.3 = (bf16[64,512]{1,0:T(8,128)(2,1)S(1)}, bf16[64,512]{1,0:T(8,128)(2,1)S(1)}, u32[]{:S(2)}, u32[]{:S(2)}) collective-permute-start(bf16[64,512]{1,0:T(8,128)(2,1)S(1)} %get-tuple-element.23), channel_id=1, source_target_pairs={{0,16},{16,0},{1,17},{17,1},{2,18},{18,2},{3,19},{19,3},{4,20},{20... | collective-permute-start | bytes 196616 | tf_op jit(solution)/shard_map/ppermute | solution.py:319
  43.4 16.7 %collective-permute-start.5 = (bf16[192,512]{1,0:T(8,128)(2,1)S(1)}, bf16[192,512]{1,0:T(8,128)(2,1)S(1)}, u32[]{:S(2)}, u32[]{:S(2)}) collective-permute-start(bf16[192,512]{1,0:T(8,128)(2,1)S(1)} %get-tuple-element.26.sent_ref), channel_id=1, source_target_pairs={{0,96},{16,48},{32,64},{48,16},{64,32},{80,112},{96,0},{112,80},{1... | collective-permute-start | bytes 589832 | tf_op jit(solution)/shard_map/ppermute | solution.py:328
  60.2 52.6 %copy-start.3 = (s32[16]{0:T(128)S(1)}, s32[16]{0:T(128)}, u32[]{:S(2)}) copy-start(s32[16]{0:T(128)} %owner_ref.1) | copy-start | bytes 196
  60.9 12.1 %all-to-all-start.1 = ((bf16[16,2,16,128]{3,2,1,0:T(8,128)(2,1)}), bf16[16,2,16,128]{3,2,1,0:T(8,128)(2,1)S(1)}, u32[]{:S(2)}, u32[]{:S(2)}) async-start(bf16[16,2,16,128]{3,2,1,0:T(8,128)(2,1)} %bitcast.9), calls=%async_computation.1 | async-start | bytes 262144 | tf_op jit(solution)/shard_map/all_to_all | solution.py:338
  65.4 7.6 %collective-permute-start.6 = (bf16[128,512]{1,0:T(8,128)(2,1)S(1)}, bf16[128,512]{1,0:T(8,128)(2,1)S(1)}, u32[]{:S(2)}, u32[]{:S(2)}) collective-permute-start(bf16[128,512]{1,0:T(8,128)(2,1)S(1)} %get-tuple-element.28), channel_id=1, source_target_pairs={{0,8},{4,12},{8,0},{12,4},{1,9},{5,13},{9,1},{13,5},{2,10},{6,14},... | collective-permute-start | bytes 393224 | tf_op jit(solution)/shard_map/ppermute | solution.py:112
  74.2 15.8 %all-to-all-start.2 = ((bf16[8,5,16,128]{3,2,1,0:T(8,128)(2,1)}), bf16[8,5,16,128]{3,2,1,0:T(8,128)(2,1)S(1)}, u32[]{:S(2)}, u32[]{:S(2)}) async-start(bf16[8,5,16,128]{3,2,1,0:T(8,128)(2,1)} %choose.1), calls=%async_computation.2 | async-start | bytes 327680 | tf_op jit(solution)/shard_map/all_to_all | solution.py:356
  82.8 7.1 %collective-permute-start.7 = (bf16[128,512]{1,0:T(8,128)(2,1)S(1)}, bf16[128,512]{1,0:T(8,128)(2,1)S(1)}, u32[]{:S(2)}, u32[]{:S(2)}) collective-permute-start(bf16[128,512]{1,0:T(8,128)(2,1)S(1)} %get-tuple-element.28), channel_id=1, source_target_pairs={{0,12},{4,0},{8,4},{12,8},{1,13},{5,1},{9,5},{13,9},{2,14},{6,2},{... | collective-permute-start | bytes 393224 | tf_op jit(solution)/shard_map/ppermute | solution.py:112
  107.5 5.2 %collective-permute-start.8 = (bf16[16,4,16,128]{3,2,1,0:T(8,128)(2,1)S(1)}, bf16[16,4,16,128]{3,2,1,0:T(8,128)(2,1)S(1)}, u32[]{:S(2)}, u32[]{:S(2)}) collective-permute-start(bf16[16,4,16,128]{3,2,1,0:T(8,128)(2,1)S(1)} %all_to_all.20), channel_id=1, source_target_pairs={{0,16},{16,0},{1,17},{17,1},{2,18},{18,2},{3,19},{19,3},{4,20},{20... | collective-permute-start | bytes 786440 | tf_op jit(solution)/shard_map/ppermute | solution.py:365

commit v13 on v12

--- a/solution.py
+++ b/solution.py
@@ -152,7 +152,8 @@
     old_low[...] = old_ref[...].astype(BF16)
 
 
-def pack_kernel(scale, keep_ref, got_ref, pieces_ref):
+def pack_kernel(scale, keep_ref, got_ref, *refs):
+    pieces_ref = refs[-1]
     grad = ((keep_ref[...] + got_ref[:PART].astype(F32)) * scale).astype(BF16)
     n_mp, n_root, cores, rows, lanes = pieces_ref.shape
     for c in range(cores):
@@ -332,7 +333,8 @@
         "pack",
         [VMEM] * 2,
         [shape((n_mp, n_root, CORE, half, lanes))],
-    )(keep, got)
+        awaited=2,
+    )(keep, got, *olds[2:])
 
     pieces = pieces.reshape((n_mp * n_root,) + pieces.shape[2:])
     blocks = lax.all_to_all(pieces, ("mp", "root"), 0, 0)
@@ -351,16 +353,14 @@
         "choose",
         [SMEM, SMEM, VMEM, VMEM],
         [shape((X * CORE, 1 + B // lanes, half, lanes))],
-        awaited=1,
-    )(info, listed, blocks, total, olds[2])
+    )(info, listed, blocks, total)
     parts = lax.all_to_all(chosen, ("x", "core"), 0, 0)
     (mine,) = kernel_call(
         spread_kernel,
         "spread",
         [SMEM, SMEM, VMEM],
         [shape((n_mp * n_root, X, half, lanes))],
-        awaited=1,
-    )(info, listed, parts, olds[3])
+    )(info, listed, parts)
     mine = lax.all_to_all(mine, ("mp", "root"), 0, 0)
     theirs = lax.ppermute(mine, "core", swap)
     gathered = [value.reshape((n_mp, n_root) + value.shape[1:]) for value in (mine, theirs)]

time: 117 us -> 111 us (0.949)
  blocking collectives: 17 us -> 28.1 us
  starting transfers between devices: 59.5 us -> 48.5 us
  waiting for transfers between devices: 26.5 us -> 21.7 us
    all_to_all x0 -> x1, blocking collectives: none -> 15.8 us  [local(): parts = lax.all_to_all(chosen, ('x', 'core'), 0, 0)]
    ppermute x1, waiting for transfers between devices: 10.6 us -> 0.01 us  [local(): got = lax.ppermute(send, ('zh', 'core'), near_far[1])]
    all_to_all x1 -> x0, starting transfers between devices: 8.62 us -> none  [local(): parts = lax.all_to_all(chosen, ('x', 'core'), 0, 0)]
    all_to_all x1, waiting for transfers between devices: 0.01 us -> 6.34 us  [local(): blocks = lax.all_to_all(pieces, ('mp', 'root'), 0, 0)]
    all_to_all x1, blocking collectives: 17 us -> 12.3 us  [local(): mine = lax.all_to_all(mine, ('mp', 'root'), 0, 0)]
    ppermute x3, starting transfers between devices: 12.4 us -> 10.7 us  [shift(): lax.ppermute(value, axis, [(at, (at + step) % size) for at in range(size)])]
  transfers between devices with their start and end apart: 12 -> 11, of which waited for: 9 -> 8; matrix products, arithmetic and copies ran while one was open for 0% -> 0% of each run, Pallas kernels for 2% -> 2%
where the time goes in v13:
time: 111 us
  starting transfers between devices  48.5 us (44%)
  blocking collectives  28.1 us (25%)
  waiting for transfers between devices  21.7 us (20%)
  Pallas kernels  11.4 us (10%)
    all_to_all x1, blocking collectives, local(): parts = lax.all_to_all(chosen, ('x', 'core'), 0, 0)  15.8 us
    all_to_all x1, blocking collectives, local(): mine = lax.all_to_all(mine, ('mp', 'root'), 0, 0)  12.3 us
    ppermute x3, starting transfers between devices, shift(): lax.ppermute(value, axis, [(at, (at + step) % size) for at in range(size)])  10.7 us
    ppermute x1, starting transfers between devices, local(): got = lax.ppermute(send, 'core', swap)  8.79 us
    all_to_all x1, waiting for transfers between devices, local(): total = lax.all_to_all(total, 'x', 0, 0)  7.45 us
    ppermute x1, starting transfers between devices, local(): got = lax.ppermute(send, ('zh', 'core'), near_far[0])  7.32 us
    all_to_all x1, waiting for transfers between devices, local(): blocks = lax.all_to_all(pieces, ('mp', 'root'), 0, 0)  6.34 us
    ppermute x1, starting transfers between devices, local(): got = lax.ppermute(send, ('zh', 'core'), near_far[1])  6.15 us
  transfers between devices with their start and end apart: 11, of which 8 were waited for; matrix products, arithmetic and copies ran while one was open for 0% of the time, Pallas kernels for 2%

profile of v13, /device:TPU:1, one launch (start us, length us, event | category | flops | bytes accessed | tf_op | source)
XLA Modules:
  0.0 110.6 jit_solution(18078573124006684347)
XLA Ops:
  0.6 2.3 %other_half.1 = (bf16[512,1024]{1,0:T(8,128)(2,1)S(1)}, bf16[512,512]{1,0:T(8,128)(2,1)S(1)}, bf16[1024,512]{1,0:T(8,128)(2,1)S(1)}) custom-call(s32[1]{0:T(128)} %bitcast.5.index_ref, bf16[1024,512]{1,0:T(8,128)(2,1)} %acts_ref.1, bf16[1024,1024]{1,0:T(8,128)(2,1)} %grads_ref.1), custom_call_target="tpu_custom_call" | custom-call | flops 536870912 | bytes 3145728 | tf_op jit(solution)/shard_map/other_half/pallas_call | solution.py:80
  2.9 0.0 copy-start.1
  2.9 8.8 %collective-permute-start = (bf16[512,512]{1,0:T(8,128)(2,1)S(1)}, bf16[512,512]{1,0:T(8,128)(2,1)S(1)}, u32[]{:S(2)}, u32[]{:S(2)}) collective-permute-start(bf16[512,512]{1,0:T(8,128)(2,1)S(1)} %get-tuple-element.19), channel_id=1, source_target_pairs={{0,16},{16,0},{1,17},{17,1},{2,18},{18,2},{3,19},{19,3},{4,20},{20... | collective-permute-start | bytes 1572872 | tf_op jit(solution)/shard_map/ppermute | solution.py:285
  11.7 0.7 own_half.1.own_ref
  12.4 0.0 copy-start.4
  12.4 0.0 copy-start
  12.5 0.8 collective-permute-done.got_ref
  13.2 0.0 copy-done.1
  13.2 1.1 join.1
  14.3 3.5 %all-to-all-start = ((bf16[4,160,512]{2,1,0:T(8,128)(2,1)}), bf16[4,160,512]{2,1,0:T(8,128)(2,1)S(1)}, u32[]{:S(2)}, u32[]{:S(2)}) async-start(bf16[4,160,512]{2,1,0:T(8,128)(2,1)} %join.1), calls=%async_computation | async-start | bytes 1310720 | tf_op jit(solution)/shard_map/all_to_all | solution.py:296
  17.8 0.0 copy-start.2
  17.8 0.0 copy-done.4
  17.9 2.3 %collective-permute-start.1 = (bf16[16,512]{1,0:T(8,128)(2,1)S(1)}, bf16[16,512]{1,0:T(8,128)(2,1)S(1)}, u32[]{:S(2)}, u32[]{:S(2)}) collective-permute-start(bf16[16,512]{1,0:T(8,128)(2,1)S(1)} %get-tuple-element.31), channel_id=1, source_target_pairs={{0,16},{16,0},{1,17},{17,1},{2,18},{18,2},{3,19},{19,3},{4,20},{20... | collective-permute-start | bytes 49160 | tf_op jit(solution)/shard_map/ppermute | solution.py:298
  20.2 0.1 stack.23.info_ref
  20.2 0.7 collective-permute-done.1.theirs_ref
  21.0 7.4 %all-to-all-done.parts_ref = bf16[4,160,512]{2,1,0:T(8,128)(2,1)S(1)} async-done(((bf16[4,160,512]{2,1,0:T(8,128)(2,1)}), bf16[4,160,512]{2,1,0:T(8,128)(2,1)S(1)}, u32[]{:S(2)}, u32[]{:S(2)}) %all-to-all-start) | async-done | bytes 655392 | tf_op jit(solution)/shard_map/all_to_all | solution.py:296
  28.4 0.0 copy-done
  28.4 0.7 sum_x.1
  29.1 7.3 %collective-permute-start.2 = (bf16[160,512]{1,0:T(8,128)(2,1)S(1)}, bf16[160,512]{1,0:T(8,128)(2,1)S(1)}, u32[]{:S(2)}, u32[]{:S(2)}) collective-permute-start(bf16[160,512]{1,0:T(8,128)(2,1)S(1)} %get-tuple-element.22), channel_id=1, source_target_pairs={{0,32},{16,112},{32,0},{48,80},{64,96},{80,48},{96,64},{112,16},{1... | collective-permute-start | bytes 491528 | tf_op jit(solution)/shard_map/ppermute | solution.py:319
  36.4 3.2 %collective-permute-start.4 = (bf16[128,512]{1,0:T(8,128)(2,1)S(1)}, bf16[128,512]{1,0:T(8,128)(2,1)S(1)}, u32[]{:S(2)}, u32[]{:S(2)}) collective-permute-start(bf16[128,512]{1,0:T(8,128)(2,1)S(1)} %get-tuple-element.24.low_ref), channel_id=1, source_target_pairs={{0,4},{4,8},{8,12},{12,0},{1,5},{5,9},{9,13},{13,1},{2,6},{6,10},{... | collective-permute-start | bytes 393224 | tf_op jit(solution)/shard_map/ppermute | solution.py:112
  39.6 1.9 %collective-permute-start.3 = (bf16[64,512]{1,0:T(8,128)(2,1)S(1)}, bf16[64,512]{1,0:T(8,128)(2,1)S(1)}, u32[]{:S(2)}, u32[]{:S(2)}) collective-permute-start(bf16[64,512]{1,0:T(8,128)(2,1)S(1)} %get-tuple-element.23), channel_id=1, source_target_pairs={{0,16},{16,0},{1,17},{17,1},{2,18},{18,2},{3,19},{19,3},{4,20},{20... | collective-permute-start | bytes 196616 | tf_op jit(solution)/shard_map/ppermute | solution.py:320
  41.5 1.2 %collective-permute-done.3.refs_0_.theirs_ref = bf16[64,512]{1,0:T(8,128)(2,1)S(1)} collective-permute-done((bf16[64,512]{1,0:T(8,128)(2,1)S(1)}, bf16[64,512]{1,0:T(8,128)(2,1)S(1)}, u32[]{:S(2)}, u32[]{:S(2)}) %collective-permute-start.3) | collective-permute-done | bytes 65568 | tf_op jit(solution)/shard_map/ppermute | solution.py:320
  42.8 0.6 collective-permute-done.4.refs_1_.one
  43.4 0.0 collective-permute-done.2.got_ref
  43.4 6.1 %collective-permute-start.5 = (bf16[192,512]{1,0:T(8,128)(2,1)S(1)}, bf16[192,512]{1,0:T(8,128)(2,1)S(1)}, u32[]{:S(2)}, u32[]{:S(2)}) collective-permute-start(bf16[192,512]{1,0:T(8,128)(2,1)S(1)} %get-tuple-element.26.sent_ref), channel_id=1, source_target_pairs={{0,96},{16,48},{32,64},{48,16},{64,32},{80,112},{96,0},{112,80},{1... | collective-permute-start | bytes 589832 | tf_op jit(solution)/shard_map/ppermute | solution.py:329
  49.6 4.8 %collective-permute-start.6 = (bf16[128,512]{1,0:T(8,128)(2,1)S(1)}, bf16[128,512]{1,0:T(8,128)(2,1)S(1)}, u32[]{:S(2)}, u32[]{:S(2)}) collective-permute-start(bf16[128,512]{1,0:T(8,128)(2,1)S(1)} %get-tuple-element.27), channel_id=1, source_target_pairs={{0,8},{4,12},{8,0},{12,4},{1,9},{5,13},{9,1},{13,5},{2,10},{6,14},... | collective-permute-start | bytes 393224 | tf_op jit(solution)/shard_map/ppermute | solution.py:112
  54.4 2.7 %collective-permute-start.7 = (bf16[128,512]{1,0:T(8,128)(2,1)S(1)}, bf16[128,512]{1,0:T(8,128)(2,1)S(1)}, u32[]{:S(2)}, u32[]{:S(2)}) collective-permute-start(bf16[128,512]{1,0:T(8,128)(2,1)S(1)} %get-tuple-element.27), channel_id=1, source_target_pairs={{0,12},{4,0},{8,4},{12,8},{1,13},{5,1},{9,5},{13,9},{2,14},{6,2},{... | collective-permute-start | bytes 393224 | tf_op jit(solution)/shard_map/ppermute | solution.py:112
  57.1 0.0 collective-permute-done.6.refs_0_.two
  57.1 4.0 %collective-permute-done.7.refs_1_.three = bf16[128,512]{1,0:T(8,128)(2,1)S(1)} collective-permute-done((bf16[128,512]{1,0:T(8,128)(2,1)S(1)}, bf16[128,512]{1,0:T(8,128)(2,1)S(1)}, u32[]{:S(2)}, u32[]{:S(2)}) %collective-permute-start.7) | collective-permute-done | bytes 131104 | tf_op jit(solution)/shard_map/ppermute | solution.py:112
  61.2 0.0 collective-permute-done.5.got_ref
  61.2 0.0 copy-start.3
  61.2 0.7 pack.1
  61.9 3.8 %all-to-all-start.1 = ((bf16[16,2,16,128]{3,2,1,0:T(8,128)(2,1)}), bf16[16,2,16,128]{3,2,1,0:T(8,128)(2,1)S(1)}, u32[]{:S(2)}, u32[]{:S(2)}) async-start(bf16[16,2,16,128]{3,2,1,0:T(8,128)(2,1)} %bitcast.9), calls=%async_computation.1 | async-start | bytes 262144 | tf_op jit(solution)/shard_map/all_to_all | solution.py:340
  65.6 0.9 update.1.total_ref
  66.5 6.3 %all-to-all-done.1.blocks_ref = bf16[16,2,16,128]{3,2,1,0:T(8,128)(2,1)S(1)} async-done(((bf16[16,2,16,128]{3,2,1,0:T(8,128)(2,1)}), bf16[16,2,16,128]{3,2,1,0:T(8,128)(2,1)S(1)}, u32[]{:S(2)}, u32[]{:S(2)}) %all-to-all-start.1) | async-done | bytes 131104 | tf_op jit(solution)/shard_map/all_to_all | solution.py:340
  72.9 0.0 copy-done.2
  72.9 0.6 choose.1
  73.5 15.8 %all_to_all.20.parts_ref = bf16[8,5,16,128]{3,2,1,0:T(8,128)(2,1)S(1)} all-to-all(bf16[8,5,16,128]{3,2,1,0:T(8,128)(2,1)S(1)} %choose.1), channel_id=1, replica_groups=mesh['x'=4,'zh'=4,'core'=2,'mp'=4,'root'=4] {'x','core'}, dimensions={0} | all-to-all | bytes 327680 | tf_op jit(solution)/shard_map/all_to_all | solution.py:357
  89.3 0.6 spread.1
  89.9 12.3 %all_to_all.21 = bf16[16,4,16,128]{3,2,1,0:T(8,128)(2,1)S(1)} all-to-all(bf16[16,4,16,128]{3,2,1,0:T(8,128)(2,1)S(1)} %spread.1), channel_id=1, replica_groups=mesh['x'=4,'zh'=4,'core'=2,'mp'=4,'root'=4] {'mp','root'}, dimensions={0} | all-to-all | bytes 524288 | tf_op jit(solution)/shard_map/all_to_all | solution.py:364
  102.1 4.1 %collective-permute-start.8 = (bf16[16,4,16,128]{3,2,1,0:T(8,128)(2,1)S(1)}, bf16[16,4,16,128]{3,2,1,0:T(8,128)(2,1)S(1)}, u32[]{:S(2)}, u32[]{:S(2)}) collective-permute-start(bf16[16,4,16,128]{3,2,1,0:T(8,128)(2,1)S(1)} %all_to_all.21), channel_id=1, source_target_pairs={{0,16},{16,0},{1,17},{17,1},{2,18},{18,2},{3,19},{19,3},{4,20},{20... | collective-permute-start | bytes 786440 | tf_op jit(solution)/shard_map/ppermute | solution.py:365
  106.2 0.6 finish.1
  106.9 0.5 collective-permute-done.8
  107.4 0.0 copy-done.3
  107.4 3.2 %refresh.1 = (f32[128,512]{1,0:T(8,128)}, f32[128,512]{1,0:T(8,128)}) custom-call(s32[5]{0:T(128)S(1)} %stack.23.info_ref, s32[16]{0:T(128)S(1)} %copy-done.3, bf16[4,4,4,16,128]{4,3,2,1,0:T(8,128)(2,1)S(1)} %bitcast.20, bf16[4,4,4,16,128]{4,3,2,1,0:T(8,128)(2,1)S(1)} %bitcast.21, f32[128,512]{1,0:T(8,128)S(1)} %bitcast.19, ...), custom_call_target="tpu_custom_call" | custom-call | flops 603979776 | bytes 1048576 | tf_op jit(solution)/shard_map/refresh/pallas_call | solution.py:369
  (2 shorter events, 0.1 us)
Async XLA Ops:
  2.9 10.3 %copy-start.1 = (bf16[1,2,16,512]{3,2,1,0:T(8,128)(2,1)S(1)}, bf16[1,2,16,512]{3,2,1,0:T(8,128)(2,1)}, u32[]{:S(2)}) copy-start(bf16[1,2,16,512]{3,2,1,0:T(8,128)(2,1)} %prec_ref.1) | copy-start | bytes 98308
  2.9 10.3 %collective-permute-start = (bf16[512,512]{1,0:T(8,128)(2,1)S(1)}, bf16[512,512]{1,0:T(8,128)(2,1)S(1)}, u32[]{:S(2)}, u32[]{:S(2)}) collective-permute-start(bf16[512,512]{1,0:T(8,128)(2,1)S(1)} %get-tuple-element.19), channel_id=1, source_target_pairs={{0,16},{16,0},{1,17},{17,1},{2,18},{18,2},{3,19},{19,3},{4,20},{20... | collective-permute-start | bytes 1572872 | tf_op jit(solution)/shard_map/ppermute | solution.py:285
  12.4 5.4 %copy-start.4 = (bf16[1,2,16,512]{3,2,1,0:T(8,128)(2,1)S(1)}, bf16[1,2,16,512]{3,2,1,0:T(8,128)(2,1)}, u32[]{:S(2)}) copy-start(bf16[1,2,16,512]{3,2,1,0:T(8,128)(2,1)} %param.10) | copy-start | bytes 98308
  12.4 16.0 %copy-start = (f32[1,128,512]{2,1,0:T(8,128)S(1)}, f32[1,128,512]{2,1,0:T(8,128)}, u32[]{:S(2)}) copy-start(f32[1,128,512]{2,1,0:T(8,128)} %param.11) | copy-start | bytes 786436
  14.3 14.1 %all-to-all-start = ((bf16[4,160,512]{2,1,0:T(8,128)(2,1)}), bf16[4,160,512]{2,1,0:T(8,128)(2,1)S(1)}, u32[]{:S(2)}, u32[]{:S(2)}) async-start(bf16[4,160,512]{2,1,0:T(8,128)(2,1)} %join.1), calls=%async_computation | async-start | bytes 1310720 | tf_op jit(solution)/shard_map/all_to_all | solution.py:296
  17.8 55.1 %copy-start.2 = (s32[16]{0:T(128)S(1)}, s32[16]{0:T(128)}, u32[]{:S(2)}) copy-start(s32[16]{0:T(128)} %listed_ref.3) | copy-start | bytes 196
  17.9 3.1 %collective-permute-start.1 = (bf16[16,512]{1,0:T(8,128)(2,1)S(1)}, bf16[16,512]{1,0:T(8,128)(2,1)S(1)}, u32[]{:S(2)}, u32[]{:S(2)}) collective-permute-start(bf16[16,512]{1,0:T(8,128)(2,1)S(1)} %get-tuple-element.31), channel_id=1, source_target_pairs={{0,16},{16,0},{1,17},{17,1},{2,18},{18,2},{3,19},{19,3},{4,20},{20... | collective-permute-start | bytes 49160 | tf_op jit(solution)/shard_map/ppermute | solution.py:298
  29.1 14.3 %collective-permute-start.2 = (bf16[160,512]{1,0:T(8,128)(2,1)S(1)}, bf16[160,512]{1,0:T(8,128)(2,1)S(1)}, u32[]{:S(2)}, u32[]{:S(2)}) collective-permute-start(bf16[160,512]{1,0:T(8,128)(2,1)S(1)} %get-tuple-element.22), channel_id=1, source_target_pairs={{0,32},{16,112},{32,0},{48,80},{64,96},{80,48},{96,64},{112,16},{1... | collective-permute-start | bytes 491528 | tf_op jit(solution)/shard_map/ppermute | solution.py:319
  36.4 7.0 %collective-permute-start.4 = (bf16[128,512]{1,0:T(8,128)(2,1)S(1)}, bf16[128,512]{1,0:T(8,128)(2,1)S(1)}, u32[]{:S(2)}, u32[]{:S(2)}) collective-permute-start(bf16[128,512]{1,0:T(8,128)(2,1)S(1)} %get-tuple-element.24.low_ref), channel_id=1, source_target_pairs={{0,4},{4,8},{8,12},{12,0},{1,5},{5,9},{9,13},{13,1},{2,6},{6,10},{... | collective-permute-start | bytes 393224 | tf_op jit(solution)/shard_map/ppermute | solution.py:112
  39.6 3.1 %collective-permute-start.3 = (bf16[64,512]{1,0:T(8,128)(2,1)S(1)}, bf16[64,512]{1,0:T(8,128)(2,1)S(1)}, u32[]{:S(2)}, u32[]{:S(2)}) collective-permute-start(bf16[64,512]{1,0:T(8,128)(2,1)S(1)} %get-tuple-element.23), channel_id=1, source_target_pairs={{0,16},{16,0},{1,17},{17,1},{2,18},{18,2},{3,19},{19,3},{4,20},{20... | collective-permute-start | bytes 196616 | tf_op jit(solution)/shard_map/ppermute | solution.py:320
  43.4 17.7 %collective-permute-start.5 = (bf16[192,512]{1,0:T(8,128)(2,1)S(1)}, bf16[192,512]{1,0:T(8,128)(2,1)S(1)}, u32[]{:S(2)}, u32[]{:S(2)}) collective-permute-start(bf16[192,512]{1,0:T(8,128)(2,1)S(1)} %get-tuple-element.26.sent_ref), channel_id=1, source_target_pairs={{0,96},{16,48},{32,64},{48,16},{64,32},{80,112},{96,0},{112,80},{1... | collective-permute-start | bytes 589832 | tf_op jit(solution)/shard_map/ppermute | solution.py:329
  49.6 7.5 %collective-permute-start.6 = (bf16[128,512]{1,0:T(8,128)(2,1)S(1)}, bf16[128,512]{1,0:T(8,128)(2,1)S(1)}, u32[]{:S(2)}, u32[]{:S(2)}) collective-permute-start(bf16[128,512]{1,0:T(8,128)(2,1)S(1)} %get-tuple-element.27), channel_id=1, source_target_pairs={{0,8},{4,12},{8,0},{12,4},{1,9},{5,13},{9,1},{13,5},{2,10},{6,14},... | collective-permute-start | bytes 393224 | tf_op jit(solution)/shard_map/ppermute | solution.py:112
  54.4 6.7 %collective-permute-start.7 = (bf16[128,512]{1,0:T(8,128)(2,1)S(1)}, bf16[128,512]{1,0:T(8,128)(2,1)S(1)}, u32[]{:S(2)}, u32[]{:S(2)}) collective-permute-start(bf16[128,512]{1,0:T(8,128)(2,1)S(1)} %get-tuple-element.27), channel_id=1, source_target_pairs={{0,12},{4,0},{8,4},{12,8},{1,13},{5,1},{9,5},{13,9},{2,14},{6,2},{... | collective-permute-start | bytes 393224 | tf_op jit(solution)/shard_map/ppermute | solution.py:112
  61.2 46.2 %copy-start.3 = (s32[16]{0:T(128)S(1)}, s32[16]{0:T(128)}, u32[]{:S(2)}) copy-start(s32[16]{0:T(128)} %owner_ref.1) | copy-start | bytes 196
  61.9 11.0 %all-to-all-start.1 = ((bf16[16,2,16,128]{3,2,1,0:T(8,128)(2,1)}), bf16[16,2,16,128]{3,2,1,0:T(8,128)(2,1)S(1)}, u32[]{:S(2)}, u32[]{:S(2)}) async-start(bf16[16,2,16,128]{3,2,1,0:T(8,128)(2,1)} %bitcast.9), calls=%async_computation.1 | async-start | bytes 262144 | tf_op jit(solution)/shard_map/all_to_all | solution.py:340
  102.1 5.2 %collective-permute-start.8 = (bf16[16,4,16,128]{3,2,1,0:T(8,128)(2,1)S(1)}, bf16[16,4,16,128]{3,2,1,0:T(8,128)(2,1)S(1)}, u32[]{:S(2)}, u32[]{:S(2)}) collective-permute-start(bf16[16,4,16,128]{3,2,1,0:T(8,128)(2,1)S(1)} %all_to_all.21), channel_id=1, source_target_pairs={{0,16},{16,0},{1,17},{17,1},{2,18},{18,2},{3,19},{19,3},{4,20},{20... | collective-permute-start | bytes 786440 | tf_op jit(solution)/shard_map/ppermute | solution.py:365

commit v14 on v13

--- a/solution.py
+++ b/solution.py
@@ -98,13 +98,33 @@
     out_ref[...] = dot(turned_ref[...], grads_ref[...])
 
 
-def join_kernel(own_ref, got_ref, prec_ref, out_ref):
-    total = (own_ref[...] + got_ref[...].astype(F32)).astype(BF16).T
+def mates(core, at, size):
+    near = at + 1 - 2 * (at % 2)
+    far = size - 1 - at
+    first = jnp.where(core == 0, near, far)
+    second = jnp.where(core == 0, far, near)
+    return first, second, far + 1 - 2 * (far % 2)
+
+
+def join_kernel(info_ref, own_ref, got_ref, prec_ref, keep_ref, send_ref, total):
+    x = info_ref[1]
+    first, second, across = mates(info_ref[0], x, X)
+    total[...] = (own_ref[...] + got_ref[...].astype(F32)).T
+    for ref, pair in ((keep_ref, (x, second)), (send_ref, (first, across))):
+        for part, mate in enumerate(pair):
+            rows = total[pl.ds(pl.multiple_of(mate * PART, PART), PART), :]
+            ref[part * PART : (part + 1) * PART] = rows.astype(ref.dtype)
     rows = prec_ref.shape[2]
-    for w in range(X):
-        out_ref[w, :PART] = total[w * PART : (w + 1) * PART]
-        for c in range(CORE):
-            out_ref[w, PART + c * rows : PART + (c + 1) * rows] = prec_ref[0, c]
+    for c in range(CORE):
+        send_ref[2 * PART + c * rows : 2 * PART + (c + 1) * rows] = prec_ref[0, c]
+
+
+def half_kernel(keep_ref, sent_ref, got_ref, out_ref, send_ref):
+    total = keep_ref[...] + got_ref[: 2 * PART].astype(F32)
+    out_ref[...] = total[:PART]
+    send_ref[:PART] = total[PART:].astype(BF16)
+    send_ref[PART : PART + ROWS] = sent_ref[2 * PART :]
+    send_ref[PART + ROWS :] = got_ref[2 * PART :]
 
 
 def shift(value, axis, step):
@@ -123,19 +143,19 @@
         out_ref[pl.ds(pl.multiple_of(at, rows), rows), :] = part[...]
 
 
-def sum_kernel(info_ref, parts_ref, mine_ref, theirs_ref, old_ref, *refs):
+def sum_kernel(info_ref, part_ref, sent_ref, got_ref, mine_ref, theirs_ref, old_ref, *refs):
     keep_ref, right_ref, left_ref, left_send, old_low, send_ref = refs
-    core = info_ref[0]
+    core, x = info_ref[0], info_ref[1]
     rows = mine_ref.shape[0]
     right_ref[pl.ds(pl.multiple_of(core * rows, rows), rows), :] = mine_ref[...]
     right_ref[pl.ds(pl.multiple_of((1 - core) * rows, rows), rows), :] = theirs_ref[...]
-    total = parts_ref[0, :PART].astype(F32)
-    for w in range(X):
+    for place_at, mate in enumerate((x, *mates(core, x, X))):
+        source = (sent_ref, got_ref)[place_at // 2]
+        start = PART + place_at % 2 * ROWS
+        to = pl.ds(pl.multiple_of(mate * rows, rows), rows)
         for ref, c in ((left_ref, core), (left_send, 1 - core)):
-            at = pl.multiple_of(PART + c * rows, rows)
-            ref[w * rows : (w + 1) * rows] = parts_ref[w, pl.ds(at, rows), :]
-        if w:
-            total = total + parts_ref[w, :PART].astype(F32)
+            ref[to, :] = source[pl.ds(pl.multiple_of(start + c * rows, rows), rows), :]
+    total = part_ref[...] + got_ref[:PART].astype(F32)
     keep_ref[...] = total
     send_ref[:PART] = total.astype(BF16)
     send_ref[PART:] = right_ref[...]
@@ -290,10 +310,29 @@
         [shape((B, B), F32)],
         work=cost(2 * acts.shape[0] * B * B, 4 * acts.shape[0] * B),
     )(turned, grads_own)
-    (total,) = kernel_call(
-        join_kernel, "join", [VMEM] * 3, [shape((X, PART + ROWS, B))]
-    )(own, got, prec_left)
-    total = lax.all_to_all(total, "x", 0, 0)
+    keep, send = kernel_call(
+        join_kernel,
+        "join",
+        [SMEM] + [VMEM] * 3,
+        [shape((2 * PART, B), F32), shape((2 * PART + ROWS, B))],
+        [pltpu.VMEM((B, B), F32)],
+    )(info, own, got, prec_left)
+    near_far = [
+        [
+            (z * CORE + c, ((z ^ 1) if c == step else X - 1 - z) * CORE + c)
+            for z in range(X)
+            for c in range(CORE)
+        ]
+        for step in range(2)
+    ]
+    got = lax.ppermute(send, ("x", "core"), near_far[0])
+    keep, send = kernel_call(
+        half_kernel,
+        "half_x",
+        [VMEM] * 3,
+        [shape((PART, B), F32), shape((PART + 2 * ROWS, B))],
+    )(keep, send, got)
+    got = lax.ppermute(send, ("x", "core"), near_far[1])
     mine = lax.dynamic_index_in_dim(prec_right[0], core, 0, keepdims=False)
     theirs = lax.ppermute(
         lax.dynamic_index_in_dim(prec_right[0], 1 - core, 0, keepdims=False), "core", swap
@@ -302,11 +341,11 @@
     keep, right_rows, left_mine, left_send, old_low, send = kernel_call(
         sum_kernel,
         "sum_x",
-        [SMEM] + [VMEM] * 4,
+        [SMEM] + [VMEM] * 6,
         [shape((PART, B), F32), shape((ROWS, B))]
         + [shape((PART // CORE, B))] * 2
         + [shape((quarter, B)), shape((PART + ROWS, B))],
-    )(info, total, mine, theirs, old_own)
+    )(info, keep, send, got, mine, theirs, old_own)
 
     near_far = [
         [

time: 111 us -> 114 us (1.027)
  blocking collectives: 28.1 us -> 29.4 us
    ppermute x0 -> x2, waiting for transfers between devices: none -> 8.42 us  [the longest x1 6.75 us: local(): got = lax.ppermute(send, ('x', 'core'), near_far[0])]
    all_to_all x1 -> x0, waiting for transfers between devices: 7.45 us -> none  [local(): total = lax.all_to_all(total, 'x', 0, 0)]
    ppermute x0 -> x2, starting transfers between devices: none -> 3.84 us  [the longest x1 1.92 us: local(): got = lax.ppermute(send, ('x', 'core'), near_far[0])]
    all_to_all x1 -> x0, starting transfers between devices: 3.48 us -> none  [local(): total = lax.all_to_all(total, 'x', 0, 0)]
    all_to_all x1, blocking collectives: 15.8 us -> 17.1 us  [local(): parts = lax.all_to_all(chosen, ('x', 'core'), 0, 0)]
  transfers between devices with their start and end apart: 11 -> 12, of which waited for: 8 -> 9; matrix products, arithmetic and copies ran while one was open for 0% -> 0% of each run, Pallas kernels for 2% -> 2%
where the time goes in v14:
time: 114 us
  starting transfers between devices  49.6 us (44%)
  blocking collectives  29.4 us (26%)
  waiting for transfers between devices  22.6 us (20%)
  Pallas kernels  11.2 us (10%)
    all_to_all x1, blocking collectives, local(): parts = lax.all_to_all(chosen, ('x', 'core'), 0, 0)  17.1 us
    all_to_all x1, blocking collectives, local(): mine = lax.all_to_all(mine, ('mp', 'root'), 0, 0)  12.3 us
    ppermute x3, starting transfers between devices, shift(): lax.ppermute(value, axis, [(at, (at + step) % size) for at in range(size)])  10.7 us
    ppermute x1, starting transfers between devices, local(): got = lax.ppermute(send, 'core', swap)  8.78 us
    ppermute x1, starting transfers between devices, local(): got = lax.ppermute(send, ('zh', 'core'), near_far[0])  8.14 us
    ppermute x1, waiting for transfers between devices, local(): got = lax.ppermute(send, ('x', 'core'), near_far[0])  6.75 us
    all_to_all x1, waiting for transfers between devices, local(): blocks = lax.all_to_all(pieces, ('mp', 'root'), 0, 0)  6.34 us
    ppermute x1, starting transfers between devices, local(): got = lax.ppermute(send, ('zh', 'core'), near_far[1])  6.14 us
  transfers between devices with their start and end apart: 12, of which 9 were waited for; matrix products, arithmetic and copies ran while one was open for 0% of the time, Pallas kernels for 2%

profile of v14, /device:TPU:1, one launch (start us, length us, event | category | flops | bytes accessed | tf_op | source)
XLA Modules:
  0.0 113.8 jit_solution(11439168107659710306)
XLA Ops:
  0.6 2.3 %other_half.1 = (bf16[512,1024]{1,0:T(8,128)(2,1)S(1)}, bf16[512,512]{1,0:T(8,128)(2,1)S(1)}, bf16[1024,512]{1,0:T(8,128)(2,1)S(1)}) custom-call(s32[1]{0:T(128)} %bitcast.5.index_ref, bf16[1024,512]{1,0:T(8,128)(2,1)} %acts_ref.1, bf16[1024,1024]{1,0:T(8,128)(2,1)} %grads_ref.1), custom_call_target="tpu_custom_call" | custom-call | flops 536870912 | bytes 3145728 | tf_op jit(solution)/shard_map/other_half/pallas_call | solution.py:80
  2.9 0.0 copy-start.1
  2.9 8.8 %collective-permute-start = (bf16[512,512]{1,0:T(8,128)(2,1)S(1)}, bf16[512,512]{1,0:T(8,128)(2,1)S(1)}, u32[]{:S(2)}, u32[]{:S(2)}) collective-permute-start(bf16[512,512]{1,0:T(8,128)(2,1)S(1)} %get-tuple-element.23), channel_id=1, source_target_pairs={{0,16},{16,0},{1,17},{17,1},{2,18},{18,2},{3,19},{19,3},{4,20},{20... | collective-permute-start | bytes 1572872 | tf_op jit(solution)/shard_map/ppermute | solution.py:305
  11.7 0.1 stack.23.info_ref
  11.8 0.7 own_half.1.own_ref
  12.5 0.0 copy-start.4
  12.5 0.0 copy-start
  12.5 0.7 collective-permute-done.got_ref
  13.2 0.0 copy-done.1
  13.2 0.9 join.1
  14.2 1.9 %collective-permute-start.1 = (bf16[288,512]{1,0:T(8,128)(2,1)S(1)}, bf16[288,512]{1,0:T(8,128)(2,1)S(1)}, u32[]{:S(2)}, u32[]{:S(2)}) collective-permute-start(bf16[288,512]{1,0:T(8,128)(2,1)S(1)} %get-tuple-element.25.sent_ref), channel_id=1, source_target_pairs={{0,128},{16,400},{128,0},{144,272},{256,384},{272,144},{384,256},{... | collective-permute-start | bytes 884744 | tf_op jit(solution)/shard_map/ppermute | solution.py:328
  16.1 6.7 %collective-permute-done.1.got_ref = bf16[288,512]{1,0:T(8,128)(2,1)S(1)} collective-permute-done((bf16[288,512]{1,0:T(8,128)(2,1)S(1)}, bf16[288,512]{1,0:T(8,128)(2,1)S(1)}, u32[]{:S(2)}, u32[]{:S(2)}) %collective-permute-start.1) | collective-permute-done | bytes 294944 | tf_op jit(solution)/shard_map/ppermute | solution.py:328
  22.9 0.0 copy-start.2
  22.9 1.9 %collective-permute-start.2 = (bf16[192,512]{1,0:T(8,128)(2,1)S(1)}, bf16[192,512]{1,0:T(8,128)(2,1)S(1)}, u32[]{:S(2)}, u32[]{:S(2)}) collective-permute-start(bf16[192,512]{1,0:T(8,128)(2,1)S(1)} %get-tuple-element.27.sent_ref), channel_id=1, source_target_pairs={{0,384},{16,144},{128,256},{144,16},{256,128},{272,400},{384,0},{4... | collective-permute-start | bytes 589832 | tf_op jit(solution)/shard_map/ppermute | solution.py:335
  24.9 0.0 copy-done.4
  24.9 2.2 %collective-permute-start.3 = (bf16[16,512]{1,0:T(8,128)(2,1)S(1)}, bf16[16,512]{1,0:T(8,128)(2,1)S(1)}, u32[]{:S(2)}, u32[]{:S(2)}) collective-permute-start(bf16[16,512]{1,0:T(8,128)(2,1)S(1)} %get-tuple-element.39), channel_id=1, source_target_pairs={{0,16},{16,0},{1,17},{17,1},{2,18},{18,2},{3,19},{19,3},{4,20},{20... | collective-permute-start | bytes 49160 | tf_op jit(solution)/shard_map/ppermute | solution.py:337
  27.1 0.8 collective-permute-done.3.theirs_ref
  28.0 1.7 %collective-permute-done.2.got_ref = bf16[192,512]{1,0:T(8,128)(2,1)S(1)} collective-permute-done((bf16[192,512]{1,0:T(8,128)(2,1)S(1)}, bf16[192,512]{1,0:T(8,128)(2,1)S(1)}, u32[]{:S(2)}, u32[]{:S(2)}) %collective-permute-start.2) | collective-permute-done | bytes 196640 | tf_op jit(solution)/shard_map/ppermute | solution.py:335
  29.6 0.0 copy-done
  29.6 0.6 sum_x.1
  30.3 8.1 %collective-permute-start.4 = (bf16[160,512]{1,0:T(8,128)(2,1)S(1)}, bf16[160,512]{1,0:T(8,128)(2,1)S(1)}, u32[]{:S(2)}, u32[]{:S(2)}) collective-permute-start(bf16[160,512]{1,0:T(8,128)(2,1)S(1)} %get-tuple-element.30), channel_id=1, source_target_pairs={{0,32},{16,112},{32,0},{48,80},{64,96},{80,48},{96,64},{112,16},{1... | collective-permute-start | bytes 491528 | tf_op jit(solution)/shard_map/ppermute | solution.py:358
  38.4 3.2 %collective-permute-start.6 = (bf16[128,512]{1,0:T(8,128)(2,1)S(1)}, bf16[128,512]{1,0:T(8,128)(2,1)S(1)}, u32[]{:S(2)}, u32[]{:S(2)}) collective-permute-start(bf16[128,512]{1,0:T(8,128)(2,1)S(1)} %get-tuple-element.32.low_ref), channel_id=1, source_target_pairs={{0,4},{4,8},{8,12},{12,0},{1,5},{5,9},{9,13},{13,1},{2,6},{6,10},{... | collective-permute-start | bytes 393224 | tf_op jit(solution)/shard_map/ppermute | solution.py:132
  41.6 1.9 %collective-permute-start.5 = (bf16[64,512]{1,0:T(8,128)(2,1)S(1)}, bf16[64,512]{1,0:T(8,128)(2,1)S(1)}, u32[]{:S(2)}, u32[]{:S(2)}) collective-permute-start(bf16[64,512]{1,0:T(8,128)(2,1)S(1)} %get-tuple-element.31), channel_id=1, source_target_pairs={{0,16},{16,0},{1,17},{17,1},{2,18},{18,2},{3,19},{19,3},{4,20},{20... | collective-permute-start | bytes 196616 | tf_op jit(solution)/shard_map/ppermute | solution.py:359
  43.5 1.2 %collective-permute-done.5.refs_0_.theirs_ref = bf16[64,512]{1,0:T(8,128)(2,1)S(1)} collective-permute-done((bf16[64,512]{1,0:T(8,128)(2,1)S(1)}, bf16[64,512]{1,0:T(8,128)(2,1)S(1)}, u32[]{:S(2)}, u32[]{:S(2)}) %collective-permute-start.5) | collective-permute-done | bytes 65568 | tf_op jit(solution)/shard_map/ppermute | solution.py:359
  44.7 0.6 collective-permute-done.6.refs_1_.one
  45.4 0.0 collective-permute-done.4.got_ref
  45.4 6.1 %collective-permute-start.7 = (bf16[192,512]{1,0:T(8,128)(2,1)S(1)}, bf16[192,512]{1,0:T(8,128)(2,1)S(1)}, u32[]{:S(2)}, u32[]{:S(2)}) collective-permute-start(bf16[192,512]{1,0:T(8,128)(2,1)S(1)} %get-tuple-element.34.sent_ref), channel_id=1, source_target_pairs={{0,96},{16,48},{32,64},{48,16},{64,32},{80,112},{96,0},{112,80},{1... | collective-permute-start | bytes 589832 | tf_op jit(solution)/shard_map/ppermute | solution.py:368
  51.6 4.8 %collective-permute-start.8 = (bf16[128,512]{1,0:T(8,128)(2,1)S(1)}, bf16[128,512]{1,0:T(8,128)(2,1)S(1)}, u32[]{:S(2)}, u32[]{:S(2)}) collective-permute-start(bf16[128,512]{1,0:T(8,128)(2,1)S(1)} %get-tuple-element.35), channel_id=1, source_target_pairs={{0,8},{4,12},{8,0},{12,4},{1,9},{5,13},{9,1},{13,5},{2,10},{6,14},... | collective-permute-start | bytes 393224 | tf_op jit(solution)/shard_map/ppermute | solution.py:132
  56.4 2.7 %collective-permute-start.9 = (bf16[128,512]{1,0:T(8,128)(2,1)S(1)}, bf16[128,512]{1,0:T(8,128)(2,1)S(1)}, u32[]{:S(2)}, u32[]{:S(2)}) collective-permute-start(bf16[128,512]{1,0:T(8,128)(2,1)S(1)} %get-tuple-element.35), channel_id=1, source_target_pairs={{0,12},{4,0},{8,4},{12,8},{1,13},{5,1},{9,5},{13,9},{2,14},{6,2},{... | collective-permute-start | bytes 393224 | tf_op jit(solution)/shard_map/ppermute | solution.py:132
  59.1 0.0 collective-permute-done.8.refs_0_.two
  59.1 4.0 %collective-permute-done.9.refs_1_.three = bf16[128,512]{1,0:T(8,128)(2,1)S(1)} collective-permute-done((bf16[128,512]{1,0:T(8,128)(2,1)S(1)}, bf16[128,512]{1,0:T(8,128)(2,1)S(1)}, u32[]{:S(2)}, u32[]{:S(2)}) %collective-permute-start.9) | collective-permute-done | bytes 131104 | tf_op jit(solution)/shard_map/ppermute | solution.py:132
  63.1 0.0 collective-permute-done.7.got_ref
  63.1 0.0 copy-start.3
  63.1 0.7 pack.1
  63.8 3.8 %all-to-all-start = ((bf16[16,2,16,128]{3,2,1,0:T(8,128)(2,1)}), bf16[16,2,16,128]{3,2,1,0:T(8,128)(2,1)S(1)}, u32[]{:S(2)}, u32[]{:S(2)}) async-start(bf16[16,2,16,128]{3,2,1,0:T(8,128)(2,1)} %bitcast.9), calls=%async_computation | async-start | bytes 262144 | tf_op jit(solution)/shard_map/all_to_all | solution.py:379
  67.5 0.9 update.1.total_ref
  68.5 6.3 %all-to-all-done.blocks_ref = bf16[16,2,16,128]{3,2,1,0:T(8,128)(2,1)S(1)} async-done(((bf16[16,2,16,128]{3,2,1,0:T(8,128)(2,1)}), bf16[16,2,16,128]{3,2,1,0:T(8,128)(2,1)S(1)}, u32[]{:S(2)}, u32[]{:S(2)}) %all-to-all-start) | async-done | bytes 131104 | tf_op jit(solution)/shard_map/all_to_all | solution.py:379
  74.8 0.0 copy-done.2
  74.8 0.6 choose.1
  75.4 17.1 %all_to_all.15.parts_ref = bf16[8,5,16,128]{3,2,1,0:T(8,128)(2,1)S(1)} all-to-all(bf16[8,5,16,128]{3,2,1,0:T(8,128)(2,1)S(1)} %choose.1), channel_id=1, replica_groups=mesh['x'=4,'zh'=4,'core'=2,'mp'=4,'root'=4] {'x','core'}, dimensions={0} | all-to-all | bytes 327680 | tf_op jit(solution)/shard_map/all_to_all | solution.py:396
  92.5 0.6 spread.1
  93.1 12.3 %all_to_all.16 = bf16[16,4,16,128]{3,2,1,0:T(8,128)(2,1)S(1)} all-to-all(bf16[16,4,16,128]{3,2,1,0:T(8,128)(2,1)S(1)} %spread.1), channel_id=1, replica_groups=mesh['x'=4,'zh'=4,'core'=2,'mp'=4,'root'=4] {'mp','root'}, dimensions={0} | all-to-all | bytes 524288 | tf_op jit(solution)/shard_map/all_to_all | solution.py:403
  105.4 4.1 %collective-permute-start.10 = (bf16[16,4,16,128]{3,2,1,0:T(8,128)(2,1)S(1)}, bf16[16,4,16,128]{3,2,1,0:T(8,128)(2,1)S(1)}, u32[]{:S(2)}, u32[]{:S(2)}) collective-permute-start(bf16[16,4,16,128]{3,2,1,0:T(8,128)(2,1)S(1)} %all_to_all.16), channel_id=1, source_target_pairs={{0,16},{16,0},{1,17},{17,1},{2,18},{18,2},{3,19},{19,3},{4,20},{20... | collective-permute-start | bytes 786440 | tf_op jit(solution)/shard_map/ppermute | solution.py:404
  109.5 0.6 finish.1
  110.1 0.5 collective-permute-done.10
  110.6 0.0 copy-done.3
  110.6 3.2 %refresh.1 = (f32[128,512]{1,0:T(8,128)}, f32[128,512]{1,0:T(8,128)}) custom-call(s32[5]{0:T(128)S(1)} %stack.23.info_ref, s32[16]{0:T(128)S(1)} %copy-done.3, bf16[4,4,4,16,128]{4,3,2,1,0:T(8,128)(2,1)S(1)} %bitcast.20, bf16[4,4,4,16,128]{4,3,2,1,0:T(8,128)(2,1)S(1)} %bitcast.21, f32[128,512]{1,0:T(8,128)S(1)} %bitcast.19, ...), custom_call_target="tpu_custom_call" | custom-call | flops 603979776 | bytes 1048576 | tf_op jit(solution)/shard_map/refresh/pallas_call | solution.py:408
  (3 shorter events, 0.1 us)
Async XLA Ops:
  2.9 10.3 %copy-start.1 = (bf16[1,2,16,512]{3,2,1,0:T(8,128)(2,1)S(1)}, bf16[1,2,16,512]{3,2,1,0:T(8,128)(2,1)}, u32[]{:S(2)}) copy-start(bf16[1,2,16,512]{3,2,1,0:T(8,128)(2,1)} %prec_ref.1) | copy-start | bytes 98308
  2.9 10.3 %collective-permute-start = (bf16[512,512]{1,0:T(8,128)(2,1)S(1)}, bf16[512,512]{1,0:T(8,128)(2,1)S(1)}, u32[]{:S(2)}, u32[]{:S(2)}) collective-permute-start(bf16[512,512]{1,0:T(8,128)(2,1)S(1)} %get-tuple-element.23), channel_id=1, source_target_pairs={{0,16},{16,0},{1,17},{17,1},{2,18},{18,2},{3,19},{19,3},{4,20},{20... | collective-permute-start | bytes 1572872 | tf_op jit(solution)/shard_map/ppermute | solution.py:305
  12.5 12.3 %copy-start.4 = (bf16[1,2,16,512]{3,2,1,0:T(8,128)(2,1)S(1)}, bf16[1,2,16,512]{3,2,1,0:T(8,128)(2,1)}, u32[]{:S(2)}) copy-start(bf16[1,2,16,512]{3,2,1,0:T(8,128)(2,1)} %param.10) | copy-start | bytes 98308
  12.5 17.1 %copy-start = (f32[1,128,512]{2,1,0:T(8,128)S(1)}, f32[1,128,512]{2,1,0:T(8,128)}, u32[]{:S(2)}) copy-start(f32[1,128,512]{2,1,0:T(8,128)} %param.11) | copy-start | bytes 786436
  14.2 8.7 %collective-permute-start.1 = (bf16[288,512]{1,0:T(8,128)(2,1)S(1)}, bf16[288,512]{1,0:T(8,128)(2,1)S(1)}, u32[]{:S(2)}, u32[]{:S(2)}) collective-permute-start(bf16[288,512]{1,0:T(8,128)(2,1)S(1)} %get-tuple-element.25.sent_ref), channel_id=1, source_target_pairs={{0,128},{16,400},{128,0},{144,272},{256,384},{272,144},{384,256},{... | collective-permute-start | bytes 884744 | tf_op jit(solution)/shard_map/ppermute | solution.py:328
  22.9 51.9 %copy-start.2 = (s32[16]{0:T(128)S(1)}, s32[16]{0:T(128)}, u32[]{:S(2)}) copy-start(s32[16]{0:T(128)} %listed_ref.3) | copy-start | bytes 196
  22.9 6.7 %collective-permute-start.2 = (bf16[192,512]{1,0:T(8,128)(2,1)S(1)}, bf16[192,512]{1,0:T(8,128)(2,1)S(1)}, u32[]{:S(2)}, u32[]{:S(2)}) collective-permute-start(bf16[192,512]{1,0:T(8,128)(2,1)S(1)} %get-tuple-element.27.sent_ref), channel_id=1, source_target_pairs={{0,384},{16,144},{128,256},{144,16},{256,128},{272,400},{384,0},{4... | collective-permute-start | bytes 589832 | tf_op jit(solution)/shard_map/ppermute | solution.py:335
  24.9 3.1 %collective-permute-start.3 = (bf16[16,512]{1,0:T(8,128)(2,1)S(1)}, bf16[16,512]{1,0:T(8,128)(2,1)S(1)}, u32[]{:S(2)}, u32[]{:S(2)}) collective-permute-start(bf16[16,512]{1,0:T(8,128)(2,1)S(1)} %get-tuple-element.39), channel_id=1, source_target_pairs={{0,16},{16,0},{1,17},{17,1},{2,18},{18,2},{3,19},{19,3},{4,20},{20... | collective-permute-start | bytes 49160 | tf_op jit(solution)/shard_map/ppermute | solution.py:337
  30.3 15.1 %collective-permute-start.4 = (bf16[160,512]{1,0:T(8,128)(2,1)S(1)}, bf16[160,512]{1,0:T(8,128)(2,1)S(1)}, u32[]{:S(2)}, u32[]{:S(2)}) collective-permute-start(bf16[160,512]{1,0:T(8,128)(2,1)S(1)} %get-tuple-element.30), channel_id=1, source_target_pairs={{0,32},{16,112},{32,0},{48,80},{64,96},{80,48},{96,64},{112,16},{1... | collective-permute-start | bytes 491528 | tf_op jit(solution)/shard_map/ppermute | solution.py:358
  38.4 7.0 %collective-permute-start.6 = (bf16[128,512]{1,0:T(8,128)(2,1)S(1)}, bf16[128,512]{1,0:T(8,128)(2,1)S(1)}, u32[]{:S(2)}, u32[]{:S(2)}) collective-permute-start(bf16[128,512]{1,0:T(8,128)(2,1)S(1)} %get-tuple-element.32.low_ref), channel_id=1, source_target_pairs={{0,4},{4,8},{8,12},{12,0},{1,5},{5,9},{9,13},{13,1},{2,6},{6,10},{... | collective-permute-start | bytes 393224 | tf_op jit(solution)/shard_map/ppermute | solution.py:132
  41.6 3.1 %collective-permute-start.5 = (bf16[64,512]{1,0:T(8,128)(2,1)S(1)}, bf16[64,512]{1,0:T(8,128)(2,1)S(1)}, u32[]{:S(2)}, u32[]{:S(2)}) collective-permute-start(bf16[64,512]{1,0:T(8,128)(2,1)S(1)} %get-tuple-element.31), channel_id=1, source_target_pairs={{0,16},{16,0},{1,17},{17,1},{2,18},{18,2},{3,19},{19,3},{4,20},{20... | collective-permute-start | bytes 196616 | tf_op jit(solution)/shard_map/ppermute | solution.py:359
  45.4 17.6 %collective-permute-start.7 = (bf16[192,512]{1,0:T(8,128)(2,1)S(1)}, bf16[192,512]{1,0:T(8,128)(2,1)S(1)}, u32[]{:S(2)}, u32[]{:S(2)}) collective-permute-start(bf16[192,512]{1,0:T(8,128)(2,1)S(1)} %get-tuple-element.34.sent_ref), channel_id=1, source_target_pairs={{0,96},{16,48},{32,64},{48,16},{64,32},{80,112},{96,0},{112,80},{1... | collective-permute-start | bytes 589832 | tf_op jit(solution)/shard_map/ppermute | solution.py:368
  51.6 7.5 %collective-permute-start.8 = (bf16[128,512]{1,0:T(8,128)(2,1)S(1)}, bf16[128,512]{1,0:T(8,128)(2,1)S(1)}, u32[]{:S(2)}, u32[]{:S(2)}) collective-permute-start(bf16[128,512]{1,0:T(8,128)(2,1)S(1)} %get-tuple-element.35), channel_id=1, source_target_pairs={{0,8},{4,12},{8,0},{12,4},{1,9},{5,13},{9,1},{13,5},{2,10},{6,14},... | collective-permute-start | bytes 393224 | tf_op jit(solution)/shard_map/ppermute | solution.py:132
  56.4 6.7 %collective-permute-start.9 = (bf16[128,512]{1,0:T(8,128)(2,1)S(1)}, bf16[128,512]{1,0:T(8,128)(2,1)S(1)}, u32[]{:S(2)}, u32[]{:S(2)}) collective-permute-start(bf16[128,512]{1,0:T(8,128)(2,1)S(1)} %get-tuple-element.35), channel_id=1, source_target_pairs={{0,12},{4,0},{8,4},{12,8},{1,13},{5,1},{9,5},{13,9},{2,14},{6,2},{... | collective-permute-start | bytes 393224 | tf_op jit(solution)/shard_map/ppermute | solution.py:132
  63.1 47.5 %copy-start.3 = (s32[16]{0:T(128)S(1)}, s32[16]{0:T(128)}, u32[]{:S(2)}) copy-start(s32[16]{0:T(128)} %owner_ref.1) | copy-start | bytes 196
  63.8 11.0 %all-to-all-start = ((bf16[16,2,16,128]{3,2,1,0:T(8,128)(2,1)}), bf16[16,2,16,128]{3,2,1,0:T(8,128)(2,1)S(1)}, u32[]{:S(2)}, u32[]{:S(2)}) async-start(bf16[16,2,16,128]{3,2,1,0:T(8,128)(2,1)} %bitcast.9), calls=%async_computation | async-start | bytes 262144 | tf_op jit(solution)/shard_map/all_to_all | solution.py:379
  105.4 5.2 %collective-permute-start.10 = (bf16[16,4,16,128]{3,2,1,0:T(8,128)(2,1)S(1)}, bf16[16,4,16,128]{3,2,1,0:T(8,128)(2,1)S(1)}, u32[]{:S(2)}, u32[]{:S(2)}) collective-permute-start(bf16[16,4,16,128]{3,2,1,0:T(8,128)(2,1)S(1)} %all_to_all.16), channel_id=1, source_target_pairs={{0,16},{16,0},{1,17},{17,1},{2,18},{18,2},{3,19},{19,3},{4,20},{20... | collective-permute-start | bytes 786440 | tf_op jit(solution)/shard_map/ppermute | solution.py:404

commit v15 on v13

--- a/solution.py
+++ b/solution.py
@@ -98,13 +98,8 @@
     out_ref[...] = dot(turned_ref[...], grads_ref[...])
 
 
-def join_kernel(own_ref, got_ref, prec_ref, out_ref):
-    total = (own_ref[...] + got_ref[...].astype(F32)).astype(BF16).T
-    rows = prec_ref.shape[2]
-    for w in range(X):
-        out_ref[w, :PART] = total[w * PART : (w + 1) * PART]
-        for c in range(CORE):
-            out_ref[w, PART + c * rows : PART + (c + 1) * rows] = prec_ref[0, c]
+def join_kernel(own_ref, got_ref, out_ref):
+    out_ref[...] = (own_ref[...] + got_ref[...].astype(F32)).astype(BF16).T
 
 
 def shift(value, axis, step):
@@ -123,33 +118,46 @@
         out_ref[pl.ds(pl.multiple_of(at, rows), rows), :] = part[...]
 
 
-def sum_kernel(info_ref, parts_ref, mine_ref, theirs_ref, old_ref, *refs):
-    keep_ref, right_ref, left_ref, left_send, old_low, send_ref = refs
+def sum_kernel(info_ref, parts_ref, mine_ref, theirs_ref, prec_ref, *refs):
+    keep_ref, right_ref, left_ref, send_ref = refs[-4:]
     core = info_ref[0]
     rows = mine_ref.shape[0]
     right_ref[pl.ds(pl.multiple_of(core * rows, rows), rows), :] = mine_ref[...]
     right_ref[pl.ds(pl.multiple_of((1 - core) * rows, rows), rows), :] = theirs_ref[...]
-    total = parts_ref[0, :PART].astype(F32)
-    for w in range(X):
-        for ref, c in ((left_ref, core), (left_send, 1 - core)):
-            at = pl.multiple_of(PART + c * rows, rows)
-            ref[w * rows : (w + 1) * rows] = parts_ref[w, pl.ds(at, rows), :]
-        if w:
-            total = total + parts_ref[w, :PART].astype(F32)
+    for c in range(CORE):
+        left_ref[c * rows : (c + 1) * rows] = prec_ref[0, c]
+    total = parts_ref[0].astype(F32)
+    for w in range(1, X):
+        total = total + parts_ref[w].astype(F32)
     keep_ref[...] = total
     send_ref[:PART] = total.astype(BF16)
     send_ref[PART:] = right_ref[...]
-    old_low[...] = old_ref[...].astype(BF16)
-
-
-def middle_kernel(keep_ref, right_ref, got_ref, old_ref, *refs):
-    out_ref, send_ref, old_low = refs[-3:]
+
+
+def middle_kernel(info_ref, keep_ref, right_ref, got_ref, old_ref, own_ref, one, two, *refs):
+    out_ref, send_ref, old_low, left_ref, left_send = refs
     total = keep_ref[...] + got_ref[:PART].astype(F32)
     out_ref[...] = total
     send_ref[:PART] = total.astype(BF16)
     send_ref[PART : PART + ROWS] = right_ref[...]
     send_ref[PART + ROWS :] = got_ref[PART:]
     old_low[...] = old_ref[...].astype(BF16)
+    core, x = info_ref[0], info_ref[1]
+    rows = ROWS // CORE
+    near = x + 1 - 2 * (x % 2)
+    far = X - 1 - x
+    across = far + 1 - 2 * (far % 2)
+    first = jnp.where(core == 0, near, far)
+    second = jnp.where(core == 0, far, near)
+    for mate, source, start in (
+        (x, own_ref, 0),
+        (first, one, 0),
+        (second, two, 0),
+        (across, two, ROWS),
+    ):
+        to = pl.ds(pl.multiple_of(mate * rows, rows), rows)
+        for ref, c in ((left_ref, core), (left_send, 1 - core)):
+            ref[to, :] = source[pl.ds(pl.multiple_of(start + c * rows, rows), rows), :]
 
 
 def pack_kernel(scale, keep_ref, got_ref, *refs):
@@ -290,23 +298,23 @@
         [shape((B, B), F32)],
         work=cost(2 * acts.shape[0] * B * B, 4 * acts.shape[0] * B),
     )(turned, grads_own)
-    (total,) = kernel_call(
-        join_kernel, "join", [VMEM] * 3, [shape((X, PART + ROWS, B))]
-    )(own, got, prec_left)
+    (total,) = kernel_call(join_kernel, "join", [VMEM] * 2, [shape((B, B))])(own, got)
+    total = total.reshape(X, PART, B)
     total = lax.all_to_all(total, "x", 0, 0)
     mine = lax.dynamic_index_in_dim(prec_right[0], core, 0, keepdims=False)
     theirs = lax.ppermute(
         lax.dynamic_index_in_dim(prec_right[0], 1 - core, 0, keepdims=False), "core", swap
     )
     old_own = stats_old[0]
-    keep, right_rows, left_mine, left_send, old_low, send = kernel_call(
+    old_low = old_own.astype(BF16)
+    olds = [old_low, shift(old_low, "mp", 1)]
+    keep, right_rows, left_rows, send = kernel_call(
         sum_kernel,
         "sum_x",
         [SMEM] + [VMEM] * 4,
-        [shape((PART, B), F32), shape((ROWS, B))]
-        + [shape((PART // CORE, B))] * 2
-        + [shape((quarter, B)), shape((PART + ROWS, B))],
-    )(info, total, mine, theirs, old_own)
+        [shape((PART, B), F32)] + [shape((ROWS, B))] * 2 + [shape((PART + ROWS, B))],
+        awaited=1,
+    )(info, total, mine, theirs, prec_left, olds[1])
 
     near_far = [
         [
@@ -317,15 +325,18 @@
         for step in range(2)
     ]
     got = lax.ppermute(send, ("zh", "core"), near_far[0])
-    left_theirs = lax.ppermute(left_send, "core", swap)
-    olds = [old_low, shift(old_low, "mp", 1)]
-    keep, send, old_later = kernel_call(
+    left_one = lax.ppermute(left_rows, ("x", "core"), near_far[0])
+    left_two = lax.ppermute(
+        jnp.concatenate([left_rows, left_one]), ("x", "core"), near_far[1]
+    )
+    keep, send, old_later, left_mine, left_send = kernel_call(
         middle_kernel,
         "middle",
-        [VMEM] * 4,
-        [shape((PART, B), F32), shape((PART + 2 * ROWS, B)), shape((quarter, B))],
-        awaited=2,
-    )(keep, right_rows, got, old_own, left_theirs, olds[1])
+        [SMEM] + [VMEM] * 7,
+        [shape((PART, B), F32), shape((PART + 2 * ROWS, B)), shape((quarter, B))]
+        + [shape((PART // CORE, B))] * 2,
+    )(info, keep, right_rows, got, old_own, left_rows, left_one, left_two)
+    left_theirs = lax.ppermute(left_send, "core", swap)
     got = lax.ppermute(send, ("zh", "core"), near_far[1])
     olds += [shift(old_later, "mp", step) for step in range(2, n_mp)]
     (pieces,) = kernel_call(

time: 111 us -> 114 us (1.027)
  starting transfers between devices: 48.5 us -> 60 us
  waiting for transfers between devices: 21.7 us -> 14.3 us
  blocking collectives: 28.1 us -> 25.8 us
    ppermute x1, starting transfers between devices: 1.92 us -> 8.34 us  [local(): left_theirs = lax.ppermute(left_send, 'core', swap)]
    all_to_all x1, waiting for transfers between devices: 6.34 us -> 0.01 us  [local(): blocks = lax.all_to_all(pieces, ('mp', 'root'), 0, 0)]
    all_to_all x1, waiting for transfers between devices: 7.45 us -> 1.33 us  [local(): total = lax.all_to_all(total, 'x', 0, 0)]
    ppermute x0 -> x2, starting transfers between devices: none -> 4.81 us  [the longest x1 2.89 us: local(): left_one = lax.ppermute(left_rows, ('x', 'core'), near_far[0])]
    ppermute x0 -> x2, waiting for transfers between devices: none -> 3.38 us  [the longest x1 3.38 us: local(): lax.ppermute(jnp.concatenate([left_rows, left_one]), ('x', 'core'), near_...]
    all_to_all x1, blocking collectives: 15.8 us -> 13.4 us  [local(): parts = lax.all_to_all(chosen, ('x', 'core'), 0, 0)]
    ppermute x3, waiting for transfers between devices: 4.66 us -> 6.6 us  [shift(): lax.ppermute(value, axis, [(at, (at + step) % size) for at in range(size)])]
    ppermute x1, starting transfers between devices: 6.15 us -> 7.69 us  [local(): got = lax.ppermute(send, ('zh', 'core'), near_far[1])]
  transfers between devices with their start and end apart: 11 -> 13, of which waited for: 8 -> 9; matrix products, arithmetic and copies ran while one was open for 0% -> 0% of each run, Pallas kernels for 2% -> 2%
where the time goes in v15:
time: 114 us; the launch traced here: 113 us
  starting transfers between devices  60 us (53%)
  blocking collectives  25.8 us (23%)
  waiting for transfers between devices  14.3 us (13%)
  Pallas kernels  11.8 us (10%)
    all_to_all x1, blocking collectives, local(): parts = lax.all_to_all(chosen, ('x', 'core'), 0, 0)  13.4 us
    all_to_all x1, blocking collectives, local(): mine = lax.all_to_all(mine, ('mp', 'root'), 0, 0)  12.4 us
    ppermute x3, starting transfers between devices, shift(): lax.ppermute(value, axis, [(at, (at + step) % size) for at in range(size)])  9.3 us
    ppermute x1, starting transfers between devices, local(): got = lax.ppermute(send, 'core', swap)  8.79 us
    ppermute x1, starting transfers between devices, local(): left_theirs = lax.ppermute(left_send, 'core', swap)  8.34 us
    ppermute x1, starting transfers between devices, local(): got = lax.ppermute(send, ('zh', 'core'), near_far[1])  7.69 us
    ppermute x1, starting transfers between devices, local(): got = lax.ppermute(send, ('zh', 'core'), near_far[0])  7.47 us
    ppermute x3, waiting for transfers between devices, shift(): lax.ppermute(value, axis, [(at, (at + step) % size) for at in range(size)])  6.6 us
  transfers between devices with their start and end apart: 13, of which 9 were waited for; matrix products, arithmetic and copies ran while one was open for 0% of the time, Pallas kernels for 2%

profile of v15, /device:TPU:1, one launch (start us, length us, event | category | flops | bytes accessed | tf_op | source)
XLA Modules:
  0.0 113.0 jit_solution(14157863884033611803)
XLA Ops:
  0.6 2.3 %other_half.1 = (bf16[512,1024]{1,0:T(8,128)(2,1)S(1)}, bf16[512,512]{1,0:T(8,128)(2,1)S(1)}, bf16[1024,512]{1,0:T(8,128)(2,1)S(1)}) custom-call(s32[1]{0:T(128)} %bitcast.5.index_ref, bf16[1024,512]{1,0:T(8,128)(2,1)} %acts_ref.1, bf16[1024,1024]{1,0:T(8,128)(2,1)} %grads_ref.1), custom_call_target="tpu_custom_call" | custom-call | flops 536870912 | bytes 3145728 | tf_op jit(solution)/shard_map/other_half/pallas_call | solution.py:80
  2.9 8.8 %collective-permute-start = (bf16[512,512]{1,0:T(8,128)(2,1)S(1)}, bf16[512,512]{1,0:T(8,128)(2,1)S(1)}, u32[]{:S(2)}, u32[]{:S(2)}) collective-permute-start(bf16[512,512]{1,0:T(8,128)(2,1)S(1)} %get-tuple-element.19), channel_id=1, source_target_pairs={{0,16},{16,0},{1,17},{17,1},{2,18},{18,2},{3,19},{19,3},{4,20},{20... | collective-permute-start | bytes 1572872 | tf_op jit(solution)/shard_map/ppermute | solution.py:293
  11.7 0.7 own_half.1.own_ref
  12.4 0.0 copy-start
  12.4 0.0 copy-start.4
  12.4 0.0 copy-start.1
  12.4 0.8 collective-permute-done.got_ref
  13.2 1.0 join.1
  14.2 3.5 %all-to-all-start = ((bf16[4,128,512]{2,1,0:T(8,128)(2,1)}), bf16[4,128,512]{2,1,0:T(8,128)(2,1)S(1)}, u32[]{:S(2)}, u32[]{:S(2)}) async-start(bf16[4,128,512]{2,1,0:T(8,128)(2,1)} %bitcast.6), calls=%async_computation | async-start | bytes 1048576 | tf_op jit(solution)/shard_map/all_to_all | solution.py:303
  17.7 0.0 copy-done
  17.8 0.0 copy-start.2
  17.8 1.9 %collective-permute-start.2 = (bf16[128,512]{1,0:T(8,128)(2,1)S(1)}, bf16[128,512]{1,0:T(8,128)(2,1)S(1)}, u32[]{:S(2)}, u32[]{:S(2)}) collective-permute-start(bf16[128,512]{1,0:T(8,128)(2,1)S(1)} %bitcast_convert_fusion.low_ref), channel_id=1, source_target_pairs={{0,4},{4,8},{8,12},{12,0},{1,5},{5,9},{9,13},{13,1},{2,6},{6,10},{... | collective-permute-start | bytes 393224 | tf_op jit(solution)/shard_map/ppermute | solution.py:107
  19.7 0.0 copy-done.4
  19.7 2.3 %collective-permute-start.1 = (bf16[16,512]{1,0:T(8,128)(2,1)S(1)}, bf16[16,512]{1,0:T(8,128)(2,1)S(1)}, u32[]{:S(2)}, u32[]{:S(2)}) collective-permute-start(bf16[16,512]{1,0:T(8,128)(2,1)S(1)} %get-tuple-element.31), channel_id=1, source_target_pairs={{0,16},{16,0},{1,17},{17,1},{2,18},{18,2},{3,19},{19,3},{4,20},{20... | collective-permute-start | bytes 49160 | tf_op jit(solution)/shard_map/ppermute | solution.py:305
  22.0 0.1 stack.23.info_ref
  22.1 0.7 collective-permute-done.1.theirs_ref
  22.8 2.7 %collective-permute-done.2.refs_0_.one = bf16[128,512]{1,0:T(8,128)(2,1)S(1)} collective-permute-done((bf16[128,512]{1,0:T(8,128)(2,1)S(1)}, bf16[128,512]{1,0:T(8,128)(2,1)S(1)}, u32[]{:S(2)}, u32[]{:S(2)}) %collective-permute-start.2) | collective-permute-done | bytes 131104 | tf_op jit(solution)/shard_map/ppermute | solution.py:107
  25.6 1.3 %all-to-all-done.parts_ref = bf16[4,128,512]{2,1,0:T(8,128)(2,1)S(1)} async-done(((bf16[4,128,512]{2,1,0:T(8,128)(2,1)}), bf16[4,128,512]{2,1,0:T(8,128)(2,1)S(1)}, u32[]{:S(2)}, u32[]{:S(2)}) %all-to-all-start) | async-done | bytes 524320 | tf_op jit(solution)/shard_map/all_to_all | solution.py:303
  26.9 0.0 copy-done.1
  26.9 0.6 sum_x.1
  27.6 2.9 %collective-permute-start.4 = (bf16[32,512]{1,0:T(8,128)(2,1)S(1)}, bf16[32,512]{1,0:T(8,128)(2,1)S(1)}, u32[]{:S(2)}, u32[]{:S(2)}) collective-permute-start(bf16[32,512]{1,0:T(8,128)(2,1)S(1)} %get-tuple-element.23.own_ref), channel_id=1, source_target_pairs={{0,128},{16,400},{128,0},{144,272},{256,384},{272,144},{384,256},{... | collective-permute-start | bytes 98312 | tf_op jit(solution)/shard_map/ppermute | solution.py:328
  30.5 7.5 %collective-permute-start.3 = (bf16[160,512]{1,0:T(8,128)(2,1)S(1)}, bf16[160,512]{1,0:T(8,128)(2,1)S(1)}, u32[]{:S(2)}, u32[]{:S(2)}) collective-permute-start(bf16[160,512]{1,0:T(8,128)(2,1)S(1)} %get-tuple-element.22), channel_id=1, source_target_pairs={{0,32},{16,112},{32,0},{48,80},{64,96},{80,48},{96,64},{112,16},{1... | collective-permute-start | bytes 491528 | tf_op jit(solution)/shard_map/ppermute | solution.py:327
  37.9 0.0 collective-permute-done.4.one
  38.0 1.9 %collective-permute-start.5 = (bf16[64,512]{1,0:T(8,128)(2,1)S(1)}, bf16[64,512]{1,0:T(8,128)(2,1)S(1)}, u32[]{:S(2)}, u32[]{:S(2)}) collective-permute-start(bf16[64,512]{1,0:T(8,128)(2,1)S(1)} %pad_maximum_fusion), channel_id=1, source_target_pairs={{0,384},{16,144},{128,256},{144,16},{256,128},{272,400},{384,0},{4... | collective-permute-start | bytes 196616 | tf_op jit(solution)/shard_map/ppermute | solution.py:329
  39.9 3.4 %collective-permute-done.5.two = bf16[64,512]{1,0:T(8,128)(2,1)S(1)} collective-permute-done((bf16[64,512]{1,0:T(8,128)(2,1)S(1)}, bf16[64,512]{1,0:T(8,128)(2,1)S(1)}, u32[]{:S(2)}, u32[]{:S(2)}) %collective-permute-start.5) | collective-permute-done | bytes 65568 | tf_op jit(solution)/shard_map/ppermute | solution.py:329
  43.3 0.1 collective-permute-done.3.got_ref
  43.4 0.6 middle.1
  44.0 7.7 %collective-permute-start.6 = (bf16[192,512]{1,0:T(8,128)(2,1)S(1)}, bf16[192,512]{1,0:T(8,128)(2,1)S(1)}, u32[]{:S(2)}, u32[]{:S(2)}) collective-permute-start(bf16[192,512]{1,0:T(8,128)(2,1)S(1)} %get-tuple-element.25.sent_ref), channel_id=1, source_target_pairs={{0,96},{16,48},{32,64},{48,16},{64,32},{80,112},{96,0},{112,80},{1... | collective-permute-start | bytes 589832 | tf_op jit(solution)/shard_map/ppermute | solution.py:340
  51.7 4.6 %collective-permute-start.7 = (bf16[128,512]{1,0:T(8,128)(2,1)S(1)}, bf16[128,512]{1,0:T(8,128)(2,1)S(1)}, u32[]{:S(2)}, u32[]{:S(2)}) collective-permute-start(bf16[128,512]{1,0:T(8,128)(2,1)S(1)} %get-tuple-element.26), channel_id=1, source_target_pairs={{0,8},{4,12},{8,0},{12,4},{1,9},{5,13},{9,1},{13,5},{2,10},{6,14},... | collective-permute-start | bytes 393224 | tf_op jit(solution)/shard_map/ppermute | solution.py:107
  56.3 2.8 %collective-permute-start.8 = (bf16[128,512]{1,0:T(8,128)(2,1)S(1)}, bf16[128,512]{1,0:T(8,128)(2,1)S(1)}, u32[]{:S(2)}, u32[]{:S(2)}) collective-permute-start(bf16[128,512]{1,0:T(8,128)(2,1)S(1)} %get-tuple-element.26), channel_id=1, source_target_pairs={{0,12},{4,0},{8,4},{12,8},{1,13},{5,1},{9,5},{13,9},{2,14},{6,2},{... | collective-permute-start | bytes 393224 | tf_op jit(solution)/shard_map/ppermute | solution.py:107
  59.1 0.0 collective-permute-done.7.refs_0_.two
  59.1 3.8 %collective-permute-done.8.refs_1_.three = bf16[128,512]{1,0:T(8,128)(2,1)S(1)} collective-permute-done((bf16[128,512]{1,0:T(8,128)(2,1)S(1)}, bf16[128,512]{1,0:T(8,128)(2,1)S(1)}, u32[]{:S(2)}, u32[]{:S(2)}) %collective-permute-start.8) | collective-permute-done | bytes 131104 | tf_op jit(solution)/shard_map/ppermute | solution.py:107
  62.9 0.0 collective-permute-done.6.got_ref
  63.0 0.7 pack.1
  63.6 3.8 %all-to-all-start.1 = ((bf16[16,2,16,128]{3,2,1,0:T(8,128)(2,1)}), bf16[16,2,16,128]{3,2,1,0:T(8,128)(2,1)S(1)}, u32[]{:S(2)}, u32[]{:S(2)}) async-start(bf16[16,2,16,128]{3,2,1,0:T(8,128)(2,1)} %bitcast.10), calls=%async_computation.1 | async-start | bytes 262144 | tf_op jit(solution)/shard_map/all_to_all | solution.py:351
  67.4 8.3 %collective-permute-start.9 = (bf16[64,512]{1,0:T(8,128)(2,1)S(1)}, bf16[64,512]{1,0:T(8,128)(2,1)S(1)}, u32[]{:S(2)}, u32[]{:S(2)}) collective-permute-start(bf16[64,512]{1,0:T(8,128)(2,1)S(1)} %get-tuple-element.28), channel_id=1, source_target_pairs={{0,16},{16,0},{1,17},{17,1},{2,18},{18,2},{3,19},{19,3},{4,20},{20... | collective-permute-start | bytes 196616 | tf_op jit(solution)/shard_map/ppermute | solution.py:339
  75.8 0.9 collective-permute-done.9.theirs_ref
  76.6 0.9 update.1.total_ref
  77.6 0.0 all-to-all-done.1.blocks_ref
  77.6 0.0 copy-done.2
  77.6 0.6 choose.1
  78.2 13.4 %all_to_all.20.parts_ref = bf16[8,5,16,128]{3,2,1,0:T(8,128)(2,1)S(1)} all-to-all(bf16[8,5,16,128]{3,2,1,0:T(8,128)(2,1)S(1)} %choose.1), channel_id=1, replica_groups=mesh['x'=4,'zh'=4,'core'=2,'mp'=4,'root'=4] {'x','core'}, dimensions={0} | all-to-all | bytes 327680 | tf_op jit(solution)/shard_map/all_to_all | solution.py:368
  91.6 0.6 spread.1
  92.2 12.4 %all_to_all.21 = bf16[16,4,16,128]{3,2,1,0:T(8,128)(2,1)S(1)} all-to-all(bf16[16,4,16,128]{3,2,1,0:T(8,128)(2,1)S(1)} %spread.1), channel_id=1, replica_groups=mesh['x'=4,'zh'=4,'core'=2,'mp'=4,'root'=4] {'mp','root'}, dimensions={0} | all-to-all | bytes 524288 | tf_op jit(solution)/shard_map/all_to_all | solution.py:375
  104.5 4.1 %collective-permute-start.10 = (bf16[16,4,16,128]{3,2,1,0:T(8,128)(2,1)S(1)}, bf16[16,4,16,128]{3,2,1,0:T(8,128)(2,1)S(1)}, u32[]{:S(2)}, u32[]{:S(2)}) collective-permute-start(bf16[16,4,16,128]{3,2,1,0:T(8,128)(2,1)S(1)} %all_to_all.21), channel_id=1, source_target_pairs={{0,16},{16,0},{1,17},{17,1},{2,18},{18,2},{3,19},{19,3},{4,20},{20... | collective-permute-start | bytes 786440 | tf_op jit(solution)/shard_map/ppermute | solution.py:376
  108.6 0.6 finish.1
  109.2 0.5 collective-permute-done.10
  109.7 3.2 %refresh.1 = (f32[128,512]{1,0:T(8,128)}, f32[128,512]{1,0:T(8,128)}) custom-call(s32[5]{0:T(128)S(1)} %stack.23.info_ref, s32[16]{0:T(128)S(1)} %copy-done.3, bf16[4,4,4,16,128]{4,3,2,1,0:T(8,128)(2,1)S(1)} %bitcast.21, bf16[4,4,4,16,128]{4,3,2,1,0:T(8,128)(2,1)S(1)} %bitcast.22, f32[128,512]{1,0:T(8,128)S(1)} %bitcast.20, ...), custom_call_target="tpu_custom_call" | custom-call | flops 603979776 | bytes 1048576 | tf_op jit(solution)/shard_map/refresh/pallas_call | solution.py:380
  (5 shorter events, 0.0 us)
Async XLA Ops:
  2.9 10.3 %collective-permute-start = (bf16[512,512]{1,0:T(8,128)(2,1)S(1)}, bf16[512,512]{1,0:T(8,128)(2,1)S(1)}, u32[]{:S(2)}, u32[]{:S(2)}) collective-permute-start(bf16[512,512]{1,0:T(8,128)(2,1)S(1)} %get-tuple-element.19), channel_id=1, source_target_pairs={{0,16},{16,0},{1,17},{17,1},{2,18},{18,2},{3,19},{19,3},{4,20},{20... | collective-permute-start | bytes 1572872 | tf_op jit(solution)/shard_map/ppermute | solution.py:293
  12.4 5.3 %copy-start = (f32[1,128,512]{2,1,0:T(8,128)S(1)}, f32[1,128,512]{2,1,0:T(8,128)}, u32[]{:S(2)}) copy-start(f32[1,128,512]{2,1,0:T(8,128)} %param.11) | copy-start | bytes 786436
  12.4 7.3 %copy-start.4 = (bf16[1,2,16,512]{3,2,1,0:T(8,128)(2,1)S(1)}, bf16[1,2,16,512]{3,2,1,0:T(8,128)(2,1)}, u32[]{:S(2)}) copy-start(bf16[1,2,16,512]{3,2,1,0:T(8,128)(2,1)} %param.10) | copy-start | bytes 98308
  12.4 14.5 %copy-start.1 = (bf16[1,2,16,512]{3,2,1,0:T(8,128)(2,1)S(1)}, bf16[1,2,16,512]{3,2,1,0:T(8,128)(2,1)}, u32[]{:S(2)}) copy-start(bf16[1,2,16,512]{3,2,1,0:T(8,128)(2,1)} %prec_ref.1) | copy-start | bytes 98308
  14.2 12.7 %all-to-all-start = ((bf16[4,128,512]{2,1,0:T(8,128)(2,1)}), bf16[4,128,512]{2,1,0:T(8,128)(2,1)S(1)}, u32[]{:S(2)}, u32[]{:S(2)}) async-start(bf16[4,128,512]{2,1,0:T(8,128)(2,1)} %bitcast.6), calls=%async_computation | async-start | bytes 1048576 | tf_op jit(solution)/shard_map/all_to_all | solution.py:303
  17.8 59.8 %copy-start.2 = (s32[16]{0:T(128)S(1)}, s32[16]{0:T(128)}, u32[]{:S(2)}) copy-start(s32[16]{0:T(128)} %listed_ref.3) | copy-start | bytes 196
  17.8 7.8 %collective-permute-start.2 = (bf16[128,512]{1,0:T(8,128)(2,1)S(1)}, bf16[128,512]{1,0:T(8,128)(2,1)S(1)}, u32[]{:S(2)}, u32[]{:S(2)}) collective-permute-start(bf16[128,512]{1,0:T(8,128)(2,1)S(1)} %bitcast_convert_fusion.low_ref), channel_id=1, source_target_pairs={{0,4},{4,8},{8,12},{12,0},{1,5},{5,9},{9,13},{13,1},{2,6},{6,10},{... | collective-permute-start | bytes 393224 | tf_op jit(solution)/shard_map/ppermute | solution.py:107
  19.7 3.1 %collective-permute-start.1 = (bf16[16,512]{1,0:T(8,128)(2,1)S(1)}, bf16[16,512]{1,0:T(8,128)(2,1)S(1)}, u32[]{:S(2)}, u32[]{:S(2)}) collective-permute-start(bf16[16,512]{1,0:T(8,128)(2,1)S(1)} %get-tuple-element.31), channel_id=1, source_target_pairs={{0,16},{16,0},{1,17},{17,1},{2,18},{18,2},{3,19},{19,3},{4,20},{20... | collective-permute-start | bytes 49160 | tf_op jit(solution)/shard_map/ppermute | solution.py:305
  27.6 10.4 %collective-permute-start.4 = (bf16[32,512]{1,0:T(8,128)(2,1)S(1)}, bf16[32,512]{1,0:T(8,128)(2,1)S(1)}, u32[]{:S(2)}, u32[]{:S(2)}) collective-permute-start(bf16[32,512]{1,0:T(8,128)(2,1)S(1)} %get-tuple-element.23.own_ref), channel_id=1, source_target_pairs={{0,128},{16,400},{128,0},{144,272},{256,384},{272,144},{384,256},{... | collective-permute-start | bytes 98312 | tf_op jit(solution)/shard_map/ppermute | solution.py:328
  30.5 12.9 %collective-permute-start.3 = (bf16[160,512]{1,0:T(8,128)(2,1)S(1)}, bf16[160,512]{1,0:T(8,128)(2,1)S(1)}, u32[]{:S(2)}, u32[]{:S(2)}) collective-permute-start(bf16[160,512]{1,0:T(8,128)(2,1)S(1)} %get-tuple-element.22), channel_id=1, source_target_pairs={{0,32},{16,112},{32,0},{48,80},{64,96},{80,48},{96,64},{112,16},{1... | collective-permute-start | bytes 491528 | tf_op jit(solution)/shard_map/ppermute | solution.py:327
  38.0 5.3 %collective-permute-start.5 = (bf16[64,512]{1,0:T(8,128)(2,1)S(1)}, bf16[64,512]{1,0:T(8,128)(2,1)S(1)}, u32[]{:S(2)}, u32[]{:S(2)}) collective-permute-start(bf16[64,512]{1,0:T(8,128)(2,1)S(1)} %pad_maximum_fusion), channel_id=1, source_target_pairs={{0,384},{16,144},{128,256},{144,16},{256,128},{272,400},{384,0},{4... | collective-permute-start | bytes 196616 | tf_op jit(solution)/shard_map/ppermute | solution.py:329
  44.0 19.0 %collective-permute-start.6 = (bf16[192,512]{1,0:T(8,128)(2,1)S(1)}, bf16[192,512]{1,0:T(8,128)(2,1)S(1)}, u32[]{:S(2)}, u32[]{:S(2)}) collective-permute-start(bf16[192,512]{1,0:T(8,128)(2,1)S(1)} %get-tuple-element.25.sent_ref), channel_id=1, source_target_pairs={{0,96},{16,48},{32,64},{48,16},{64,32},{80,112},{96,0},{112,80},{1... | collective-permute-start | bytes 589832 | tf_op jit(solution)/shard_map/ppermute | solution.py:340
  51.7 7.4 %collective-permute-start.7 = (bf16[128,512]{1,0:T(8,128)(2,1)S(1)}, bf16[128,512]{1,0:T(8,128)(2,1)S(1)}, u32[]{:S(2)}, u32[]{:S(2)}) collective-permute-start(bf16[128,512]{1,0:T(8,128)(2,1)S(1)} %get-tuple-element.26), channel_id=1, source_target_pairs={{0,8},{4,12},{8,0},{12,4},{1,9},{5,13},{9,1},{13,5},{2,10},{6,14},... | collective-permute-start | bytes 393224 | tf_op jit(solution)/shard_map/ppermute | solution.py:107
  56.3 6.7 %collective-permute-start.8 = (bf16[128,512]{1,0:T(8,128)(2,1)S(1)}, bf16[128,512]{1,0:T(8,128)(2,1)S(1)}, u32[]{:S(2)}, u32[]{:S(2)}) collective-permute-start(bf16[128,512]{1,0:T(8,128)(2,1)S(1)} %get-tuple-element.26), channel_id=1, source_target_pairs={{0,12},{4,0},{8,4},{12,8},{1,13},{5,1},{9,5},{13,9},{2,14},{6,2},{... | collective-permute-start | bytes 393224 | tf_op jit(solution)/shard_map/ppermute | solution.py:107
  62.9 46.8 %copy-start.3 = (s32[16]{0:T(128)S(1)}, s32[16]{0:T(128)}, u32[]{:S(2)}) copy-start(s32[16]{0:T(128)} %owner_ref.1) | copy-start | bytes 196
  63.6 13.9 %all-to-all-start.1 = ((bf16[16,2,16,128]{3,2,1,0:T(8,128)(2,1)}), bf16[16,2,16,128]{3,2,1,0:T(8,128)(2,1)S(1)}, u32[]{:S(2)}, u32[]{:S(2)}) async-start(bf16[16,2,16,128]{3,2,1,0:T(8,128)(2,1)} %bitcast.10), calls=%async_computation.1 | async-start | bytes 262144 | tf_op jit(solution)/shard_map/all_to_all | solution.py:351
  67.4 9.2 %collective-permute-start.9 = (bf16[64,512]{1,0:T(8,128)(2,1)S(1)}, bf16[64,512]{1,0:T(8,128)(2,1)S(1)}, u32[]{:S(2)}, u32[]{:S(2)}) collective-permute-start(bf16[64,512]{1,0:T(8,128)(2,1)S(1)} %get-tuple-element.28), channel_id=1, source_target_pairs={{0,16},{16,0},{1,17},{17,1},{2,18},{18,2},{3,19},{19,3},{4,20},{20... | collective-permute-start | bytes 196616 | tf_op jit(solution)/shard_map/ppermute | solution.py:339
  104.5 5.2 %collective-permute-start.10 = (bf16[16,4,16,128]{3,2,1,0:T(8,128)(2,1)S(1)}, bf16[16,4,16,128]{3,2,1,0:T(8,128)(2,1)S(1)}, u32[]{:S(2)}, u32[]{:S(2)}) collective-permute-start(bf16[16,4,16,128]{3,2,1,0:T(8,128)(2,1)S(1)} %all_to_all.21), channel_id=1, source_target_pairs={{0,16},{16,0},{1,17},{17,1},{2,18},{18,2},{3,19},{19,3},{4,20},{20... | collective-permute-start | bytes 786440 | tf_op jit(solution)/shard_map/ppermute | solution.py:376
